TPU v7x, 32 devices: a whole 2x2x4 slice. The times are simulated.
32 devices in a mesh: seq: 8 (over z, x), tensor: 4 (over y, core).
Axes of the slice: x: 2, y: 2, z: 4, core: 2. Of those that a mesh axis runs over, the one named last changes fastest.
Arguments:
- hidden_in: bfloat16 [1024, 4096], P(('seq', 'tensor')), may hold values from -30 to 30
- prev_amax: float32 [], replicated, may hold values from 5 to 9
- w_x: bfloat16 [4096, 8192], P('seq', 'tensor'), may hold values from -0.09375 to 0.09375
- w_bc: bfloat16 [4096, 8, 2, 128], P('seq', 'tensor'), may hold values from -0.046875 to 0.046875
- w_dt: bfloat16 [4096, 128], P('seq', 'tensor'), may hold values from -0.09375 to 0.09375
- conv_x: float32 [4, 8192], P(None, 'tensor'), may hold values from -4 to 4
- conv_bc: float32 [4, 8, 2, 128], P(None, 'tensor'), may hold values from -4 to 4
- conv_state_x: bfloat16 [3, 8192], P(None, 'tensor'), may hold values from -6 to 6
- conv_state_bc: bfloat16 [3, 8, 2, 128], P(None, 'tensor'), may hold values from -3 to 3
- dt_bias: float32 [128], P('tensor'), may hold values from -2 to 1
- decay_rate: float32 [128], P('tensor'), may hold values from 9.765625e-05 to 0.12
- skip: float32 [128], P('tensor'), may hold values from 0.5 to 4
- init_state: float32 [128, 64, 128], P('tensor'), may hold values from -48 to 48
- norm_gain: float32 [8192], P('tensor'), may hold values from 0.1 to 1.9
- w_out: bfloat16 [8192, 4096], P('tensor', 'seq'), may hold values from -0.0625 to 0.0625
Outputs:
- layer_out: bfloat16 [1024, 4096], P(('seq', 'tensor'))
- abs_max: float32 [], replicated
All inputs are finite; a program needn't handle non-finite values.
Results may differ from a plain program's by a relative error of at most 0.019.
Values may be sent and summed in bfloat16 or wider, within the bound.
No kernel may reach another device: no remote copies, remote signals or barrier semaphores. Data moves between devices by JAX's collectives and lax.ppermute only.
A program may use at most 64 MiB of HBM per device.

v0:
```python
import functools

import jax
import jax.numpy as jnp
from jax import lax
from jax.experimental import pallas as pl
from jax.experimental.pallas import tpu as pltpu
from jax.sharding import PartitionSpec as P

HEADS = 128
HEAD_DIM = 64
STATE = 128
GROUPS = 8
KERNEL = 4
SPAN = 128


epsilon = 1e-05
quant_range = 448.0


def from_behind(value, axis, steps):
    count = lax.axis_size(axis)
    first, last = (max(0, -steps), min(count, count - steps))
    return lax.ppermute(value, axis, [(source, source + steps) for source in range(first, last)])


def carried_in(shard, axis, combine, identity):
    count, here = (lax.axis_size(axis), lax.axis_index(axis))
    everything = jax.tree.map(
        lambda part, kind: lax.all_gather(part.astype(kind), axis),
        shard,
        (jnp.bfloat16, jnp.bfloat16),
    )
    start = jax.tree.map(
        lambda part, zero: jnp.broadcast_to(jnp.asarray(zero, part.dtype), part.shape),
        shard,
        identity,
    )

    def turn(k, before):
        reached = k < here
        new = combine(
            before, jax.tree.map(lambda part, own: part[k].astype(own.dtype), everything, shard)
        )
        return jax.tree.map(lambda a, b: jnp.where(reached, a, b), new, before)

    return lax.fori_loop(0, count, turn, start)


def depthwise(before, projected, conv_taps, length):
    extended = jnp.concatenate([before, projected], axis=0)
    summed = conv_taps[0] * extended[0:length]
    for offset in range(1, KERNEL):
        summed = summed + conv_taps[offset] * extended[offset : offset + length]
    return jax.nn.silu(summed).astype(jnp.bfloat16)


def combine(earlier, later):
    return (earlier[0] * later[0], later[0][:, None, None] * earlier[1] + later[1])


def by_tokens(
    hidden_in,
    prev_amax,
    w_x,
    w_bc,
    w_dt,
    conv_x,
    conv_bc,
    conv_state_x,
    conv_state_bc,
    dt_bias,
    decay_rate,
    skip,
    init_state,
    norm_gain,
    w_out,
):
    margin = KERNEL - 1
    gathered = lax.all_gather(hidden_in, "tensor", axis=0, tiled=True)
    abs_max = lax.pmax(jnp.max(jnp.abs(gathered.astype(jnp.float32))), "seq")
    in_scale = prev_amax / quant_range
    leading = lax.axis_index("seq") == 0
    row_count = gathered.shape[0]
    bc_width = w_bc.shape[1] * w_bc.shape[2] * w_bc.shape[3]
    bc_rows = jnp.reshape(w_bc, (w_bc.shape[0], bc_width))
    scaled = gathered.astype(jnp.float32) * (quant_range / prev_amax)
    quant = jnp.clip(scaled, -quant_range, quant_range).astype(jnp.bfloat16)
    pieces = (
        lax.all_gather(w_x, "seq", axis=0, tiled=True),
        lax.all_gather(bc_rows, "seq", axis=0, tiled=True),
        lax.all_gather(w_dt, "seq", axis=0, tiled=True),
    )
    x_proj, bc_proj, dt_proj = tuple(
        (
            jnp.dot(quant, weight_piece, preferred_element_type=jnp.float32)
            for weight_piece in pieces
        )
    )
    x_whole = (x_proj * in_scale).astype(jnp.bfloat16)
    bc_whole = (bc_proj * in_scale).astype(jnp.bfloat16)
    dt_raw = dt_proj * in_scale
    state_bc = jnp.reshape(conv_state_bc, (margin, bc_width))
    received = from_behind(
        (x_whole[row_count - margin :], bc_whole[row_count - margin :]), "seq", 1
    )
    x_edge = jnp.where(leading, conv_state_x, received[0])
    bc_edge = jnp.where(leading, state_bc, received[1])
    x_act = depthwise(x_edge, x_whole, conv_x, row_count)
    bc_act = depthwise(bc_edge, bc_whole, jnp.reshape(conv_bc, (KERNEL, bc_width)), row_count)
    step_size = jax.nn.softplus(dt_raw + dt_bias)
    heads_here = step_size.shape[1]
    groups_here = w_bc.shape[1]
    per_group = HEADS // GROUPS
    blocks = row_count // SPAN
    x_blocks = x_act.reshape(blocks, SPAN, heads_here, HEAD_DIM)
    bc_blocks = bc_act.reshape(blocks, SPAN, groups_here, 2, STATE)
    in_map = bc_blocks[:, :, :, 0]
    out_map = bc_blocks[:, :, :, 1]
    step_blocks = step_size.reshape(blocks, SPAN, heads_here)
    cum_blocks = jnp.cumsum(-step_blocks * decay_rate, axis=1)
    index_row = jnp.arange(SPAN, dtype=jnp.int32)
    lower_mask = index_row[:, None] >= index_row[None, :]
    intersection = jnp.einsum(
        "ctgn,cugn->cgtu", out_map, in_map, preferred_element_type=jnp.float32
    )
    intersection = jnp.repeat(intersection, per_group, axis=1)
    cum_heads = jnp.transpose(cum_blocks, (0, 2, 1))
    log_gap = cum_heads[:, :, :, None] - cum_heads[:, :, None, :]
    decay = jnp.exp(jnp.where(lower_mask[None, None], log_gap, -1e30))
    step_heads = jnp.transpose(step_blocks, (0, 2, 1))
    weights = (intersection * decay * step_heads[:, :, None, :]).astype(jnp.bfloat16)
    local_part = jnp.einsum(
        "chtu,cuhp->cthp", weights, x_blocks, preferred_element_type=jnp.float32
    )
    last_cum = cum_blocks[:, SPAN - 1, :]
    x_weighted = (
        x_blocks.astype(jnp.float32)
        * (step_blocks * jnp.exp(last_cum[:, None, :] - cum_blocks))[:, :, :, None]
    ).astype(jnp.bfloat16)
    in_heads = jnp.repeat(in_map, per_group, axis=2)
    added = jnp.einsum("cuhp,cuhn->chpn", x_weighted, in_heads, preferred_element_type=jnp.float32)

    def carry_on(carried, element):
        block_decay, block_added = element
        return (block_decay[:, None, None] * carried + block_added, carried)

    empty_state = jnp.zeros((heads_here, HEAD_DIM, STATE), jnp.float32)
    device_state, entering = lax.scan(carry_on, empty_state, (jnp.exp(last_cum), added))
    device_decay = jnp.exp(jnp.sum(last_cum, axis=0))
    seeded = device_state + jnp.where(leading, device_decay[:, None, None] * init_state, 0.0)
    identity = (jnp.ones_like(device_decay), jnp.zeros_like(device_state))
    scanned = carried_in((device_decay, seeded), "seq", combine, identity)
    incoming = jnp.where(leading, init_state, scanned[1])
    prefix = jnp.exp(jnp.cumsum(last_cum, axis=0) - last_cum)
    states_in = entering + prefix[:, :, None, None] * incoming[None]
    out_heads = jnp.repeat(out_map, per_group, axis=2).astype(jnp.float32)
    carried_part = (
        jnp.einsum("cthn,chpn->cthp", out_heads, states_in, precision=lax.Precision.HIGHEST)
        * jnp.exp(cum_blocks)[:, :, :, None]
    )
    ssm_out = local_part + carried_part + skip[None, None, :, None] * x_blocks.astype(jnp.float32)
    ssm_out = ssm_out.reshape(row_count, heads_here * HEAD_DIM)
    squares = lax.psum(jnp.sum(ssm_out * ssm_out, axis=1), "tensor")
    mean_sq = squares / (HEADS * HEAD_DIM)
    normed = (ssm_out * lax.rsqrt(mean_sq + epsilon)[:, None] * norm_gain).astype(jnp.bfloat16)
    partial_out = jnp.dot(
        normed, lax.all_gather(w_out, "seq", axis=1, tiled=True), preferred_element_type=jnp.float32
    )
    layer_out = lax.psum_scatter(
        partial_out.astype(jnp.bfloat16), "tensor", scatter_dimension=0, tiled=True
    )
    return (layer_out, abs_max)


PAIR = 2
LINE = 4
ROWS = 8
SMEM = pl.BlockSpec(memory_space=pltpu.SMEM)
HIGHEST = lax.Precision.HIGHEST


def splits(mesh):
    count, ranks = (mesh.shape["seq"], mesh.shape["tensor"])
    heads_all, groups_here = (HEADS // ranks, GROUPS // ranks)
    if count != PAIR * LINE or groups_here != PAIR or ranks & (ranks - 1):
        return False
    heads_here = heads_all // count
    return 2 * heads_here == ROWS and heads_here * HEAD_DIM == 2 * SPAN


def nt_dot(a, b, **kw):
    return lax.dot_general(
        a, b, (((1,), (1,)), ((), ())), preferred_element_type=jnp.float32, **kw
    )


def project_kernel(ranks, place_ref, factor_ref, *refs):
    hidden = [refs[x * ranks : (x + 1) * ranks] for x in range(PAIR)]
    refs = refs[PAIR * ranks :]
    own_x, x_far, own_bc, other_bc, own_dt, other_dt = refs[:6]
    far_refs = refs[6 : 6 + LINE // 2]
    near_refs = refs[6 + LINE // 2 : 6 + LINE]
    sent_refs = refs[6 + LINE : 6 + LINE + LINE // 2]
    bc_ref, largest_ref, quant_ref, near_dt, all_dt = refs[6 + LINE + LINE // 2 :]
    side, z = (place_ref[1], place_ref[2])
    step = pl.program_id(0)
    factor = factor_ref[0]
    depth = own_x.shape[0]
    largest = None
    each = hidden[0][0].shape[0]
    for x in range(PAIR):
        for k in range(each):
            block = (k ^ (z % each)) * PAIR + (side ^ x)
            for j in range(ranks):
                for half in range(PAIR):
                    cut = slice(half * depth, (half + 1) * depth)
                    values = hidden[x][j][k, :, cut].astype(jnp.float32)
                    scaled = jnp.clip(values * factor, -quant_range, quant_range)
                    quant_ref[half, block, j] = scaled.astype(jnp.bfloat16)
                    top = jnp.max(jnp.abs(values).reshape(-1, ROWS, depth), axis=0)
                    largest = top if largest is None else jnp.maximum(largest, top)
    width = largest_ref.shape[1]
    top = largest[:, :width]
    for at in range(width, depth, width):
        top = jnp.maximum(top, largest[:, at : at + width])

    @pl.when(step == 0)
    def _():
        largest_ref[...] = top

    @pl.when(step > 0)
    def _():
        largest_ref[...] = jnp.maximum(largest_ref[...], top)

    rows = quant_ref.shape[1] * quant_ref.shape[2] * quant_ref.shape[3]
    near = quant_ref[side].reshape(rows, depth)
    far = quant_ref[1 - side].reshape(rows, depth)

    def both(own, other):
        return jnp.dot(near, own, preferred_element_type=jnp.float32) + jnp.dot(
            far, other, preferred_element_type=jnp.float32
        )

    at_rows = pl.ds(pl.multiple_of(step * rows, rows), rows)
    ours = nt_dot(own_dt[...], near)
    near_dt[...] = ours.reshape(near_dt.shape)
    all_dt[...] = (ours + nt_dot(other_dt[...], far)).reshape(all_dt.shape)
    channels = near_refs[0].shape[1]
    tokens = pl.num_programs(0) * rows
    extra = rows // channels * ROWS
    upper = lax.broadcasted_iota(jnp.int32, (ROWS, channels), 0) < ROWS // 2

    def steps_of(dt_ref, run):
        dt = dt_ref[run // 2]
        pieces = []
        for at in range(0, rows, channels):
            piece = dt[:, at : at + channels]
            turned = pltpu.roll(piece, ROWS // 2, 0)
            lower_run = jnp.where(upper, piece, turned)
            upper_run = jnp.where(upper, turned, piece)
            pieces.append(split_parts(jnp.where(run % 2 == 0, lower_run, upper_run), upper))
        return jnp.concatenate(pieces, axis=0).astype(jnp.bfloat16)

    extra_rows = pl.ds(pl.multiple_of(tokens + step * extra, 16), extra)

    def columns(run):
        return pl.ds(pl.multiple_of(run * channels, channels), channels)

    bc_ref[at_rows] = both(own_bc[...], other_bc[...]).astype(jnp.bfloat16)
    for m in range(LINE // 2):
        owner = z ^ (m + LINE // 2)
        run = side * LINE + owner
        other = x_far[:, columns(owner % (LINE // 2))]
        far_refs[m][at_rows] = both(own_x[:, columns(run)], other).astype(jnp.bfloat16)
        far_refs[m][extra_rows] = steps_of(all_dt, run)
        for out_refs, way in ((near_refs, side), (sent_refs, 1 - side)):
            run = way * LINE + (z ^ m)
            product = jnp.dot(near, own_x[:, columns(run)], preferred_element_type=jnp.float32)
            out_refs[m][at_rows] = product.astype(jnp.bfloat16)
            out_refs[m][extra_rows] = steps_of(near_dt, run)


def split_parts(values, upper):
    top = values.astype(jnp.bfloat16).astype(jnp.float32)
    return jnp.where(upper, top, values - top)


def project(place, factor, hidden, w_x, weights):
    line, own, wide = hidden[0].shape
    ranks = len(hidden) // PAIR
    depth, x_wide = (weights[0].shape[0], 2 * weights[0].shape[1])
    channels, maps_wide = (x_wide // LINE, weights[1].shape[1])
    steps = 2
    each = line // steps
    tokens = line * PAIR * ranks * own
    extra = tokens // channels * ROWS

    def fixed(array):
        return pl.BlockSpec(array.shape, lambda i, p: (0,) * array.ndim)

    dt_shape = (weights[-1].shape[0] // ROWS, ROWS, tokens // steps)
    payload = jax.ShapeDtypeStruct((tokens + extra, channels), jnp.bfloat16)
    maps = jax.ShapeDtypeStruct((tokens, maps_wide), jnp.bfloat16)
    largest = jax.ShapeDtypeStruct((ROWS, 128), jnp.float32)
    outs = [payload] * (LINE + LINE // 2) + [maps, largest]
    rows_of = pl.BlockSpec((each, own, wide), lambda i, p: (i ^ (p[2] // each), 0, 0))
    return pl.pallas_call(
        functools.partial(project_kernel, ranks),
        grid_spec=pltpu.PrefetchScalarGridSpec(
            num_scalar_prefetch=1,
            grid=(steps,),
            in_specs=[SMEM]
            + [rows_of] * (PAIR * ranks)
            + [fixed(w) for w in (w_x, *weights)],
            out_specs=[fixed(out) for out in outs],
            scratch_shapes=[
                pltpu.VMEM((PAIR, each * PAIR, ranks, own, depth), jnp.bfloat16),
                pltpu.VMEM(dt_shape, jnp.float32),
                pltpu.VMEM(dt_shape, jnp.float32),
            ],
        ),
        out_shape=outs,
        compiler_params=pltpu.CompilerParams(vmem_limit_bytes=26 * 2**20),
        cost_estimate=pl.CostEstimate(
            flops=2 * tokens * wide * (x_wide + maps_wide),
            bytes_accessed=2 * tokens * (wide + x_wide),
            transcendentals=0,
        ),
        name="project",
    )(place, factor, *hidden, w_x, *weights)


def onward_kernel(own_ref, received_ref, out_ref):
    rows, channels = own_ref.shape
    tokens = rows * channels // (channels + ROWS)
    total = own_ref[:tokens].astype(jnp.float32) + received_ref[:tokens].astype(jnp.float32)
    out_ref[:tokens] = total.astype(jnp.bfloat16)
    upper = lax.broadcasted_iota(jnp.int32, (ROWS, channels), 0) < ROWS // 2
    extra = own_ref[tokens:].astype(jnp.float32) + received_ref[tokens:].astype(jnp.float32)
    pieces = []
    for at in range(0, rows - tokens, ROWS):
        piece = extra[at : at + ROWS]
        pieces.append(split_parts(piece + pltpu.roll(piece, ROWS // 2, 0), upper))
    out_ref[tokens:] = jnp.concatenate(pieces, axis=0).astype(jnp.bfloat16)


def onward(own, received):
    whole = pl.BlockSpec(own.shape, lambda: (0, 0))
    return pl.pallas_call(
        onward_kernel,
        in_specs=[whole, whole],
        out_specs=whole,
        out_shape=jax.ShapeDtypeStruct(own.shape, own.dtype),
        compiler_params=pltpu.CompilerParams(vmem_limit_bytes=8 * 2**20),
        cost_estimate=pl.CostEstimate(
            flops=own.size, bytes_accessed=6 * own.size, transcendentals=0
        ),
        name="onward",
    )(own, received)


def turned_rank(rank, ranks):
    turned = 0
    while ranks > 1:
        turned, rank, ranks = (2 * turned + rank % 2, rank // 2, ranks // 2)
    return turned


def scan_kernel(place_ref, scale_ref, *refs):
    x_refs, bc_refs = (refs[:-9], refs[-9:-6])
    small_ref, largest_ref, state_ref, out_ref, x_buf, bc_buf = refs[-6:]
    tokens, channels = bc_refs[0].shape
    blocks = tokens // SPAN
    heads = channels // HEAD_DIM
    rank, z = (place_ref[0], place_ref[2])
    ranks = place_ref.shape[0] - 3
    own = SPAN // ranks
    edge = ROWS
    in_scale = scale_ref[0]
    at_end = (z == 0) | (z == LINE - 1)
    x_buf[:edge] = small_ref[:edge]
    bc_buf[:edge] = small_ref[edge : 2 * edge]
    state = state_ref[...].T

    for block in range(blocks):
        for true_rank in range(ranks):
            source = block * SPAN + (true_rank ^ rank) * own
            source = pl.ds(pl.multiple_of(source, own), own)
            at = edge + block * SPAN + true_rank * own
            at = slice(at, at + own)
            total = sum(ref[source].astype(jnp.float32) for ref in x_refs) * in_scale
            x_buf[at] = total.astype(jnp.bfloat16).astype(jnp.float32)
            near, far, done = (ref[source].astype(jnp.float32) for ref in bc_refs)
            total = ((near + far) * in_scale).astype(jnp.bfloat16).astype(jnp.float32)
            bc_buf[at] = jnp.where(at_end, done, total)

    taps = 2 * edge

    def activate(buf, row, block):
        start = edge - (KERNEL - 1) + block * SPAN
        summed = small_ref[row : row + 1] * buf[start : start + SPAN]
        for k in range(1, KERNEL):
            summed = summed + small_ref[row + k : row + k + 1] * buf[start + k : start + k + SPAN]
        return (summed / (1.0 + jnp.exp(-summed))).astype(jnp.bfloat16)

    skip = small_ref[taps + 2 * KERNEL : taps + 2 * KERNEL + 1]
    gain = small_ref[taps + 2 * KERNEL + 1 : taps + 2 * KERNEL + 2]
    bias = small_ref[4 * edge :, :SPAN]
    rate = small_ref[4 * edge :, SPAN:]

    up = lax.broadcasted_iota(jnp.int32, (SPAN, SPAN), 0)
    across = lax.broadcasted_iota(jnp.int32, (SPAN, SPAN), 1)
    lane = lax.broadcasted_iota(jnp.int32, (SPAN, channels), 1)
    lower = up >= across
    upper = (up <= across).astype(jnp.float32)
    lanes = across[:ROWS]

    dt = sum(ref[tokens:].astype(jnp.float32) for ref in x_refs)
    steps = []
    wide = channels // SPAN
    for block in range(blocks):
        tile = dt[block // wide * ROWS : (block // wide + 1) * ROWS]
        cut = tile[:, block % wide * SPAN : (block % wide + 1) * SPAN]
        cut = (cut + pltpu.roll(cut, ROWS // 2, 0)) * in_scale
        bit = 1
        while bit < ranks:
            shift = bit * own
            flipped = jnp.where(
                (lanes // shift) % 2 == 1,
                pltpu.roll(cut, shift, 1),
                pltpu.roll(cut, SPAN - shift, 1),
            )
            cut = jnp.where((rank & bit) != 0, flipped, cut)
            bit *= 2
        raw = cut + bias
        steps.append(jnp.maximum(raw, 0.0) + jnp.log1p(jnp.exp(-jnp.abs(raw))))
    drops = jnp.concatenate([-step * rate for step in steps], axis=0)
    cums = jnp.dot(drops, upper, precision=HIGHEST, preferred_element_type=jnp.float32)

    sums = jnp.zeros((SPAN, SPAN), jnp.float32)
    for block in range(blocks):
        x_act = activate(x_buf, taps, block)
        bc_act = activate(bc_buf, taps + KERNEL, block)
        in_map, out_map = (bc_act[:, :STATE], bc_act[:, STATE:])
        step, cum = (steps[block], cums[block * ROWS : (block + 1) * ROWS])
        last = cum[:, SPAN - 1 : SPAN]
        turned = jnp.concatenate(
            [
                cum,
                step * jnp.exp(last - cum),
                jnp.exp(cum),
                jnp.zeros((SPAN - 3 * ROWS, SPAN), jnp.float32),
            ],
            axis=0,
        ).T

        def spread(row):
            result = jnp.broadcast_to(turned[:, row : row + 1], (SPAN, channels))
            for h in range(1, heads):
                result = jnp.where(lane >= h * HEAD_DIM, turned[:, row + h : row + h + 1], result)
            return result

        inner = jnp.where(lower, nt_dot(out_map, in_map), 0.0)
        x_wide = x_act.astype(jnp.float32)
        weights, spaced = ([], [])
        for h in range(heads):
            gap = jnp.where(lower, turned[:, h : h + 1] - cum[h : h + 1], 0.0)
            weights.append((inner * jnp.exp(gap) * step[h : h + 1]).astype(jnp.bfloat16))
            inside = (lane >= h * HEAD_DIM) & (lane < (h + 1) * HEAD_DIM)
            spaced.append(jnp.where(inside, x_wide, 0.0).astype(jnp.bfloat16))
        local_part = jnp.dot(
            jnp.concatenate(weights, axis=1),
            jnp.concatenate(spaced, axis=0),
            preferred_element_type=jnp.float32,
        )
        grown = spread(2 * ROWS)
        x_weighted = (x_wide * spread(ROWS)).astype(jnp.bfloat16)
        added = lax.dot_general(
            in_map, x_weighted, (((0,), (0,)), ((), ())), preferred_element_type=jnp.float32
        )
        high = state.astype(jnp.bfloat16)
        rest = (state - high.astype(jnp.float32)).astype(jnp.bfloat16)
        carried = jnp.dot(
            jnp.concatenate([out_map, out_map], axis=1),
            jnp.concatenate([high, rest], axis=0),
            preferred_element_type=jnp.float32,
        )
        ssm_out = local_part + grown * carried + skip * x_wide
        state = grown[SPAN - 1 : SPAN] * state + added
        gained = (ssm_out * gain).astype(jnp.bfloat16)
        for true_rank in range(ranks):
            at = (turned_rank(true_rank, ranks) * blocks + block) * own
            out_ref[at : at + own] = gained[true_rank * own : (true_rank + 1) * own]
        summed = jnp.sum(ssm_out * ssm_out, axis=1, keepdims=True)
        sums = jnp.where(across == block, summed, sums)

    whole = sums.T[:ROWS]
    top = whole.astype(jnp.bfloat16).astype(jnp.float32)
    largest = jnp.broadcast_to(jnp.max(largest_ref[...]), (ROWS, channels))
    extra = jnp.concatenate([jnp.concatenate([top, whole - top], axis=1), largest], axis=0)
    out_ref[tokens:] = extra.astype(jnp.bfloat16)


def scan(place, in_scale, sums, maps, small, largest, state):
    channels = sums[0].shape[1]
    tokens = maps[0].shape[0]

    def fixed(array):
        return pl.BlockSpec(array.shape, lambda i, p: (0, 0))

    out = jax.ShapeDtypeStruct((tokens + 2 * ROWS, channels), jnp.bfloat16)
    return pl.pallas_call(
        scan_kernel,
        grid_spec=pltpu.PrefetchScalarGridSpec(
            num_scalar_prefetch=1,
            grid=(1,),
            in_specs=[SMEM]
            + [fixed(array) for array in (*sums, *maps, small, largest, state)],
            out_specs=fixed(out),
            scratch_shapes=[
                pltpu.VMEM((tokens + ROWS, channels), jnp.float32),
                pltpu.VMEM((tokens + ROWS, 2 * STATE), jnp.float32),
            ],
        ),
        out_shape=out,
        compiler_params=pltpu.CompilerParams(vmem_limit_bytes=20 * 2**20),
        cost_estimate=pl.CostEstimate(
            flops=8 * tokens * SPAN * channels,
            bytes_accessed=8 * tokens * channels,
            transcendentals=tokens * (channels + 8 * SPAN),
        ),
        name="scan",
    )(place, in_scale, *sums, *maps, small, largest, state)


def by_heads(
    hidden_in,
    prev_amax,
    w_x,
    w_bc,
    w_dt,
    conv_x,
    conv_bc,
    conv_state_x,
    conv_state_bc,
    dt_bias,
    decay_rate,
    skip,
    init_state,
    norm_gain,
    w_out,
):
    margin = KERNEL - 1
    count, here = (lax.axis_size("seq"), lax.axis_index("seq"))
    ranks, rank = (lax.axis_size("tensor"), lax.axis_index("tensor"))
    z, side = (here // PAIR, here % PAIR)
    place_of = side * LINE + z
    f32, bf16 = (jnp.float32, jnp.bfloat16)
    own, width = hidden_in.shape
    depth = w_x.shape[0]
    channels = w_x.shape[1] // count
    heads_here = w_dt.shape[1] // count
    in_scale = (prev_amax / quant_range).reshape(1)
    factor = (quant_range / prev_amax).reshape(1)
    place = jnp.stack([rank, side, z] + [rank] * ranks).astype(jnp.int32)

    def pick(array, axis, index):
        return lax.dynamic_index_in_dim(array, index, axis, keepdims=False)

    def along(value, pairs):
        moves = [(a * PAIR + x, b * PAIR + x) for a, b in pairs for x in range(PAIR)]
        return lax.ppermute(value, "seq", moves)

    def across(value):
        return lax.ppermute(value, "seq", [(s, s ^ 1) for s in range(count)])

    def of_heads(array):
        return jnp.repeat(array, HEAD_DIM)[None]

    by_channel = jnp.concatenate(
        [conv_state_x.astype(f32), conv_x, of_heads(skip), norm_gain[None]], axis=0
    )
    by_channel = lax.dynamic_slice_in_dim(by_channel, place_of * channels, channels, axis=1)
    by_map = jnp.concatenate([conv_state_bc.astype(f32), conv_bc], axis=0)
    by_map = pick(by_map, 1, side).reshape(margin + KERNEL, 2 * STATE)
    by_head = jnp.stack([dt_bias, decay_rate]).reshape(2, count, heads_here)
    by_head = jnp.tile(pick(by_head, 1, place_of).T, (ROWS // heads_here, 1))
    by_head = jnp.repeat(by_head, SPAN, axis=1)
    blank = jnp.zeros((ROWS - margin, channels), f32)
    small = jnp.concatenate(
        [
            blank,
            by_channel[:margin],
            blank,
            by_map[:margin],
            by_channel[margin : margin + KERNEL],
            by_map[margin:],
            by_channel[margin + KERNEL :],
            jnp.zeros((2 * ROWS - 2 * KERNEL - 2, channels), f32),
            by_head,
        ],
        axis=0,
    )

    start_state = lax.dynamic_slice_in_dim(
        init_state, place_of * heads_here, heads_here, axis=0
    ).reshape(channels, STATE)

    tie = lax.optimization_barrier
    half_run = LINE // 2 * channels
    opposite = (z // (LINE // 2)) ^ 1
    at = ((1 - side) * 2 + opposite) * half_run
    x_sent = lax.dynamic_slice_in_dim(w_x, at, half_run, axis=1)
    x_sent, hidden_in = tie((x_sent, hidden_in))
    x_far = across(x_sent)
    x_far, maps_sent, dt_sent = tie(
        (x_far, pick(w_bc, 1, 1 - side).reshape(depth, 2 * STATE), w_dt.T)
    )
    bc_other, dt_other = (across(maps_sent), across(dt_sent))
    bc_own = pick(w_bc, 1, side).reshape(depth, 2 * STATE)

    def line_columns(m):
        return lax.dynamic_slice_in_dim(hidden_in, (z ^ m) * PAIR * depth, PAIR * depth, axis=1)

    arrived = [line_columns(0)]
    for m in range(1, LINE):
        arrived.append(along(line_columns(m), [(s, s ^ m) for s in range(LINE)]))
    stacked = jnp.stack(arrived)
    beyond_pair = across(stacked)
    beyond_pair, small, start_state, bc_own, dt_sent = tie(
        (beyond_pair, small, start_state, bc_own, dt_sent)
    )
    rows = []
    for mine in (stacked, beyond_pair):
        ours = [mine]
        for j in range(1, ranks):
            bit = j & -j
            pairs = [(t, t ^ bit) for t in range(ranks)]
            ours.append(lax.ppermute(ours[j - bit], "tensor", pairs))
        rows.extend(ours)

    start, end = (0, LINE - 1)
    at_end = (z == start) | (z == end)
    next_start, next_end = (1, LINE - 2)
    inward = [(start, next_start), (end, next_end)]
    outward = [(next_start, start), (next_end, end)]
    middle = [(next_start, next_end), (next_end, next_start)]
    over_middle = [(next_start, end), (next_end, start)]
    beside_pairs = [(s, s ^ 1) for s in range(LINE)]
    weights = (x_far, bc_own, bc_other, dt_sent, dt_other)
    over, far, mine, near, mine_sent, near_sent, maps, largest = project(
        place, factor, rows, w_x, weights
    )

    map_hop = along(maps, inward)
    hop_far = along(far, inward)
    hop_over = along(over, inward)
    near = onward(near, across(near_sent))
    got_mine = across(mine_sent)
    near_out = along(near, outward)
    near_in = along(near, inward)
    map_sum = (maps.astype(f32) + map_hop.astype(f32)).astype(bf16)
    map_far = along(map_sum, middle)
    map_done = ((map_sum.astype(f32) + map_far.astype(f32)) * in_scale).astype(bf16)
    hop_far, near_out = tie((hop_far, near_out))
    sent_end = onward(over, hop_far)
    got_end = along(sent_end, over_middle)
    hop_over, unused = tie((hop_over, sent_end))
    got_next = along(onward(far, hop_over), middle)
    map_done, got_end, got_mine = tie((map_done, got_end, got_mine))
    map_done = along(map_done, outward)
    gained = scan(
        place,
        in_scale,
        [mine, got_mine, near_out, near_in, got_end, got_next],
        [map_sum, map_far, map_done],
        small,
        largest,
        start_state,
    )

    tokens = gained.shape[0] - 2 * ROWS
    beside = along(gained, beside_pairs)
    facing = along(gained, middle)
    second = jnp.where(at_end, along(facing, outward), facing)
    beyond = along(beside, middle)
    third = jnp.where(at_end, along(beyond, outward), beyond)
    far_own = across(gained)
    far_beside = across(beside)
    second, far_own = tie((second, far_own))
    far_second = across(second)
    third, far_beside = tie((third, far_beside))
    far_third = across(third)
    two, three = (jnp.where(at_end, 2, 3), jnp.where(at_end, 3, 2))

    def rows_for(x, m):
        at = ((side ^ x) * LINE + (z ^ m)) * channels
        return lax.dynamic_slice_in_dim(w_out, at, channels, axis=0)

    total = None
    tails = [far_third[tokens:]]
    for x, m, piece in (
        (0, 0, gained),
        (1, 0, far_own),
        (0, 1, beside),
        (1, 1, far_beside),
        (0, two, second),
        (1, two, far_second),
        (0, three, third),
    ):
        product = jnp.dot(piece, rows_for(x, m), preferred_element_type=f32)
        total = product if total is None else total + product
        tails.append(piece[tokens:])
    total, far_third = tie((total, far_third))
    last_rows = rows_for(1, three)
    tails = [tail.astype(f32) for tail in tails]
    squares = sum(tail[:ROWS, :SPAN] + tail[:ROWS, SPAN:] for tail in tails)
    top = functools.reduce(jnp.maximum, [tail[ROWS:, :SPAN] for tail in tails])

    def run_of(array, index, run):
        return lax.dynamic_slice_in_dim(array, index * run, run, axis=0)

    def first_sum(index):
        block, so_far = (run_of(far_third, index, run), run_of(total, index, run))
        return so_far + jnp.dot(block, last_rows, preferred_element_type=f32)

    run = tokens // 2
    keeps = rank % 2
    pairs = [(t, t ^ 1) for t in range(ranks)]
    received = lax.ppermute(first_sum(1 - keeps).astype(bf16), "tensor", pairs)
    kept = first_sum(keeps)
    squares = squares + lax.ppermute(squares, "tensor", pairs)
    bit = 2
    while bit < ranks:
        run //= 2
        keeps = (rank // bit) % 2
        pairs = [(t, t ^ bit) for t in range(ranks)]
        sent = run_of(kept, 1 - keeps, run) + run_of(received, 1 - keeps, run).astype(f32)
        kept = run_of(kept, keeps, run) + run_of(received, keeps, run).astype(f32)
        received = lax.ppermute(sent.astype(bf16), "tensor", pairs)
        squares = squares + lax.ppermute(squares, "tensor", pairs)
        bit *= 2
    mean_sq = squares.reshape(count, ranks, own) / (HEADS * HEAD_DIM)
    factors = lax.rsqrt(pick(mean_sq, 1, rank) + epsilon)
    final = (kept + received.astype(f32)).reshape(count, own, -1) * factors[:, :, None]
    final = lax.all_to_all(final.astype(bf16), "seq", split_axis=0, concat_axis=0, tiled=True)
    layer_out = final.transpose(1, 0, 2).reshape(own, count * final.shape[2])
    return (layer_out, jnp.max(top))


def solution(mesh):
    return jax.shard_map(
        by_heads if splits(mesh) else by_tokens,
        mesh=mesh,
        in_specs=(
            P(("seq", "tensor"), None),
            P(),
            P("seq", "tensor"),
            P("seq", "tensor", None, None),
            P("seq", "tensor"),
            P(None, "tensor"),
            P(None, "tensor", None, None),
            P(None, "tensor"),
            P(None, "tensor", None, None),
            P("tensor"),
            P("tensor"),
            P("tensor"),
            P("tensor", None, None),
            P("tensor"),
            P("tensor", "seq"),
        ),
        out_specs=(P(("seq", "tensor"), None), P()),
        check_vma=False,
    )
```

profile of v0, /device:TPU:0, one launch (start us, length us, event | category | flops | bytes accessed | tf_op | source)
XLA Modules:
  0.0 195.0 jit_solution(3982849622930200237)
XLA Ops:
  0.7 2.0 %constant_dynamic-slice_fusion.9 = bf16[512,512]{1,0:T(8,128)(2,1)} fusion(bf16[512,2048]{1,0:T(8,128)(2,1)} %refs_8_.1, s32[]{:T(128)S(6)} %select_n.123), kind=kLoop, calls=%fused_computation.63 | loop fusion | bytes 1048580 | tf_op jit(solution)/shard_map/dynamic_slice | solution.py:615
  2.7 2.9 %collective-permute-start.7 = (bf16[512,512]{1,0:T(8,128)(2,1)}, bf16[512,512]{1,0:T(8,128)(2,1)S(1)}, u32[]{:S(2)}, u32[]{:S(2)}) collective-permute-start(bf16[512,512]{1,0:T(8,128)(2,1)} %constant_dynamic-slice_fusion.9), channel_id=1, source_target_pairs={{0,4},{4,0},{8,12},{12,8},{16,20},{20,16},{24,28},{28,24},{1,5},{5... | collective-permute-start | bytes 1572872 | tf_op jit(solution)/shard_map/ppermute | solution.py:577
  5.7 1.6 dynamic-slice_bitcast_fusion
  7.3 1.6 collective-permute-start
  8.8 2.6 %collective-permute-start.1 = (bf16[32,1024]{1,0:T(8,128)(2,1)S(1)}, bf16[32,1024]{1,0:T(8,128)(2,1)}, u32[]{:S(2)}, u32[]{:S(2)}) collective-permute-start(bf16[32,1024]{1,0:T(8,128)(2,1)S(1)} %get-tuple-element.66), channel_id=1, source_target_pairs={{0,16},{4,20},{8,24},{12,28},{16,0},{20,4},{24,8},{28,12},{1,17},{... | collective-permute-start | bytes 196616 | tf_op jit(solution)/shard_map/ppermute | solution.py:574
  20.2 1.8 collective-permute-start.4
  22.0 3.9 %collective-permute-done.6.refs_4_ = bf16[4,32,1024]{2,1,0:T(8,128)(2,1)} collective-permute-done((bf16[4,32,1024]{2,1,0:T(8,128)(2,1)S(1)}, bf16[4,32,1024]{2,1,0:T(8,128)(2,1)}, u32[]{:S(2)}, u32[]{:S(2)}) %collective-permute-start.6) | collective-permute-done | bytes 262176 | tf_op jit(solution)/shard_map/ppermute | solution.py:577
  28.4 2.2 %collective-permute-start.11 = (bf16[512,256]{1,0:T(8,128)(2,1)}, bf16[512,256]{1,0:T(8,128)(2,1)}, u32[]{:S(2)}, u32[]{:S(2)}) collective-permute-start(bf16[512,256]{1,0:T(8,128)(2,1)} %bitcast.62), channel_id=1, source_target_pairs={{0,4},{4,0},{8,12},{12,8},{16,20},{20,16},{24,28},{28,24},{1,5},{5... | collective-permute-start | bytes 786440 | tf_op jit(solution)/shard_map/ppermute | solution.py:577
  30.6 2.3 %collective-permute-done.9.refs_6_ = bf16[4,32,1024]{2,1,0:T(8,128)(2,1)} collective-permute-done((bf16[4,32,1024]{2,1,0:T(8,128)(2,1)}, bf16[4,32,1024]{2,1,0:T(8,128)(2,1)}, u32[]{:S(2)}, u32[]{:S(2)}) %collective-permute-start.9) | collective-permute-done | bytes 262176 | tf_op jit(solution)/shard_map/ppermute | solution.py:641
  35.9 2.1 %collective-permute-done.12.refs_13_ = bf16[32,512]{1,0:T(8,128)(2,1)S(1)} collective-permute-done((bf16[32,512]{1,0:T(8,128)(2,1)S(1)}, bf16[32,512]{1,0:T(8,128)(2,1)S(1)}, u32[]{:S(2)}, u32[]{:S(2)}) %collective-permute-start.12) | collective-permute-done | bytes 32800 | tf_op jit(solution)/shard_map/ppermute | solution.py:577
  38.0 1.6 copy-done.10
  40.6 7.0 %project.1 = (bf16[1056,256]{1,0:T(8,128)(2,1)}, bf16[1056,256]{1,0:T(8,128)(2,1)S(1)}, bf16[1056,256]{1,0:T(8,128)(2,1)S(1)}, bf16[1056,256]{1,0:T(8,128)(2,1)S...) custom-call(s32[7]{0:T(128)S(1)} %stack.43.place_ref, ...), custom_call_target="tpu_custom_call" | custom-call | flops 2684354560 | bytes 4194304 | tf_op jit(solution)/shard_map/project/pallas_call | solution.py:309
  47.6 1.8 collective-permute-start.16
  49.4 2.8 %collective-permute-start.13 = (bf16[1024,256]{1,0:T(8,128)(2,1)S(1)}, bf16[1024,256]{1,0:T(8,128)(2,1)S(1)}, u32[]{:S(2)}, u32[]{:S(2)}) collective-permute-start(bf16[1024,256]{1,0:T(8,128)(2,1)S(1)} %get-tuple-element.41), channel_id=1, source_target_pairs={{0,8},{4,12},{24,16},{28,20},{1,9},{5,13},{25,17},{29,21},{2,10},{... | collective-permute-start | bytes 1572872 | tf_op jit(solution)/shard_map/ppermute | solution.py:574
  53.6 8.0 %collective-permute-done.16.received_ref = bf16[1056,256]{1,0:T(8,128)(2,1)S(1)} collective-permute-done((bf16[1056,256]{1,0:T(8,128)(2,1)S(1)}, bf16[1056,256]{1,0:T(8,128)(2,1)S(1)}, u32[]{:S(2)}, u32[]{:S(2)}) %collective-permute-start.16) | collective-permute-done | bytes 540704 | tf_op jit(solution)/shard_map/ppermute | solution.py:577
  63.0 5.4 %collective-permute-start.21 = (bf16[1056,256]{1,0:T(8,128)(2,1)}, bf16[1056,256]{1,0:T(8,128)(2,1)}, u32[]{:S(2)}, u32[]{:S(2)}) collective-permute-start(bf16[1056,256]{1,0:T(8,128)(2,1)} %get-tuple-element.42.own_ref), channel_id=1, source_target_pairs={{0,8},{4,12},{24,16},{28,20},{1,9},{5,13},{25,17},{29,21},{2,10},{... | collective-permute-start | bytes 1622024 | tf_op jit(solution)/shard_map/ppermute | solution.py:574
  69.3 1.6 collective-permute-start.19
  70.8 5.3 %collective-permute-done.15.received_ref = bf16[1056,256]{1,0:T(8,128)(2,1)S(1)} collective-permute-done((bf16[1056,256]{1,0:T(8,128)(2,1)S(1)}, bf16[1056,256]{1,0:T(8,128)(2,1)S(1)}, u32[]{:S(2)}, u32[]{:S(2)}) %collective-permute-start.15) | collective-permute-done | bytes 540704 | tf_op jit(solution)/shard_map/ppermute | solution.py:574
  76.6 2.2 %onward.4 = bf16[1056,256]{1,0:T(8,128)(2,1)} custom-call(bf16[1056,256]{1,0:T(8,128)(2,1)} %get-tuple-element.42.own_ref, bf16[1056,256]{1,0:T(8,128)(2,1)S(1)} %collective-permute-done.15.received_ref), custom_call_target="tpu_custom_call" | custom-call | flops 270336 | bytes 1622016 | tf_op jit(solution)/shard_map/onward/pallas_call | solution.py:351
  80.2 7.4 %collective-permute-start.20 = (bf16[1056,256]{1,0:T(8,128)(2,1)}, bf16[1056,256]{1,0:T(8,128)(2,1)S(1)}, u32[]{:S(2)}, u32[]{:S(2)}) collective-permute-start(bf16[1056,256]{1,0:T(8,128)(2,1)} %copy-done.5), channel_id=1, source_target_pairs={{0,8},{4,12},{24,16},{28,20},{1,9},{5,13},{25,17},{29,21},{2,10},{... | collective-permute-start | bytes 1622024 | tf_op jit(solution)/shard_map/ppermute | solution.py:574
  90.8 4.7 %collective-permute-done.18.refs_4_ = bf16[1056,256]{1,0:T(8,128)(2,1)} collective-permute-done((bf16[1056,256]{1,0:T(8,128)(2,1)}, bf16[1056,256]{1,0:T(8,128)(2,1)}, u32[]{:S(2)}, u32[]{:S(2)}) %collective-permute-start.18) | collective-permute-done | bytes 540704 | tf_op jit(solution)/shard_map/ppermute | solution.py:574
  97.4 9.6 %collective-permute-done.23.refs_8_ = bf16[1024,256]{1,0:T(8,128)(2,1)S(1)} collective-permute-done((bf16[1024,256]{1,0:T(8,128)(2,1)S(1)}, bf16[1024,256]{1,0:T(8,128)(2,1)S(1)}, u32[]{:S(2)}, u32[]{:S(2)}) %collective-permute-start.23) | collective-permute-done | bytes 524320 | tf_op jit(solution)/shard_map/ppermute | solution.py:574
  108.0 9.0 %scan.1 = bf16[1040,256]{1,0:T(8,128)(2,1)S(1)} custom-call(s32[7]{0:T(128)S(1)} %stack.43.place_ref, f32[1]{0:T(128)} %bitcast.3.scale_ref, bf16[1056,256]{1,0:T(8,128)(2,1)S(1)} %copy-done.7, bf16[1056,256]{1,0:T(8,128)(2,1)} %collective-permute-done.19.refs_1_, bf16[1056,256]{1,0:T(8,128)(2,1)S(1)} %copy-done.9, ...), custom_call_target="tpu_custom_call" | custom-call | flops 268435456 | bytes 2097152 | tf_op jit(solution)/shard_map/scan/pallas_call | solution.py:514
  118.5 2.7 %collective-permute-start.27 = (bf16[1040,256]{1,0:T(8,128)(2,1)S(1)}, bf16[1040,256]{1,0:T(8,128)(2,1)S(1)}, u32[]{:S(2)}, u32[]{:S(2)}) collective-permute-start(bf16[1040,256]{1,0:T(8,128)(2,1)S(1)} %scan.1), channel_id=1, source_target_pairs={{0,8},{4,12},{8,0},{12,4},{16,24},{20,28},{24,16},{28,20},{1,9},{5... | collective-permute-start | bytes 1597448 | tf_op jit(solution)/shard_map/ppermute | solution.py:574
  123.1 8.0 %collective-permute-done.27 = bf16[1040,256]{1,0:T(8,128)(2,1)S(1)} collective-permute-done((bf16[1040,256]{1,0:T(8,128)(2,1)S(1)}, bf16[1040,256]{1,0:T(8,128)(2,1)S(1)}, u32[]{:S(2)}, u32[]{:S(2)}) %collective-permute-start.27) | collective-permute-done | bytes 532512 | tf_op jit(solution)/shard_map/ppermute | solution.py:574
  133.0 8.4 %collective-permute-done.25 = bf16[1040,256]{1,0:T(8,128)(2,1)S(1)} collective-permute-done((bf16[1040,256]{1,0:T(8,128)(2,1)}, bf16[1040,256]{1,0:T(8,128)(2,1)S(1)}, u32[]{:S(2)}, u32[]{:S(2)}) %collective-permute-start.25) | collective-permute-done | bytes 532512 | tf_op jit(solution)/shard_map/ppermute | solution.py:574
  145.4 10.1 %collective-permute-done.29 = bf16[1040,256]{1,0:T(8,128)(2,1)S(1)} collective-permute-done((bf16[1040,256]{1,0:T(8,128)(2,1)S(1)}, bf16[1040,256]{1,0:T(8,128)(2,1)S(1)}, u32[]{:S(2)}, u32[]{:S(2)}) %collective-permute-start.29) | collective-permute-done | bytes 532512 | tf_op jit(solution)/shard_map/ppermute | solution.py:574
  157.9 7.8 %collective-permute-done.32 = bf16[1040,256]{1,0:T(8,128)(2,1)S(1)} collective-permute-done((bf16[1040,256]{1,0:T(8,128)(2,1)S(1)}, bf16[1040,256]{1,0:T(8,128)(2,1)S(1)}, u32[]{:S(2)}, u32[]{:S(2)}) %collective-permute-start.32) | collective-permute-done | bytes 532512 | tf_op jit(solution)/shard_map/ppermute | solution.py:577
  169.5 1.7 add_convert_fusion.2
  173.1 6.4 %collective-permute-done.34 = bf16[256,512]{1,0:T(8,128)(2,1)S(1)} collective-permute-done((bf16[256,512]{1,0:T(8,128)(2,1)}, bf16[256,512]{1,0:T(8,128)(2,1)S(1)}, u32[]{:S(2)}, u32[]{:S(2)}) %collective-permute-start.34) | collective-permute-done | bytes 262176 | tf_op jit(solution)/shard_map/ppermute | solution.py:742
  181.3 4.7 %all-to-all-start = ((bf16[8,32,512]{2,1,0:T(8,128)(2,1)}), bf16[8,32,512]{2,1,0:T(8,128)(2,1)S(1)}, u32[]{:S(2)}, u32[]{:S(2)}) async-start(bf16[8,32,512]{2,1,0:T(8,128)(2,1)} %multiply_convert_fusion.1), calls=%async_computation | async-start | bytes 524288 | tf_op jit(solution)/shard_map/all_to_all | solution.py:748
  186.6 7.6 %all-to-all-done = bf16[8,32,512]{2,1,0:T(8,128)(2,1)S(1)} async-done(((bf16[8,32,512]{2,1,0:T(8,128)(2,1)}), bf16[8,32,512]{2,1,0:T(8,128)(2,1)S(1)}, u32[]{:S(2)}, u32[]{:S(2)}) %all-to-all-start) | async-done | bytes 262176 | tf_op jit(solution)/shard_map/all_to_all | solution.py:748
  (140 shorter events, 46.1 us)
Async XLA Ops:
  2.7 19.3 %collective-permute-start.7 = (bf16[512,512]{1,0:T(8,128)(2,1)}, bf16[512,512]{1,0:T(8,128)(2,1)S(1)}, u32[]{:S(2)}, u32[]{:S(2)}) collective-permute-start(bf16[512,512]{1,0:T(8,128)(2,1)} %constant_dynamic-slice_fusion.9), channel_id=1, source_target_pairs={{0,4},{4,0},{8,12},{12,8},{16,20},{20,16},{24,28},{28,24},{1,5},{5... | collective-permute-start | bytes 1572872 | tf_op jit(solution)/shard_map/ppermute | solution.py:577
  7.3 10.6 %collective-permute-start = (bf16[32,1024]{1,0:T(8,128)(2,1)}, bf16[32,1024]{1,0:T(8,128)(2,1)S(1)}, u32[]{:S(2)}, u32[]{:S(2)}) collective-permute-start(bf16[32,1024]{1,0:T(8,128)(2,1)} %get-tuple-element.67), channel_id=1, source_target_pairs={{0,8},{4,12},{8,0},{12,4},{16,24},{20,28},{24,16},{28,20},{1,9},{5... | collective-permute-start | bytes 196616 | tf_op jit(solution)/shard_map/ppermute | solution.py:574
  8.8 9.0 %collective-permute-start.1 = (bf16[32,1024]{1,0:T(8,128)(2,1)S(1)}, bf16[32,1024]{1,0:T(8,128)(2,1)}, u32[]{:S(2)}, u32[]{:S(2)}) collective-permute-start(bf16[32,1024]{1,0:T(8,128)(2,1)S(1)} %get-tuple-element.66), channel_id=1, source_target_pairs={{0,16},{4,20},{8,24},{12,28},{16,0},{20,4},{24,8},{28,12},{1,17},{... | collective-permute-start | bytes 196616 | tf_op jit(solution)/shard_map/ppermute | solution.py:574
  11.4 6.4 %collective-permute-start.2 = (bf16[32,1024]{1,0:T(8,128)(2,1)S(1)}, bf16[32,1024]{1,0:T(8,128)(2,1)}, u32[]{:S(2)}, u32[]{:S(2)}) collective-permute-start(bf16[32,1024]{1,0:T(8,128)(2,1)S(1)} %get-tuple-element.65), channel_id=1, source_target_pairs={{0,24},{4,28},{8,16},{12,20},{16,8},{20,12},{24,0},{28,4},{1,25},{... | collective-permute-start | bytes 196616 | tf_op jit(solution)/shard_map/ppermute | solution.py:574
  18.8 7.2 %collective-permute-start.6 = (bf16[4,32,1024]{2,1,0:T(8,128)(2,1)S(1)}, bf16[4,32,1024]{2,1,0:T(8,128)(2,1)}, u32[]{:S(2)}, u32[]{:S(2)}) collective-permute-start(bf16[4,32,1024]{2,1,0:T(8,128)(2,1)S(1)} %pad_maximum_fusion.refs_0_), channel_id=1, source_target_pairs={{0,4},{4,0},{8,12},{12,8},{16,20},{20,16},{24,28},{28,24},{1,5},{5... | collective-permute-start | bytes 786440 | tf_op jit(solution)/shard_map/ppermute | solution.py:577
  20.2 7.7 %collective-permute-start.4 = (bf16[4,32,1024]{2,1,0:T(8,128)(2,1)S(1)}, bf16[4,32,1024]{2,1,0:T(8,128)(2,1)}, u32[]{:S(2)}, u32[]{:S(2)}) collective-permute-start(bf16[4,32,1024]{2,1,0:T(8,128)(2,1)S(1)} %pad_maximum_fusion.refs_0_), channel_id=1, source_target_pairs={{0,2},{1,3},{2,0},{3,1},{4,6},{5,7},{6,4},{7,5},{8,10},{9,11},{10,... | collective-permute-start | bytes 786440 | tf_op jit(solution)/shard_map/ppermute | solution.py:641
  25.9 7.0 %collective-permute-start.9 = (bf16[4,32,1024]{2,1,0:T(8,128)(2,1)}, bf16[4,32,1024]{2,1,0:T(8,128)(2,1)}, u32[]{:S(2)}, u32[]{:S(2)}) collective-permute-start(bf16[4,32,1024]{2,1,0:T(8,128)(2,1)} %collective-permute-done.6.refs_4_), channel_id=1, source_target_pairs={{0,2},{1,3},{2,0},{3,1},{4,6},{5,7},{6,4},{7,5},{8,10},{9,11},{10,... | collective-permute-start | bytes 786440 | tf_op jit(solution)/shard_map/ppermute | solution.py:641
  27.4 5.5 %collective-permute-start.3 = (bf16[4,32,1024]{2,1,0:T(8,128)(2,1)S(1)}, bf16[4,32,1024]{2,1,0:T(8,128)(2,1)S(1)}, u32[]{:S(2)}, u32[]{:S(2)}) collective-permute-start(bf16[4,32,1024]{2,1,0:T(8,128)(2,1)S(1)} %pad_maximum_fusion.refs_0_), channel_id=1, source_target_pairs={{0,1},{1,0},{2,3},{3,2},{4,5},{5,4},{6,7},{7,6},{8,9},{9,8},{10,11... | collective-permute-start | bytes 786440 | tf_op jit(solution)/shard_map/ppermute | solution.py:641
  27.9 10.1 %collective-permute-start.5 = (bf16[4,32,1024]{2,1,0:T(8,128)(2,1)}, bf16[4,32,1024]{2,1,0:T(8,128)(2,1)}, u32[]{:S(2)}, u32[]{:S(2)}) collective-permute-start(bf16[4,32,1024]{2,1,0:T(8,128)(2,1)} %collective-permute-done.4.refs_2_), channel_id=1, source_target_pairs={{0,1},{1,0},{2,3},{3,2},{4,5},{5,4},{6,7},{7,6},{8,9},{9,8},{10,11... | collective-permute-start | bytes 786440 | tf_op jit(solution)/shard_map/ppermute | solution.py:641
  28.0 10.1 %collective-permute-start.8 = (bf16[4,32,1024]{2,1,0:T(8,128)(2,1)}, bf16[4,32,1024]{2,1,0:T(8,128)(2,1)}, u32[]{:S(2)}, u32[]{:S(2)}) collective-permute-start(bf16[4,32,1024]{2,1,0:T(8,128)(2,1)} %collective-permute-done.6.refs_4_), channel_id=1, source_target_pairs={{0,1},{1,0},{2,3},{3,2},{4,5},{5,4},{6,7},{7,6},{8,9},{9,8},{10,11... | collective-permute-start | bytes 786440 | tf_op jit(solution)/shard_map/ppermute | solution.py:641
  28.4 9.6 %collective-permute-start.11 = (bf16[512,256]{1,0:T(8,128)(2,1)}, bf16[512,256]{1,0:T(8,128)(2,1)}, u32[]{:S(2)}, u32[]{:S(2)}) collective-permute-start(bf16[512,256]{1,0:T(8,128)(2,1)} %bitcast.62), channel_id=1, source_target_pairs={{0,4},{4,0},{8,12},{12,8},{16,20},{20,16},{24,28},{28,24},{1,5},{5... | collective-permute-start | bytes 786440 | tf_op jit(solution)/shard_map/ppermute | solution.py:577
  47.6 14.0 %collective-permute-start.16 = (bf16[1056,256]{1,0:T(8,128)(2,1)S(1)}, bf16[1056,256]{1,0:T(8,128)(2,1)S(1)}, u32[]{:S(2)}, u32[]{:S(2)}) collective-permute-start(bf16[1056,256]{1,0:T(8,128)(2,1)S(1)} %get-tuple-element.45), channel_id=1, source_target_pairs={{0,4},{4,0},{8,12},{12,8},{16,20},{20,16},{24,28},{28,24},{1,5},{5... | collective-permute-start | bytes 1622024 | tf_op jit(solution)/shard_map/ppermute | solution.py:577
  49.4 19.0 %collective-permute-start.13 = (bf16[1024,256]{1,0:T(8,128)(2,1)S(1)}, bf16[1024,256]{1,0:T(8,128)(2,1)S(1)}, u32[]{:S(2)}, u32[]{:S(2)}) collective-permute-start(bf16[1024,256]{1,0:T(8,128)(2,1)S(1)} %get-tuple-element.41), channel_id=1, source_target_pairs={{0,8},{4,12},{24,16},{28,20},{1,9},{5,13},{25,17},{29,21},{2,10},{... | collective-permute-start | bytes 1572872 | tf_op jit(solution)/shard_map/ppermute | solution.py:574
  52.2 23.9 %collective-permute-start.15 = (bf16[1056,256]{1,0:T(8,128)(2,1)S(1)}, bf16[1056,256]{1,0:T(8,128)(2,1)S(1)}, u32[]{:S(2)}, u32[]{:S(2)}) collective-permute-start(bf16[1056,256]{1,0:T(8,128)(2,1)S(1)} %get-tuple-element.43.own_ref), channel_id=1, source_target_pairs={{0,8},{4,12},{24,16},{28,20},{1,9},{5,13},{25,17},{29,21},{2,10},{... | collective-permute-start | bytes 1622024 | tf_op jit(solution)/shard_map/ppermute | solution.py:574
  61.7 14.9 %collective-permute-start.17 = (bf16[1056,256]{1,0:T(8,128)(2,1)S(1)}, bf16[1056,256]{1,0:T(8,128)(2,1)S(1)}, u32[]{:S(2)}, u32[]{:S(2)}) collective-permute-start(bf16[1056,256]{1,0:T(8,128)(2,1)S(1)} %onward.3), channel_id=1, source_target_pairs={{8,0},{12,4},{16,24},{20,28},{9,1},{13,5},{17,25},{21,29},{10,2},{... | collective-permute-start | bytes 1622024 | tf_op jit(solution)/shard_map/ppermute | solution.py:574
  63.0 24.5 %collective-permute-start.21 = (bf16[1056,256]{1,0:T(8,128)(2,1)}, bf16[1056,256]{1,0:T(8,128)(2,1)}, u32[]{:S(2)}, u32[]{:S(2)}) collective-permute-start(bf16[1056,256]{1,0:T(8,128)(2,1)} %get-tuple-element.42.own_ref), channel_id=1, source_target_pairs={{0,8},{4,12},{24,16},{28,20},{1,9},{5,13},{25,17},{29,21},{2,10},{... | collective-permute-start | bytes 1622024 | tf_op jit(solution)/shard_map/ppermute | solution.py:574
  68.6 22.0 %collective-permute-start.14 = (bf16[1024,256]{1,0:T(8,128)(2,1)S(1)}, bf16[1024,256]{1,0:T(8,128)(2,1)S(1)}, u32[]{:S(2)}, u32[]{:S(2)}) collective-permute-start(bf16[1024,256]{1,0:T(8,128)(2,1)S(1)} %add_convert_fusion.1.refs_6_), channel_id=1, source_target_pairs={{8,16},{12,20},{16,8},{20,12},{9,17},{13,21},{17,9},{21,13},{10,18... | collective-permute-start | bytes 1572872 | tf_op jit(solution)/shard_map/ppermute | solution.py:574
  69.3 21.5 %collective-permute-start.19 = (bf16[1056,256]{1,0:T(8,128)(2,1)}, bf16[1056,256]{1,0:T(8,128)(2,1)}, u32[]{:S(2)}, u32[]{:S(2)}) collective-permute-start(bf16[1056,256]{1,0:T(8,128)(2,1)} %get-tuple-element.47), channel_id=1, source_target_pairs={{0,4},{4,0},{8,12},{12,8},{16,20},{20,16},{24,28},{28,24},{1,5},{5... | collective-permute-start | bytes 1622024 | tf_op jit(solution)/shard_map/ppermute | solution.py:577
  78.9 16.7 %collective-permute-start.18 = (bf16[1056,256]{1,0:T(8,128)(2,1)}, bf16[1056,256]{1,0:T(8,128)(2,1)}, u32[]{:S(2)}, u32[]{:S(2)}) collective-permute-start(bf16[1056,256]{1,0:T(8,128)(2,1)} %onward.4), channel_id=1, source_target_pairs={{8,24},{12,28},{16,0},{20,4},{9,25},{13,29},{17,1},{21,5},{10,26},... | collective-permute-start | bytes 1622024 | tf_op jit(solution)/shard_map/ppermute | solution.py:574
  80.2 17.2 %collective-permute-start.20 = (bf16[1056,256]{1,0:T(8,128)(2,1)}, bf16[1056,256]{1,0:T(8,128)(2,1)S(1)}, u32[]{:S(2)}, u32[]{:S(2)}) collective-permute-start(bf16[1056,256]{1,0:T(8,128)(2,1)} %copy-done.5), channel_id=1, source_target_pairs={{0,8},{4,12},{24,16},{28,20},{1,9},{5,13},{25,17},{29,21},{2,10},{... | collective-permute-start | bytes 1622024 | tf_op jit(solution)/shard_map/ppermute | solution.py:574
  89.9 7.5 %collective-permute-start.22 = (bf16[1056,256]{1,0:T(8,128)(2,1)S(1)}, bf16[1056,256]{1,0:T(8,128)(2,1)S(1)}, u32[]{:S(2)}, u32[]{:S(2)}) collective-permute-start(bf16[1056,256]{1,0:T(8,128)(2,1)S(1)} %onward.5), channel_id=1, source_target_pairs={{8,16},{12,20},{16,8},{20,12},{9,17},{13,21},{17,9},{21,13},{10,18... | collective-permute-start | bytes 1622024 | tf_op jit(solution)/shard_map/ppermute | solution.py:574
  95.5 11.4 %collective-permute-start.23 = (bf16[1024,256]{1,0:T(8,128)(2,1)S(1)}, bf16[1024,256]{1,0:T(8,128)(2,1)S(1)}, u32[]{:S(2)}, u32[]{:S(2)}) collective-permute-start(bf16[1024,256]{1,0:T(8,128)(2,1)S(1)} %multiply_convert_fusion), channel_id=1, source_target_pairs={{8,0},{12,4},{16,24},{20,28},{9,1},{13,5},{17,25},{21,29},{10,2},{... | collective-permute-start | bytes 1572872 | tf_op jit(solution)/shard_map/ppermute | solution.py:574
  118.5 12.7 %collective-permute-start.27 = (bf16[1040,256]{1,0:T(8,128)(2,1)S(1)}, bf16[1040,256]{1,0:T(8,128)(2,1)S(1)}, u32[]{:S(2)}, u32[]{:S(2)}) collective-permute-start(bf16[1040,256]{1,0:T(8,128)(2,1)S(1)} %scan.1), channel_id=1, source_target_pairs={{0,8},{4,12},{8,0},{12,4},{16,24},{20,28},{24,16},{28,20},{1,9},{5... | collective-permute-start | bytes 1597448 | tf_op jit(solution)/shard_map/ppermute | solution.py:574
  121.2 20.2 %collective-permute-start.26 = (bf16[1040,256]{1,0:T(8,128)(2,1)S(1)}, bf16[1040,256]{1,0:T(8,128)(2,1)S(1)}, u32[]{:S(2)}, u32[]{:S(2)}) collective-permute-start(bf16[1040,256]{1,0:T(8,128)(2,1)S(1)} %scan.1), channel_id=1, source_target_pairs={{0,4},{4,0},{8,12},{12,8},{16,20},{20,16},{24,28},{28,24},{1,5},{5... | collective-permute-start | bytes 1597448 | tf_op jit(solution)/shard_map/ppermute | solution.py:577
  121.8 19.6 %collective-permute-start.25 = (bf16[1040,256]{1,0:T(8,128)(2,1)}, bf16[1040,256]{1,0:T(8,128)(2,1)S(1)}, u32[]{:S(2)}, u32[]{:S(2)}) collective-permute-start(bf16[1040,256]{1,0:T(8,128)(2,1)} %collective-permute-done.24), channel_id=1, source_target_pairs={{8,0},{12,4},{16,24},{20,28},{9,1},{13,5},{17,25},{21,29},{10,2},{... | collective-permute-start | bytes 1597448 | tf_op jit(solution)/shard_map/ppermute | solution.py:574
  131.1 12.1 %collective-permute-start.28 = (bf16[1040,256]{1,0:T(8,128)(2,1)S(1)}, bf16[1040,256]{1,0:T(8,128)(2,1)S(1)}, u32[]{:S(2)}, u32[]{:S(2)}) collective-permute-start(bf16[1040,256]{1,0:T(8,128)(2,1)S(1)} %collective-permute-done.27), channel_id=1, source_target_pairs={{8,16},{12,20},{16,8},{20,12},{9,17},{13,21},{17,9},{21,13},{10,18... | collective-permute-start | bytes 1597448 | tf_op jit(solution)/shard_map/ppermute | solution.py:574
  131.8 23.8 %collective-permute-start.30 = (bf16[1040,256]{1,0:T(8,128)(2,1)S(1)}, bf16[1040,256]{1,0:T(8,128)(2,1)S(1)}, u32[]{:S(2)}, u32[]{:S(2)}) collective-permute-start(bf16[1040,256]{1,0:T(8,128)(2,1)S(1)} %collective-permute-done.27), channel_id=1, source_target_pairs={{0,4},{4,0},{8,12},{12,8},{16,20},{20,16},{24,28},{28,24},{1,5},{5... | collective-permute-start | bytes 1597448 | tf_op jit(solution)/shard_map/ppermute | solution.py:577
  141.5 15.0 %collective-permute-start.31 = (bf16[1040,256]{1,0:T(8,128)(2,1)S(1)}, bf16[1040,256]{1,0:T(8,128)(2,1)S(1)}, u32[]{:S(2)}, u32[]{:S(2)}) collective-permute-start(bf16[1040,256]{1,0:T(8,128)(2,1)S(1)} %broadcast_select_fusion.1), channel_id=1, source_target_pairs={{0,4},{4,0},{8,12},{12,8},{16,20},{20,16},{24,28},{28,24},{1,5},{5... | collective-permute-start | bytes 1597448 | tf_op jit(solution)/shard_map/ppermute | solution.py:577
  143.2 12.3 %collective-permute-start.29 = (bf16[1040,256]{1,0:T(8,128)(2,1)S(1)}, bf16[1040,256]{1,0:T(8,128)(2,1)S(1)}, u32[]{:S(2)}, u32[]{:S(2)}) collective-permute-start(bf16[1040,256]{1,0:T(8,128)(2,1)S(1)} %collective-permute-done.28), channel_id=1, source_target_pairs={{8,0},{12,4},{16,24},{20,28},{9,1},{13,5},{17,25},{21,29},{10,2},{... | collective-permute-start | bytes 1597448 | tf_op jit(solution)/shard_map/ppermute | solution.py:574
  155.6 10.0 %collective-permute-start.32 = (bf16[1040,256]{1,0:T(8,128)(2,1)S(1)}, bf16[1040,256]{1,0:T(8,128)(2,1)S(1)}, u32[]{:S(2)}, u32[]{:S(2)}) collective-permute-start(bf16[1040,256]{1,0:T(8,128)(2,1)S(1)} %broadcast_select_fusion), channel_id=1, source_target_pairs={{0,4},{4,0},{8,12},{12,8},{16,20},{20,16},{24,28},{28,24},{1,5},{5... | collective-permute-start | bytes 1597448 | tf_op jit(solution)/shard_map/ppermute | solution.py:577
  171.2 8.3 %collective-permute-start.34 = (bf16[256,512]{1,0:T(8,128)(2,1)}, bf16[256,512]{1,0:T(8,128)(2,1)S(1)}, u32[]{:S(2)}, u32[]{:S(2)}) collective-permute-start(bf16[256,512]{1,0:T(8,128)(2,1)} %add_convert_fusion.2), channel_id=1, source_target_pairs={{0,2},{1,3},{2,0},{3,1},{4,6},{5,7},{6,4},{7,5},{8,10},{9,11},{10,... | collective-permute-start | bytes 786440 | tf_op jit(solution)/shard_map/ppermute | solution.py:742
  181.3 12.9 %all-to-all-start = ((bf16[8,32,512]{2,1,0:T(8,128)(2,1)}), bf16[8,32,512]{2,1,0:T(8,128)(2,1)S(1)}, u32[]{:S(2)}, u32[]{:S(2)}) async-start(bf16[8,32,512]{2,1,0:T(8,128)(2,1)} %multiply_convert_fusion.1), calls=%async_computation | async-start | bytes 524288 | tf_op jit(solution)/shard_map/all_to_all | solution.py:748
  (22 other events, 357.7 us)
where the time goes:
time: 196 us; the launch traced here: 195 us
  waiting for transfers between devices  86.8 us (44%)
  starting transfers between devices  59.2 us (30%)
  Pallas kernels  19.6 us (10%)
  local copies, waits for them, and re-layouts  14.8 us (8%)
  other arithmetic  9.05 us (5%)
  matrix products  3.66 us (2%)
    ppermute x17, waiting for transfers between devices, along(): return lax.ppermute(value, 'seq', moves)  47.1 us
    ppermute x17, starting transfers between devices, along(): return lax.ppermute(value, 'seq', moves)  34.2 us
    ppermute x10, waiting for transfers between devices, across(): return lax.ppermute(value, 'seq', [(s, s ^ 1) for s in range(count)])  21.8 us
    ppermute x10, starting transfers between devices, across(): return lax.ppermute(value, 'seq', [(s, s ^ 1) for s in range(count)])  13.9 us
    pallas_call x1, Pallas kernels, scan(): pl.pallas_call(scan_kernel, grid_spec=pltpu.PrefetchScalarGridSpec(num_sc...  8.96 us
    all_to_all x1, waiting for transfers between devices, by_heads(): lax.all_to_all(final.astype(bf16), 'seq', split_axis=0, concat_axis=0, ti...  7.62 us
    pallas_call x1, Pallas kernels, project(): pl.pallas_call(functools.partial(project_kernel, ranks), grid_spec=pltpu....  7.02 us
    ppermute x1, waiting for transfers between devices, by_heads(): received = lax.ppermute(sent.astype(bf16), 'tensor', pairs)  6.4 us
  transfers between devices with their start and end apart: 38, of which 17 were waited for; matrix products, arithmetic and copies ran while one was open for 9% of the time, Pallas kernels for 2%

commit v1 on v0

--- a/solution.py
+++ b/solution.py
@@ -177,7 +177,9 @@
 PAIR = 2
 LINE = 4
 ROWS = 8
+CUTS = 2
 SMEM = pl.BlockSpec(memory_space=pltpu.SMEM)
+VMEM = pl.BlockSpec(memory_space=pltpu.VMEM)
 HIGHEST = lax.Precision.HIGHEST
 
 
@@ -205,14 +207,12 @@
     sent_refs = refs[6 + LINE : 6 + LINE + LINE // 2]
     bc_ref, largest_ref, quant_ref, near_dt, all_dt = refs[6 + LINE + LINE // 2 :]
     side, z = (place_ref[1], place_ref[2])
-    step = pl.program_id(0)
     factor = factor_ref[0]
     depth = own_x.shape[0]
     largest = None
-    each = hidden[0][0].shape[0]
     for x in range(PAIR):
-        for k in range(each):
-            block = (k ^ (z % each)) * PAIR + (side ^ x)
+        for k in range(LINE):
+            block = (k ^ z) * PAIR + (side ^ x)
             for j in range(ranks):
                 for half in range(PAIR):
                     cut = slice(half * depth, (half + 1) * depth)
@@ -225,30 +225,12 @@
     top = largest[:, :width]
     for at in range(width, depth, width):
         top = jnp.maximum(top, largest[:, at : at + width])
-
-    @pl.when(step == 0)
-    def _():
-        largest_ref[...] = top
-
-    @pl.when(step > 0)
-    def _():
-        largest_ref[...] = jnp.maximum(largest_ref[...], top)
-
-    rows = quant_ref.shape[1] * quant_ref.shape[2] * quant_ref.shape[3]
-    near = quant_ref[side].reshape(rows, depth)
-    far = quant_ref[1 - side].reshape(rows, depth)
-
-    def both(own, other):
-        return jnp.dot(near, own, preferred_element_type=jnp.float32) + jnp.dot(
-            far, other, preferred_element_type=jnp.float32
-        )
-
-    at_rows = pl.ds(pl.multiple_of(step * rows, rows), rows)
-    ours = nt_dot(own_dt[...], near)
-    near_dt[...] = ours.reshape(near_dt.shape)
-    all_dt[...] = (ours + nt_dot(other_dt[...], far)).reshape(all_dt.shape)
+    largest_ref[...] = top
+
     channels = near_refs[0].shape[1]
-    tokens = pl.num_programs(0) * rows
+    tokens = bc_ref.shape[0]
+    rows = tokens // CUTS
+    blocks = quant_ref.shape[1] // CUTS
     extra = rows // channels * ROWS
     upper = lax.broadcasted_iota(jnp.int32, (ROWS, channels), 0) < ROWS // 2
 
@@ -263,23 +245,36 @@
             pieces.append(split_parts(jnp.where(run % 2 == 0, lower_run, upper_run), upper))
         return jnp.concatenate(pieces, axis=0).astype(jnp.bfloat16)
 
-    extra_rows = pl.ds(pl.multiple_of(tokens + step * extra, 16), extra)
-
     def columns(run):
         return pl.ds(pl.multiple_of(run * channels, channels), channels)
 
-    bc_ref[at_rows] = both(own_bc[...], other_bc[...]).astype(jnp.bfloat16)
-    for m in range(LINE // 2):
-        owner = z ^ (m + LINE // 2)
-        run = side * LINE + owner
-        other = x_far[:, columns(owner % (LINE // 2))]
-        far_refs[m][at_rows] = both(own_x[:, columns(run)], other).astype(jnp.bfloat16)
-        far_refs[m][extra_rows] = steps_of(all_dt, run)
-        for out_refs, way in ((near_refs, side), (sent_refs, 1 - side)):
-            run = way * LINE + (z ^ m)
-            product = jnp.dot(near, own_x[:, columns(run)], preferred_element_type=jnp.float32)
-            out_refs[m][at_rows] = product.astype(jnp.bfloat16)
-            out_refs[m][extra_rows] = steps_of(near_dt, run)
+    for cut in range(CUTS):
+        part = slice(cut * blocks, (cut + 1) * blocks)
+        near = quant_ref[side, part].reshape(rows, depth)
+        far = quant_ref[1 - side, part].reshape(rows, depth)
+
+        def both(own, other):
+            return jnp.dot(near, own, preferred_element_type=jnp.float32) + jnp.dot(
+                far, other, preferred_element_type=jnp.float32
+            )
+
+        at_rows = slice(cut * rows, (cut + 1) * rows)
+        extra_rows = slice(tokens + cut * extra, tokens + (cut + 1) * extra)
+        ours = nt_dot(own_dt[...], near)
+        near_dt[...] = ours.reshape(near_dt.shape)
+        all_dt[...] = (ours + nt_dot(other_dt[...], far)).reshape(all_dt.shape)
+        bc_ref[at_rows] = both(own_bc[...], other_bc[...]).astype(jnp.bfloat16)
+        for m in range(LINE // 2):
+            owner = z ^ (m + LINE // 2)
+            run = side * LINE + owner
+            other = x_far[:, columns(owner % (LINE // 2))]
+            far_refs[m][at_rows] = both(own_x[:, columns(run)], other).astype(jnp.bfloat16)
+            far_refs[m][extra_rows] = steps_of(all_dt, run)
+            for out_refs, way in ((near_refs, side), (sent_refs, 1 - side)):
+                run = way * LINE + (z ^ m)
+                product = jnp.dot(near, own_x[:, columns(run)], preferred_element_type=jnp.float32)
+                out_refs[m][at_rows] = product.astype(jnp.bfloat16)
+                out_refs[m][extra_rows] = steps_of(near_dt, run)
 
 
 def split_parts(values, upper):
@@ -292,37 +287,24 @@
     ranks = len(hidden) // PAIR
     depth, x_wide = (weights[0].shape[0], 2 * weights[0].shape[1])
     channels, maps_wide = (x_wide // LINE, weights[1].shape[1])
-    steps = 2
-    each = line // steps
     tokens = line * PAIR * ranks * own
     extra = tokens // channels * ROWS
-
-    def fixed(array):
-        return pl.BlockSpec(array.shape, lambda i, p: (0,) * array.ndim)
-
-    dt_shape = (weights[-1].shape[0] // ROWS, ROWS, tokens // steps)
+    dt_shape = (weights[-1].shape[0] // ROWS, ROWS, tokens // CUTS)
     payload = jax.ShapeDtypeStruct((tokens + extra, channels), jnp.bfloat16)
     maps = jax.ShapeDtypeStruct((tokens, maps_wide), jnp.bfloat16)
     largest = jax.ShapeDtypeStruct((ROWS, 128), jnp.float32)
     outs = [payload] * (LINE + LINE // 2) + [maps, largest]
-    rows_of = pl.BlockSpec((each, own, wide), lambda i, p: (i ^ (p[2] // each), 0, 0))
     return pl.pallas_call(
         functools.partial(project_kernel, ranks),
-        grid_spec=pltpu.PrefetchScalarGridSpec(
-            num_scalar_prefetch=1,
-            grid=(steps,),
-            in_specs=[SMEM]
-            + [rows_of] * (PAIR * ranks)
-            + [fixed(w) for w in (w_x, *weights)],
-            out_specs=[fixed(out) for out in outs],
-            scratch_shapes=[
-                pltpu.VMEM((PAIR, each * PAIR, ranks, own, depth), jnp.bfloat16),
-                pltpu.VMEM(dt_shape, jnp.float32),
-                pltpu.VMEM(dt_shape, jnp.float32),
-            ],
-        ),
+        in_specs=[SMEM, SMEM] + [VMEM] * (len(hidden) + 1 + len(weights)),
+        out_specs=[VMEM] * len(outs),
+        scratch_shapes=[
+            pltpu.VMEM((PAIR, line * PAIR, ranks, own, depth), jnp.bfloat16),
+            pltpu.VMEM(dt_shape, jnp.float32),
+            pltpu.VMEM(dt_shape, jnp.float32),
+        ],
         out_shape=outs,
-        compiler_params=pltpu.CompilerParams(vmem_limit_bytes=26 * 2**20),
+        compiler_params=pltpu.CompilerParams(vmem_limit_bytes=32 * 2**20),
         cost_estimate=pl.CostEstimate(
             flops=2 * tokens * wide * (x_wide + maps_wide),
             bytes_accessed=2 * tokens * (wide + x_wide),
@@ -347,11 +329,10 @@
 
 
 def onward(own, received):
-    whole = pl.BlockSpec(own.shape, lambda: (0, 0))
     return pl.pallas_call(
         onward_kernel,
-        in_specs=[whole, whole],
-        out_specs=whole,
+        in_specs=[VMEM, VMEM],
+        out_specs=VMEM,
         out_shape=jax.ShapeDtypeStruct(own.shape, own.dtype),
         compiler_params=pltpu.CompilerParams(vmem_limit_bytes=8 * 2**20),
         cost_estimate=pl.CostEstimate(
@@ -507,23 +488,15 @@
     channels = sums[0].shape[1]
     tokens = maps[0].shape[0]
 
-    def fixed(array):
-        return pl.BlockSpec(array.shape, lambda i, p: (0, 0))
-
     out = jax.ShapeDtypeStruct((tokens + 2 * ROWS, channels), jnp.bfloat16)
     return pl.pallas_call(
         scan_kernel,
-        grid_spec=pltpu.PrefetchScalarGridSpec(
-            num_scalar_prefetch=1,
-            grid=(1,),
-            in_specs=[SMEM]
-            + [fixed(array) for array in (*sums, *maps, small, largest, state)],
-            out_specs=fixed(out),
-            scratch_shapes=[
-                pltpu.VMEM((tokens + ROWS, channels), jnp.float32),
-                pltpu.VMEM((tokens + ROWS, 2 * STATE), jnp.float32),
-            ],
-        ),
+        in_specs=[SMEM, SMEM] + [VMEM] * (len(sums) + len(maps) + 3),
+        out_specs=VMEM,
+        scratch_shapes=[
+            pltpu.VMEM((tokens + ROWS, channels), jnp.float32),
+            pltpu.VMEM((tokens + ROWS, 2 * STATE), jnp.float32),
+        ],
         out_shape=out,
         compiler_params=pltpu.CompilerParams(vmem_limit_bytes=20 * 2**20),
         cost_estimate=pl.CostEstimate(
@@ -664,10 +637,9 @@
     map_sum = (maps.astype(f32) + map_hop.astype(f32)).astype(bf16)
     map_far = along(map_sum, middle)
     map_done = ((map_sum.astype(f32) + map_far.astype(f32)) * in_scale).astype(bf16)
-    hop_far, near_out = tie((hop_far, near_out))
     sent_end = onward(over, hop_far)
     got_end = along(sent_end, over_middle)
-    hop_over, unused = tie((hop_over, sent_end))
+    hop_over, near_out, unused = tie((hop_over, near_out, sent_end))
     got_next = along(onward(far, hop_over), middle)
     map_done, got_end, got_mine = tie((map_done, got_end, got_mine))
     map_done = along(map_done, outward)

time: 196 us -> 194 us (0.990)
  starting transfers between devices: 59.2 us -> 52.8 us
  waiting for transfers between devices: 86.8 us -> 91.8 us
    ppermute x17, starting transfers between devices: 34.2 us -> 27 us  [along(): return lax.ppermute(value, 'seq', moves)]
    ppermute x17, waiting for transfers between devices: 47.1 us -> 54 us  [along(): return lax.ppermute(value, 'seq', moves)]
    unnamed x38 -> x32, local copies, waits for them, and re-layouts: 6.14 us -> 6.93 us
  transfers between devices with their start and end apart: 38 -> 38, of which waited for: 17 -> 18; matrix products, arithmetic and copies ran while one was open for 9% -> 9% of each run, Pallas kernels for 2% -> 2%
where the time goes in v1:
time: 194 us; the launch traced here: 193 us
  waiting for transfers between devices  91.8 us (47%)
  starting transfers between devices  52.8 us (27%)
  Pallas kernels  18.5 us (10%)
  local copies, waits for them, and re-layouts  15.6 us (8%)
  other arithmetic  9.05 us (5%)
  matrix products  3.68 us (2%)
    ppermute x17, waiting for transfers between devices, along(): return lax.ppermute(value, 'seq', moves)  54 us
    ppermute x17, starting transfers between devices, along(): return lax.ppermute(value, 'seq', moves)  27 us
    ppermute x10, waiting for transfers between devices, across(): return lax.ppermute(value, 'seq', [(s, s ^ 1) for s in range(count)])  20 us
    ppermute x10, starting transfers between devices, across(): return lax.ppermute(value, 'seq', [(s, s ^ 1) for s in range(count)])  15.4 us
    pallas_call x1, Pallas kernels, scan(): pl.pallas_call(scan_kernel, in_specs=[SMEM, SMEM] + [VMEM] * (len(sums) +...  8.64 us
    all_to_all x1, waiting for transfers between devices, by_heads(): lax.all_to_all(final.astype(bf16), 'seq', split_axis=0, concat_axis=0, ti...  7.62 us
    unnamed x32, local copies, waits for them, and re-layouts  6.93 us
    ppermute x1, waiting for transfers between devices, by_heads(): received = lax.ppermute(sent.astype(bf16), 'tensor', pairs)  6.42 us
  transfers between devices with their start and end apart: 38, of which 18 were waited for; matrix products, arithmetic and copies ran while one was open for 9% of the time, Pallas kernels for 2%

profile of v1, /device:TPU:0, one launch (start us, length us, event | category | flops | bytes accessed | tf_op | source)
XLA Modules:
  0.0 193.2 jit_solution(14784716827201218207)
XLA Ops:
  0.7 2.0 %constant_dynamic-slice_fusion.9 = bf16[512,512]{1,0:T(8,128)(2,1)} fusion(bf16[512,2048]{1,0:T(8,128)(2,1)} %refs_8_.1, s32[]{:T(128)S(6)} %select_n.123), kind=kLoop, calls=%fused_computation.63 | loop fusion | bytes 1048580 | tf_op jit(solution)/shard_map/dynamic_slice | solution.py:588
  2.7 2.9 %collective-permute-start.7 = (bf16[512,512]{1,0:T(8,128)(2,1)}, bf16[512,512]{1,0:T(8,128)(2,1)S(1)}, u32[]{:S(2)}, u32[]{:S(2)}) collective-permute-start(bf16[512,512]{1,0:T(8,128)(2,1)} %constant_dynamic-slice_fusion.9), channel_id=1, source_target_pairs={{0,4},{4,0},{8,12},{12,8},{16,20},{20,16},{24,28},{28,24},{1,5},{5... | collective-permute-start | bytes 1572872 | tf_op jit(solution)/shard_map/ppermute | solution.py:550
  8.8 2.6 %collective-permute-start.1 = (bf16[32,1024]{1,0:T(8,128)(2,1)S(1)}, bf16[32,1024]{1,0:T(8,128)(2,1)}, u32[]{:S(2)}, u32[]{:S(2)}) collective-permute-start(bf16[32,1024]{1,0:T(8,128)(2,1)S(1)} %get-tuple-element.64), channel_id=1, source_target_pairs={{0,16},{4,20},{8,24},{12,28},{16,0},{20,4},{24,8},{28,12},{1,17},{... | collective-permute-start | bytes 196616 | tf_op jit(solution)/shard_map/ppermute | solution.py:547
  20.2 1.8 collective-permute-start.4
  22.0 3.9 %collective-permute-done.6.refs_4_ = bf16[4,32,1024]{2,1,0:T(8,128)(2,1)} collective-permute-done((bf16[4,32,1024]{2,1,0:T(8,128)(2,1)S(1)}, bf16[4,32,1024]{2,1,0:T(8,128)(2,1)}, u32[]{:S(2)}, u32[]{:S(2)}) %collective-permute-start.6) | collective-permute-done | bytes 262176 | tf_op jit(solution)/shard_map/ppermute | solution.py:550
  28.4 2.2 %collective-permute-start.11 = (bf16[512,256]{1,0:T(8,128)(2,1)}, bf16[512,256]{1,0:T(8,128)(2,1)}, u32[]{:S(2)}, u32[]{:S(2)}) collective-permute-start(bf16[512,256]{1,0:T(8,128)(2,1)} %bitcast.62), channel_id=1, source_target_pairs={{0,4},{4,0},{8,12},{12,8},{16,20},{20,16},{24,28},{28,24},{1,5},{5... | collective-permute-start | bytes 786440 | tf_op jit(solution)/shard_map/ppermute | solution.py:550
  30.6 2.3 %collective-permute-done.9.refs_6_ = bf16[4,32,1024]{2,1,0:T(8,128)(2,1)} collective-permute-done((bf16[4,32,1024]{2,1,0:T(8,128)(2,1)}, bf16[4,32,1024]{2,1,0:T(8,128)(2,1)}, u32[]{:S(2)}, u32[]{:S(2)}) %collective-permute-start.9) | collective-permute-done | bytes 262176 | tf_op jit(solution)/shard_map/ppermute | solution.py:614
  35.9 2.1 %collective-permute-done.12.refs_13_ = bf16[32,512]{1,0:T(8,128)(2,1)S(1)} collective-permute-done((bf16[32,512]{1,0:T(8,128)(2,1)S(1)}, bf16[32,512]{1,0:T(8,128)(2,1)S(1)}, u32[]{:S(2)}, u32[]{:S(2)}) %collective-permute-start.12) | collective-permute-done | bytes 32800 | tf_op jit(solution)/shard_map/ppermute | solution.py:550
  38.0 1.6 copy-done.7
  40.6 5.7 %project.1 = (bf16[1056,256]{1,0:T(8,128)(2,1)}, bf16[1056,256]{1,0:T(8,128)(2,1)S(1)}, bf16[1056,256]{1,0:T(8,128)(2,1)S(1)}, bf16[1056,256]{1,0:T(8,128)(2,1)S...) custom-call(s32[7]{0:T(128)S(1)} %stack.43.place_ref, ...), custom_call_target="tpu_custom_call" | custom-call | flops 2684354560 | bytes 4194304 | tf_op jit(solution)/shard_map/project/pallas_call | solution.py:297
  47.1 1.7 collective-permute-start.19
  48.8 2.8 %collective-permute-start.13 = (bf16[1024,256]{1,0:T(8,128)(2,1)S(1)}, bf16[1024,256]{1,0:T(8,128)(2,1)S(1)}, u32[]{:S(2)}, u32[]{:S(2)}) collective-permute-start(bf16[1024,256]{1,0:T(8,128)(2,1)S(1)} %get-tuple-element.40), channel_id=1, source_target_pairs={{0,8},{4,12},{24,16},{28,20},{1,9},{5,13},{25,17},{29,21},{2,10},{... | collective-permute-start | bytes 1572872 | tf_op jit(solution)/shard_map/ppermute | solution.py:547
  53.0 2.1 %collective-permute-start.18 = (bf16[1056,256]{1,0:T(8,128)(2,1)}, bf16[1056,256]{1,0:T(8,128)(2,1)}, u32[]{:S(2)}, u32[]{:S(2)}) collective-permute-start(bf16[1056,256]{1,0:T(8,128)(2,1)} %get-tuple-element.41.own_ref), channel_id=1, source_target_pairs={{0,8},{4,12},{24,16},{28,20},{1,9},{5,13},{25,17},{29,21},{2,10},{... | collective-permute-start | bytes 1622024 | tf_op jit(solution)/shard_map/ppermute | solution.py:547
  55.1 5.9 %collective-permute-done.19.received_ref = bf16[1056,256]{1,0:T(8,128)(2,1)S(1)} collective-permute-done((bf16[1056,256]{1,0:T(8,128)(2,1)S(1)}, bf16[1056,256]{1,0:T(8,128)(2,1)S(1)}, u32[]{:S(2)}, u32[]{:S(2)}) %collective-permute-start.19) | collective-permute-done | bytes 540704 | tf_op jit(solution)/shard_map/ppermute | solution.py:550
  65.6 10.0 %collective-permute-done.15.received_ref = bf16[1056,256]{1,0:T(8,128)(2,1)S(1)} collective-permute-done((bf16[1056,256]{1,0:T(8,128)(2,1)S(1)}, bf16[1056,256]{1,0:T(8,128)(2,1)S(1)}, u32[]{:S(2)}, u32[]{:S(2)}) %collective-permute-start.15) | collective-permute-done | bytes 540704 | tf_op jit(solution)/shard_map/ppermute | solution.py:547
  75.6 2.0 %onward.3 = bf16[1056,256]{1,0:T(8,128)(2,1)} custom-call(bf16[1056,256]{1,0:T(8,128)(2,1)} %get-tuple-element.41.own_ref, bf16[1056,256]{1,0:T(8,128)(2,1)S(1)} %collective-permute-done.15.received_ref), custom_call_target="tpu_custom_call" | custom-call | flops 270336 | bytes 1622016 | tf_op jit(solution)/shard_map/onward/pallas_call | solution.py:332
  78.8 6.4 %collective-permute-done.18.received_ref = bf16[1056,256]{1,0:T(8,128)(2,1)} collective-permute-done((bf16[1056,256]{1,0:T(8,128)(2,1)}, bf16[1056,256]{1,0:T(8,128)(2,1)}, u32[]{:S(2)}, u32[]{:S(2)}) %collective-permute-start.18) | collective-permute-done | bytes 540704 | tf_op jit(solution)/shard_map/ppermute | solution.py:547
  85.2 4.4 %collective-permute-start.21 = (bf16[1056,256]{1,0:T(8,128)(2,1)}, bf16[1056,256]{1,0:T(8,128)(2,1)S(1)}, u32[]{:S(2)}, u32[]{:S(2)}) collective-permute-start(bf16[1056,256]{1,0:T(8,128)(2,1)} %onward.4), channel_id=1, source_target_pairs={{0,8},{4,12},{24,16},{28,20},{1,9},{5,13},{25,17},{29,21},{2,10},{... | collective-permute-start | bytes 1622024 | tf_op jit(solution)/shard_map/ppermute | solution.py:547
  94.5 5.1 %collective-permute-done.21.refs_3_ = bf16[1056,256]{1,0:T(8,128)(2,1)S(1)} collective-permute-done((bf16[1056,256]{1,0:T(8,128)(2,1)}, bf16[1056,256]{1,0:T(8,128)(2,1)S(1)}, u32[]{:S(2)}, u32[]{:S(2)}) %collective-permute-start.21) | collective-permute-done | bytes 540704 | tf_op jit(solution)/shard_map/ppermute | solution.py:547
  99.6 6.7 %collective-permute-done.23.refs_8_ = bf16[1024,256]{1,0:T(8,128)(2,1)S(1)} collective-permute-done((bf16[1024,256]{1,0:T(8,128)(2,1)S(1)}, bf16[1024,256]{1,0:T(8,128)(2,1)S(1)}, u32[]{:S(2)}, u32[]{:S(2)}) %collective-permute-start.23) | collective-permute-done | bytes 524320 | tf_op jit(solution)/shard_map/ppermute | solution.py:547
  107.4 8.6 %scan.1 = bf16[1040,256]{1,0:T(8,128)(2,1)S(1)} custom-call(s32[7]{0:T(128)S(1)} %stack.43.place_ref, f32[1]{0:T(128)} %bitcast.3.scale_ref, bf16[1056,256]{1,0:T(8,128)(2,1)S(1)} %copy-done.6, bf16[1056,256]{1,0:T(8,128)(2,1)} %collective-permute-done.17.refs_1_, bf16[1056,256]{1,0:T(8,128)(2,1)} %collective-permute-done.20.refs_2_, ...), custom_call_target="tpu_custom_call" | custom-call | flops 268435456 | bytes 2097152 | tf_op jit(solution)/shard_map/scan/pallas_call | solution.py:492
  117.5 1.9 collective-permute-start.27
  121.9 7.7 %collective-permute-done.27 = bf16[1040,256]{1,0:T(8,128)(2,1)S(1)} collective-permute-done((bf16[1040,256]{1,0:T(8,128)(2,1)S(1)}, bf16[1040,256]{1,0:T(8,128)(2,1)S(1)}, u32[]{:S(2)}, u32[]{:S(2)}) %collective-permute-start.27) | collective-permute-done | bytes 532512 | tf_op jit(solution)/shard_map/ppermute | solution.py:547
  130.3 2.0 %collective-permute-start.30 = (bf16[1040,256]{1,0:T(8,128)(2,1)S(1)}, bf16[1040,256]{1,0:T(8,128)(2,1)S(1)}, u32[]{:S(2)}, u32[]{:S(2)}) collective-permute-start(bf16[1040,256]{1,0:T(8,128)(2,1)S(1)} %collective-permute-done.27), channel_id=1, source_target_pairs={{0,4},{4,0},{8,12},{12,8},{16,20},{20,16},{24,28},{28,24},{1,5},{5... | collective-permute-start | bytes 1597448 | tf_op jit(solution)/shard_map/ppermute | solution.py:550
  132.7 6.8 %collective-permute-done.25 = bf16[1040,256]{1,0:T(8,128)(2,1)S(1)} collective-permute-done((bf16[1040,256]{1,0:T(8,128)(2,1)}, bf16[1040,256]{1,0:T(8,128)(2,1)S(1)}, u32[]{:S(2)}, u32[]{:S(2)}) %collective-permute-start.25) | collective-permute-done | bytes 532512 | tf_op jit(solution)/shard_map/ppermute | solution.py:547
  139.6 2.2 %collective-permute-start.31 = (bf16[1040,256]{1,0:T(8,128)(2,1)S(1)}, bf16[1040,256]{1,0:T(8,128)(2,1)S(1)}, u32[]{:S(2)}, u32[]{:S(2)}) collective-permute-start(bf16[1040,256]{1,0:T(8,128)(2,1)S(1)} %broadcast_select_fusion.1), channel_id=1, source_target_pairs={{0,4},{4,0},{8,12},{12,8},{16,20},{20,16},{24,28},{28,24},{1,5},{5... | collective-permute-start | bytes 1597448 | tf_op jit(solution)/shard_map/ppermute | solution.py:550
  144.5 10.4 %collective-permute-done.29 = bf16[1040,256]{1,0:T(8,128)(2,1)S(1)} collective-permute-done((bf16[1040,256]{1,0:T(8,128)(2,1)S(1)}, bf16[1040,256]{1,0:T(8,128)(2,1)S(1)}, u32[]{:S(2)}, u32[]{:S(2)}) %collective-permute-start.29) | collective-permute-done | bytes 532512 | tf_op jit(solution)/shard_map/ppermute | solution.py:547
  156.6 8.1 %collective-permute-done.32 = bf16[1040,256]{1,0:T(8,128)(2,1)S(1)} collective-permute-done((bf16[1040,256]{1,0:T(8,128)(2,1)S(1)}, bf16[1040,256]{1,0:T(8,128)(2,1)S(1)}, u32[]{:S(2)}, u32[]{:S(2)}) %collective-permute-start.32) | collective-permute-done | bytes 532512 | tf_op jit(solution)/shard_map/ppermute | solution.py:550
  168.5 1.7 add_convert_fusion.2
  172.1 6.4 %collective-permute-done.34 = bf16[256,512]{1,0:T(8,128)(2,1)S(1)} collective-permute-done((bf16[256,512]{1,0:T(8,128)(2,1)}, bf16[256,512]{1,0:T(8,128)(2,1)S(1)}, u32[]{:S(2)}, u32[]{:S(2)}) %collective-permute-start.34) | collective-permute-done | bytes 262176 | tf_op jit(solution)/shard_map/ppermute | solution.py:714
  180.4 3.9 %all-to-all-start = ((bf16[8,32,512]{2,1,0:T(8,128)(2,1)}), bf16[8,32,512]{2,1,0:T(8,128)(2,1)S(1)}, u32[]{:S(2)}, u32[]{:S(2)}) async-start(bf16[8,32,512]{2,1,0:T(8,128)(2,1)} %multiply_convert_fusion.1), calls=%async_computation | async-start | bytes 524288 | tf_op jit(solution)/shard_map/all_to_all | solution.py:720
  184.9 7.6 %all-to-all-done = bf16[8,32,512]{2,1,0:T(8,128)(2,1)S(1)} async-done(((bf16[8,32,512]{2,1,0:T(8,128)(2,1)}), bf16[8,32,512]{2,1,0:T(8,128)(2,1)S(1)}, u32[]{:S(2)}, u32[]{:S(2)}) %all-to-all-start) | async-done | bytes 262176 | tf_op jit(solution)/shard_map/all_to_all | solution.py:720
  (134 shorter events, 50.0 us)
Async XLA Ops:
  2.7 19.3 %collective-permute-start.7 = (bf16[512,512]{1,0:T(8,128)(2,1)}, bf16[512,512]{1,0:T(8,128)(2,1)S(1)}, u32[]{:S(2)}, u32[]{:S(2)}) collective-permute-start(bf16[512,512]{1,0:T(8,128)(2,1)} %constant_dynamic-slice_fusion.9), channel_id=1, source_target_pairs={{0,4},{4,0},{8,12},{12,8},{16,20},{20,16},{24,28},{28,24},{1,5},{5... | collective-permute-start | bytes 1572872 | tf_op jit(solution)/shard_map/ppermute | solution.py:550
  7.3 10.6 %collective-permute-start = (bf16[32,1024]{1,0:T(8,128)(2,1)}, bf16[32,1024]{1,0:T(8,128)(2,1)S(1)}, u32[]{:S(2)}, u32[]{:S(2)}) collective-permute-start(bf16[32,1024]{1,0:T(8,128)(2,1)} %get-tuple-element.65), channel_id=1, source_target_pairs={{0,8},{4,12},{8,0},{12,4},{16,24},{20,28},{24,16},{28,20},{1,9},{5... | collective-permute-start | bytes 196616 | tf_op jit(solution)/shard_map/ppermute | solution.py:547
  8.8 9.0 %collective-permute-start.1 = (bf16[32,1024]{1,0:T(8,128)(2,1)S(1)}, bf16[32,1024]{1,0:T(8,128)(2,1)}, u32[]{:S(2)}, u32[]{:S(2)}) collective-permute-start(bf16[32,1024]{1,0:T(8,128)(2,1)S(1)} %get-tuple-element.64), channel_id=1, source_target_pairs={{0,16},{4,20},{8,24},{12,28},{16,0},{20,4},{24,8},{28,12},{1,17},{... | collective-permute-start | bytes 196616 | tf_op jit(solution)/shard_map/ppermute | solution.py:547
  11.4 6.4 %collective-permute-start.2 = (bf16[32,1024]{1,0:T(8,128)(2,1)S(1)}, bf16[32,1024]{1,0:T(8,128)(2,1)}, u32[]{:S(2)}, u32[]{:S(2)}) collective-permute-start(bf16[32,1024]{1,0:T(8,128)(2,1)S(1)} %get-tuple-element.63), channel_id=1, source_target_pairs={{0,24},{4,28},{8,16},{12,20},{16,8},{20,12},{24,0},{28,4},{1,25},{... | collective-permute-start | bytes 196616 | tf_op jit(solution)/shard_map/ppermute | solution.py:547
  18.8 7.2 %collective-permute-start.6 = (bf16[4,32,1024]{2,1,0:T(8,128)(2,1)S(1)}, bf16[4,32,1024]{2,1,0:T(8,128)(2,1)}, u32[]{:S(2)}, u32[]{:S(2)}) collective-permute-start(bf16[4,32,1024]{2,1,0:T(8,128)(2,1)S(1)} %pad_maximum_fusion.refs_0_), channel_id=1, source_target_pairs={{0,4},{4,0},{8,12},{12,8},{16,20},{20,16},{24,28},{28,24},{1,5},{5... | collective-permute-start | bytes 786440 | tf_op jit(solution)/shard_map/ppermute | solution.py:550
  20.2 7.7 %collective-permute-start.4 = (bf16[4,32,1024]{2,1,0:T(8,128)(2,1)S(1)}, bf16[4,32,1024]{2,1,0:T(8,128)(2,1)}, u32[]{:S(2)}, u32[]{:S(2)}) collective-permute-start(bf16[4,32,1024]{2,1,0:T(8,128)(2,1)S(1)} %pad_maximum_fusion.refs_0_), channel_id=1, source_target_pairs={{0,2},{1,3},{2,0},{3,1},{4,6},{5,7},{6,4},{7,5},{8,10},{9,11},{10,... | collective-permute-start | bytes 786440 | tf_op jit(solution)/shard_map/ppermute | solution.py:614
  25.9 7.0 %collective-permute-start.9 = (bf16[4,32,1024]{2,1,0:T(8,128)(2,1)}, bf16[4,32,1024]{2,1,0:T(8,128)(2,1)}, u32[]{:S(2)}, u32[]{:S(2)}) collective-permute-start(bf16[4,32,1024]{2,1,0:T(8,128)(2,1)} %collective-permute-done.6.refs_4_), channel_id=1, source_target_pairs={{0,2},{1,3},{2,0},{3,1},{4,6},{5,7},{6,4},{7,5},{8,10},{9,11},{10,... | collective-permute-start | bytes 786440 | tf_op jit(solution)/shard_map/ppermute | solution.py:614
  27.4 5.5 %collective-permute-start.3 = (bf16[4,32,1024]{2,1,0:T(8,128)(2,1)S(1)}, bf16[4,32,1024]{2,1,0:T(8,128)(2,1)S(1)}, u32[]{:S(2)}, u32[]{:S(2)}) collective-permute-start(bf16[4,32,1024]{2,1,0:T(8,128)(2,1)S(1)} %pad_maximum_fusion.refs_0_), channel_id=1, source_target_pairs={{0,1},{1,0},{2,3},{3,2},{4,5},{5,4},{6,7},{7,6},{8,9},{9,8},{10,11... | collective-permute-start | bytes 786440 | tf_op jit(solution)/shard_map/ppermute | solution.py:614
  27.9 10.1 %collective-permute-start.5 = (bf16[4,32,1024]{2,1,0:T(8,128)(2,1)}, bf16[4,32,1024]{2,1,0:T(8,128)(2,1)}, u32[]{:S(2)}, u32[]{:S(2)}) collective-permute-start(bf16[4,32,1024]{2,1,0:T(8,128)(2,1)} %collective-permute-done.4.refs_2_), channel_id=1, source_target_pairs={{0,1},{1,0},{2,3},{3,2},{4,5},{5,4},{6,7},{7,6},{8,9},{9,8},{10,11... | collective-permute-start | bytes 786440 | tf_op jit(solution)/shard_map/ppermute | solution.py:614
  28.0 10.1 %collective-permute-start.8 = (bf16[4,32,1024]{2,1,0:T(8,128)(2,1)}, bf16[4,32,1024]{2,1,0:T(8,128)(2,1)}, u32[]{:S(2)}, u32[]{:S(2)}) collective-permute-start(bf16[4,32,1024]{2,1,0:T(8,128)(2,1)} %collective-permute-done.6.refs_4_), channel_id=1, source_target_pairs={{0,1},{1,0},{2,3},{3,2},{4,5},{5,4},{6,7},{7,6},{8,9},{9,8},{10,11... | collective-permute-start | bytes 786440 | tf_op jit(solution)/shard_map/ppermute | solution.py:614
  28.4 9.6 %collective-permute-start.11 = (bf16[512,256]{1,0:T(8,128)(2,1)}, bf16[512,256]{1,0:T(8,128)(2,1)}, u32[]{:S(2)}, u32[]{:S(2)}) collective-permute-start(bf16[512,256]{1,0:T(8,128)(2,1)} %bitcast.62), channel_id=1, source_target_pairs={{0,4},{4,0},{8,12},{12,8},{16,20},{20,16},{24,28},{28,24},{1,5},{5... | collective-permute-start | bytes 786440 | tf_op jit(solution)/shard_map/ppermute | solution.py:550
  47.1 13.9 %collective-permute-start.19 = (bf16[1056,256]{1,0:T(8,128)(2,1)S(1)}, bf16[1056,256]{1,0:T(8,128)(2,1)S(1)}, u32[]{:S(2)}, u32[]{:S(2)}) collective-permute-start(bf16[1056,256]{1,0:T(8,128)(2,1)S(1)} %get-tuple-element.46), channel_id=1, source_target_pairs={{0,4},{4,0},{8,12},{12,8},{16,20},{20,16},{24,28},{28,24},{1,5},{5... | collective-permute-start | bytes 1622024 | tf_op jit(solution)/shard_map/ppermute | solution.py:550
  48.8 15.2 %collective-permute-start.13 = (bf16[1024,256]{1,0:T(8,128)(2,1)S(1)}, bf16[1024,256]{1,0:T(8,128)(2,1)S(1)}, u32[]{:S(2)}, u32[]{:S(2)}) collective-permute-start(bf16[1024,256]{1,0:T(8,128)(2,1)S(1)} %get-tuple-element.40), channel_id=1, source_target_pairs={{0,8},{4,12},{24,16},{28,20},{1,9},{5,13},{25,17},{29,21},{2,10},{... | collective-permute-start | bytes 1572872 | tf_op jit(solution)/shard_map/ppermute | solution.py:547
  51.7 23.9 %collective-permute-start.15 = (bf16[1056,256]{1,0:T(8,128)(2,1)S(1)}, bf16[1056,256]{1,0:T(8,128)(2,1)S(1)}, u32[]{:S(2)}, u32[]{:S(2)}) collective-permute-start(bf16[1056,256]{1,0:T(8,128)(2,1)S(1)} %get-tuple-element.42.own_ref), channel_id=1, source_target_pairs={{0,8},{4,12},{24,16},{28,20},{1,9},{5,13},{25,17},{29,21},{2,10},{... | collective-permute-start | bytes 1622024 | tf_op jit(solution)/shard_map/ppermute | solution.py:547
  53.0 32.2 %collective-permute-start.18 = (bf16[1056,256]{1,0:T(8,128)(2,1)}, bf16[1056,256]{1,0:T(8,128)(2,1)}, u32[]{:S(2)}, u32[]{:S(2)}) collective-permute-start(bf16[1056,256]{1,0:T(8,128)(2,1)} %get-tuple-element.41.own_ref), channel_id=1, source_target_pairs={{0,8},{4,12},{24,16},{28,20},{1,9},{5,13},{25,17},{29,21},{2,10},{... | collective-permute-start | bytes 1622024 | tf_op jit(solution)/shard_map/ppermute | solution.py:547
  61.9 27.7 %collective-permute-start.20 = (bf16[1056,256]{1,0:T(8,128)(2,1)}, bf16[1056,256]{1,0:T(8,128)(2,1)}, u32[]{:S(2)}, u32[]{:S(2)}) collective-permute-start(bf16[1056,256]{1,0:T(8,128)(2,1)} %onward.4), channel_id=1, source_target_pairs={{8,0},{12,4},{16,24},{20,28},{9,1},{13,5},{17,25},{21,29},{10,2},{... | collective-permute-start | bytes 1622024 | tf_op jit(solution)/shard_map/ppermute | solution.py:547
  64.1 28.5 %collective-permute-start.14 = (bf16[1024,256]{1,0:T(8,128)(2,1)S(1)}, bf16[1024,256]{1,0:T(8,128)(2,1)S(1)}, u32[]{:S(2)}, u32[]{:S(2)}) collective-permute-start(bf16[1024,256]{1,0:T(8,128)(2,1)S(1)} %add_convert_fusion.1.refs_6_), channel_id=1, source_target_pairs={{8,16},{12,20},{16,8},{20,12},{9,17},{13,21},{17,9},{21,13},{10,18... | collective-permute-start | bytes 1572872 | tf_op jit(solution)/shard_map/ppermute | solution.py:547
  64.8 28.0 %collective-permute-start.17 = (bf16[1056,256]{1,0:T(8,128)(2,1)}, bf16[1056,256]{1,0:T(8,128)(2,1)}, u32[]{:S(2)}, u32[]{:S(2)}) collective-permute-start(bf16[1056,256]{1,0:T(8,128)(2,1)} %get-tuple-element.43), channel_id=1, source_target_pairs={{0,4},{4,0},{8,12},{12,8},{16,20},{20,16},{24,28},{28,24},{1,5},{5... | collective-permute-start | bytes 1622024 | tf_op jit(solution)/shard_map/ppermute | solution.py:550
  77.6 15.5 %collective-permute-start.16 = (bf16[1056,256]{1,0:T(8,128)(2,1)}, bf16[1056,256]{1,0:T(8,128)(2,1)}, u32[]{:S(2)}, u32[]{:S(2)}) collective-permute-start(bf16[1056,256]{1,0:T(8,128)(2,1)} %onward.3), channel_id=1, source_target_pairs={{8,24},{12,28},{16,0},{20,4},{9,25},{13,29},{17,1},{21,5},{10,26},... | collective-permute-start | bytes 1622024 | tf_op jit(solution)/shard_map/ppermute | solution.py:547
  85.2 14.4 %collective-permute-start.21 = (bf16[1056,256]{1,0:T(8,128)(2,1)}, bf16[1056,256]{1,0:T(8,128)(2,1)S(1)}, u32[]{:S(2)}, u32[]{:S(2)}) collective-permute-start(bf16[1056,256]{1,0:T(8,128)(2,1)} %onward.4), channel_id=1, source_target_pairs={{0,8},{4,12},{24,16},{28,20},{1,9},{5,13},{25,17},{29,21},{2,10},{... | collective-permute-start | bytes 1622024 | tf_op jit(solution)/shard_map/ppermute | solution.py:547
  91.9 14.4 %collective-permute-start.22 = (bf16[1056,256]{1,0:T(8,128)(2,1)S(1)}, bf16[1056,256]{1,0:T(8,128)(2,1)S(1)}, u32[]{:S(2)}, u32[]{:S(2)}) collective-permute-start(bf16[1056,256]{1,0:T(8,128)(2,1)S(1)} %onward.5), channel_id=1, source_target_pairs={{8,16},{12,20},{16,8},{20,12},{9,17},{13,21},{17,9},{21,13},{10,18... | collective-permute-start | bytes 1622024 | tf_op jit(solution)/shard_map/ppermute | solution.py:547
  93.0 13.3 %collective-permute-start.23 = (bf16[1024,256]{1,0:T(8,128)(2,1)S(1)}, bf16[1024,256]{1,0:T(8,128)(2,1)S(1)}, u32[]{:S(2)}, u32[]{:S(2)}) collective-permute-start(bf16[1024,256]{1,0:T(8,128)(2,1)S(1)} %multiply_convert_fusion), channel_id=1, source_target_pairs={{8,0},{12,4},{16,24},{20,28},{9,1},{13,5},{17,25},{21,29},{10,2},{... | collective-permute-start | bytes 1572872 | tf_op jit(solution)/shard_map/ppermute | solution.py:547
  117.5 12.1 %collective-permute-start.27 = (bf16[1040,256]{1,0:T(8,128)(2,1)S(1)}, bf16[1040,256]{1,0:T(8,128)(2,1)S(1)}, u32[]{:S(2)}, u32[]{:S(2)}) collective-permute-start(bf16[1040,256]{1,0:T(8,128)(2,1)S(1)} %scan.1), channel_id=1, source_target_pairs={{0,8},{4,12},{8,0},{12,4},{16,24},{20,28},{24,16},{28,20},{1,9},{5... | collective-permute-start | bytes 1597448 | tf_op jit(solution)/shard_map/ppermute | solution.py:547
  119.3 20.3 %collective-permute-start.26 = (bf16[1040,256]{1,0:T(8,128)(2,1)S(1)}, bf16[1040,256]{1,0:T(8,128)(2,1)S(1)}, u32[]{:S(2)}, u32[]{:S(2)}) collective-permute-start(bf16[1040,256]{1,0:T(8,128)(2,1)S(1)} %scan.1), channel_id=1, source_target_pairs={{0,4},{4,0},{8,12},{12,8},{16,20},{20,16},{24,28},{28,24},{1,5},{5... | collective-permute-start | bytes 1597448 | tf_op jit(solution)/shard_map/ppermute | solution.py:550
  120.6 18.9 %collective-permute-start.25 = (bf16[1040,256]{1,0:T(8,128)(2,1)}, bf16[1040,256]{1,0:T(8,128)(2,1)S(1)}, u32[]{:S(2)}, u32[]{:S(2)}) collective-permute-start(bf16[1040,256]{1,0:T(8,128)(2,1)} %collective-permute-done.24), channel_id=1, source_target_pairs={{8,0},{12,4},{16,24},{20,28},{9,1},{13,5},{17,25},{21,29},{10,2},{... | collective-permute-start | bytes 1597448 | tf_op jit(solution)/shard_map/ppermute | solution.py:547
  129.6 12.6 %collective-permute-start.28 = (bf16[1040,256]{1,0:T(8,128)(2,1)S(1)}, bf16[1040,256]{1,0:T(8,128)(2,1)S(1)}, u32[]{:S(2)}, u32[]{:S(2)}) collective-permute-start(bf16[1040,256]{1,0:T(8,128)(2,1)S(1)} %collective-permute-done.27), channel_id=1, source_target_pairs={{8,16},{12,20},{16,8},{20,12},{9,17},{13,21},{17,9},{21,13},{10,18... | collective-permute-start | bytes 1597448 | tf_op jit(solution)/shard_map/ppermute | solution.py:547
  130.3 24.6 %collective-permute-start.30 = (bf16[1040,256]{1,0:T(8,128)(2,1)S(1)}, bf16[1040,256]{1,0:T(8,128)(2,1)S(1)}, u32[]{:S(2)}, u32[]{:S(2)}) collective-permute-start(bf16[1040,256]{1,0:T(8,128)(2,1)S(1)} %collective-permute-done.27), channel_id=1, source_target_pairs={{0,4},{4,0},{8,12},{12,8},{16,20},{20,16},{24,28},{28,24},{1,5},{5... | collective-permute-start | bytes 1597448 | tf_op jit(solution)/shard_map/ppermute | solution.py:550
  139.6 15.6 %collective-permute-start.31 = (bf16[1040,256]{1,0:T(8,128)(2,1)S(1)}, bf16[1040,256]{1,0:T(8,128)(2,1)S(1)}, u32[]{:S(2)}, u32[]{:S(2)}) collective-permute-start(bf16[1040,256]{1,0:T(8,128)(2,1)S(1)} %broadcast_select_fusion.1), channel_id=1, source_target_pairs={{0,4},{4,0},{8,12},{12,8},{16,20},{20,16},{24,28},{28,24},{1,5},{5... | collective-permute-start | bytes 1597448 | tf_op jit(solution)/shard_map/ppermute | solution.py:550
  142.2 12.6 %collective-permute-start.29 = (bf16[1040,256]{1,0:T(8,128)(2,1)S(1)}, bf16[1040,256]{1,0:T(8,128)(2,1)S(1)}, u32[]{:S(2)}, u32[]{:S(2)}) collective-permute-start(bf16[1040,256]{1,0:T(8,128)(2,1)S(1)} %collective-permute-done.28), channel_id=1, source_target_pairs={{8,0},{12,4},{16,24},{20,28},{9,1},{13,5},{17,25},{21,29},{10,2},{... | collective-permute-start | bytes 1597448 | tf_op jit(solution)/shard_map/ppermute | solution.py:547
  154.9 9.8 %collective-permute-start.32 = (bf16[1040,256]{1,0:T(8,128)(2,1)S(1)}, bf16[1040,256]{1,0:T(8,128)(2,1)S(1)}, u32[]{:S(2)}, u32[]{:S(2)}) collective-permute-start(bf16[1040,256]{1,0:T(8,128)(2,1)S(1)} %broadcast_select_fusion), channel_id=1, source_target_pairs={{0,4},{4,0},{8,12},{12,8},{16,20},{20,16},{24,28},{28,24},{1,5},{5... | collective-permute-start | bytes 1597448 | tf_op jit(solution)/shard_map/ppermute | solution.py:550
  170.3 8.3 %collective-permute-start.34 = (bf16[256,512]{1,0:T(8,128)(2,1)}, bf16[256,512]{1,0:T(8,128)(2,1)S(1)}, u32[]{:S(2)}, u32[]{:S(2)}) collective-permute-start(bf16[256,512]{1,0:T(8,128)(2,1)} %add_convert_fusion.2), channel_id=1, source_target_pairs={{0,2},{1,3},{2,0},{3,1},{4,6},{5,7},{6,4},{7,5},{8,10},{9,11},{10,... | collective-permute-start | bytes 786440 | tf_op jit(solution)/shard_map/ppermute | solution.py:714
  180.4 12.1 %all-to-all-start = ((bf16[8,32,512]{2,1,0:T(8,128)(2,1)}), bf16[8,32,512]{2,1,0:T(8,128)(2,1)S(1)}, u32[]{:S(2)}, u32[]{:S(2)}) async-start(bf16[8,32,512]{2,1,0:T(8,128)(2,1)} %multiply_convert_fusion.1), calls=%async_computation | async-start | bytes 524288 | tf_op jit(solution)/shard_map/all_to_all | solution.py:720
  (19 other events, 285.7 us)

commit v2 on v1

--- a/solution.py
+++ b/solution.py
@@ -180,6 +180,7 @@
 CUTS = 2
 SMEM = pl.BlockSpec(memory_space=pltpu.SMEM)
 VMEM = pl.BlockSpec(memory_space=pltpu.VMEM)
+HBM = pl.BlockSpec(memory_space=pltpu.HBM)
 HIGHEST = lax.Precision.HIGHEST
 
 
@@ -199,24 +200,39 @@
 
 
 def project_kernel(ranks, place_ref, factor_ref, *refs):
-    hidden = [refs[x * ranks : (x + 1) * ranks] for x in range(PAIR)]
+    hidden_in = [refs[x * ranks : (x + 1) * ranks] for x in range(PAIR)]
     refs = refs[PAIR * ranks :]
-    own_x, x_far, own_bc, other_bc, own_dt, other_dt = refs[:6]
-    far_refs = refs[6 : 6 + LINE // 2]
-    near_refs = refs[6 + LINE // 2 : 6 + LINE]
-    sent_refs = refs[6 + LINE : 6 + LINE + LINE // 2]
-    bc_ref, largest_ref, quant_ref, near_dt, all_dt = refs[6 + LINE + LINE // 2 :]
+    w_in, x_far, own_bc, other_bc, own_dt, other_dt = refs[:6]
+    far_refs = [refs[6 + m * CUTS : 6 + (m + 1) * CUTS] for m in range(LINE // 2)]
+    refs = refs[6 + CUTS * (LINE // 2) :]
+    near_refs, sent_refs = (refs[: LINE // 2], refs[LINE // 2 : LINE])
+    bc_ref, largest_ref, hidden_buf, own_x, quant_ref, near_dt, all_dt, arrived = refs[LINE:]
+    copies = [
+        [
+            pltpu.make_async_copy(
+                hidden_in[x][j], hidden_buf.at[x, j], arrived.at[x * ranks + j]
+            )
+            for j in range(ranks)
+        ]
+        for x in range(PAIR)
+    ]
+    own_copy = pltpu.make_async_copy(w_in, own_x, arrived.at[PAIR * ranks])
+    for row in copies:
+        for copy in row:
+            copy.start()
+    own_copy.start()
     side, z = (place_ref[1], place_ref[2])
     factor = factor_ref[0]
     depth = own_x.shape[0]
     largest = None
     for x in range(PAIR):
-        for k in range(LINE):
-            block = (k ^ z) * PAIR + (side ^ x)
-            for j in range(ranks):
+        for j in range(ranks):
+            copies[x][j].wait()
+            for k in range(LINE):
+                block = (k ^ z) * PAIR + (side ^ x)
                 for half in range(PAIR):
                     cut = slice(half * depth, (half + 1) * depth)
-                    values = hidden[x][j][k, :, cut].astype(jnp.float32)
+                    values = hidden_buf[x, j, k, :, cut].astype(jnp.float32)
                     scaled = jnp.clip(values * factor, -quant_range, quant_range)
                     quant_ref[half, block, j] = scaled.astype(jnp.bfloat16)
                     top = jnp.max(jnp.abs(values).reshape(-1, ROWS, depth), axis=0)
@@ -226,6 +242,7 @@
     for at in range(width, depth, width):
         top = jnp.maximum(top, largest[:, at : at + width])
     largest_ref[...] = top
+    own_copy.wait()
 
     channels = near_refs[0].shape[1]
     tokens = bc_ref.shape[0]
@@ -268,8 +285,9 @@
             owner = z ^ (m + LINE // 2)
             run = side * LINE + owner
             other = x_far[:, columns(owner % (LINE // 2))]
-            far_refs[m][at_rows] = both(own_x[:, columns(run)], other).astype(jnp.bfloat16)
-            far_refs[m][extra_rows] = steps_of(all_dt, run)
+            far_ref = far_refs[m][cut]
+            far_ref[:rows] = both(own_x[:, columns(run)], other).astype(jnp.bfloat16)
+            far_ref[rows:] = steps_of(all_dt, run)
             for out_refs, way in ((near_refs, side), (sent_refs, 1 - side)):
                 run = way * LINE + (z ^ m)
                 product = jnp.dot(near, own_x[:, columns(run)], preferred_element_type=jnp.float32)
@@ -293,15 +311,19 @@
     payload = jax.ShapeDtypeStruct((tokens + extra, channels), jnp.bfloat16)
     maps = jax.ShapeDtypeStruct((tokens, maps_wide), jnp.bfloat16)
     largest = jax.ShapeDtypeStruct((ROWS, 128), jnp.float32)
-    outs = [payload] * (LINE + LINE // 2) + [maps, largest]
+    run = jax.ShapeDtypeStruct(((tokens + extra) // CUTS, channels), jnp.bfloat16)
+    outs = [run] * (CUTS * (LINE // 2)) + [payload] * LINE + [maps, largest]
     return pl.pallas_call(
         functools.partial(project_kernel, ranks),
-        in_specs=[SMEM, SMEM] + [VMEM] * (len(hidden) + 1 + len(weights)),
+        in_specs=[SMEM, SMEM] + [HBM] * (len(hidden) + 1) + [VMEM] * len(weights),
         out_specs=[VMEM] * len(outs),
         scratch_shapes=[
+            pltpu.VMEM((PAIR, ranks, line, own, wide), jnp.bfloat16),
+            pltpu.VMEM(w_x.shape, w_x.dtype),
             pltpu.VMEM((PAIR, line * PAIR, ranks, own, depth), jnp.bfloat16),
             pltpu.VMEM(dt_shape, jnp.float32),
             pltpu.VMEM(dt_shape, jnp.float32),
+            pltpu.SemaphoreType.DMA((PAIR * ranks + 1,)),
         ],
         out_shape=outs,
         compiler_params=pltpu.CompilerParams(vmem_limit_bytes=32 * 2**20),
@@ -349,11 +371,12 @@
     return turned
 
 
-def scan_kernel(place_ref, scale_ref, *refs):
-    x_refs, bc_refs = (refs[:-9], refs[-9:-6])
+def scan_kernel(wholes, place_ref, scale_ref, *refs):
+    x_refs, run_refs, bc_refs = (refs[:wholes], refs[wholes:-9], refs[-9:-6])
     small_ref, largest_ref, state_ref, out_ref, x_buf, bc_buf = refs[-6:]
     tokens, channels = bc_refs[0].shape
     blocks = tokens // SPAN
+    run_blocks = blocks // CUTS
     heads = channels // HEAD_DIM
     rank, z = (place_ref[0], place_ref[2])
     ranks = place_ref.shape[0] - 3
@@ -367,11 +390,15 @@
 
     for block in range(blocks):
         for true_rank in range(ranks):
-            source = block * SPAN + (true_rank ^ rank) * own
-            source = pl.ds(pl.multiple_of(source, own), own)
+            turn = (true_rank ^ rank) * own
+            source = pl.ds(pl.multiple_of(block * SPAN + turn, own), own)
             at = edge + block * SPAN + true_rank * own
             at = slice(at, at + own)
-            total = sum(ref[source].astype(jnp.float32) for ref in x_refs) * in_scale
+            total = sum(ref[source].astype(jnp.float32) for ref in x_refs)
+            inside = pl.ds(pl.multiple_of(block % run_blocks * SPAN + turn, own), own)
+            for ref in run_refs[block // run_blocks :: CUTS]:
+                total = total + ref[inside].astype(jnp.float32)
+            total = total * in_scale
             x_buf[at] = total.astype(jnp.bfloat16).astype(jnp.float32)
             near, far, done = (ref[source].astype(jnp.float32) for ref in bc_refs)
             total = ((near + far) * in_scale).astype(jnp.bfloat16).astype(jnp.float32)
@@ -399,6 +426,11 @@
     lanes = across[:ROWS]
 
     dt = sum(ref[tokens:].astype(jnp.float32) for ref in x_refs)
+    run = tokens // CUTS
+    runs = [
+        sum(ref[run:].astype(jnp.float32) for ref in run_refs[cut::CUTS]) for cut in range(CUTS)
+    ]
+    dt = dt + jnp.concatenate(runs, axis=0)
     steps = []
     wide = channels // SPAN
     for block in range(blocks):
@@ -484,14 +516,14 @@
     out_ref[tokens:] = extra.astype(jnp.bfloat16)
 
 
-def scan(place, in_scale, sums, maps, small, largest, state):
+def scan(place, in_scale, sums, runs, maps, small, largest, state):
     channels = sums[0].shape[1]
     tokens = maps[0].shape[0]
 
     out = jax.ShapeDtypeStruct((tokens + 2 * ROWS, channels), jnp.bfloat16)
     return pl.pallas_call(
-        scan_kernel,
-        in_specs=[SMEM, SMEM] + [VMEM] * (len(sums) + len(maps) + 3),
+        functools.partial(scan_kernel, len(sums)),
+        in_specs=[SMEM, SMEM] + [VMEM] * (len(sums) + len(runs) + len(maps) + 3),
         out_specs=VMEM,
         scratch_shapes=[
             pltpu.VMEM((tokens + ROWS, channels), jnp.float32),
@@ -505,7 +537,7 @@
             transcendentals=tokens * (channels + 8 * SPAN),
         ),
         name="scan",
-    )(place, in_scale, *sums, *maps, small, largest, state)
+    )(place, in_scale, *sums, *runs, *maps, small, largest, state)
 
 
 def by_heads(
@@ -611,6 +643,8 @@
         for j in range(1, ranks):
             bit = j & -j
             pairs = [(t, t ^ bit) for t in range(ranks)]
+            if mine is beyond_pair and j == ranks - 1:
+                ours[j - bit], dt_other = tie((ours[j - bit], dt_other))
             ours.append(lax.ppermute(ours[j - bit], "tensor", pairs))
         rows.extend(ours)
 
@@ -623,30 +657,37 @@
     over_middle = [(next_start, end), (next_end, start)]
     beside_pairs = [(s, s ^ 1) for s in range(LINE)]
     weights = (x_far, bc_own, bc_other, dt_sent, dt_other)
-    over, far, mine, near, mine_sent, near_sent, maps, largest = project(
-        place, factor, rows, w_x, weights
-    )
+    shares = project(place, factor, rows, w_x, weights)
+    over, far = (shares[:CUTS], shares[CUTS : 2 * CUTS])
+    mine, near, mine_sent, near_sent, maps, largest = shares[2 * CUTS :]
 
     map_hop = along(maps, inward)
-    hop_far = along(far, inward)
-    hop_over = along(over, inward)
+    hops_far = [along(run, inward) for run in far]
+    hops_over = [along(run, inward) for run in over]
     near = onward(near, across(near_sent))
     got_mine = across(mine_sent)
     near_out = along(near, outward)
-    near_in = along(near, inward)
     map_sum = (maps.astype(f32) + map_hop.astype(f32)).astype(bf16)
     map_far = along(map_sum, middle)
     map_done = ((map_sum.astype(f32) + map_far.astype(f32)) * in_scale).astype(bf16)
-    sent_end = onward(over, hop_far)
-    got_end = along(sent_end, over_middle)
-    hop_over, near_out, unused = tie((hop_over, near_out, sent_end))
-    got_next = along(onward(far, hop_over), middle)
-    map_done, got_end, got_mine = tie((map_done, got_end, got_mine))
+    got_end, got_next = ([], [])
+    for own_run, hop in zip(over, hops_far):
+        value = onward(own_run, hop)
+        got_end.append(along(value, over_middle))
+    hops_over[0], near_out, unused = tie((hops_over[0], near_out, value))
+    for own_run, hop in zip(far, hops_over):
+        value = onward(own_run, hop)
+        got_next.append(along(value, middle))
+        if len(got_next) == 1:
+            near, unused = tie((near, value))
+            near_in = along(near, inward)
+    map_done, got_end[0], got_mine = tie((map_done, got_end[0], got_mine))
     map_done = along(map_done, outward)
     gained = scan(
         place,
         in_scale,
-        [mine, got_mine, near_out, near_in, got_end, got_next],
+        [mine, got_mine, near_out, near_in],
+        [*got_end, *got_next],
         [map_sum, map_far, map_done],
         small,
         largest,

time: 194 us -> 209 us (1.077)
  starting transfers between devices: 52.8 us -> 64.9 us
  local copies, waits for them, and re-layouts: 15.6 us -> 21.8 us
  waiting for transfers between devices: 91.8 us -> 86.6 us
    ppermute x17 -> x21, starting transfers between devices: 27 us -> 43.1 us  [along(): return lax.ppermute(value, 'seq', moves)]
    ppermute x17 -> x21, waiting for transfers between devices: 54 us -> 45.6 us  [along(): return lax.ppermute(value, 'seq', moves)]
    ppermute x10, starting transfers between devices: 15.4 us -> 11.3 us  [across(): return lax.ppermute(value, 'seq', [(s, s ^ 1) for s in range(count)])]
    unnamed x32 -> x52, local copies, waits for them, and re-layouts: 6.93 us -> 10.5 us
    concatenate x1, local copies, waits for them, and re-layouts: 0.08 us -> 3.7 us  [by_heads(): jnp.concatenate([blank, by_channel[:margin], blank, by_map[:margin], by_c...]
    ppermute x6, waiting for transfers between devices: 2.75 us -> 5.78 us  [by_heads(): ours.append(lax.ppermute(ours[j - bit], 'tensor', pairs))]
    pallas_call x3 -> x5, Pallas kernels: 4.15 us -> 4.83 us  [onward(): pl.pallas_call(onward_kernel, in_specs=[VMEM, VMEM], out_specs=VMEM, out_...]
  transfers between devices with their start and end apart: 38 -> 42, of which waited for: 18 -> 16; matrix products, arithmetic and copies ran while one was open for 9% -> 10% of each run, Pallas kernels for 2% -> 2%
where the time goes in v2:
time: 209 us; the launch traced here: 208 us
  waiting for transfers between devices  86.6 us (41%)
  starting transfers between devices  64.9 us (31%)
  local copies, waits for them, and re-layouts  21.8 us (10%)
  Pallas kernels  19.7 us (9%)
  other arithmetic  9.06 us (4%)
  matrix products  3.67 us (2%)
    ppermute x21, waiting for transfers between devices, along(): return lax.ppermute(value, 'seq', moves)  45.6 us
    ppermute x21, starting transfers between devices, along(): return lax.ppermute(value, 'seq', moves)  43.1 us
    ppermute x10, waiting for transfers between devices, across(): return lax.ppermute(value, 'seq', [(s, s ^ 1) for s in range(count)])  20.2 us
    ppermute x10, starting transfers between devices, across(): return lax.ppermute(value, 'seq', [(s, s ^ 1) for s in range(count)])  11.3 us
    unnamed x52, local copies, waits for them, and re-layouts  10.5 us
    pallas_call x1, Pallas kernels, scan(): pl.pallas_call(functools.partial(scan_kernel, len(sums)), in_specs=[SMEM,...  8.33 us
    all_to_all x1, waiting for transfers between devices, by_heads(): lax.all_to_all(final.astype(bf16), 'seq', split_axis=0, concat_axis=0, ti...  7.62 us
    pallas_call x1, Pallas kernels, project(): pl.pallas_call(functools.partial(project_kernel, ranks), in_specs=[SMEM,...  6.57 us
  transfers between devices with their start and end apart: 42, of which 16 were waited for; matrix products, arithmetic and copies ran while one was open for 10% of the time, Pallas kernels for 2%

profile of v2, /device:TPU:0, one launch (start us, length us, event | category | flops | bytes accessed | tf_op | source)
XLA Modules:
  0.0 207.8 jit_solution(17137934099088808289)
XLA Ops:
  0.7 2.0 constant_dynamic-slice_fusion.9
  2.8 2.9 %collective-permute-start.7 = (bf16[512,512]{1,0:T(8,128)(2,1)}, bf16[512,512]{1,0:T(8,128)(2,1)S(1)}, u32[]{:S(2)}, u32[]{:S(2)}) collective-permute-start(bf16[512,512]{1,0:T(8,128)(2,1)} %constant_dynamic-slice_fusion.9), channel_id=1, source_target_pairs={{0,4},{4,0},{8,12},{12,8},{16,20},{20,16},{24,28},{28,24},{1,5},{5... | collective-permute-start | bytes 1572872 | tf_op jit(solution)/shard_map/ppermute | solution.py:582
  6.7 1.6 collective-permute-start
  8.3 2.6 %collective-permute-start.1 = (bf16[32,1024]{1,0:T(8,128)(2,1)S(1)}, bf16[32,1024]{1,0:T(8,128)(2,1)}, u32[]{:S(2)}, u32[]{:S(2)}) collective-permute-start(bf16[32,1024]{1,0:T(8,128)(2,1)S(1)} %get-tuple-element.74), channel_id=1, source_target_pairs={{0,16},{4,20},{8,24},{12,28},{16,0},{20,4},{24,8},{28,12},{1,17},{... | collective-permute-start | bytes 196616 | tf_op jit(solution)/shard_map/ppermute | solution.py:579
  18.7 3.7 %concatenate.12.refs_11_ = f32[40,256]{1,0:T(8,128)} concatenate(f32[5,256]{1,0:T(8,128)S(1)} %broadcast_in_dim.16, f32[3,256]{1,0:T(4,128)S(1)} %slice.156, f32[5,256]{1,0:T(8,128)S(1)} %broadcast_in_dim.16, f32[3,256]{1,0:T(4,128)S(1)} %bitcast.66, f32[4,256]{1,0:T(4,128)S(1)} %slice.158, f32[4,256]{1,0:T(4,128)S(1)} %bitcast.67, f32[2,256]{1,0:T(2,128)} %slice.160, ...), dimensions={0} | concatenate | bytes 81920 | tf_op jit(solution)/shard_map/concatenate | solution.py:597
  23.3 1.6 collective-permute-start.4
  26.9 5.8 %collective-permute-done.4.refs_2_ = bf16[4,32,1024]{2,1,0:T(8,128)(2,1)} collective-permute-done((bf16[4,32,1024]{2,1,0:T(8,128)(2,1)S(1)}, bf16[4,32,1024]{2,1,0:T(8,128)(2,1)}, u32[]{:S(2)}, u32[]{:S(2)}) %collective-permute-start.4) | collective-permute-done | bytes 262176 | tf_op jit(solution)/shard_map/ppermute | solution.py:648
  36.8 6.2 %collective-permute-done.12.refs_11_ = bf16[512,256]{1,0:T(8,128)(2,1)} collective-permute-done((bf16[512,256]{1,0:T(8,128)(2,1)}, bf16[512,256]{1,0:T(8,128)(2,1)}, u32[]{:S(2)}, u32[]{:S(2)}) %collective-permute-start.12) | collective-permute-done | bytes 262176 | tf_op jit(solution)/shard_map/ppermute | solution.py:582
  43.1 1.6 copy-done.10
  47.1 6.6 %project.1 = (bf16[528,256]{1,0:T(8,128)(2,1)}, bf16[528,256]{1,0:T(8,128)(2,1)}, bf16[528,256]{1,0:T(8,128)(2,1)S(1)}, bf16[528,256]{1,0:T(8,128)(2,1)S(1)}, bf...) custom-call(s32[7]{0:T(128)S(1)} %stack.43.place_ref, ...), custom_call_target="tpu_custom_call" | custom-call | flops 2684354560 | bytes 4194304 | tf_op jit(solution)/shard_map/project/pallas_call | solution.py:316
  53.7 1.6 collective-permute-start.19
  55.3 2.4 %collective-permute-start.13 = (bf16[1024,256]{1,0:T(8,128)(2,1)S(1)}, bf16[1024,256]{1,0:T(8,128)(2,1)S(1)}, u32[]{:S(2)}, u32[]{:S(2)}) collective-permute-start(bf16[1024,256]{1,0:T(8,128)(2,1)S(1)} %get-tuple-element.47), channel_id=1, source_target_pairs={{0,8},{4,12},{24,16},{28,20},{1,9},{5,13},{25,17},{29,21},{2,10},{... | collective-permute-start | bytes 1572872 | tf_op jit(solution)/shard_map/ppermute | solution.py:579
  59.0 8.1 %collective-permute-done.19.received_ref = bf16[1056,256]{1,0:T(8,128)(2,1)S(1)} collective-permute-done((bf16[1056,256]{1,0:T(8,128)(2,1)S(1)}, bf16[1056,256]{1,0:T(8,128)(2,1)S(1)}, u32[]{:S(2)}, u32[]{:S(2)}) %collective-permute-start.19) | collective-permute-done | bytes 540704 | tf_op jit(solution)/shard_map/ppermute | solution.py:582
  71.8 9.1 %collective-permute-start.21 = (bf16[528,256]{1,0:T(8,128)(2,1)S(1)}, bf16[528,256]{1,0:T(8,128)(2,1)S(1)}, u32[]{:S(2)}, u32[]{:S(2)}) collective-permute-start(bf16[528,256]{1,0:T(8,128)(2,1)S(1)} %get-tuple-element.55.own_ref), channel_id=1, source_target_pairs={{0,8},{4,12},{24,16},{28,20},{1,9},{5,13},{25,17},{29,21},{2,10},{... | collective-permute-start | bytes 811016 | tf_op jit(solution)/shard_map/ppermute | solution.py:579
  80.9 2.0 collective-permute-start.18
  82.9 1.7 onward.5
  84.7 2.4 %collective-permute-done.21.received_ref = bf16[528,256]{1,0:T(8,128)(2,1)S(1)} collective-permute-done((bf16[528,256]{1,0:T(8,128)(2,1)S(1)}, bf16[528,256]{1,0:T(8,128)(2,1)S(1)}, u32[]{:S(2)}, u32[]{:S(2)}) %collective-permute-start.21) | collective-permute-done | bytes 270368 | tf_op jit(solution)/shard_map/ppermute | solution.py:579
  91.1 5.1 %collective-permute-start.25 = (bf16[528,256]{1,0:T(8,128)(2,1)}, bf16[528,256]{1,0:T(8,128)(2,1)S(1)}, u32[]{:S(2)}, u32[]{:S(2)}) collective-permute-start(bf16[528,256]{1,0:T(8,128)(2,1)} %get-tuple-element.54.own_ref), channel_id=1, source_target_pairs={{0,8},{4,12},{24,16},{28,20},{1,9},{5,13},{25,17},{29,21},{2,10},{... | collective-permute-start | bytes 811016 | tf_op jit(solution)/shard_map/ppermute | solution.py:579
  101.1 2.2 %collective-permute-done.25.received_ref = bf16[528,256]{1,0:T(8,128)(2,1)S(1)} collective-permute-done((bf16[528,256]{1,0:T(8,128)(2,1)}, bf16[528,256]{1,0:T(8,128)(2,1)S(1)}, u32[]{:S(2)}, u32[]{:S(2)}) %collective-permute-start.25) | collective-permute-done | bytes 270368 | tf_op jit(solution)/shard_map/ppermute | solution.py:579
  106.2 10.2 %collective-permute-done.23.refs_5_ = bf16[528,256]{1,0:T(8,128)(2,1)S(1)} collective-permute-done((bf16[528,256]{1,0:T(8,128)(2,1)S(1)}, bf16[528,256]{1,0:T(8,128)(2,1)S(1)}, u32[]{:S(2)}, u32[]{:S(2)}) %collective-permute-start.23) | collective-permute-done | bytes 270368 | tf_op jit(solution)/shard_map/ppermute | solution.py:579
  118.2 8.3 %scan.1 = bf16[1040,256]{1,0:T(8,128)(2,1)S(1)} custom-call(s32[7]{0:T(128)S(1)} %copy-done.14, f32[1]{0:T(128)} %bitcast.3.scale_ref, bf16[1056,256]{1,0:T(8,128)(2,1)S(1)} %copy-done.4, bf16[1056,256]{1,0:T(8,128)(2,1)} %collective-permute-done.17.refs_1_, bf16[1056,256]{1,0:T(8,128)(2,1)} %collective-permute-done.20.refs_2_, ...), custom_call_target="tpu_custom_call" | custom-call | flops 268435456 | bytes 2097152 | tf_op jit(solution)/shard_map/scan/pallas_call | solution.py:524
  128.0 5.4 %collective-permute-start.31 = (bf16[1040,256]{1,0:T(8,128)(2,1)S(1)}, bf16[1040,256]{1,0:T(8,128)(2,1)S(1)}, u32[]{:S(2)}, u32[]{:S(2)}) collective-permute-start(bf16[1040,256]{1,0:T(8,128)(2,1)S(1)} %scan.1), channel_id=1, source_target_pairs={{0,8},{4,12},{8,0},{12,4},{16,24},{20,28},{24,16},{28,20},{1,9},{5... | collective-permute-start | bytes 1597448 | tf_op jit(solution)/shard_map/ppermute | solution.py:579
  135.2 10.0 %collective-permute-done.31 = bf16[1040,256]{1,0:T(8,128)(2,1)S(1)} collective-permute-done((bf16[1040,256]{1,0:T(8,128)(2,1)S(1)}, bf16[1040,256]{1,0:T(8,128)(2,1)S(1)}, u32[]{:S(2)}, u32[]{:S(2)}) %collective-permute-start.31) | collective-permute-done | bytes 532512 | tf_op jit(solution)/shard_map/ppermute | solution.py:579
  146.9 10.9 %collective-permute-done.29 = bf16[1040,256]{1,0:T(8,128)(2,1)S(1)} collective-permute-done((bf16[1040,256]{1,0:T(8,128)(2,1)}, bf16[1040,256]{1,0:T(8,128)(2,1)S(1)}, u32[]{:S(2)}, u32[]{:S(2)}) %collective-permute-start.29) | collective-permute-done | bytes 532512 | tf_op jit(solution)/shard_map/ppermute | solution.py:579
  160.6 9.0 %collective-permute-done.33 = bf16[1040,256]{1,0:T(8,128)(2,1)S(1)} collective-permute-done((bf16[1040,256]{1,0:T(8,128)(2,1)S(1)}, bf16[1040,256]{1,0:T(8,128)(2,1)S(1)}, u32[]{:S(2)}, u32[]{:S(2)}) %collective-permute-start.33) | collective-permute-done | bytes 532512 | tf_op jit(solution)/shard_map/ppermute | solution.py:579
  169.6 2.1 collective-permute-start.36
  173.9 5.1 %collective-permute-done.36 = bf16[1040,256]{1,0:T(8,128)(2,1)S(1)} collective-permute-done((bf16[1040,256]{1,0:T(8,128)(2,1)S(1)}, bf16[1040,256]{1,0:T(8,128)(2,1)S(1)}, u32[]{:S(2)}, u32[]{:S(2)}) %collective-permute-start.36) | collective-permute-done | bytes 532512 | tf_op jit(solution)/shard_map/ppermute | solution.py:582
  181.2 1.5 collective-permute-start.40
  182.8 1.7 add_convert_fusion.2
  186.4 6.4 %collective-permute-done.38 = bf16[256,512]{1,0:T(8,128)(2,1)S(1)} collective-permute-done((bf16[256,512]{1,0:T(8,128)(2,1)}, bf16[256,512]{1,0:T(8,128)(2,1)S(1)}, u32[]{:S(2)}, u32[]{:S(2)}) %collective-permute-start.38) | collective-permute-done | bytes 262176 | tf_op jit(solution)/shard_map/ppermute | solution.py:755
  194.6 4.2 %all-to-all-start = ((bf16[8,32,512]{2,1,0:T(8,128)(2,1)}), bf16[8,32,512]{2,1,0:T(8,128)(2,1)S(1)}, u32[]{:S(2)}, u32[]{:S(2)}) async-start(bf16[8,32,512]{2,1,0:T(8,128)(2,1)} %multiply_convert_fusion.1), calls=%async_computation | async-start | bytes 524288 | tf_op jit(solution)/shard_map/all_to_all | solution.py:761
  199.5 7.6 %all-to-all-done = bf16[8,32,512]{2,1,0:T(8,128)(2,1)S(1)} async-done(((bf16[8,32,512]{2,1,0:T(8,128)(2,1)}), bf16[8,32,512]{2,1,0:T(8,128)(2,1)S(1)}, u32[]{:S(2)}, u32[]{:S(2)}) %all-to-all-start) | async-done | bytes 262176 | tf_op jit(solution)/shard_map/all_to_all | solution.py:761
  (164 shorter events, 54.1 us)
Async XLA Ops:
  2.8 22.1 %collective-permute-start.7 = (bf16[512,512]{1,0:T(8,128)(2,1)}, bf16[512,512]{1,0:T(8,128)(2,1)S(1)}, u32[]{:S(2)}, u32[]{:S(2)}) collective-permute-start(bf16[512,512]{1,0:T(8,128)(2,1)} %constant_dynamic-slice_fusion.9), channel_id=1, source_target_pairs={{0,4},{4,0},{8,12},{12,8},{16,20},{20,16},{24,28},{28,24},{1,5},{5... | collective-permute-start | bytes 1572872 | tf_op jit(solution)/shard_map/ppermute | solution.py:582
  6.7 10.2 %collective-permute-start = (bf16[32,1024]{1,0:T(8,128)(2,1)S(1)}, bf16[32,1024]{1,0:T(8,128)(2,1)S(1)}, u32[]{:S(2)}, u32[]{:S(2)}) collective-permute-start(bf16[32,1024]{1,0:T(8,128)(2,1)S(1)} %get-tuple-element.75), channel_id=1, source_target_pairs={{0,8},{4,12},{8,0},{12,4},{16,24},{20,28},{24,16},{28,20},{1,9},{5... | collective-permute-start | bytes 196616 | tf_op jit(solution)/shard_map/ppermute | solution.py:579
  8.3 8.6 %collective-permute-start.1 = (bf16[32,1024]{1,0:T(8,128)(2,1)S(1)}, bf16[32,1024]{1,0:T(8,128)(2,1)}, u32[]{:S(2)}, u32[]{:S(2)}) collective-permute-start(bf16[32,1024]{1,0:T(8,128)(2,1)S(1)} %get-tuple-element.74), channel_id=1, source_target_pairs={{0,16},{4,20},{8,24},{12,28},{16,0},{20,4},{24,8},{28,12},{1,17},{... | collective-permute-start | bytes 196616 | tf_op jit(solution)/shard_map/ppermute | solution.py:579
  23.3 9.4 %collective-permute-start.4 = (bf16[4,32,1024]{2,1,0:T(8,128)(2,1)S(1)}, bf16[4,32,1024]{2,1,0:T(8,128)(2,1)}, u32[]{:S(2)}, u32[]{:S(2)}) collective-permute-start(bf16[4,32,1024]{2,1,0:T(8,128)(2,1)S(1)} %pad_maximum_fusion.refs_0_), channel_id=1, source_target_pairs={{0,2},{1,3},{2,0},{3,1},{4,6},{5,7},{6,4},{7,5},{8,10},{9,11},{10,... | collective-permute-start | bytes 786440 | tf_op jit(solution)/shard_map/ppermute | solution.py:648
  24.9 11.2 %collective-permute-start.9 = (bf16[4,32,1024]{2,1,0:T(8,128)(2,1)S(1)}, bf16[4,32,1024]{2,1,0:T(8,128)(2,1)}, u32[]{:S(2)}, u32[]{:S(2)}) collective-permute-start(bf16[4,32,1024]{2,1,0:T(8,128)(2,1)S(1)} %collective-permute-done.6.refs_4_), channel_id=1, source_target_pairs={{0,2},{1,3},{2,0},{3,1},{4,6},{5,7},{6,4},{7,5},{8,10},{9,11},{10,... | collective-permute-start | bytes 786440 | tf_op jit(solution)/shard_map/ppermute | solution.py:648
  26.4 7.5 %collective-permute-start.10 = (bf16[32,512]{1,0:T(8,128)(2,1)}, bf16[32,512]{1,0:T(8,128)(2,1)S(1)}, u32[]{:S(2)}, u32[]{:S(2)}) collective-permute-start(bf16[32,512]{1,0:T(8,128)(2,1)} %bitcast.56), channel_id=1, source_target_pairs={{0,4},{4,0},{8,12},{12,8},{16,20},{20,16},{24,28},{28,24},{1,5},{5... | collective-permute-start | bytes 98312 | tf_op jit(solution)/shard_map/ppermute | solution.py:582
  26.9 9.9 %collective-permute-start.3 = (bf16[4,32,1024]{2,1,0:T(8,128)(2,1)S(1)}, bf16[4,32,1024]{2,1,0:T(8,128)(2,1)}, u32[]{:S(2)}, u32[]{:S(2)}) collective-permute-start(bf16[4,32,1024]{2,1,0:T(8,128)(2,1)S(1)} %pad_maximum_fusion.refs_0_), channel_id=1, source_target_pairs={{0,1},{1,0},{2,3},{3,2},{4,5},{5,4},{6,7},{7,6},{8,9},{9,8},{10,11... | collective-permute-start | bytes 786440 | tf_op jit(solution)/shard_map/ppermute | solution.py:648
  34.5 8.5 %collective-permute-start.12 = (bf16[512,256]{1,0:T(8,128)(2,1)}, bf16[512,256]{1,0:T(8,128)(2,1)}, u32[]{:S(2)}, u32[]{:S(2)}) collective-permute-start(bf16[512,256]{1,0:T(8,128)(2,1)} %bitcast.62), channel_id=1, source_target_pairs={{0,4},{4,0},{8,12},{12,8},{16,20},{20,16},{24,28},{28,24},{1,5},{5... | collective-permute-start | bytes 786440 | tf_op jit(solution)/shard_map/ppermute | solution.py:582
  53.7 13.4 %collective-permute-start.19 = (bf16[1056,256]{1,0:T(8,128)(2,1)S(1)}, bf16[1056,256]{1,0:T(8,128)(2,1)S(1)}, u32[]{:S(2)}, u32[]{:S(2)}) collective-permute-start(bf16[1056,256]{1,0:T(8,128)(2,1)S(1)} %get-tuple-element.53), channel_id=1, source_target_pairs={{0,4},{4,0},{8,12},{12,8},{16,20},{20,16},{24,28},{28,24},{1,5},{5... | collective-permute-start | bytes 1622024 | tf_op jit(solution)/shard_map/ppermute | solution.py:582
  55.3 14.7 %collective-permute-start.13 = (bf16[1024,256]{1,0:T(8,128)(2,1)S(1)}, bf16[1024,256]{1,0:T(8,128)(2,1)S(1)}, u32[]{:S(2)}, u32[]{:S(2)}) collective-permute-start(bf16[1024,256]{1,0:T(8,128)(2,1)S(1)} %get-tuple-element.47), channel_id=1, source_target_pairs={{0,8},{4,12},{24,16},{28,20},{1,9},{5,13},{25,17},{29,21},{2,10},{... | collective-permute-start | bytes 1572872 | tf_op jit(solution)/shard_map/ppermute | solution.py:579
  57.7 23.2 %collective-permute-start.15 = (bf16[528,256]{1,0:T(8,128)(2,1)S(1)}, bf16[528,256]{1,0:T(8,128)(2,1)S(1)}, u32[]{:S(2)}, u32[]{:S(2)}) collective-permute-start(bf16[528,256]{1,0:T(8,128)(2,1)S(1)} %get-tuple-element.49.own_ref), channel_id=1, source_target_pairs={{0,8},{4,12},{24,16},{28,20},{1,9},{5,13},{25,17},{29,21},{2,10},{... | collective-permute-start | bytes 811016 | tf_op jit(solution)/shard_map/ppermute | solution.py:579
  68.1 28.2 %collective-permute-start.20 = (bf16[1056,256]{1,0:T(8,128)(2,1)}, bf16[1056,256]{1,0:T(8,128)(2,1)}, u32[]{:S(2)}, u32[]{:S(2)}) collective-permute-start(bf16[1056,256]{1,0:T(8,128)(2,1)} %onward.6), channel_id=1, source_target_pairs={{8,0},{12,4},{16,24},{20,28},{9,1},{13,5},{17,25},{21,29},{10,2},{... | collective-permute-start | bytes 1622024 | tf_op jit(solution)/shard_map/ppermute | solution.py:579
  70.2 29.4 %collective-permute-start.14 = (bf16[1024,256]{1,0:T(8,128)(2,1)S(1)}, bf16[1024,256]{1,0:T(8,128)(2,1)S(1)}, u32[]{:S(2)}, u32[]{:S(2)}) collective-permute-start(bf16[1024,256]{1,0:T(8,128)(2,1)S(1)} %add_convert_fusion.1.refs_8_), channel_id=1, source_target_pairs={{8,16},{12,20},{16,8},{20,12},{9,17},{13,21},{17,9},{21,13},{10,18... | collective-permute-start | bytes 1572872 | tf_op jit(solution)/shard_map/ppermute | solution.py:579
  70.9 28.9 %collective-permute-start.17 = (bf16[1056,256]{1,0:T(8,128)(2,1)}, bf16[1056,256]{1,0:T(8,128)(2,1)}, u32[]{:S(2)}, u32[]{:S(2)}) collective-permute-start(bf16[1056,256]{1,0:T(8,128)(2,1)} %get-tuple-element.50), channel_id=1, source_target_pairs={{0,4},{4,0},{8,12},{12,8},{16,20},{20,16},{24,28},{28,24},{1,5},{5... | collective-permute-start | bytes 1622024 | tf_op jit(solution)/shard_map/ppermute | solution.py:582
  71.8 15.2 %collective-permute-start.21 = (bf16[528,256]{1,0:T(8,128)(2,1)S(1)}, bf16[528,256]{1,0:T(8,128)(2,1)S(1)}, u32[]{:S(2)}, u32[]{:S(2)}) collective-permute-start(bf16[528,256]{1,0:T(8,128)(2,1)S(1)} %get-tuple-element.55.own_ref), channel_id=1, source_target_pairs={{0,8},{4,12},{24,16},{28,20},{1,9},{5,13},{25,17},{29,21},{2,10},{... | collective-permute-start | bytes 811016 | tf_op jit(solution)/shard_map/ppermute | solution.py:579
  80.9 10.2 %collective-permute-start.18 = (bf16[528,256]{1,0:T(8,128)(2,1)}, bf16[528,256]{1,0:T(8,128)(2,1)}, u32[]{:S(2)}, u32[]{:S(2)}) collective-permute-start(bf16[528,256]{1,0:T(8,128)(2,1)} %get-tuple-element.48.own_ref), channel_id=1, source_target_pairs={{0,8},{4,12},{24,16},{28,20},{1,9},{5,13},{25,17},{29,21},{2,10},{... | collective-permute-start | bytes 811016 | tf_op jit(solution)/shard_map/ppermute | solution.py:579
  87.8 12.0 %collective-permute-start.16 = (bf16[528,256]{1,0:T(8,128)(2,1)}, bf16[528,256]{1,0:T(8,128)(2,1)}, u32[]{:S(2)}, u32[]{:S(2)}) collective-permute-start(bf16[528,256]{1,0:T(8,128)(2,1)} %onward.5), channel_id=1, source_target_pairs={{8,24},{12,28},{16,0},{20,4},{9,25},{13,29},{17,1},{21,5},{10,26},... | collective-permute-start | bytes 811016 | tf_op jit(solution)/shard_map/ppermute | solution.py:579
  91.1 12.2 %collective-permute-start.25 = (bf16[528,256]{1,0:T(8,128)(2,1)}, bf16[528,256]{1,0:T(8,128)(2,1)S(1)}, u32[]{:S(2)}, u32[]{:S(2)}) collective-permute-start(bf16[528,256]{1,0:T(8,128)(2,1)} %get-tuple-element.54.own_ref), channel_id=1, source_target_pairs={{0,8},{4,12},{24,16},{28,20},{1,9},{5,13},{25,17},{29,21},{2,10},{... | collective-permute-start | bytes 811016 | tf_op jit(solution)/shard_map/ppermute | solution.py:579
  98.2 18.2 %collective-permute-start.22 = (bf16[1056,256]{1,0:T(8,128)(2,1)}, bf16[1056,256]{1,0:T(8,128)(2,1)S(1)}, u32[]{:S(2)}, u32[]{:S(2)}) collective-permute-start(bf16[1056,256]{1,0:T(8,128)(2,1)} %onward.6), channel_id=1, source_target_pairs={{0,8},{4,12},{24,16},{28,20},{1,9},{5,13},{25,17},{29,21},{2,10},{... | collective-permute-start | bytes 1622024 | tf_op jit(solution)/shard_map/ppermute | solution.py:579
  99.8 16.7 %collective-permute-start.27 = (bf16[1024,256]{1,0:T(8,128)(2,1)S(1)}, bf16[1024,256]{1,0:T(8,128)(2,1)S(1)}, u32[]{:S(2)}, u32[]{:S(2)}) collective-permute-start(bf16[1024,256]{1,0:T(8,128)(2,1)S(1)} %multiply_convert_fusion), channel_id=1, source_target_pairs={{8,0},{12,4},{16,24},{20,28},{9,1},{13,5},{17,25},{21,29},{10,2},{... | collective-permute-start | bytes 1572872 | tf_op jit(solution)/shard_map/ppermute | solution.py:579
  104.1 12.4 %collective-permute-start.23 = (bf16[528,256]{1,0:T(8,128)(2,1)S(1)}, bf16[528,256]{1,0:T(8,128)(2,1)S(1)}, u32[]{:S(2)}, u32[]{:S(2)}) collective-permute-start(bf16[528,256]{1,0:T(8,128)(2,1)S(1)} %onward.7), channel_id=1, source_target_pairs={{8,24},{12,28},{16,0},{20,4},{9,25},{13,29},{17,1},{21,5},{10,26},... | collective-permute-start | bytes 811016 | tf_op jit(solution)/shard_map/ppermute | solution.py:579
  105.4 11.1 %collective-permute-start.24 = (bf16[528,256]{1,0:T(8,128)(2,1)S(1)}, bf16[528,256]{1,0:T(8,128)(2,1)S(1)}, u32[]{:S(2)}, u32[]{:S(2)}) collective-permute-start(bf16[528,256]{1,0:T(8,128)(2,1)S(1)} %onward.8), channel_id=1, source_target_pairs={{8,16},{12,20},{16,8},{20,12},{9,17},{13,21},{17,9},{21,13},{10,18... | collective-permute-start | bytes 811016 | tf_op jit(solution)/shard_map/ppermute | solution.py:579
  128.0 17.2 %collective-permute-start.31 = (bf16[1040,256]{1,0:T(8,128)(2,1)S(1)}, bf16[1040,256]{1,0:T(8,128)(2,1)S(1)}, u32[]{:S(2)}, u32[]{:S(2)}) collective-permute-start(bf16[1040,256]{1,0:T(8,128)(2,1)S(1)} %scan.1), channel_id=1, source_target_pairs={{0,8},{4,12},{8,0},{12,4},{16,24},{20,28},{24,16},{28,20},{1,9},{5... | collective-permute-start | bytes 1597448 | tf_op jit(solution)/shard_map/ppermute | solution.py:579
  133.3 24.5 %collective-permute-start.30 = (bf16[1040,256]{1,0:T(8,128)(2,1)S(1)}, bf16[1040,256]{1,0:T(8,128)(2,1)S(1)}, u32[]{:S(2)}, u32[]{:S(2)}) collective-permute-start(bf16[1040,256]{1,0:T(8,128)(2,1)S(1)} %scan.1), channel_id=1, source_target_pairs={{0,4},{4,0},{8,12},{12,8},{16,20},{20,16},{24,28},{28,24},{1,5},{5... | collective-permute-start | bytes 1597448 | tf_op jit(solution)/shard_map/ppermute | solution.py:582
  133.9 23.9 %collective-permute-start.29 = (bf16[1040,256]{1,0:T(8,128)(2,1)}, bf16[1040,256]{1,0:T(8,128)(2,1)S(1)}, u32[]{:S(2)}, u32[]{:S(2)}) collective-permute-start(bf16[1040,256]{1,0:T(8,128)(2,1)} %collective-permute-done.28), channel_id=1, source_target_pairs={{8,0},{12,4},{16,24},{20,28},{9,1},{13,5},{17,25},{21,29},{10,2},{... | collective-permute-start | bytes 1597448 | tf_op jit(solution)/shard_map/ppermute | solution.py:579
  145.2 13.2 %collective-permute-start.32 = (bf16[1040,256]{1,0:T(8,128)(2,1)S(1)}, bf16[1040,256]{1,0:T(8,128)(2,1)S(1)}, u32[]{:S(2)}, u32[]{:S(2)}) collective-permute-start(bf16[1040,256]{1,0:T(8,128)(2,1)S(1)} %collective-permute-done.31), channel_id=1, source_target_pairs={{8,16},{12,20},{16,8},{20,12},{9,17},{13,21},{17,9},{21,13},{10,18... | collective-permute-start | bytes 1597448 | tf_op jit(solution)/shard_map/ppermute | solution.py:579
  145.9 23.7 %collective-permute-start.34 = (bf16[1040,256]{1,0:T(8,128)(2,1)S(1)}, bf16[1040,256]{1,0:T(8,128)(2,1)S(1)}, u32[]{:S(2)}, u32[]{:S(2)}) collective-permute-start(bf16[1040,256]{1,0:T(8,128)(2,1)S(1)} %collective-permute-done.31), channel_id=1, source_target_pairs={{0,4},{4,0},{8,12},{12,8},{16,20},{20,16},{24,28},{28,24},{1,5},{5... | collective-permute-start | bytes 1597448 | tf_op jit(solution)/shard_map/ppermute | solution.py:582
  157.9 14.6 %collective-permute-start.35 = (bf16[1040,256]{1,0:T(8,128)(2,1)S(1)}, bf16[1040,256]{1,0:T(8,128)(2,1)S(1)}, u32[]{:S(2)}, u32[]{:S(2)}) collective-permute-start(bf16[1040,256]{1,0:T(8,128)(2,1)S(1)} %broadcast_select_fusion.1), channel_id=1, source_target_pairs={{0,4},{4,0},{8,12},{12,8},{16,20},{20,16},{24,28},{28,24},{1,5},{5... | collective-permute-start | bytes 1597448 | tf_op jit(solution)/shard_map/ppermute | solution.py:582
  158.4 11.2 %collective-permute-start.33 = (bf16[1040,256]{1,0:T(8,128)(2,1)S(1)}, bf16[1040,256]{1,0:T(8,128)(2,1)S(1)}, u32[]{:S(2)}, u32[]{:S(2)}) collective-permute-start(bf16[1040,256]{1,0:T(8,128)(2,1)S(1)} %collective-permute-done.32), channel_id=1, source_target_pairs={{8,0},{12,4},{16,24},{20,28},{9,1},{13,5},{17,25},{21,29},{10,2},{... | collective-permute-start | bytes 1597448 | tf_op jit(solution)/shard_map/ppermute | solution.py:579
  169.6 9.3 %collective-permute-start.36 = (bf16[1040,256]{1,0:T(8,128)(2,1)S(1)}, bf16[1040,256]{1,0:T(8,128)(2,1)S(1)}, u32[]{:S(2)}, u32[]{:S(2)}) collective-permute-start(bf16[1040,256]{1,0:T(8,128)(2,1)S(1)} %broadcast_select_fusion), channel_id=1, source_target_pairs={{0,4},{4,0},{8,12},{12,8},{16,20},{20,16},{24,28},{28,24},{1,5},{5... | collective-permute-start | bytes 1597448 | tf_op jit(solution)/shard_map/ppermute | solution.py:582
  184.5 8.3 %collective-permute-start.38 = (bf16[256,512]{1,0:T(8,128)(2,1)}, bf16[256,512]{1,0:T(8,128)(2,1)S(1)}, u32[]{:S(2)}, u32[]{:S(2)}) collective-permute-start(bf16[256,512]{1,0:T(8,128)(2,1)} %add_convert_fusion.2), channel_id=1, source_target_pairs={{0,2},{1,3},{2,0},{3,1},{4,6},{5,7},{6,4},{7,5},{8,10},{9,11},{10,... | collective-permute-start | bytes 786440 | tf_op jit(solution)/shard_map/ppermute | solution.py:755
  194.6 12.5 %all-to-all-start = ((bf16[8,32,512]{2,1,0:T(8,128)(2,1)}), bf16[8,32,512]{2,1,0:T(8,128)(2,1)S(1)}, u32[]{:S(2)}, u32[]{:S(2)}) async-start(bf16[8,32,512]{2,1,0:T(8,128)(2,1)} %multiply_convert_fusion.1), calls=%async_computation | async-start | bytes 524288 | tf_op jit(solution)/shard_map/all_to_all | solution.py:761
  (33 other events, 444.0 us)

commit v3 on v1

--- a/solution.py
+++ b/solution.py
@@ -198,14 +198,30 @@
     )
 
 
-def project_kernel(ranks, place_ref, factor_ref, *refs):
+def pair_columns(owner, channels):
+    at = owner % (LINE // 2) * channels
+    return pl.ds(pl.multiple_of(at, channels), channels)
+
+
+def steps_of(dt, run, upper):
+    channels = upper.shape[1]
+    dt = dt[run // 2]
+    pieces = []
+    for at in range(0, dt.shape[1], channels):
+        piece = dt[:, at : at + channels]
+        turned = pltpu.roll(piece, ROWS // 2, 0)
+        lower_run = jnp.where(upper, piece, turned)
+        upper_run = jnp.where(upper, turned, piece)
+        pieces.append(split_parts(jnp.where(run % 2 == 0, lower_run, upper_run), upper))
+    return jnp.concatenate(pieces, axis=0).astype(jnp.bfloat16)
+
+
+def far_kernel(ranks, place_ref, factor_ref, *refs):
     hidden = [refs[x * ranks : (x + 1) * ranks] for x in range(PAIR)]
     refs = refs[PAIR * ranks :]
-    own_x, x_far, own_bc, other_bc, own_dt, other_dt = refs[:6]
-    far_refs = refs[6 : 6 + LINE // 2]
-    near_refs = refs[6 + LINE // 2 : 6 + LINE]
-    sent_refs = refs[6 + LINE : 6 + LINE + LINE // 2]
-    bc_ref, largest_ref, quant_ref, near_dt, all_dt = refs[6 + LINE + LINE // 2 :]
+    own_x, other_x, own_bc, other_bc, own_dt, other_dt = refs[:6]
+    x_refs = refs[6 : 6 + LINE // 2]
+    bc_ref, largest_ref, quant_ref, dt_buf = refs[6 + LINE // 2 :]
     side, z = (place_ref[1], place_ref[2])
     factor = factor_ref[0]
     depth = own_x.shape[0]
@@ -227,27 +243,12 @@
         top = jnp.maximum(top, largest[:, at : at + width])
     largest_ref[...] = top
 
-    channels = near_refs[0].shape[1]
+    channels = x_refs[0].shape[1]
     tokens = bc_ref.shape[0]
     rows = tokens // CUTS
     blocks = quant_ref.shape[1] // CUTS
     extra = rows // channels * ROWS
     upper = lax.broadcasted_iota(jnp.int32, (ROWS, channels), 0) < ROWS // 2
-
-    def steps_of(dt_ref, run):
-        dt = dt_ref[run // 2]
-        pieces = []
-        for at in range(0, rows, channels):
-            piece = dt[:, at : at + channels]
-            turned = pltpu.roll(piece, ROWS // 2, 0)
-            lower_run = jnp.where(upper, piece, turned)
-            upper_run = jnp.where(upper, turned, piece)
-            pieces.append(split_parts(jnp.where(run % 2 == 0, lower_run, upper_run), upper))
-        return jnp.concatenate(pieces, axis=0).astype(jnp.bfloat16)
-
-    def columns(run):
-        return pl.ds(pl.multiple_of(run * channels, channels), channels)
-
     for cut in range(CUTS):
         part = slice(cut * blocks, (cut + 1) * blocks)
         near = quant_ref[side, part].reshape(rows, depth)
@@ -260,21 +261,38 @@
 
         at_rows = slice(cut * rows, (cut + 1) * rows)
         extra_rows = slice(tokens + cut * extra, tokens + (cut + 1) * extra)
-        ours = nt_dot(own_dt[...], near)
-        near_dt[...] = ours.reshape(near_dt.shape)
-        all_dt[...] = (ours + nt_dot(other_dt[...], far)).reshape(all_dt.shape)
         bc_ref[at_rows] = both(own_bc[...], other_bc[...]).astype(jnp.bfloat16)
+        dt = nt_dot(own_dt[...], near) + nt_dot(other_dt[...], far)
+        dt_buf[...] = dt.reshape(dt_buf.shape)
         for m in range(LINE // 2):
             owner = z ^ (m + LINE // 2)
-            run = side * LINE + owner
-            other = x_far[:, columns(owner % (LINE // 2))]
-            far_refs[m][at_rows] = both(own_x[:, columns(run)], other).astype(jnp.bfloat16)
-            far_refs[m][extra_rows] = steps_of(all_dt, run)
-            for out_refs, way in ((near_refs, side), (sent_refs, 1 - side)):
-                run = way * LINE + (z ^ m)
-                product = jnp.dot(near, own_x[:, columns(run)], preferred_element_type=jnp.float32)
+            columns = pair_columns(owner, channels)
+            product = both(own_x[:, columns], other_x[:, columns])
+            x_refs[m][at_rows] = product.astype(jnp.bfloat16)
+            x_refs[m][extra_rows] = steps_of(dt_buf, side * LINE + owner, upper)
+
+
+def near_kernel(place_ref, quant_ref, own_x, sent_x, own_dt, *refs):
+    near_refs, sent_refs, dt_buf = (refs[: LINE // 2], refs[LINE // 2 : LINE], refs[LINE])
+    side, z = (place_ref[1], place_ref[2])
+    depth, channels = (own_x.shape[0], near_refs[0].shape[1])
+    blocks = quant_ref.shape[1] // CUTS
+    rows = blocks * quant_ref.shape[2] * quant_ref.shape[3]
+    tokens = rows * CUTS
+    extra = rows // channels * ROWS
+    upper = lax.broadcasted_iota(jnp.int32, (ROWS, channels), 0) < ROWS // 2
+    for cut in range(CUTS):
+        near = quant_ref[side, cut * blocks : (cut + 1) * blocks].reshape(rows, depth)
+        at_rows = slice(cut * rows, (cut + 1) * rows)
+        extra_rows = slice(tokens + cut * extra, tokens + (cut + 1) * extra)
+        dt_buf[...] = nt_dot(own_dt[...], near).reshape(dt_buf.shape)
+        for x_ref, out_refs, way in ((own_x, near_refs, side), (sent_x, sent_refs, 1 - side)):
+            for m in range(LINE // 2):
+                owner = z ^ m
+                weight = x_ref[:, pair_columns(owner, channels)]
+                product = jnp.dot(near, weight, preferred_element_type=jnp.float32)
                 out_refs[m][at_rows] = product.astype(jnp.bfloat16)
-                out_refs[m][extra_rows] = steps_of(near_dt, run)
+                out_refs[m][extra_rows] = steps_of(dt_buf, way * LINE + owner, upper)
 
 
 def split_parts(values, upper):
@@ -282,36 +300,48 @@
     return jnp.where(upper, top, values - top)
 
 
-def project(place, factor, hidden, w_x, weights):
+def project(place, factor, hidden, far_weights, near_weights):
     line, own, wide = hidden[0].shape
     ranks = len(hidden) // PAIR
-    depth, x_wide = (weights[0].shape[0], 2 * weights[0].shape[1])
-    channels, maps_wide = (x_wide // LINE, weights[1].shape[1])
+    depth, x_wide = far_weights[0].shape
+    channels, maps_wide = (x_wide // (LINE // 2), far_weights[2].shape[1])
     tokens = line * PAIR * ranks * own
     extra = tokens // channels * ROWS
-    dt_shape = (weights[-1].shape[0] // ROWS, ROWS, tokens // CUTS)
     payload = jax.ShapeDtypeStruct((tokens + extra, channels), jnp.bfloat16)
     maps = jax.ShapeDtypeStruct((tokens, maps_wide), jnp.bfloat16)
     largest = jax.ShapeDtypeStruct((ROWS, 128), jnp.float32)
-    outs = [payload] * (LINE + LINE // 2) + [maps, largest]
-    return pl.pallas_call(
-        functools.partial(project_kernel, ranks),
-        in_specs=[SMEM, SMEM] + [VMEM] * (len(hidden) + 1 + len(weights)),
+    quant = jax.ShapeDtypeStruct((PAIR, line * PAIR, ranks, own, depth), jnp.bfloat16)
+    dt_buf = pltpu.VMEM((near_weights[-1].shape[0] // ROWS, ROWS, tokens // CUTS), jnp.float32)
+    outs = [payload] * (LINE // 2) + [maps, largest, quant]
+    over, far, maps, largest, quant = pl.pallas_call(
+        functools.partial(far_kernel, ranks),
+        in_specs=[SMEM, SMEM] + [VMEM] * (len(hidden) + len(far_weights)),
         out_specs=[VMEM] * len(outs),
-        scratch_shapes=[
-            pltpu.VMEM((PAIR, line * PAIR, ranks, own, depth), jnp.bfloat16),
-            pltpu.VMEM(dt_shape, jnp.float32),
-            pltpu.VMEM(dt_shape, jnp.float32),
-        ],
+        scratch_shapes=[dt_buf],
         out_shape=outs,
-        compiler_params=pltpu.CompilerParams(vmem_limit_bytes=32 * 2**20),
+        compiler_params=pltpu.CompilerParams(vmem_limit_bytes=24 * 2**20),
         cost_estimate=pl.CostEstimate(
             flops=2 * tokens * wide * (x_wide + maps_wide),
             bytes_accessed=2 * tokens * (wide + x_wide),
             transcendentals=0,
         ),
-        name="project",
-    )(place, factor, *hidden, w_x, *weights)
+        name="far",
+    )(place, factor, *hidden, *far_weights)
+    mine, near, mine_sent, near_sent = pl.pallas_call(
+        near_kernel,
+        in_specs=[SMEM] + [VMEM] * (1 + len(near_weights)),
+        out_specs=[VMEM] * LINE,
+        scratch_shapes=[dt_buf],
+        out_shape=[payload] * LINE,
+        compiler_params=pltpu.CompilerParams(vmem_limit_bytes=24 * 2**20),
+        cost_estimate=pl.CostEstimate(
+            flops=2 * tokens * wide * x_wide,
+            bytes_accessed=2 * tokens * (wide + 2 * x_wide),
+            transcendentals=0,
+        ),
+        name="near",
+    )(place, quant, *near_weights)
+    return over, far, mine, near, mine_sent, near_sent, maps, largest
 
 
 def onward_kernel(own_ref, received_ref, out_ref):
@@ -584,8 +614,13 @@
     tie = lax.optimization_barrier
     half_run = LINE // 2 * channels
     opposite = (z // (LINE // 2)) ^ 1
-    at = ((1 - side) * 2 + opposite) * half_run
-    x_sent = lax.dynamic_slice_in_dim(w_x, at, half_run, axis=1)
+
+    def half_columns(side_of, pair_of):
+        return lax.dynamic_slice_in_dim(
+            w_x, (side_of * 2 + pair_of) * half_run, half_run, axis=1
+        )
+
+    x_sent = half_columns(1 - side, opposite)
     x_sent, hidden_in = tie((x_sent, hidden_in))
     x_far = across(x_sent)
     x_far, maps_sent, dt_sent = tie(
@@ -602,8 +637,13 @@
         arrived.append(along(line_columns(m), [(s, s ^ m) for s in range(LINE)]))
     stacked = jnp.stack(arrived)
     beyond_pair = across(stacked)
-    beyond_pair, small, start_state, bc_own, dt_sent = tie(
-        (beyond_pair, small, start_state, bc_own, dt_sent)
+    w_far, w_near, w_near_sent = (
+        half_columns(side, opposite),
+        half_columns(side, 1 - opposite),
+        half_columns(1 - side, 1 - opposite),
+    )
+    beyond_pair, small, start_state, bc_own, dt_sent, w_far, w_near, w_near_sent = tie(
+        (beyond_pair, small, start_state, bc_own, dt_sent, w_far, w_near, w_near_sent)
     )
     rows = []
     for mine in (stacked, beyond_pair):
@@ -622,9 +662,12 @@
     middle = [(next_start, next_end), (next_end, next_start)]
     over_middle = [(next_start, end), (next_end, start)]
     beside_pairs = [(s, s ^ 1) for s in range(LINE)]
-    weights = (x_far, bc_own, bc_other, dt_sent, dt_other)
     over, far, mine, near, mine_sent, near_sent, maps, largest = project(
-        place, factor, rows, w_x, weights
+        place,
+        factor,
+        rows,
+        (w_far, x_far, bc_own, bc_other, dt_sent, dt_other),
+        (w_near, w_near_sent, dt_sent),
     )
 
     map_hop = along(maps, inward)
@@ -633,14 +676,16 @@
     near = onward(near, across(near_sent))
     got_mine = across(mine_sent)
     near_out = along(near, outward)
-    near_in = along(near, inward)
     map_sum = (maps.astype(f32) + map_hop.astype(f32)).astype(bf16)
     map_far = along(map_sum, middle)
     map_done = ((map_sum.astype(f32) + map_far.astype(f32)) * in_scale).astype(bf16)
     sent_end = onward(over, hop_far)
     got_end = along(sent_end, over_middle)
     hop_over, near_out, unused = tie((hop_over, near_out, sent_end))
-    got_next = along(onward(far, hop_over), middle)
+    sent_next = onward(far, hop_over)
+    got_next = along(sent_next, middle)
+    near, unused = tie((near, sent_next))
+    near_in = along(near, inward)
     map_done, got_end, got_mine = tie((map_done, got_end, got_mine))
     map_done = along(map_done, outward)
     gained = scan(
@@ -703,7 +748,6 @@
     pairs = [(t, t ^ 1) for t in range(ranks)]
     received = lax.ppermute(first_sum(1 - keeps).astype(bf16), "tensor", pairs)
     kept = first_sum(keeps)
-    squares = squares + lax.ppermute(squares, "tensor", pairs)
     bit = 2
     while bit < ranks:
         run //= 2
@@ -711,13 +755,18 @@
         pairs = [(t, t ^ bit) for t in range(ranks)]
         sent = run_of(kept, 1 - keeps, run) + run_of(received, 1 - keeps, run).astype(f32)
         kept = run_of(kept, keeps, run) + run_of(received, keeps, run).astype(f32)
-        received = lax.ppermute(sent.astype(bf16), "tensor", pairs)
-        squares = squares + lax.ppermute(squares, "tensor", pairs)
+        sent = sent.astype(bf16)
+        squares, unused = tie((squares, sent))
+        received = lax.ppermute(sent, "tensor", pairs)
+        bit *= 2
+    bit = 1
+    while bit < ranks:
+        squares = squares + lax.ppermute(squares, "tensor", [(t, t ^ bit) for t in range(ranks)])
         bit *= 2
     mean_sq = squares.reshape(count, ranks, own) / (HEADS * HEAD_DIM)
-    factors = lax.rsqrt(pick(mean_sq, 1, rank) + epsilon)
-    final = (kept + received.astype(f32)).reshape(count, own, -1) * factors[:, :, None]
-    final = lax.all_to_all(final.astype(bf16), "seq", split_axis=0, concat_axis=0, tiled=True)
+    factors = lax.rsqrt(pick(mean_sq, 1, rank) + epsilon).reshape(run, 1)
+    final = ((kept + received.astype(f32)) * factors).astype(bf16).reshape(count, own, -1)
+    final = lax.all_to_all(final, "seq", split_axis=0, concat_axis=0, tiled=True)
     layer_out = final.transpose(1, 0, 2).reshape(own, count * final.shape[2])
     return (layer_out, jnp.max(top))
 

time: 194 us -> 203 us (1.046)
  waiting for transfers between devices: 91.8 us -> 97.5 us
  local copies, waits for them, and re-layouts: 15.6 us -> 18.1 us
  Pallas kernels: 18.5 us -> 21 us
  starting transfers between devices: 52.8 us -> 50.5 us
    ppermute x6, waiting for transfers between devices: 2.75 us -> 6.23 us  [by_heads(): ours.append(lax.ppermute(ours[j - bit], 'tensor', pairs))]
    ppermute x17, waiting for transfers between devices: 54 us -> 57 us  [along(): return lax.ppermute(value, 'seq', moves)]
    concatenate x1, local copies, waits for them, and re-layouts: 0.08 us -> 3.04 us  [by_heads(): jnp.concatenate([blank, by_channel[:margin], blank, by_map[:margin], by_c...]
    ppermute x10, starting transfers between devices: 15.4 us -> 12.8 us  [across(): return lax.ppermute(value, 'seq', [(s, s ^ 1) for s in range(count)])]
    pallas_call x1 -> x2, Pallas kernels: 5.69 us -> 8.21 us  [the longest x1 5.31 us: project(): pl.pallas_call(functools.partial(far_kernel, ranks), in_specs=[SMEM, SMEM...]
    unnamed x32 -> x52, local copies, waits for them, and re-layouts: 6.93 us -> 6.38 us
where the time goes in v3:
time: 203 us; the launch traced here: 202 us
  waiting for transfers between devices  97.5 us (48%)
  starting transfers between devices  50.5 us (25%)
  Pallas kernels  21 us (10%)
  local copies, waits for them, and re-layouts  18.1 us (9%)
  other arithmetic  8.22 us (4%)
  matrix products  4.76 us (2%)
    ppermute x17, waiting for transfers between devices, along(): return lax.ppermute(value, 'seq', moves)  57 us
    ppermute x17, starting transfers between devices, along(): return lax.ppermute(value, 'seq', moves)  28.3 us
    ppermute x10, waiting for transfers between devices, across(): return lax.ppermute(value, 'seq', [(s, s ^ 1) for s in range(count)])  18.2 us
    ppermute x10, starting transfers between devices, across(): return lax.ppermute(value, 'seq', [(s, s ^ 1) for s in range(count)])  12.8 us
    pallas_call x1, Pallas kernels, scan(): pl.pallas_call(scan_kernel, in_specs=[SMEM, SMEM] + [VMEM] * (len(sums) +...  8.68 us
    all_to_all x1, waiting for transfers between devices, by_heads(): lax.all_to_all(final, 'seq', split_axis=0, concat_axis=0, tiled=True)  7.92 us
    ppermute x2, waiting for transfers between devices, by_heads(): lax.ppermute(squares, 'tensor', [(t, t ^ bit) for t in range(ranks)])  6.52 us
    unnamed x52, local copies, waits for them, and re-layouts  6.38 us
  transfers between devices with their start and end apart: 38, of which 18 were waited for; matrix products, arithmetic and copies ran while one was open for 9% of the time, Pallas kernels for 2%

profile of v3, /device:TPU:0, one launch (start us, length us, event | category | flops | bytes accessed | tf_op | source)
XLA Modules:
  0.0 202.0 jit_solution(13477441250988940767)
XLA Ops:
  0.8 2.8 %constant_dynamic-slice_fusion.2 = (bf16[512,512]{1,0:T(8,128)(2,1)S(1)}, bf16[512,512]{1,0:T(8,128)(2,1)}, bf16[512,512]{1,0:T(8,128)(2,1)}, bf16[512,512]{1,0:T(8,128)(2,1)S(1)}) fusion(bf16[512,2048]{1,0:T(8,128)(2,1)} %param.17, s32[]{:T(128)S(6)} %select_n.144, s32[]{:T(128)S(6)} %select_n.142, s32[]{:T(128)S(6)} %select_n.132, s32[]{:T(128)S(6)} %select_n.143), kind=kLoop, calls=%fused_computation.55 | loop fusion | bytes 4194320 | tf_op jit(solution)/shard_map/dynamic_slice | solution.py:619
  3.6 2.9 %collective-permute-start.7 = (bf16[512,512]{1,0:T(8,128)(2,1)}, bf16[512,512]{1,0:T(8,128)(2,1)}, u32[]{:S(2)}, u32[]{:S(2)}) collective-permute-start(bf16[512,512]{1,0:T(8,128)(2,1)} %get-tuple-element.38), channel_id=1, source_target_pairs={{0,4},{4,0},{8,12},{12,8},{16,20},{20,16},{24,28},{28,24},{1,5},{5... | collective-permute-start | bytes 1572872 | tf_op jit(solution)/shard_map/ppermute | solution.py:580
  7.3 1.6 collective-permute-start
  8.9 2.6 %collective-permute-start.1 = (bf16[32,1024]{1,0:T(8,128)(2,1)}, bf16[32,1024]{1,0:T(8,128)(2,1)}, u32[]{:S(2)}, u32[]{:S(2)}) collective-permute-start(bf16[32,1024]{1,0:T(8,128)(2,1)} %get-tuple-element.80), channel_id=1, source_target_pairs={{0,16},{4,20},{8,24},{12,28},{16,0},{20,4},{24,8},{28,12},{1,17},{... | collective-permute-start | bytes 196616 | tf_op jit(solution)/shard_map/ppermute | solution.py:577
  14.5 1.6 collective-permute-done.1
  16.1 1.7 collective-permute-done.2
  17.8 1.6 pad_maximum_fusion.refs_0_
  20.1 3.0 %concatenate.12.refs_9_ = f32[40,256]{1,0:T(8,128)} concatenate(f32[5,256]{1,0:T(8,128)S(1)} %broadcast_in_dim.15, f32[3,256]{1,0:T(4,128)S(1)} %slice.156, f32[5,256]{1,0:T(8,128)S(1)} %broadcast_in_dim.15, f32[3,256]{1,0:T(4,128)S(1)} %bitcast.63, f32[4,256]{1,0:T(4,128)S(1)} %slice.158, f32[4,256]{1,0:T(4,128)S(1)} %bitcast.64, f32[2,256]{1,0:T(2,128)S(1)} %slice.160, ...), dimensions={0} | concatenate | bytes 81920 | tf_op jit(solution)/shard_map/concatenate | solution.py:595
  24.0 1.6 collective-permute-start.4
  27.7 5.4 %collective-permute-done.4.refs_2_ = bf16[4,32,1024]{2,1,0:T(8,128)(2,1)} collective-permute-done((bf16[4,32,1024]{2,1,0:T(8,128)(2,1)}, bf16[4,32,1024]{2,1,0:T(8,128)(2,1)}, u32[]{:S(2)}, u32[]{:S(2)}) %collective-permute-start.4) | collective-permute-done | bytes 262176 | tf_op jit(solution)/shard_map/ppermute | solution.py:654
  38.9 4.0 %collective-permute-done.12.refs_13_ = bf16[32,512]{1,0:T(8,128)(2,1)} collective-permute-done((bf16[32,512]{1,0:T(8,128)(2,1)}, bf16[32,512]{1,0:T(8,128)(2,1)}, u32[]{:S(2)}, u32[]{:S(2)}) %collective-permute-start.12) | collective-permute-done | bytes 32800 | tf_op jit(solution)/shard_map/ppermute | solution.py:580
  45.6 5.3 %far.1 = (bf16[1056,256]{1,0:T(8,128)(2,1)}, bf16[1056,256]{1,0:T(8,128)(2,1)S(1)}, bf16[1024,256]{1,0:T(8,128)(2,1)S(1)}, f32[8,128]{1,0:T(8,128)S(1)}, bf16[2,8,4,32,512]{4,3,2,1,0:T(8,128)(2,1)S(1)}) custom-call(s32[7]{0:T(128)S(1)} %stack.43.place_ref, f32[1]{0:T(128)} %bitcast.4.factor_ref, bf16[4,32,1024]{2,1,0:T(8,128)(2,1)} %pad_maximum_fusion.refs_0_, ...), custom_call_target="tpu_custom_call" | custom-call | flops 1610612736 | bytes 3145728 | tf_op jit(solution)/shard_map/far/pallas_call | solution.py:316
  50.9 2.9 %near.1 = (bf16[1056,256]{1,0:T(8,128)(2,1)S(1)}, bf16[1056,256]{1,0:T(8,128)(2,1)S(1)}, bf16[1056,256]{1,0:T(8,128)(2,1)}, bf16[1056,256]{1,0:T(8,128)(2,1)S(1)}) custom-call(s32[7]{0:T(128)S(1)} %stack.43.place_ref, bf16[2,8,4,32,512]{4,3,2,1,0:T(8,128)(2,1)S(1)} %get-tuple-element.46.quant_ref, bf16[512,512]{1,0:T(8,128)(2,1)S(1)} %get-tuple-element.47.own_x, ...), custom_call_target="tpu_custom_call" | custom-call | flops 1073741824 | bytes 4194304 | tf_op jit(solution)/shard_map/near/pallas_call | solution.py:330
  55.3 1.7 collective-permute-start.13
  58.4 2.1 %collective-permute-start.18 = (bf16[1056,256]{1,0:T(8,128)(2,1)}, bf16[1056,256]{1,0:T(8,128)(2,1)}, u32[]{:S(2)}, u32[]{:S(2)}) collective-permute-start(bf16[1056,256]{1,0:T(8,128)(2,1)} %get-tuple-element.51.own_ref), channel_id=1, source_target_pairs={{0,8},{4,12},{24,16},{28,20},{1,9},{5,13},{25,17},{29,21},{2,10},{... | collective-permute-start | bytes 1622024 | tf_op jit(solution)/shard_map/ppermute | solution.py:577
  60.5 6.6 %collective-permute-done.19.received_ref = bf16[1056,256]{1,0:T(8,128)(2,1)S(1)} collective-permute-done((bf16[1056,256]{1,0:T(8,128)(2,1)S(1)}, bf16[1056,256]{1,0:T(8,128)(2,1)S(1)}, u32[]{:S(2)}, u32[]{:S(2)}) %collective-permute-start.19) | collective-permute-done | bytes 540704 | tf_op jit(solution)/shard_map/ppermute | solution.py:580
  71.8 9.2 %collective-permute-done.15.received_ref = bf16[1056,256]{1,0:T(8,128)(2,1)S(1)} collective-permute-done((bf16[1056,256]{1,0:T(8,128)(2,1)S(1)}, bf16[1056,256]{1,0:T(8,128)(2,1)S(1)}, u32[]{:S(2)}, u32[]{:S(2)}) %collective-permute-start.15) | collective-permute-done | bytes 540704 | tf_op jit(solution)/shard_map/ppermute | solution.py:577
  81.0 2.0 onward.3
  84.2 6.3 %collective-permute-done.18.received_ref = bf16[1056,256]{1,0:T(8,128)(2,1)} collective-permute-done((bf16[1056,256]{1,0:T(8,128)(2,1)}, bf16[1056,256]{1,0:T(8,128)(2,1)}, u32[]{:S(2)}, u32[]{:S(2)}) %collective-permute-start.18) | collective-permute-done | bytes 540704 | tf_op jit(solution)/shard_map/ppermute | solution.py:577
  93.5 8.3 %collective-permute-start.21 = (bf16[1056,256]{1,0:T(8,128)(2,1)}, bf16[1056,256]{1,0:T(8,128)(2,1)S(1)}, u32[]{:S(2)}, u32[]{:S(2)}) collective-permute-start(bf16[1056,256]{1,0:T(8,128)(2,1)} %onward.4), channel_id=1, source_target_pairs={{0,8},{4,12},{24,16},{28,20},{1,9},{5,13},{25,17},{29,21},{2,10},{... | collective-permute-start | bytes 1622024 | tf_op jit(solution)/shard_map/ppermute | solution.py:577
  103.5 11.6 %collective-permute-done.23.refs_8_ = bf16[1024,256]{1,0:T(8,128)(2,1)S(1)} collective-permute-done((bf16[1024,256]{1,0:T(8,128)(2,1)S(1)}, bf16[1024,256]{1,0:T(8,128)(2,1)S(1)}, u32[]{:S(2)}, u32[]{:S(2)}) %collective-permute-start.23) | collective-permute-done | bytes 524320 | tf_op jit(solution)/shard_map/ppermute | solution.py:577
  116.2 8.7 %scan.1 = bf16[1040,256]{1,0:T(8,128)(2,1)S(1)} custom-call(s32[7]{0:T(128)S(1)} %stack.43.place_ref, f32[1]{0:T(128)} %bitcast.3.scale_ref, bf16[1056,256]{1,0:T(8,128)(2,1)S(1)} %copy-done.6, bf16[1056,256]{1,0:T(8,128)(2,1)} %collective-permute-done.17.refs_1_, bf16[1056,256]{1,0:T(8,128)(2,1)} %collective-permute-done.20.refs_2_, ...), custom_call_target="tpu_custom_call" | custom-call | flops 268435456 | bytes 2097152 | tf_op jit(solution)/shard_map/scan/pallas_call | solution.py:522
  128.5 10.4 %collective-permute-done.27 = bf16[1040,256]{1,0:T(8,128)(2,1)} collective-permute-done((bf16[1040,256]{1,0:T(8,128)(2,1)S(1)}, bf16[1040,256]{1,0:T(8,128)(2,1)}, u32[]{:S(2)}, u32[]{:S(2)}) %collective-permute-start.27) | collective-permute-done | bytes 532512 | tf_op jit(solution)/shard_map/ppermute | solution.py:577
  142.4 5.8 %collective-permute-done.25 = bf16[1040,256]{1,0:T(8,128)(2,1)S(1)} collective-permute-done((bf16[1040,256]{1,0:T(8,128)(2,1)}, bf16[1040,256]{1,0:T(8,128)(2,1)S(1)}, u32[]{:S(2)}, u32[]{:S(2)}) %collective-permute-start.25) | collective-permute-done | bytes 532512 | tf_op jit(solution)/shard_map/ppermute | solution.py:577
  151.5 10.4 %collective-permute-done.29 = bf16[1040,256]{1,0:T(8,128)(2,1)S(1)} collective-permute-done((bf16[1040,256]{1,0:T(8,128)(2,1)S(1)}, bf16[1040,256]{1,0:T(8,128)(2,1)S(1)}, u32[]{:S(2)}, u32[]{:S(2)}) %collective-permute-start.29) | collective-permute-done | bytes 532512 | tf_op jit(solution)/shard_map/ppermute | solution.py:577
  164.9 7.0 %collective-permute-done.32 = bf16[1040,256]{1,0:T(8,128)(2,1)S(1)} collective-permute-done((bf16[1040,256]{1,0:T(8,128)(2,1)S(1)}, bf16[1040,256]{1,0:T(8,128)(2,1)S(1)}, u32[]{:S(2)}, u32[]{:S(2)}) %collective-permute-start.32) | collective-permute-done | bytes 532512 | tf_op jit(solution)/shard_map/ppermute | solution.py:580
  172.7 1.7 collective-permute-done.33
  174.4 1.7 add_convert_fusion.2
  179.4 5.4 %collective-permute-done.36 = f32[8,128]{1,0:T(8,128)S(1)} collective-permute-done((f32[8,128]{1,0:T(8,128)S(1)}, f32[8,128]{1,0:T(8,128)S(1)}, u32[]{:S(2)}, u32[]{:S(2)}) %collective-permute-start.36) | collective-permute-done | bytes 4128 | tf_op jit(solution)/shard_map/ppermute | solution.py:764
  187.5 1.8 multiply_convert_fusion.1
  189.2 3.6 %all-to-all-start = ((bf16[8,32,512]{2,1,0:T(8,128)(2,1)}), bf16[8,32,512]{2,1,0:T(8,128)(2,1)S(1)}, u32[]{:S(2)}, u32[]{:S(2)}) async-start(bf16[8,32,512]{2,1,0:T(8,128)(2,1)} %bitcast.15), calls=%async_computation | async-start | bytes 524288 | tf_op jit(solution)/shard_map/all_to_all | solution.py:769
  193.4 7.9 %all-to-all-done = bf16[8,32,512]{2,1,0:T(8,128)(2,1)S(1)} async-done(((bf16[8,32,512]{2,1,0:T(8,128)(2,1)}), bf16[8,32,512]{2,1,0:T(8,128)(2,1)S(1)}, u32[]{:S(2)}, u32[]{:S(2)}) %all-to-all-start) | async-done | bytes 262176 | tf_op jit(solution)/shard_map/all_to_all | solution.py:769
  (155 shorter events, 50.9 us)
Async XLA Ops:
  3.6 22.0 %collective-permute-start.7 = (bf16[512,512]{1,0:T(8,128)(2,1)}, bf16[512,512]{1,0:T(8,128)(2,1)}, u32[]{:S(2)}, u32[]{:S(2)}) collective-permute-start(bf16[512,512]{1,0:T(8,128)(2,1)} %get-tuple-element.38), channel_id=1, source_target_pairs={{0,4},{4,0},{8,12},{12,8},{16,20},{20,16},{24,28},{28,24},{1,5},{5... | collective-permute-start | bytes 1572872 | tf_op jit(solution)/shard_map/ppermute | solution.py:580
  7.3 7.3 %collective-permute-start = (bf16[32,1024]{1,0:T(8,128)(2,1)}, bf16[32,1024]{1,0:T(8,128)(2,1)}, u32[]{:S(2)}, u32[]{:S(2)}) collective-permute-start(bf16[32,1024]{1,0:T(8,128)(2,1)} %get-tuple-element.81), channel_id=1, source_target_pairs={{0,8},{4,12},{8,0},{12,4},{16,24},{20,28},{24,16},{28,20},{1,9},{5... | collective-permute-start | bytes 196616 | tf_op jit(solution)/shard_map/ppermute | solution.py:577
  8.9 7.3 %collective-permute-start.1 = (bf16[32,1024]{1,0:T(8,128)(2,1)}, bf16[32,1024]{1,0:T(8,128)(2,1)}, u32[]{:S(2)}, u32[]{:S(2)}) collective-permute-start(bf16[32,1024]{1,0:T(8,128)(2,1)} %get-tuple-element.80), channel_id=1, source_target_pairs={{0,16},{4,20},{8,24},{12,28},{16,0},{20,4},{24,8},{28,12},{1,17},{... | collective-permute-start | bytes 196616 | tf_op jit(solution)/shard_map/ppermute | solution.py:577
  19.5 6.7 %collective-permute-start.6 = (bf16[4,32,1024]{2,1,0:T(8,128)(2,1)}, bf16[4,32,1024]{2,1,0:T(8,128)(2,1)}, u32[]{:S(2)}, u32[]{:S(2)}) collective-permute-start(bf16[4,32,1024]{2,1,0:T(8,128)(2,1)} %pad_maximum_fusion.refs_0_), channel_id=1, source_target_pairs={{0,4},{4,0},{8,12},{12,8},{16,20},{20,16},{24,28},{28,24},{1,5},{5... | collective-permute-start | bytes 786440 | tf_op jit(solution)/shard_map/ppermute | solution.py:580
  24.0 9.1 %collective-permute-start.4 = (bf16[4,32,1024]{2,1,0:T(8,128)(2,1)}, bf16[4,32,1024]{2,1,0:T(8,128)(2,1)}, u32[]{:S(2)}, u32[]{:S(2)}) collective-permute-start(bf16[4,32,1024]{2,1,0:T(8,128)(2,1)} %pad_maximum_fusion.refs_0_), channel_id=1, source_target_pairs={{0,2},{1,3},{2,0},{3,1},{4,6},{5,7},{6,4},{7,5},{8,10},{9,11},{10,... | collective-permute-start | bytes 786440 | tf_op jit(solution)/shard_map/ppermute | solution.py:654
  26.2 9.7 %collective-permute-start.9 = (bf16[4,32,1024]{2,1,0:T(8,128)(2,1)}, bf16[4,32,1024]{2,1,0:T(8,128)(2,1)}, u32[]{:S(2)}, u32[]{:S(2)}) collective-permute-start(bf16[4,32,1024]{2,1,0:T(8,128)(2,1)} %collective-permute-done.6.refs_4_), channel_id=1, source_target_pairs={{0,2},{1,3},{2,0},{3,1},{4,6},{5,7},{6,4},{7,5},{8,10},{9,11},{10,... | collective-permute-start | bytes 786440 | tf_op jit(solution)/shard_map/ppermute | solution.py:654
  27.7 8.2 %collective-permute-start.3 = (bf16[4,32,1024]{2,1,0:T(8,128)(2,1)}, bf16[4,32,1024]{2,1,0:T(8,128)(2,1)S(1)}, u32[]{:S(2)}, u32[]{:S(2)}) collective-permute-start(bf16[4,32,1024]{2,1,0:T(8,128)(2,1)} %pad_maximum_fusion.refs_0_), channel_id=1, source_target_pairs={{0,1},{1,0},{2,3},{3,2},{4,5},{5,4},{6,7},{7,6},{8,9},{9,8},{10,11... | collective-permute-start | bytes 786440 | tf_op jit(solution)/shard_map/ppermute | solution.py:654
  33.1 9.7 %collective-permute-start.5 = (bf16[4,32,1024]{2,1,0:T(8,128)(2,1)}, bf16[4,32,1024]{2,1,0:T(8,128)(2,1)}, u32[]{:S(2)}, u32[]{:S(2)}) collective-permute-start(bf16[4,32,1024]{2,1,0:T(8,128)(2,1)} %collective-permute-done.4.refs_2_), channel_id=1, source_target_pairs={{0,1},{1,0},{2,3},{3,2},{4,5},{5,4},{6,7},{7,6},{8,9},{9,8},{10,11... | collective-permute-start | bytes 786440 | tf_op jit(solution)/shard_map/ppermute | solution.py:654
  33.1 9.7 %collective-permute-start.8 = (bf16[4,32,1024]{2,1,0:T(8,128)(2,1)}, bf16[4,32,1024]{2,1,0:T(8,128)(2,1)}, u32[]{:S(2)}, u32[]{:S(2)}) collective-permute-start(bf16[4,32,1024]{2,1,0:T(8,128)(2,1)} %collective-permute-done.6.refs_4_), channel_id=1, source_target_pairs={{0,1},{1,0},{2,3},{3,2},{4,5},{5,4},{6,7},{7,6},{8,9},{9,8},{10,11... | collective-permute-start | bytes 786440 | tf_op jit(solution)/shard_map/ppermute | solution.py:654
  33.6 9.2 %collective-permute-start.11 = (bf16[512,256]{1,0:T(8,128)(2,1)}, bf16[512,256]{1,0:T(8,128)(2,1)}, u32[]{:S(2)}, u32[]{:S(2)}) collective-permute-start(bf16[512,256]{1,0:T(8,128)(2,1)} %bitcast.61), channel_id=1, source_target_pairs={{0,4},{4,0},{8,12},{12,8},{16,20},{20,16},{24,28},{28,24},{1,5},{5... | collective-permute-start | bytes 786440 | tf_op jit(solution)/shard_map/ppermute | solution.py:580
  35.9 7.0 %collective-permute-start.10 = (bf16[4,32,1024]{2,1,0:T(8,128)(2,1)}, bf16[4,32,1024]{2,1,0:T(8,128)(2,1)}, u32[]{:S(2)}, u32[]{:S(2)}) collective-permute-start(bf16[4,32,1024]{2,1,0:T(8,128)(2,1)} %collective-permute-done.9.refs_6_), channel_id=1, source_target_pairs={{0,1},{1,0},{2,3},{3,2},{4,5},{5,4},{6,7},{7,6},{8,9},{9,8},{10,11... | collective-permute-start | bytes 786440 | tf_op jit(solution)/shard_map/ppermute | solution.py:654
  53.8 13.3 %collective-permute-start.19 = (bf16[1056,256]{1,0:T(8,128)(2,1)S(1)}, bf16[1056,256]{1,0:T(8,128)(2,1)S(1)}, u32[]{:S(2)}, u32[]{:S(2)}) collective-permute-start(bf16[1056,256]{1,0:T(8,128)(2,1)S(1)} %get-tuple-element.56), channel_id=1, source_target_pairs={{0,4},{4,0},{8,12},{12,8},{16,20},{20,16},{24,28},{28,24},{1,5},{5... | collective-permute-start | bytes 1622024 | tf_op jit(solution)/shard_map/ppermute | solution.py:580
  55.3 14.1 %collective-permute-start.13 = (bf16[1024,256]{1,0:T(8,128)(2,1)S(1)}, bf16[1024,256]{1,0:T(8,128)(2,1)S(1)}, u32[]{:S(2)}, u32[]{:S(2)}) collective-permute-start(bf16[1024,256]{1,0:T(8,128)(2,1)S(1)} %get-tuple-element.50), channel_id=1, source_target_pairs={{0,8},{4,12},{24,16},{28,20},{1,9},{5,13},{25,17},{29,21},{2,10},{... | collective-permute-start | bytes 1572872 | tf_op jit(solution)/shard_map/ppermute | solution.py:577
  57.1 23.9 %collective-permute-start.15 = (bf16[1056,256]{1,0:T(8,128)(2,1)S(1)}, bf16[1056,256]{1,0:T(8,128)(2,1)S(1)}, u32[]{:S(2)}, u32[]{:S(2)}) collective-permute-start(bf16[1056,256]{1,0:T(8,128)(2,1)S(1)} %get-tuple-element.52.own_ref), channel_id=1, source_target_pairs={{0,8},{4,12},{24,16},{28,20},{1,9},{5,13},{25,17},{29,21},{2,10},{... | collective-permute-start | bytes 1622024 | tf_op jit(solution)/shard_map/ppermute | solution.py:577
  58.4 32.1 %collective-permute-start.18 = (bf16[1056,256]{1,0:T(8,128)(2,1)}, bf16[1056,256]{1,0:T(8,128)(2,1)}, u32[]{:S(2)}, u32[]{:S(2)}) collective-permute-start(bf16[1056,256]{1,0:T(8,128)(2,1)} %get-tuple-element.51.own_ref), channel_id=1, source_target_pairs={{0,8},{4,12},{24,16},{28,20},{1,9},{5,13},{25,17},{29,21},{2,10},{... | collective-permute-start | bytes 1622024 | tf_op jit(solution)/shard_map/ppermute | solution.py:577
  68.1 22.4 %collective-permute-start.20 = (bf16[1056,256]{1,0:T(8,128)(2,1)}, bf16[1056,256]{1,0:T(8,128)(2,1)}, u32[]{:S(2)}, u32[]{:S(2)}) collective-permute-start(bf16[1056,256]{1,0:T(8,128)(2,1)} %onward.4), channel_id=1, source_target_pairs={{8,0},{12,4},{16,24},{20,28},{9,1},{13,5},{17,25},{21,29},{10,2},{... | collective-permute-start | bytes 1622024 | tf_op jit(solution)/shard_map/ppermute | solution.py:577
  69.6 32.2 %collective-permute-start.14 = (bf16[1024,256]{1,0:T(8,128)(2,1)S(1)}, bf16[1024,256]{1,0:T(8,128)(2,1)S(1)}, u32[]{:S(2)}, u32[]{:S(2)}) collective-permute-start(bf16[1024,256]{1,0:T(8,128)(2,1)S(1)} %add_convert_fusion.1.refs_6_), channel_id=1, source_target_pairs={{8,16},{12,20},{16,8},{20,12},{9,17},{13,21},{17,9},{21,13},{10,18... | collective-permute-start | bytes 1572872 | tf_op jit(solution)/shard_map/ppermute | solution.py:577
  70.3 31.7 %collective-permute-start.17 = (bf16[1056,256]{1,0:T(8,128)(2,1)}, bf16[1056,256]{1,0:T(8,128)(2,1)}, u32[]{:S(2)}, u32[]{:S(2)}) collective-permute-start(bf16[1056,256]{1,0:T(8,128)(2,1)} %get-tuple-element.53), channel_id=1, source_target_pairs={{0,4},{4,0},{8,12},{12,8},{16,20},{20,16},{24,28},{28,24},{1,5},{5... | collective-permute-start | bytes 1622024 | tf_op jit(solution)/shard_map/ppermute | solution.py:580
  82.9 19.0 %collective-permute-start.16 = (bf16[1056,256]{1,0:T(8,128)(2,1)}, bf16[1056,256]{1,0:T(8,128)(2,1)}, u32[]{:S(2)}, u32[]{:S(2)}) collective-permute-start(bf16[1056,256]{1,0:T(8,128)(2,1)} %onward.3), channel_id=1, source_target_pairs={{8,24},{12,28},{16,0},{20,4},{9,25},{13,29},{17,1},{21,5},{10,26},... | collective-permute-start | bytes 1622024 | tf_op jit(solution)/shard_map/ppermute | solution.py:577
  92.8 22.3 %collective-permute-start.22 = (bf16[1056,256]{1,0:T(8,128)(2,1)S(1)}, bf16[1056,256]{1,0:T(8,128)(2,1)S(1)}, u32[]{:S(2)}, u32[]{:S(2)}) collective-permute-start(bf16[1056,256]{1,0:T(8,128)(2,1)S(1)} %onward.5), channel_id=1, source_target_pairs={{8,16},{12,20},{16,8},{20,12},{9,17},{13,21},{17,9},{21,13},{10,18... | collective-permute-start | bytes 1622024 | tf_op jit(solution)/shard_map/ppermute | solution.py:577
  93.5 21.6 %collective-permute-start.21 = (bf16[1056,256]{1,0:T(8,128)(2,1)}, bf16[1056,256]{1,0:T(8,128)(2,1)S(1)}, u32[]{:S(2)}, u32[]{:S(2)}) collective-permute-start(bf16[1056,256]{1,0:T(8,128)(2,1)} %onward.4), channel_id=1, source_target_pairs={{0,8},{4,12},{24,16},{28,20},{1,9},{5,13},{25,17},{29,21},{2,10},{... | collective-permute-start | bytes 1622024 | tf_op jit(solution)/shard_map/ppermute | solution.py:577
  102.0 13.1 %collective-permute-start.23 = (bf16[1024,256]{1,0:T(8,128)(2,1)S(1)}, bf16[1024,256]{1,0:T(8,128)(2,1)S(1)}, u32[]{:S(2)}, u32[]{:S(2)}) collective-permute-start(bf16[1024,256]{1,0:T(8,128)(2,1)S(1)} %multiply_convert_fusion), channel_id=1, source_target_pairs={{8,0},{12,4},{16,24},{20,28},{9,1},{13,5},{17,25},{21,29},{10,2},{... | collective-permute-start | bytes 1572872 | tf_op jit(solution)/shard_map/ppermute | solution.py:577
  126.3 12.6 %collective-permute-start.27 = (bf16[1040,256]{1,0:T(8,128)(2,1)S(1)}, bf16[1040,256]{1,0:T(8,128)(2,1)}, u32[]{:S(2)}, u32[]{:S(2)}) collective-permute-start(bf16[1040,256]{1,0:T(8,128)(2,1)S(1)} %scan.1), channel_id=1, source_target_pairs={{0,8},{4,12},{8,0},{12,4},{16,24},{20,28},{24,16},{28,20},{1,9},{5... | collective-permute-start | bytes 1597448 | tf_op jit(solution)/shard_map/ppermute | solution.py:577
  126.7 21.6 %collective-permute-start.26 = (bf16[1040,256]{1,0:T(8,128)(2,1)S(1)}, bf16[1040,256]{1,0:T(8,128)(2,1)S(1)}, u32[]{:S(2)}, u32[]{:S(2)}) collective-permute-start(bf16[1040,256]{1,0:T(8,128)(2,1)S(1)} %scan.1), channel_id=1, source_target_pairs={{0,4},{4,0},{8,12},{12,8},{16,20},{20,16},{24,28},{28,24},{1,5},{5... | collective-permute-start | bytes 1597448 | tf_op jit(solution)/shard_map/ppermute | solution.py:580
  127.2 21.0 %collective-permute-start.25 = (bf16[1040,256]{1,0:T(8,128)(2,1)}, bf16[1040,256]{1,0:T(8,128)(2,1)S(1)}, u32[]{:S(2)}, u32[]{:S(2)}) collective-permute-start(bf16[1040,256]{1,0:T(8,128)(2,1)} %collective-permute-done.24), channel_id=1, source_target_pairs={{8,0},{12,4},{16,24},{20,28},{9,1},{13,5},{17,25},{21,29},{10,2},{... | collective-permute-start | bytes 1597448 | tf_op jit(solution)/shard_map/ppermute | solution.py:577
  138.9 10.4 %collective-permute-start.28 = (bf16[1040,256]{1,0:T(8,128)(2,1)}, bf16[1040,256]{1,0:T(8,128)(2,1)S(1)}, u32[]{:S(2)}, u32[]{:S(2)}) collective-permute-start(bf16[1040,256]{1,0:T(8,128)(2,1)} %collective-permute-done.27), channel_id=1, source_target_pairs={{8,16},{12,20},{16,8},{20,12},{9,17},{13,21},{17,9},{21,13},{10,18... | collective-permute-start | bytes 1597448 | tf_op jit(solution)/shard_map/ppermute | solution.py:577
  139.6 22.4 %collective-permute-start.30 = (bf16[1040,256]{1,0:T(8,128)(2,1)}, bf16[1040,256]{1,0:T(8,128)(2,1)S(1)}, u32[]{:S(2)}, u32[]{:S(2)}) collective-permute-start(bf16[1040,256]{1,0:T(8,128)(2,1)} %collective-permute-done.27), channel_id=1, source_target_pairs={{0,4},{4,0},{8,12},{12,8},{16,20},{20,16},{24,28},{28,24},{1,5},{5... | collective-permute-start | bytes 1597448 | tf_op jit(solution)/shard_map/ppermute | solution.py:580
  148.3 15.3 %collective-permute-start.31 = (bf16[1040,256]{1,0:T(8,128)(2,1)S(1)}, bf16[1040,256]{1,0:T(8,128)(2,1)S(1)}, u32[]{:S(2)}, u32[]{:S(2)}) collective-permute-start(bf16[1040,256]{1,0:T(8,128)(2,1)S(1)} %broadcast_select_fusion.1), channel_id=1, source_target_pairs={{0,4},{4,0},{8,12},{12,8},{16,20},{20,16},{24,28},{28,24},{1,5},{5... | collective-permute-start | bytes 1597448 | tf_op jit(solution)/shard_map/ppermute | solution.py:580
  149.3 12.6 %collective-permute-start.29 = (bf16[1040,256]{1,0:T(8,128)(2,1)S(1)}, bf16[1040,256]{1,0:T(8,128)(2,1)S(1)}, u32[]{:S(2)}, u32[]{:S(2)}) collective-permute-start(bf16[1040,256]{1,0:T(8,128)(2,1)S(1)} %collective-permute-done.28), channel_id=1, source_target_pairs={{8,0},{12,4},{16,24},{20,28},{9,1},{13,5},{17,25},{21,29},{10,2},{... | collective-permute-start | bytes 1597448 | tf_op jit(solution)/shard_map/ppermute | solution.py:577
  162.0 10.0 %collective-permute-start.32 = (bf16[1040,256]{1,0:T(8,128)(2,1)S(1)}, bf16[1040,256]{1,0:T(8,128)(2,1)S(1)}, u32[]{:S(2)}, u32[]{:S(2)}) collective-permute-start(bf16[1040,256]{1,0:T(8,128)(2,1)S(1)} %broadcast_select_fusion), channel_id=1, source_target_pairs={{0,4},{4,0},{8,12},{12,8},{16,20},{20,16},{24,28},{28,24},{1,5},{5... | collective-permute-start | bytes 1597448 | tf_op jit(solution)/shard_map/ppermute | solution.py:580
  176.1 11.4 %collective-permute-start.34 = (bf16[256,512]{1,0:T(8,128)(2,1)}, bf16[256,512]{1,0:T(8,128)(2,1)S(1)}, u32[]{:S(2)}, u32[]{:S(2)}) collective-permute-start(bf16[256,512]{1,0:T(8,128)(2,1)} %add_convert_fusion.2), channel_id=1, source_target_pairs={{0,2},{1,3},{2,0},{3,1},{4,6},{5,7},{6,4},{7,5},{8,10},{9,11},{10,... | collective-permute-start | bytes 786440 | tf_op jit(solution)/shard_map/ppermute | solution.py:760
  189.2 12.1 %all-to-all-start = ((bf16[8,32,512]{2,1,0:T(8,128)(2,1)}), bf16[8,32,512]{2,1,0:T(8,128)(2,1)S(1)}, u32[]{:S(2)}, u32[]{:S(2)}) async-start(bf16[8,32,512]{2,1,0:T(8,128)(2,1)} %bitcast.15), calls=%async_computation | async-start | bytes 524288 | tf_op jit(solution)/shard_map/all_to_all | solution.py:769
  (29 other events, 406.9 us)

commit v4 on v1

--- a/solution.py
+++ b/solution.py
@@ -304,7 +304,7 @@
             pltpu.VMEM(dt_shape, jnp.float32),
         ],
         out_shape=outs,
-        compiler_params=pltpu.CompilerParams(vmem_limit_bytes=32 * 2**20),
+        compiler_params=pltpu.CompilerParams(vmem_limit_bytes=10 * 2**20),
         cost_estimate=pl.CostEstimate(
             flops=2 * tokens * wide * (x_wide + maps_wide),
             bytes_accessed=2 * tokens * (wide + x_wide),
@@ -334,7 +334,7 @@
         in_specs=[VMEM, VMEM],
         out_specs=VMEM,
         out_shape=jax.ShapeDtypeStruct(own.shape, own.dtype),
-        compiler_params=pltpu.CompilerParams(vmem_limit_bytes=8 * 2**20),
+        compiler_params=pltpu.CompilerParams(vmem_limit_bytes=4 * 2**20),
         cost_estimate=pl.CostEstimate(
             flops=own.size, bytes_accessed=6 * own.size, transcendentals=0
         ),
@@ -498,7 +498,7 @@
             pltpu.VMEM((tokens + ROWS, 2 * STATE), jnp.float32),
         ],
         out_shape=out,
-        compiler_params=pltpu.CompilerParams(vmem_limit_bytes=20 * 2**20),
+        compiler_params=pltpu.CompilerParams(vmem_limit_bytes=8 * 2**20),
         cost_estimate=pl.CostEstimate(
             flops=8 * tokens * SPAN * channels,
             bytes_accessed=8 * tokens * channels,
@@ -633,7 +633,6 @@
     near = onward(near, across(near_sent))
     got_mine = across(mine_sent)
     near_out = along(near, outward)
-    near_in = along(near, inward)
     map_sum = (maps.astype(f32) + map_hop.astype(f32)).astype(bf16)
     map_far = along(map_sum, middle)
     map_done = ((map_sum.astype(f32) + map_far.astype(f32)) * in_scale).astype(bf16)
@@ -641,7 +640,9 @@
     got_end = along(sent_end, over_middle)
     hop_over, near_out, unused = tie((hop_over, near_out, sent_end))
     got_next = along(onward(far, hop_over), middle)
-    map_done, got_end, got_mine = tie((map_done, got_end, got_mine))
+    near, got_end = tie((near, got_end))
+    near_in = along(near, inward)
+    map_done, got_mine, unused = tie((map_done, got_mine, hop_over))
     map_done = along(map_done, outward)
     gained = scan(
         place,

time: 194 us -> 196 us (1.010)
  waiting for transfers between devices: 91.8 us -> 96.7 us
  starting transfers between devices: 52.8 us -> 49.5 us
    ppermute x17, waiting for transfers between devices: 54 us -> 60.1 us  [along(): return lax.ppermute(value, 'seq', moves)]
    ppermute x10, starting transfers between devices: 15.4 us -> 12.9 us  [across(): return lax.ppermute(value, 'seq', [(s, s ^ 1) for s in range(count)])]
  transfers between devices with their start and end apart: 38 -> 38, of which waited for: 18 -> 17; matrix products, arithmetic and copies ran while one was open for 9% -> 9% of each run, Pallas kernels for 2% -> 2%
where the time goes in v4:
time: 196 us; the launch traced here: 195 us
  waiting for transfers between devices  96.7 us (49%)
  starting transfers between devices  49.5 us (25%)
  Pallas kernels  18.5 us (9%)
  local copies, waits for them, and re-layouts  15.6 us (8%)
  other arithmetic  9.05 us (5%)
  matrix products  3.68 us (2%)
    ppermute x17, waiting for transfers between devices, along(): return lax.ppermute(value, 'seq', moves)  60.1 us
    ppermute x17, starting transfers between devices, along(): return lax.ppermute(value, 'seq', moves)  26.4 us
    ppermute x10, waiting for transfers between devices, across(): return lax.ppermute(value, 'seq', [(s, s ^ 1) for s in range(count)])  18.8 us
    ppermute x10, starting transfers between devices, across(): return lax.ppermute(value, 'seq', [(s, s ^ 1) for s in range(count)])  12.9 us
    pallas_call x1, Pallas kernels, scan(): pl.pallas_call(scan_kernel, in_specs=[SMEM, SMEM] + [VMEM] * (len(sums) +...  8.64 us
    all_to_all x1, waiting for transfers between devices, by_heads(): lax.all_to_all(final.astype(bf16), 'seq', split_axis=0, concat_axis=0, ti...  7.62 us
    unnamed x32, local copies, waits for them, and re-layouts  6.93 us
    ppermute x1, waiting for transfers between devices, by_heads(): received = lax.ppermute(sent.astype(bf16), 'tensor', pairs)  6.4 us
  transfers between devices with their start and end apart: 38, of which 17 were waited for; matrix products, arithmetic and copies ran while one was open for 9% of the time, Pallas kernels for 2%

profile of v4, /device:TPU:0, one launch (start us, length us, event | category | flops | bytes accessed | tf_op | source)
XLA Modules:
  0.0 194.9 jit_solution(16956379527206244000)
XLA Ops:
  0.7 2.0 %constant_dynamic-slice_fusion.9 = bf16[512,512]{1,0:T(8,128)(2,1)} fusion(bf16[512,2048]{1,0:T(8,128)(2,1)} %refs_8_.1, s32[]{:T(128)S(6)} %select_n.123), kind=kLoop, calls=%fused_computation.63 | loop fusion | bytes 1048580 | tf_op jit(solution)/shard_map/dynamic_slice | solution.py:588
  2.7 2.9 %collective-permute-start.7 = (bf16[512,512]{1,0:T(8,128)(2,1)}, bf16[512,512]{1,0:T(8,128)(2,1)S(1)}, u32[]{:S(2)}, u32[]{:S(2)}) collective-permute-start(bf16[512,512]{1,0:T(8,128)(2,1)} %constant_dynamic-slice_fusion.9), channel_id=1, source_target_pairs={{0,4},{4,0},{8,12},{12,8},{16,20},{20,16},{24,28},{28,24},{1,5},{5... | collective-permute-start | bytes 1572872 | tf_op jit(solution)/shard_map/ppermute | solution.py:550
  5.7 1.6 dynamic-slice_bitcast_fusion
  7.3 1.6 collective-permute-start
  8.8 2.6 %collective-permute-start.1 = (bf16[32,1024]{1,0:T(8,128)(2,1)S(1)}, bf16[32,1024]{1,0:T(8,128)(2,1)}, u32[]{:S(2)}, u32[]{:S(2)}) collective-permute-start(bf16[32,1024]{1,0:T(8,128)(2,1)S(1)} %get-tuple-element.66), channel_id=1, source_target_pairs={{0,16},{4,20},{8,24},{12,28},{16,0},{20,4},{24,8},{28,12},{1,17},{... | collective-permute-start | bytes 196616 | tf_op jit(solution)/shard_map/ppermute | solution.py:547
  20.2 1.8 collective-permute-start.4
  22.0 3.9 %collective-permute-done.6.refs_4_ = bf16[4,32,1024]{2,1,0:T(8,128)(2,1)} collective-permute-done((bf16[4,32,1024]{2,1,0:T(8,128)(2,1)S(1)}, bf16[4,32,1024]{2,1,0:T(8,128)(2,1)}, u32[]{:S(2)}, u32[]{:S(2)}) %collective-permute-start.6) | collective-permute-done | bytes 262176 | tf_op jit(solution)/shard_map/ppermute | solution.py:550
  28.4 2.2 %collective-permute-start.11 = (bf16[512,256]{1,0:T(8,128)(2,1)}, bf16[512,256]{1,0:T(8,128)(2,1)}, u32[]{:S(2)}, u32[]{:S(2)}) collective-permute-start(bf16[512,256]{1,0:T(8,128)(2,1)} %bitcast.62), channel_id=1, source_target_pairs={{0,4},{4,0},{8,12},{12,8},{16,20},{20,16},{24,28},{28,24},{1,5},{5... | collective-permute-start | bytes 786440 | tf_op jit(solution)/shard_map/ppermute | solution.py:550
  30.6 2.3 %collective-permute-done.9.refs_6_ = bf16[4,32,1024]{2,1,0:T(8,128)(2,1)} collective-permute-done((bf16[4,32,1024]{2,1,0:T(8,128)(2,1)}, bf16[4,32,1024]{2,1,0:T(8,128)(2,1)}, u32[]{:S(2)}, u32[]{:S(2)}) %collective-permute-start.9) | collective-permute-done | bytes 262176 | tf_op jit(solution)/shard_map/ppermute | solution.py:614
  35.9 2.1 %collective-permute-done.12.refs_13_ = bf16[32,512]{1,0:T(8,128)(2,1)S(1)} collective-permute-done((bf16[32,512]{1,0:T(8,128)(2,1)S(1)}, bf16[32,512]{1,0:T(8,128)(2,1)S(1)}, u32[]{:S(2)}, u32[]{:S(2)}) %collective-permute-start.12) | collective-permute-done | bytes 32800 | tf_op jit(solution)/shard_map/ppermute | solution.py:550
  38.0 1.6 copy-done.7
  40.6 5.7 %project.1 = (bf16[1056,256]{1,0:T(8,128)(2,1)}, bf16[1056,256]{1,0:T(8,128)(2,1)S(1)}, bf16[1056,256]{1,0:T(8,128)(2,1)S(1)}, bf16[1056,256]{1,0:T(8,128)(2,1)S...) custom-call(s32[7]{0:T(128)S(1)} %stack.43.place_ref, ...), custom_call_target="tpu_custom_call" | custom-call | flops 2684354560 | bytes 4194304 | tf_op jit(solution)/shard_map/project/pallas_call | solution.py:297
  47.1 1.7 collective-permute-start.17
  48.8 2.8 %collective-permute-start.19 = (bf16[1056,256]{1,0:T(8,128)(2,1)S(1)}, bf16[1056,256]{1,0:T(8,128)(2,1)S(1)}, u32[]{:S(2)}, u32[]{:S(2)}) collective-permute-start(bf16[1056,256]{1,0:T(8,128)(2,1)S(1)} %get-tuple-element.46.own_ref), channel_id=1, source_target_pairs={{0,8},{4,12},{24,16},{28,20},{1,9},{5,13},{25,17},{29,21},{2,10},{... | collective-permute-start | bytes 1622024 | tf_op jit(solution)/shard_map/ppermute | solution.py:547
  53.0 2.1 %collective-permute-start.16 = (bf16[1056,256]{1,0:T(8,128)(2,1)}, bf16[1056,256]{1,0:T(8,128)(2,1)}, u32[]{:S(2)}, u32[]{:S(2)}) collective-permute-start(bf16[1056,256]{1,0:T(8,128)(2,1)} %get-tuple-element.43.own_ref), channel_id=1, source_target_pairs={{0,8},{4,12},{24,16},{28,20},{1,9},{5,13},{25,17},{29,21},{2,10},{... | collective-permute-start | bytes 1622024 | tf_op jit(solution)/shard_map/ppermute | solution.py:547
  55.1 5.9 %collective-permute-done.17.received_ref = bf16[1056,256]{1,0:T(8,128)(2,1)S(1)} collective-permute-done((bf16[1056,256]{1,0:T(8,128)(2,1)S(1)}, bf16[1056,256]{1,0:T(8,128)(2,1)S(1)}, u32[]{:S(2)}, u32[]{:S(2)}) %collective-permute-start.17) | collective-permute-done | bytes 540704 | tf_op jit(solution)/shard_map/ppermute | solution.py:550
  64.3 2.0 %onward.4 = bf16[1056,256]{1,0:T(8,128)(2,1)} custom-call(bf16[1056,256]{1,0:T(8,128)(2,1)} %get-tuple-element.43.own_ref, bf16[1056,256]{1,0:T(8,128)(2,1)S(1)} %collective-permute-done.19.received_ref), custom_call_target="tpu_custom_call" | custom-call | flops 270336 | bytes 1622016 | tf_op jit(solution)/shard_map/onward/pallas_call | solution.py:332
  67.6 8.0 %collective-permute-done.13 = bf16[1024,256]{1,0:T(8,128)(2,1)S(1)} collective-permute-done((bf16[1024,256]{1,0:T(8,128)(2,1)S(1)}, bf16[1024,256]{1,0:T(8,128)(2,1)S(1)}, u32[]{:S(2)}, u32[]{:S(2)}) %collective-permute-start.13) | collective-permute-done | bytes 524320 | tf_op jit(solution)/shard_map/ppermute | solution.py:547
  76.8 8.4 %collective-permute-done.16.received_ref = bf16[1056,256]{1,0:T(8,128)(2,1)} collective-permute-done((bf16[1056,256]{1,0:T(8,128)(2,1)}, bf16[1056,256]{1,0:T(8,128)(2,1)}, u32[]{:S(2)}, u32[]{:S(2)}) %collective-permute-start.16) | collective-permute-done | bytes 540704 | tf_op jit(solution)/shard_map/ppermute | solution.py:547
  85.2 3.5 %collective-permute-done.18.refs_2_ = bf16[1056,256]{1,0:T(8,128)(2,1)} collective-permute-done((bf16[1056,256]{1,0:T(8,128)(2,1)}, bf16[1056,256]{1,0:T(8,128)(2,1)}, u32[]{:S(2)}, u32[]{:S(2)}) %collective-permute-start.18) | collective-permute-done | bytes 540704 | tf_op jit(solution)/shard_map/ppermute | solution.py:547
  91.7 5.3 %collective-permute-start.21 = (bf16[1056,256]{1,0:T(8,128)(2,1)}, bf16[1056,256]{1,0:T(8,128)(2,1)S(1)}, u32[]{:S(2)}, u32[]{:S(2)}) collective-permute-start(bf16[1056,256]{1,0:T(8,128)(2,1)} %onward.3), channel_id=1, source_target_pairs={{0,8},{4,12},{24,16},{28,20},{1,9},{5,13},{25,17},{29,21},{2,10},{... | collective-permute-start | bytes 1622024 | tf_op jit(solution)/shard_map/ppermute | solution.py:547
  98.7 11.4 %collective-permute-done.23.refs_8_ = bf16[1024,256]{1,0:T(8,128)(2,1)S(1)} collective-permute-done((bf16[1024,256]{1,0:T(8,128)(2,1)S(1)}, bf16[1024,256]{1,0:T(8,128)(2,1)S(1)}, u32[]{:S(2)}, u32[]{:S(2)}) %collective-permute-start.23) | collective-permute-done | bytes 524320 | tf_op jit(solution)/shard_map/ppermute | solution.py:547
  111.2 8.6 %scan.1 = bf16[1040,256]{1,0:T(8,128)(2,1)S(1)} custom-call(s32[7]{0:T(128)S(1)} %stack.43.place_ref, f32[1]{0:T(128)} %bitcast.3.scale_ref, bf16[1056,256]{1,0:T(8,128)(2,1)S(1)} %copy-done.6, bf16[1056,256]{1,0:T(8,128)(2,1)} %collective-permute-done.15.refs_1_, bf16[1056,256]{1,0:T(8,128)(2,1)} %collective-permute-done.18.refs_2_, ...), custom_call_target="tpu_custom_call" | custom-call | flops 268435456 | bytes 2097152 | tf_op jit(solution)/shard_map/scan/pallas_call | solution.py:492
  123.7 10.0 %collective-permute-done.27 = bf16[1040,256]{1,0:T(8,128)(2,1)S(1)} collective-permute-done((bf16[1040,256]{1,0:T(8,128)(2,1)S(1)}, bf16[1040,256]{1,0:T(8,128)(2,1)S(1)}, u32[]{:S(2)}, u32[]{:S(2)}) %collective-permute-start.27) | collective-permute-done | bytes 532512 | tf_op jit(solution)/shard_map/ppermute | solution.py:547
  135.7 7.3 %collective-permute-done.25 = bf16[1040,256]{1,0:T(8,128)(2,1)S(1)} collective-permute-done((bf16[1040,256]{1,0:T(8,128)(2,1)}, bf16[1040,256]{1,0:T(8,128)(2,1)S(1)}, u32[]{:S(2)}, u32[]{:S(2)}) %collective-permute-start.25) | collective-permute-done | bytes 532512 | tf_op jit(solution)/shard_map/ppermute | solution.py:547
  146.2 10.4 %collective-permute-done.29 = bf16[1040,256]{1,0:T(8,128)(2,1)S(1)} collective-permute-done((bf16[1040,256]{1,0:T(8,128)(2,1)S(1)}, bf16[1040,256]{1,0:T(8,128)(2,1)S(1)}, u32[]{:S(2)}, u32[]{:S(2)}) %collective-permute-start.29) | collective-permute-done | bytes 532512 | tf_op jit(solution)/shard_map/ppermute | solution.py:547
  156.6 1.7 collective-permute-start.32
  159.6 6.9 %collective-permute-done.32 = bf16[1040,256]{1,0:T(8,128)(2,1)S(1)} collective-permute-done((bf16[1040,256]{1,0:T(8,128)(2,1)S(1)}, bf16[1040,256]{1,0:T(8,128)(2,1)S(1)}, u32[]{:S(2)}, u32[]{:S(2)}) %collective-permute-start.32) | collective-permute-done | bytes 532512 | tf_op jit(solution)/shard_map/ppermute | solution.py:550
  170.4 1.7 add_convert_fusion.2
  174.0 6.4 %collective-permute-done.34 = bf16[256,512]{1,0:T(8,128)(2,1)S(1)} collective-permute-done((bf16[256,512]{1,0:T(8,128)(2,1)}, bf16[256,512]{1,0:T(8,128)(2,1)S(1)}, u32[]{:S(2)}, u32[]{:S(2)}) %collective-permute-start.34) | collective-permute-done | bytes 262176 | tf_op jit(solution)/shard_map/ppermute | solution.py:715
  182.2 3.7 %all-to-all-start = ((bf16[8,32,512]{2,1,0:T(8,128)(2,1)}), bf16[8,32,512]{2,1,0:T(8,128)(2,1)S(1)}, u32[]{:S(2)}, u32[]{:S(2)}) async-start(bf16[8,32,512]{2,1,0:T(8,128)(2,1)} %multiply_convert_fusion.1), calls=%async_computation | async-start | bytes 524288 | tf_op jit(solution)/shard_map/all_to_all | solution.py:721
  186.5 7.6 %all-to-all-done = bf16[8,32,512]{2,1,0:T(8,128)(2,1)S(1)} async-done(((bf16[8,32,512]{2,1,0:T(8,128)(2,1)}), bf16[8,32,512]{2,1,0:T(8,128)(2,1)S(1)}, u32[]{:S(2)}, u32[]{:S(2)}) %all-to-all-start) | async-done | bytes 262176 | tf_op jit(solution)/shard_map/all_to_all | solution.py:721
  (134 shorter events, 47.3 us)
Async XLA Ops:
  2.7 19.3 %collective-permute-start.7 = (bf16[512,512]{1,0:T(8,128)(2,1)}, bf16[512,512]{1,0:T(8,128)(2,1)S(1)}, u32[]{:S(2)}, u32[]{:S(2)}) collective-permute-start(bf16[512,512]{1,0:T(8,128)(2,1)} %constant_dynamic-slice_fusion.9), channel_id=1, source_target_pairs={{0,4},{4,0},{8,12},{12,8},{16,20},{20,16},{24,28},{28,24},{1,5},{5... | collective-permute-start | bytes 1572872 | tf_op jit(solution)/shard_map/ppermute | solution.py:550
  7.3 10.6 %collective-permute-start = (bf16[32,1024]{1,0:T(8,128)(2,1)}, bf16[32,1024]{1,0:T(8,128)(2,1)S(1)}, u32[]{:S(2)}, u32[]{:S(2)}) collective-permute-start(bf16[32,1024]{1,0:T(8,128)(2,1)} %get-tuple-element.67), channel_id=1, source_target_pairs={{0,8},{4,12},{8,0},{12,4},{16,24},{20,28},{24,16},{28,20},{1,9},{5... | collective-permute-start | bytes 196616 | tf_op jit(solution)/shard_map/ppermute | solution.py:547
  8.8 9.0 %collective-permute-start.1 = (bf16[32,1024]{1,0:T(8,128)(2,1)S(1)}, bf16[32,1024]{1,0:T(8,128)(2,1)}, u32[]{:S(2)}, u32[]{:S(2)}) collective-permute-start(bf16[32,1024]{1,0:T(8,128)(2,1)S(1)} %get-tuple-element.66), channel_id=1, source_target_pairs={{0,16},{4,20},{8,24},{12,28},{16,0},{20,4},{24,8},{28,12},{1,17},{... | collective-permute-start | bytes 196616 | tf_op jit(solution)/shard_map/ppermute | solution.py:547
  11.4 6.4 %collective-permute-start.2 = (bf16[32,1024]{1,0:T(8,128)(2,1)S(1)}, bf16[32,1024]{1,0:T(8,128)(2,1)}, u32[]{:S(2)}, u32[]{:S(2)}) collective-permute-start(bf16[32,1024]{1,0:T(8,128)(2,1)S(1)} %get-tuple-element.65), channel_id=1, source_target_pairs={{0,24},{4,28},{8,16},{12,20},{16,8},{20,12},{24,0},{28,4},{1,25},{... | collective-permute-start | bytes 196616 | tf_op jit(solution)/shard_map/ppermute | solution.py:547
  18.8 7.2 %collective-permute-start.6 = (bf16[4,32,1024]{2,1,0:T(8,128)(2,1)S(1)}, bf16[4,32,1024]{2,1,0:T(8,128)(2,1)}, u32[]{:S(2)}, u32[]{:S(2)}) collective-permute-start(bf16[4,32,1024]{2,1,0:T(8,128)(2,1)S(1)} %pad_maximum_fusion.refs_0_), channel_id=1, source_target_pairs={{0,4},{4,0},{8,12},{12,8},{16,20},{20,16},{24,28},{28,24},{1,5},{5... | collective-permute-start | bytes 786440 | tf_op jit(solution)/shard_map/ppermute | solution.py:550
  20.2 7.7 %collective-permute-start.4 = (bf16[4,32,1024]{2,1,0:T(8,128)(2,1)S(1)}, bf16[4,32,1024]{2,1,0:T(8,128)(2,1)}, u32[]{:S(2)}, u32[]{:S(2)}) collective-permute-start(bf16[4,32,1024]{2,1,0:T(8,128)(2,1)S(1)} %pad_maximum_fusion.refs_0_), channel_id=1, source_target_pairs={{0,2},{1,3},{2,0},{3,1},{4,6},{5,7},{6,4},{7,5},{8,10},{9,11},{10,... | collective-permute-start | bytes 786440 | tf_op jit(solution)/shard_map/ppermute | solution.py:614
  25.9 7.0 %collective-permute-start.9 = (bf16[4,32,1024]{2,1,0:T(8,128)(2,1)}, bf16[4,32,1024]{2,1,0:T(8,128)(2,1)}, u32[]{:S(2)}, u32[]{:S(2)}) collective-permute-start(bf16[4,32,1024]{2,1,0:T(8,128)(2,1)} %collective-permute-done.6.refs_4_), channel_id=1, source_target_pairs={{0,2},{1,3},{2,0},{3,1},{4,6},{5,7},{6,4},{7,5},{8,10},{9,11},{10,... | collective-permute-start | bytes 786440 | tf_op jit(solution)/shard_map/ppermute | solution.py:614
  27.4 5.5 %collective-permute-start.3 = (bf16[4,32,1024]{2,1,0:T(8,128)(2,1)S(1)}, bf16[4,32,1024]{2,1,0:T(8,128)(2,1)S(1)}, u32[]{:S(2)}, u32[]{:S(2)}) collective-permute-start(bf16[4,32,1024]{2,1,0:T(8,128)(2,1)S(1)} %pad_maximum_fusion.refs_0_), channel_id=1, source_target_pairs={{0,1},{1,0},{2,3},{3,2},{4,5},{5,4},{6,7},{7,6},{8,9},{9,8},{10,11... | collective-permute-start | bytes 786440 | tf_op jit(solution)/shard_map/ppermute | solution.py:614
  27.9 10.1 %collective-permute-start.5 = (bf16[4,32,1024]{2,1,0:T(8,128)(2,1)}, bf16[4,32,1024]{2,1,0:T(8,128)(2,1)}, u32[]{:S(2)}, u32[]{:S(2)}) collective-permute-start(bf16[4,32,1024]{2,1,0:T(8,128)(2,1)} %collective-permute-done.4.refs_2_), channel_id=1, source_target_pairs={{0,1},{1,0},{2,3},{3,2},{4,5},{5,4},{6,7},{7,6},{8,9},{9,8},{10,11... | collective-permute-start | bytes 786440 | tf_op jit(solution)/shard_map/ppermute | solution.py:614
  28.0 10.1 %collective-permute-start.8 = (bf16[4,32,1024]{2,1,0:T(8,128)(2,1)}, bf16[4,32,1024]{2,1,0:T(8,128)(2,1)}, u32[]{:S(2)}, u32[]{:S(2)}) collective-permute-start(bf16[4,32,1024]{2,1,0:T(8,128)(2,1)} %collective-permute-done.6.refs_4_), channel_id=1, source_target_pairs={{0,1},{1,0},{2,3},{3,2},{4,5},{5,4},{6,7},{7,6},{8,9},{9,8},{10,11... | collective-permute-start | bytes 786440 | tf_op jit(solution)/shard_map/ppermute | solution.py:614
  28.4 9.6 %collective-permute-start.11 = (bf16[512,256]{1,0:T(8,128)(2,1)}, bf16[512,256]{1,0:T(8,128)(2,1)}, u32[]{:S(2)}, u32[]{:S(2)}) collective-permute-start(bf16[512,256]{1,0:T(8,128)(2,1)} %bitcast.62), channel_id=1, source_target_pairs={{0,4},{4,0},{8,12},{12,8},{16,20},{20,16},{24,28},{28,24},{1,5},{5... | collective-permute-start | bytes 786440 | tf_op jit(solution)/shard_map/ppermute | solution.py:550
  47.1 13.9 %collective-permute-start.17 = (bf16[1056,256]{1,0:T(8,128)(2,1)S(1)}, bf16[1056,256]{1,0:T(8,128)(2,1)S(1)}, u32[]{:S(2)}, u32[]{:S(2)}) collective-permute-start(bf16[1056,256]{1,0:T(8,128)(2,1)S(1)} %get-tuple-element.45), channel_id=1, source_target_pairs={{0,4},{4,0},{8,12},{12,8},{16,20},{20,16},{24,28},{28,24},{1,5},{5... | collective-permute-start | bytes 1622024 | tf_op jit(solution)/shard_map/ppermute | solution.py:550
  48.8 15.5 %collective-permute-start.19 = (bf16[1056,256]{1,0:T(8,128)(2,1)S(1)}, bf16[1056,256]{1,0:T(8,128)(2,1)S(1)}, u32[]{:S(2)}, u32[]{:S(2)}) collective-permute-start(bf16[1056,256]{1,0:T(8,128)(2,1)S(1)} %get-tuple-element.46.own_ref), channel_id=1, source_target_pairs={{0,8},{4,12},{24,16},{28,20},{1,9},{5,13},{25,17},{29,21},{2,10},{... | collective-permute-start | bytes 1622024 | tf_op jit(solution)/shard_map/ppermute | solution.py:547
  51.7 23.9 %collective-permute-start.13 = (bf16[1024,256]{1,0:T(8,128)(2,1)S(1)}, bf16[1024,256]{1,0:T(8,128)(2,1)S(1)}, u32[]{:S(2)}, u32[]{:S(2)}) collective-permute-start(bf16[1024,256]{1,0:T(8,128)(2,1)S(1)} %get-tuple-element.41), channel_id=1, source_target_pairs={{0,8},{4,12},{24,16},{28,20},{1,9},{5,13},{25,17},{29,21},{2,10},{... | collective-permute-start | bytes 1572872 | tf_op jit(solution)/shard_map/ppermute | solution.py:547
  53.0 32.2 %collective-permute-start.16 = (bf16[1056,256]{1,0:T(8,128)(2,1)}, bf16[1056,256]{1,0:T(8,128)(2,1)}, u32[]{:S(2)}, u32[]{:S(2)}) collective-permute-start(bf16[1056,256]{1,0:T(8,128)(2,1)} %get-tuple-element.43.own_ref), channel_id=1, source_target_pairs={{0,8},{4,12},{24,16},{28,20},{1,9},{5,13},{25,17},{29,21},{2,10},{... | collective-permute-start | bytes 1622024 | tf_op jit(solution)/shard_map/ppermute | solution.py:547
  61.9 26.8 %collective-permute-start.18 = (bf16[1056,256]{1,0:T(8,128)(2,1)}, bf16[1056,256]{1,0:T(8,128)(2,1)}, u32[]{:S(2)}, u32[]{:S(2)}) collective-permute-start(bf16[1056,256]{1,0:T(8,128)(2,1)} %onward.3), channel_id=1, source_target_pairs={{8,0},{12,4},{16,24},{20,28},{9,1},{13,5},{17,25},{21,29},{10,2},{... | collective-permute-start | bytes 1622024 | tf_op jit(solution)/shard_map/ppermute | solution.py:547
  66.3 25.4 %collective-permute-start.20 = (bf16[1056,256]{1,0:T(8,128)(2,1)}, bf16[1056,256]{1,0:T(8,128)(2,1)}, u32[]{:S(2)}, u32[]{:S(2)}) collective-permute-start(bf16[1056,256]{1,0:T(8,128)(2,1)} %onward.4), channel_id=1, source_target_pairs={{8,24},{12,28},{16,0},{20,4},{9,25},{13,29},{17,1},{21,5},{10,26},... | collective-permute-start | bytes 1622024 | tf_op jit(solution)/shard_map/ppermute | solution.py:547
  75.7 21.3 %collective-permute-start.14 = (bf16[1024,256]{1,0:T(8,128)(2,1)S(1)}, bf16[1024,256]{1,0:T(8,128)(2,1)S(1)}, u32[]{:S(2)}, u32[]{:S(2)}) collective-permute-start(bf16[1024,256]{1,0:T(8,128)(2,1)S(1)} %add_convert_fusion.1.refs_6_), channel_id=1, source_target_pairs={{8,16},{12,20},{16,8},{20,12},{9,17},{13,21},{17,9},{21,13},{10,18... | collective-permute-start | bytes 1572872 | tf_op jit(solution)/shard_map/ppermute | solution.py:547
  76.4 20.8 %collective-permute-start.15 = (bf16[1056,256]{1,0:T(8,128)(2,1)}, bf16[1056,256]{1,0:T(8,128)(2,1)}, u32[]{:S(2)}, u32[]{:S(2)}) collective-permute-start(bf16[1056,256]{1,0:T(8,128)(2,1)} %get-tuple-element.42), channel_id=1, source_target_pairs={{0,4},{4,0},{8,12},{12,8},{16,20},{20,16},{24,28},{28,24},{1,5},{5... | collective-permute-start | bytes 1622024 | tf_op jit(solution)/shard_map/ppermute | solution.py:550
  91.0 19.1 %collective-permute-start.22 = (bf16[1056,256]{1,0:T(8,128)(2,1)S(1)}, bf16[1056,256]{1,0:T(8,128)(2,1)S(1)}, u32[]{:S(2)}, u32[]{:S(2)}) collective-permute-start(bf16[1056,256]{1,0:T(8,128)(2,1)S(1)} %onward.5), channel_id=1, source_target_pairs={{8,16},{12,20},{16,8},{20,12},{9,17},{13,21},{17,9},{21,13},{10,18... | collective-permute-start | bytes 1622024 | tf_op jit(solution)/shard_map/ppermute | solution.py:547
  91.7 18.4 %collective-permute-start.21 = (bf16[1056,256]{1,0:T(8,128)(2,1)}, bf16[1056,256]{1,0:T(8,128)(2,1)S(1)}, u32[]{:S(2)}, u32[]{:S(2)}) collective-permute-start(bf16[1056,256]{1,0:T(8,128)(2,1)} %onward.3), channel_id=1, source_target_pairs={{0,8},{4,12},{24,16},{28,20},{1,9},{5,13},{25,17},{29,21},{2,10},{... | collective-permute-start | bytes 1622024 | tf_op jit(solution)/shard_map/ppermute | solution.py:547
  97.2 12.9 %collective-permute-start.23 = (bf16[1024,256]{1,0:T(8,128)(2,1)S(1)}, bf16[1024,256]{1,0:T(8,128)(2,1)S(1)}, u32[]{:S(2)}, u32[]{:S(2)}) collective-permute-start(bf16[1024,256]{1,0:T(8,128)(2,1)S(1)} %multiply_convert_fusion), channel_id=1, source_target_pairs={{8,0},{12,4},{16,24},{20,28},{9,1},{13,5},{17,25},{21,29},{10,2},{... | collective-permute-start | bytes 1572872 | tf_op jit(solution)/shard_map/ppermute | solution.py:547
  121.3 12.5 %collective-permute-start.27 = (bf16[1040,256]{1,0:T(8,128)(2,1)S(1)}, bf16[1040,256]{1,0:T(8,128)(2,1)S(1)}, u32[]{:S(2)}, u32[]{:S(2)}) collective-permute-start(bf16[1040,256]{1,0:T(8,128)(2,1)S(1)} %scan.1), channel_id=1, source_target_pairs={{0,8},{4,12},{8,0},{12,4},{16,24},{20,28},{24,16},{28,20},{1,9},{5... | collective-permute-start | bytes 1597448 | tf_op jit(solution)/shard_map/ppermute | solution.py:547
  121.6 21.4 %collective-permute-start.26 = (bf16[1040,256]{1,0:T(8,128)(2,1)S(1)}, bf16[1040,256]{1,0:T(8,128)(2,1)S(1)}, u32[]{:S(2)}, u32[]{:S(2)}) collective-permute-start(bf16[1040,256]{1,0:T(8,128)(2,1)S(1)} %scan.1), channel_id=1, source_target_pairs={{0,4},{4,0},{8,12},{12,8},{16,20},{20,16},{24,28},{28,24},{1,5},{5... | collective-permute-start | bytes 1597448 | tf_op jit(solution)/shard_map/ppermute | solution.py:550
  122.4 20.6 %collective-permute-start.25 = (bf16[1040,256]{1,0:T(8,128)(2,1)}, bf16[1040,256]{1,0:T(8,128)(2,1)S(1)}, u32[]{:S(2)}, u32[]{:S(2)}) collective-permute-start(bf16[1040,256]{1,0:T(8,128)(2,1)} %collective-permute-done.24), channel_id=1, source_target_pairs={{8,0},{12,4},{16,24},{20,28},{9,1},{13,5},{17,25},{21,29},{10,2},{... | collective-permute-start | bytes 1597448 | tf_op jit(solution)/shard_map/ppermute | solution.py:547
  133.7 10.2 %collective-permute-start.28 = (bf16[1040,256]{1,0:T(8,128)(2,1)S(1)}, bf16[1040,256]{1,0:T(8,128)(2,1)S(1)}, u32[]{:S(2)}, u32[]{:S(2)}) collective-permute-start(bf16[1040,256]{1,0:T(8,128)(2,1)S(1)} %collective-permute-done.27), channel_id=1, source_target_pairs={{8,16},{12,20},{16,8},{20,12},{9,17},{13,21},{17,9},{21,13},{10,18... | collective-permute-start | bytes 1597448 | tf_op jit(solution)/shard_map/ppermute | solution.py:547
  134.4 22.2 %collective-permute-start.30 = (bf16[1040,256]{1,0:T(8,128)(2,1)S(1)}, bf16[1040,256]{1,0:T(8,128)(2,1)S(1)}, u32[]{:S(2)}, u32[]{:S(2)}) collective-permute-start(bf16[1040,256]{1,0:T(8,128)(2,1)S(1)} %collective-permute-done.27), channel_id=1, source_target_pairs={{0,4},{4,0},{8,12},{12,8},{16,20},{20,16},{24,28},{28,24},{1,5},{5... | collective-permute-start | bytes 1597448 | tf_op jit(solution)/shard_map/ppermute | solution.py:550
  143.0 15.3 %collective-permute-start.31 = (bf16[1040,256]{1,0:T(8,128)(2,1)S(1)}, bf16[1040,256]{1,0:T(8,128)(2,1)S(1)}, u32[]{:S(2)}, u32[]{:S(2)}) collective-permute-start(bf16[1040,256]{1,0:T(8,128)(2,1)S(1)} %broadcast_select_fusion.1), channel_id=1, source_target_pairs={{0,4},{4,0},{8,12},{12,8},{16,20},{20,16},{24,28},{28,24},{1,5},{5... | collective-permute-start | bytes 1597448 | tf_op jit(solution)/shard_map/ppermute | solution.py:550
  144.0 12.6 %collective-permute-start.29 = (bf16[1040,256]{1,0:T(8,128)(2,1)S(1)}, bf16[1040,256]{1,0:T(8,128)(2,1)S(1)}, u32[]{:S(2)}, u32[]{:S(2)}) collective-permute-start(bf16[1040,256]{1,0:T(8,128)(2,1)S(1)} %collective-permute-done.28), channel_id=1, source_target_pairs={{8,0},{12,4},{16,24},{20,28},{9,1},{13,5},{17,25},{21,29},{10,2},{... | collective-permute-start | bytes 1597448 | tf_op jit(solution)/shard_map/ppermute | solution.py:547
  156.6 9.9 %collective-permute-start.32 = (bf16[1040,256]{1,0:T(8,128)(2,1)S(1)}, bf16[1040,256]{1,0:T(8,128)(2,1)S(1)}, u32[]{:S(2)}, u32[]{:S(2)}) collective-permute-start(bf16[1040,256]{1,0:T(8,128)(2,1)S(1)} %broadcast_select_fusion), channel_id=1, source_target_pairs={{0,4},{4,0},{8,12},{12,8},{16,20},{20,16},{24,28},{28,24},{1,5},{5... | collective-permute-start | bytes 1597448 | tf_op jit(solution)/shard_map/ppermute | solution.py:550
  172.1 8.3 %collective-permute-start.34 = (bf16[256,512]{1,0:T(8,128)(2,1)}, bf16[256,512]{1,0:T(8,128)(2,1)S(1)}, u32[]{:S(2)}, u32[]{:S(2)}) collective-permute-start(bf16[256,512]{1,0:T(8,128)(2,1)} %add_convert_fusion.2), channel_id=1, source_target_pairs={{0,2},{1,3},{2,0},{3,1},{4,6},{5,7},{6,4},{7,5},{8,10},{9,11},{10,... | collective-permute-start | bytes 786440 | tf_op jit(solution)/shard_map/ppermute | solution.py:715
  182.2 11.9 %all-to-all-start = ((bf16[8,32,512]{2,1,0:T(8,128)(2,1)}), bf16[8,32,512]{2,1,0:T(8,128)(2,1)S(1)}, u32[]{:S(2)}, u32[]{:S(2)}) async-start(bf16[8,32,512]{2,1,0:T(8,128)(2,1)} %multiply_convert_fusion.1), calls=%async_computation | async-start | bytes 524288 | tf_op jit(solution)/shard_map/all_to_all | solution.py:721
  (19 other events, 288.8 us)

commit v5 on v1

--- a/solution.py
+++ b/solution.py
@@ -350,10 +350,12 @@
 
 
 def scan_kernel(place_ref, scale_ref, *refs):
-    x_refs, bc_refs = (refs[:-9], refs[-9:-6])
-    small_ref, largest_ref, state_ref, out_ref, x_buf, bc_buf = refs[-6:]
+    x_refs, bc_refs = (refs[:-10], refs[-10:-7])
+    small_ref, largest_ref, state_ref = refs[-7:-4]
+    out_refs, x_buf, bc_buf = (refs[-4:-2], *refs[-2:])
     tokens, channels = bc_refs[0].shape
     blocks = tokens // SPAN
+    run_blocks = blocks // CUTS
     heads = channels // HEAD_DIM
     rank, z = (place_ref[0], place_ref[2])
     ranks = place_ref.shape[0] - 3
@@ -472,7 +474,8 @@
         state = grown[SPAN - 1 : SPAN] * state + added
         gained = (ssm_out * gain).astype(jnp.bfloat16)
         for true_rank in range(ranks):
-            at = (turned_rank(true_rank, ranks) * blocks + block) * own
+            at = (turned_rank(true_rank, ranks) * run_blocks + block % run_blocks) * own
+            out_ref = out_refs[block // run_blocks]
             out_ref[at : at + own] = gained[true_rank * own : (true_rank + 1) * own]
         summed = jnp.sum(ssm_out * ssm_out, axis=1, keepdims=True)
         sums = jnp.where(across == block, summed, sums)
@@ -481,23 +484,26 @@
     top = whole.astype(jnp.bfloat16).astype(jnp.float32)
     largest = jnp.broadcast_to(jnp.max(largest_ref[...]), (ROWS, channels))
     extra = jnp.concatenate([jnp.concatenate([top, whole - top], axis=1), largest], axis=0)
-    out_ref[tokens:] = extra.astype(jnp.bfloat16)
+    out_refs[-1][tokens // CUTS :] = extra.astype(jnp.bfloat16)
 
 
 def scan(place, in_scale, sums, maps, small, largest, state):
     channels = sums[0].shape[1]
     tokens = maps[0].shape[0]
 
-    out = jax.ShapeDtypeStruct((tokens + 2 * ROWS, channels), jnp.bfloat16)
+    outs = [
+        jax.ShapeDtypeStruct((tokens // CUTS + 2 * ROWS * last, channels), jnp.bfloat16)
+        for last in (False, True)
+    ]
     return pl.pallas_call(
         scan_kernel,
         in_specs=[SMEM, SMEM] + [VMEM] * (len(sums) + len(maps) + 3),
-        out_specs=VMEM,
+        out_specs=[VMEM] * len(outs),
         scratch_shapes=[
             pltpu.VMEM((tokens + ROWS, channels), jnp.float32),
             pltpu.VMEM((tokens + ROWS, 2 * STATE), jnp.float32),
         ],
-        out_shape=out,
+        out_shape=outs,
         compiler_params=pltpu.CompilerParams(vmem_limit_bytes=20 * 2**20),
         cost_estimate=pl.CostEstimate(
             flops=8 * tokens * SPAN * channels,
@@ -653,71 +659,88 @@
         start_state,
     )
 
-    tokens = gained.shape[0] - 2 * ROWS
-    beside = along(gained, beside_pairs)
-    facing = along(gained, middle)
-    second = jnp.where(at_end, along(facing, outward), facing)
-    beyond = along(beside, middle)
-    third = jnp.where(at_end, along(beyond, outward), beyond)
-    far_own = across(gained)
-    far_beside = across(beside)
-    second, far_own = tie((second, far_own))
-    far_second = across(second)
-    third, far_beside = tie((third, far_beside))
-    far_third = across(third)
+    run = maps.shape[0] // CUTS
     two, three = (jnp.where(at_end, 2, 3), jnp.where(at_end, 3, 2))
 
     def rows_for(x, m):
         at = ((side ^ x) * LINE + (z ^ m)) * channels
         return lax.dynamic_slice_in_dim(w_out, at, channels, axis=0)
 
-    total = None
-    tails = [far_third[tokens:]]
-    for x, m, piece in (
-        (0, 0, gained),
-        (1, 0, far_own),
-        (0, 1, beside),
-        (1, 1, far_beside),
-        (0, two, second),
-        (1, two, far_second),
-        (0, three, third),
-    ):
-        product = jnp.dot(piece, rows_for(x, m), preferred_element_type=f32)
-        total = product if total is None else total + product
-        tails.append(piece[tokens:])
-    total, far_third = tie((total, far_third))
-    last_rows = rows_for(1, three)
-    tails = [tail.astype(f32) for tail in tails]
+    def gather(block):
+        beside = along(block, beside_pairs)
+        facing = along(block, middle)
+        outer = along(facing, outward)
+        second = jnp.where(at_end, outer, facing)
+        beyond = along(beside, middle)
+        beyond, unused = tie((beyond, outer))
+        third = jnp.where(at_end, along(beyond, outward), beyond)
+        far_own = across(block)
+        far_beside = across(beside)
+        second, far_own = tie((second, far_own))
+        far_second = across(second)
+        third, far_beside = tie((third, far_beside))
+        far_third = across(third)
+        return (
+            (0, 0, block),
+            (1, 0, far_own),
+            (0, 1, beside),
+            (1, 1, far_beside),
+            (0, two, second),
+            (1, two, far_second),
+            (0, three, third),
+            (1, three, far_third),
+        )
+
+    def run_of(array, index, length):
+        return lax.dynamic_slice_in_dim(array, index * length, length, axis=0)
+
+    def reduced(pieces, after):
+        total = None
+        for x, m, piece in pieces[:-1]:
+            product = jnp.dot(piece, rows_for(x, m), preferred_element_type=f32)
+            total = product if total is None else total + product
+        x, m, last = pieces[-1]
+        total, last, unused = tie((total, last, after))
+        length = run // 2
+
+        def first_sum(index):
+            product = jnp.dot(
+                run_of(last, index, length), rows_for(x, m), preferred_element_type=f32
+            )
+            return run_of(total, index, length) + product
+
+        keeps = rank % 2
+        pairs = [(t, t ^ 1) for t in range(ranks)]
+        received = lax.ppermute(first_sum(1 - keeps).astype(bf16), "tensor", pairs)
+        kept = first_sum(keeps)
+        bit = 2
+        while bit < ranks:
+            length //= 2
+            keeps = (rank // bit) % 2
+            pairs = [(t, t ^ bit) for t in range(ranks)]
+            sent = run_of(kept, 1 - keeps, length) + run_of(received, 1 - keeps, length)
+            kept = run_of(kept, keeps, length) + run_of(received, keeps, length)
+            sent = sent.astype(bf16)
+            received = lax.ppermute(sent, "tensor", pairs)
+            bit *= 2
+        return kept, received, sent
+
+    gathered = [gather(block) for block in gained]
+    halves = []
+    for pieces in gathered:
+        halves.append(reduced(pieces, halves[-1][-1] if halves else ()))
+    tails = [piece[run:].astype(f32) for x, m, piece in gathered[-1]]
     squares = sum(tail[:ROWS, :SPAN] + tail[:ROWS, SPAN:] for tail in tails)
     top = functools.reduce(jnp.maximum, [tail[ROWS:, :SPAN] for tail in tails])
-
-    def run_of(array, index, run):
-        return lax.dynamic_slice_in_dim(array, index * run, run, axis=0)
-
-    def first_sum(index):
-        block, so_far = (run_of(far_third, index, run), run_of(total, index, run))
-        return so_far + jnp.dot(block, last_rows, preferred_element_type=f32)
-
-    run = tokens // 2
-    keeps = rank % 2
-    pairs = [(t, t ^ 1) for t in range(ranks)]
-    received = lax.ppermute(first_sum(1 - keeps).astype(bf16), "tensor", pairs)
-    kept = first_sum(keeps)
-    squares = squares + lax.ppermute(squares, "tensor", pairs)
-    bit = 2
+    bit = 1
     while bit < ranks:
-        run //= 2
-        keeps = (rank // bit) % 2
-        pairs = [(t, t ^ bit) for t in range(ranks)]
-        sent = run_of(kept, 1 - keeps, run) + run_of(received, 1 - keeps, run).astype(f32)
-        kept = run_of(kept, keeps, run) + run_of(received, keeps, run).astype(f32)
-        received = lax.ppermute(sent.astype(bf16), "tensor", pairs)
-        squares = squares + lax.ppermute(squares, "tensor", pairs)
+        squares = squares + lax.ppermute(squares, "tensor", [(t, t ^ bit) for t in range(ranks)])
         bit *= 2
     mean_sq = squares.reshape(count, ranks, own) / (HEADS * HEAD_DIM)
-    factors = lax.rsqrt(pick(mean_sq, 1, rank) + epsilon)
-    final = (kept + received.astype(f32)).reshape(count, own, -1) * factors[:, :, None]
-    final = lax.all_to_all(final.astype(bf16), "seq", split_axis=0, concat_axis=0, tiled=True)
+    factors = lax.rsqrt(pick(mean_sq, 1, rank) + epsilon)[:, :, None]
+    final = jnp.concatenate([kept + received.astype(f32) for kept, received, _ in halves], axis=0)
+    final = (final.reshape(count, own, -1) * factors).astype(bf16)
+    final = lax.all_to_all(final, "seq", split_axis=0, concat_axis=0, tiled=True)
     layer_out = final.transpose(1, 0, 2).reshape(own, count * final.shape[2])
     return (layer_out, jnp.max(top))
 

time: 194 us -> 217 us (1.12)
  starting transfers between devices: 52.8 us -> 65.6 us
  local copies, waits for them, and re-layouts: 15.6 us -> 22 us
  matrix products: 3.68 us -> 6.8 us
  waiting for transfers between devices: 91.8 us -> 89.6 us
    ppermute x10 -> x14, waiting for transfers between devices: 20 us -> 12.4 us  [across(): return lax.ppermute(value, 'seq', [(s, s ^ 1) for s in range(count)])]
    ppermute x17 -> x22, starting transfers between devices: 27 us -> 33.3 us  [along(): return lax.ppermute(value, 'seq', moves)]
    ppermute x6, waiting for transfers between devices: 2.75 us -> 6.99 us  [by_heads(): ours.append(lax.ppermute(ours[j - bit], 'tensor', pairs))]
    concatenate x1, local copies, waits for them, and re-layouts: 0.08 us -> 3.68 us  [by_heads(): jnp.concatenate([blank, by_channel[:margin], blank, by_map[:margin], by_c...]
    ppermute x10 -> x14, starting transfers between devices: 15.4 us -> 18.8 us  [across(): return lax.ppermute(value, 'seq', [(s, s ^ 1) for s in range(count)])]
    ppermute x17 -> x22, waiting for transfers between devices: 54 us -> 57.4 us  [along(): return lax.ppermute(value, 'seq', moves)]
    dot_general x9 -> x18, matrix products: 3.68 us -> 6.8 us  [the longest x14 5.17 us: reduced(): product = jnp.dot(piece, rows_for(x, m), preferred_element_type=f32)]
    ppermute x4 -> x6, waiting for transfers between devices: 7.45 us -> 5.6 us  [the longest x2 4.3 us: reduced(): received = lax.ppermute(sent, 'tensor', pairs)]
  transfers between devices with their start and end apart: 38 -> 49, of which waited for: 18 -> 22; matrix products, arithmetic and copies ran while one was open for 9% -> 14% of each run, Pallas kernels for 2% -> 2%
where the time goes in v5:
time: 217 us; the launch traced here: 215 us
  waiting for transfers between devices  89.6 us (41%)
  starting transfers between devices  65.6 us (30%)
  local copies, waits for them, and re-layouts  22 us (10%)
  Pallas kernels  18.6 us (9%)
  other arithmetic  10.8 us (5%)
  matrix products  6.8 us (3%)
    ppermute x22, waiting for transfers between devices, along(): return lax.ppermute(value, 'seq', moves)  57.4 us
    ppermute x22, starting transfers between devices, along(): return lax.ppermute(value, 'seq', moves)  33.3 us
    ppermute x14, starting transfers between devices, across(): return lax.ppermute(value, 'seq', [(s, s ^ 1) for s in range(count)])  18.8 us
    ppermute x14, waiting for transfers between devices, across(): return lax.ppermute(value, 'seq', [(s, s ^ 1) for s in range(count)])  12.4 us
    pallas_call x1, Pallas kernels, scan(): pl.pallas_call(scan_kernel, in_specs=[SMEM, SMEM] + [VMEM] * (len(sums) +...  8.91 us
    unnamed x38, local copies, waits for them, and re-layouts  8.48 us
    all_to_all x1, waiting for transfers between devices, by_heads(): lax.all_to_all(final, 'seq', split_axis=0, concat_axis=0, tiled=True)  7.21 us
    ppermute x6, waiting for transfers between devices, by_heads(): ours.append(lax.ppermute(ours[j - bit], 'tensor', pairs))  6.99 us
  transfers between devices with their start and end apart: 49, of which 22 were waited for; matrix products, arithmetic and copies ran while one was open for 14% of the time, Pallas kernels for 2%

profile of v5, /device:TPU:0, one launch (start us, length us, event | category | flops | bytes accessed | tf_op | source)
XLA Modules:
  0.0 215.3 jit_solution(9144253218101528536)
XLA Ops:
  0.7 2.0 constant_dynamic-slice_fusion.9
  2.7 2.9 %collective-permute-start.7 = (bf16[512,512]{1,0:T(8,128)(2,1)}, bf16[512,512]{1,0:T(8,128)(2,1)S(1)}, u32[]{:S(2)}, u32[]{:S(2)}) collective-permute-start(bf16[512,512]{1,0:T(8,128)(2,1)} %constant_dynamic-slice_fusion.9), channel_id=1, source_target_pairs={{0,4},{4,0},{8,12},{12,8},{16,20},{20,16},{24,28},{28,24},{1,5},{5... | collective-permute-start | bytes 1572872 | tf_op jit(solution)/shard_map/ppermute | solution.py:556
  8.3 2.6 %collective-permute-start.1 = (bf16[32,1024]{1,0:T(8,128)(2,1)S(1)}, bf16[32,1024]{1,0:T(8,128)(2,1)S(1)}, u32[]{:S(2)}, u32[]{:S(2)}) collective-permute-start(bf16[32,1024]{1,0:T(8,128)(2,1)S(1)} %get-tuple-element.84), channel_id=1, source_target_pairs={{0,16},{4,20},{8,24},{12,28},{16,0},{20,4},{24,8},{28,12},{1,17},{... | collective-permute-start | bytes 196616 | tf_op jit(solution)/shard_map/ppermute | solution.py:553
  22.3 3.7 %concatenate.15.refs_9_ = f32[40,256]{1,0:T(8,128)} concatenate(f32[5,256]{1,0:T(8,128)S(1)} %broadcast_in_dim.16, f32[3,256]{1,0:T(4,128)S(1)} %slice.156, f32[5,256]{1,0:T(8,128)S(1)} %broadcast_in_dim.16, f32[3,256]{1,0:T(4,128)S(1)} %bitcast.74, f32[4,256]{1,0:T(4,128)S(1)} %slice.158, f32[4,256]{1,0:T(4,128)S(1)} %bitcast.75, f32[2,256]{1,0:T(2,128)} %slice.160, ...), dimensions={0} | concatenate | bytes 81920 | tf_op jit(solution)/shard_map/concatenate | solution.py:571
  26.9 1.8 collective-permute-start.4
  30.4 5.9 %collective-permute-done.4.refs_2_ = bf16[4,32,1024]{2,1,0:T(8,128)(2,1)} collective-permute-done((bf16[4,32,1024]{2,1,0:T(8,128)(2,1)S(1)}, bf16[4,32,1024]{2,1,0:T(8,128)(2,1)}, u32[]{:S(2)}, u32[]{:S(2)}) %collective-permute-start.4) | collective-permute-done | bytes 262176 | tf_op jit(solution)/shard_map/ppermute | solution.py:620
  36.8 1.7 collective-permute-start.11
  42.6 3.5 %collective-permute-done.12.refs_13_ = bf16[32,512]{1,0:T(8,128)(2,1)} collective-permute-done((bf16[32,512]{1,0:T(8,128)(2,1)}, bf16[32,512]{1,0:T(8,128)(2,1)}, u32[]{:S(2)}, u32[]{:S(2)}) %collective-permute-start.12) | collective-permute-done | bytes 32800 | tf_op jit(solution)/shard_map/ppermute | solution.py:556
  49.4 5.6 %project.1 = (bf16[1056,256]{1,0:T(8,128)(2,1)}, bf16[1056,256]{1,0:T(8,128)(2,1)S(1)}, bf16[1056,256]{1,0:T(8,128)(2,1)S(1)}, bf16[1056,256]{1,0:T(8,128)(2,1)S...) custom-call(s32[7]{0:T(128)S(1)} %stack.43.place_ref, ...), custom_call_target="tpu_custom_call" | custom-call | flops 2684354560 | bytes 4194304 | tf_op jit(solution)/shard_map/project/pallas_call | solution.py:297
  55.0 1.7 collective-permute-start.19
  56.7 2.6 %collective-permute-start.13 = (bf16[1024,256]{1,0:T(8,128)(2,1)S(1)}, bf16[1024,256]{1,0:T(8,128)(2,1)S(1)}, u32[]{:S(2)}, u32[]{:S(2)}) collective-permute-start(bf16[1024,256]{1,0:T(8,128)(2,1)S(1)} %get-tuple-element.50), channel_id=1, source_target_pairs={{0,8},{4,12},{24,16},{28,20},{1,9},{5,13},{25,17},{29,21},{2,10},{... | collective-permute-start | bytes 1572872 | tf_op jit(solution)/shard_map/ppermute | solution.py:553
  60.7 2.1 collective-permute-start.18
  62.8 5.5 %collective-permute-done.19.received_ref = bf16[1056,256]{1,0:T(8,128)(2,1)S(1)} collective-permute-done((bf16[1056,256]{1,0:T(8,128)(2,1)S(1)}, bf16[1056,256]{1,0:T(8,128)(2,1)S(1)}, u32[]{:S(2)}, u32[]{:S(2)}) %collective-permute-start.19) | collective-permute-done | bytes 540704 | tf_op jit(solution)/shard_map/ppermute | solution.py:556
  73.2 10.0 %collective-permute-done.15.received_ref = bf16[1056,256]{1,0:T(8,128)(2,1)S(1)} collective-permute-done((bf16[1056,256]{1,0:T(8,128)(2,1)S(1)}, bf16[1056,256]{1,0:T(8,128)(2,1)S(1)}, u32[]{:S(2)}, u32[]{:S(2)}) %collective-permute-start.15) | collective-permute-done | bytes 540704 | tf_op jit(solution)/shard_map/ppermute | solution.py:553
  83.3 2.0 onward.3
  86.6 6.2 %collective-permute-done.18.received_ref = bf16[1056,256]{1,0:T(8,128)(2,1)} collective-permute-done((bf16[1056,256]{1,0:T(8,128)(2,1)}, bf16[1056,256]{1,0:T(8,128)(2,1)}, u32[]{:S(2)}, u32[]{:S(2)}) %collective-permute-start.18) | collective-permute-done | bytes 540704 | tf_op jit(solution)/shard_map/ppermute | solution.py:553
  92.8 4.4 %collective-permute-start.21 = (bf16[1056,256]{1,0:T(8,128)(2,1)}, bf16[1056,256]{1,0:T(8,128)(2,1)S(1)}, u32[]{:S(2)}, u32[]{:S(2)}) collective-permute-start(bf16[1056,256]{1,0:T(8,128)(2,1)} %onward.4), channel_id=1, source_target_pairs={{0,8},{4,12},{24,16},{28,20},{1,9},{5,13},{25,17},{29,21},{2,10},{... | collective-permute-start | bytes 1622024 | tf_op jit(solution)/shard_map/ppermute | solution.py:553
  101.8 5.3 %collective-permute-done.21.refs_3_ = bf16[1056,256]{1,0:T(8,128)(2,1)S(1)} collective-permute-done((bf16[1056,256]{1,0:T(8,128)(2,1)}, bf16[1056,256]{1,0:T(8,128)(2,1)S(1)}, u32[]{:S(2)}, u32[]{:S(2)}) %collective-permute-start.21) | collective-permute-done | bytes 540704 | tf_op jit(solution)/shard_map/ppermute | solution.py:553
  107.1 6.6 %collective-permute-done.23.refs_8_ = bf16[1024,256]{1,0:T(8,128)(2,1)S(1)} collective-permute-done((bf16[1024,256]{1,0:T(8,128)(2,1)S(1)}, bf16[1024,256]{1,0:T(8,128)(2,1)S(1)}, u32[]{:S(2)}, u32[]{:S(2)}) %collective-permute-start.23) | collective-permute-done | bytes 524320 | tf_op jit(solution)/shard_map/ppermute | solution.py:553
  114.5 8.9 %scan.1 = (bf16[512,256]{1,0:T(8,128)(2,1)}, bf16[528,256]{1,0:T(8,128)(2,1)S(1)}) custom-call(s32[7]{0:T(128)S(1)} %stack.43.place_ref, f32[1]{0:T(128)} %bitcast.3.scale_ref, bf16[1056,256]{1,0:T(8,128)(2,1)S(1)} %copy-done.2, bf16[1056,256]{1,0:T(8,128)(2,1)} %collective-permute-done.17.refs_1_, bf16[1056,256]{1,0:T(8,128)(2,1)} %collective-permute-done.20.refs_2_, ...), custom_call_target="tpu_custom_call" | custom-call | flops 268435456 | bytes 2097152 | tf_op jit(solution)/shard_map/scan/pallas_call | solution.py:498
  124.1 5.1 %collective-permute-start.38 = (bf16[528,256]{1,0:T(8,128)(2,1)S(1)}, bf16[528,256]{1,0:T(8,128)(2,1)S(1)}, u32[]{:S(2)}, u32[]{:S(2)}) collective-permute-start(bf16[528,256]{1,0:T(8,128)(2,1)S(1)} %get-tuple-element.72), channel_id=1, source_target_pairs={{0,8},{4,12},{8,0},{12,4},{16,24},{20,28},{24,16},{28,20},{1,9},{5... | collective-permute-start | bytes 811016 | tf_op jit(solution)/shard_map/ppermute | solution.py:553
  136.6 10.7 %collective-permute-done.25 = bf16[512,256]{1,0:T(8,128)(2,1)S(1)} collective-permute-done((bf16[512,256]{1,0:T(8,128)(2,1)S(1)}, bf16[512,256]{1,0:T(8,128)(2,1)S(1)}, u32[]{:S(2)}, u32[]{:S(2)}) %collective-permute-start.25) | collective-permute-done | bytes 262176 | tf_op jit(solution)/shard_map/ppermute | solution.py:553
  153.3 4.7 %collective-permute-done.36 = bf16[528,256]{1,0:T(8,128)(2,1)S(1)} collective-permute-done((bf16[528,256]{1,0:T(8,128)(2,1)S(1)}, bf16[528,256]{1,0:T(8,128)(2,1)S(1)}, u32[]{:S(2)}, u32[]{:S(2)}) %collective-permute-start.36) | collective-permute-done | bytes 270368 | tf_op jit(solution)/shard_map/ppermute | solution.py:553
  160.7 1.7 collective-permute-start.42
  162.4 6.2 %collective-permute-done.29 = bf16[512,256]{1,0:T(8,128)(2,1)S(1)} collective-permute-done((bf16[512,256]{1,0:T(8,128)(2,1)S(1)}, bf16[512,256]{1,0:T(8,128)(2,1)S(1)}, u32[]{:S(2)}, u32[]{:S(2)}) %collective-permute-start.29) | collective-permute-done | bytes 262176 | tf_op jit(solution)/shard_map/ppermute | solution.py:553
  169.9 2.1 collective-permute-start.32
  172.9 4.0 %collective-permute-done.40 = bf16[528,256]{1,0:T(8,128)(2,1)S(1)} collective-permute-done((bf16[528,256]{1,0:T(8,128)(2,1)S(1)}, bf16[528,256]{1,0:T(8,128)(2,1)S(1)}, u32[]{:S(2)}, u32[]{:S(2)}) %collective-permute-start.40) | collective-permute-done | bytes 270368 | tf_op jit(solution)/shard_map/ppermute | solution.py:553
  177.0 2.1 collective-permute-start.43
  180.3 3.2 %collective-permute-done.43 = bf16[528,256]{1,0:T(8,128)(2,1)S(1)} collective-permute-done((bf16[528,256]{1,0:T(8,128)(2,1)S(1)}, bf16[528,256]{1,0:T(8,128)(2,1)S(1)}, u32[]{:S(2)}, u32[]{:S(2)}) %collective-permute-start.43) | collective-permute-done | bytes 270368 | tf_op jit(solution)/shard_map/ppermute | solution.py:556
  193.2 3.3 %collective-permute-done.34 = bf16[128,512]{1,0:T(8,128)(2,1)S(1)} collective-permute-done((bf16[128,512]{1,0:T(8,128)(2,1)}, bf16[128,512]{1,0:T(8,128)(2,1)S(1)}, u32[]{:S(2)}, u32[]{:S(2)}) %collective-permute-start.34) | collective-permute-done | bytes 131104 | tf_op jit(solution)/shard_map/ppermute | solution.py:724
  200.2 5.8 %all-to-all-start = ((bf16[8,32,512]{2,1,0:T(8,128)(2,1)}), bf16[8,32,512]{2,1,0:T(8,128)(2,1)S(1)}, u32[]{:S(2)}, u32[]{:S(2)}) async-start(bf16[8,32,512]{2,1,0:T(8,128)(2,1)} %multiply_convert_fusion.1), calls=%async_computation | async-start | bytes 524288 | tf_op jit(solution)/shard_map/all_to_all | solution.py:743
  207.3 7.2 %all-to-all-done = bf16[8,32,512]{2,1,0:T(8,128)(2,1)S(1)} async-done(((bf16[8,32,512]{2,1,0:T(8,128)(2,1)}), bf16[8,32,512]{2,1,0:T(8,128)(2,1)S(1)}, u32[]{:S(2)}, u32[]{:S(2)}) %all-to-all-start) | async-done | bytes 262176 | tf_op jit(solution)/shard_map/all_to_all | solution.py:743
  (176 shorter events, 72.2 us)
Async XLA Ops:
  2.7 26.0 %collective-permute-start.7 = (bf16[512,512]{1,0:T(8,128)(2,1)}, bf16[512,512]{1,0:T(8,128)(2,1)S(1)}, u32[]{:S(2)}, u32[]{:S(2)}) collective-permute-start(bf16[512,512]{1,0:T(8,128)(2,1)} %constant_dynamic-slice_fusion.9), channel_id=1, source_target_pairs={{0,4},{4,0},{8,12},{12,8},{16,20},{20,16},{24,28},{28,24},{1,5},{5... | collective-permute-start | bytes 1572872 | tf_op jit(solution)/shard_map/ppermute | solution.py:556
  6.6 14.4 %collective-permute-start = (bf16[32,1024]{1,0:T(8,128)(2,1)S(1)}, bf16[32,1024]{1,0:T(8,128)(2,1)S(1)}, u32[]{:S(2)}, u32[]{:S(2)}) collective-permute-start(bf16[32,1024]{1,0:T(8,128)(2,1)S(1)} %get-tuple-element.85), channel_id=1, source_target_pairs={{0,8},{4,12},{8,0},{12,4},{16,24},{20,28},{24,16},{28,20},{1,9},{5... | collective-permute-start | bytes 196616 | tf_op jit(solution)/shard_map/ppermute | solution.py:553
  8.3 12.7 %collective-permute-start.1 = (bf16[32,1024]{1,0:T(8,128)(2,1)S(1)}, bf16[32,1024]{1,0:T(8,128)(2,1)S(1)}, u32[]{:S(2)}, u32[]{:S(2)}) collective-permute-start(bf16[32,1024]{1,0:T(8,128)(2,1)S(1)} %get-tuple-element.84), channel_id=1, source_target_pairs={{0,16},{4,20},{8,24},{12,28},{16,0},{20,4},{24,8},{28,12},{1,17},{... | collective-permute-start | bytes 196616 | tf_op jit(solution)/shard_map/ppermute | solution.py:553
  10.8 10.1 %collective-permute-start.2 = (bf16[32,1024]{1,0:T(8,128)(2,1)S(1)}, bf16[32,1024]{1,0:T(8,128)(2,1)}, u32[]{:S(2)}, u32[]{:S(2)}) collective-permute-start(bf16[32,1024]{1,0:T(8,128)(2,1)S(1)} %get-tuple-element.83), channel_id=1, source_target_pairs={{0,24},{4,28},{8,16},{12,20},{16,8},{20,12},{24,0},{28,4},{1,25},{... | collective-permute-start | bytes 196616 | tf_op jit(solution)/shard_map/ppermute | solution.py:553
  28.9 10.7 %collective-permute-start.9 = (bf16[4,32,1024]{2,1,0:T(8,128)(2,1)S(1)}, bf16[4,32,1024]{2,1,0:T(8,128)(2,1)}, u32[]{:S(2)}, u32[]{:S(2)}) collective-permute-start(bf16[4,32,1024]{2,1,0:T(8,128)(2,1)S(1)} %collective-permute-done.6.refs_4_), channel_id=1, source_target_pairs={{0,2},{1,3},{2,0},{3,1},{4,6},{5,7},{6,4},{7,5},{8,10},{9,11},{10,... | collective-permute-start | bytes 786440 | tf_op jit(solution)/shard_map/ppermute | solution.py:620
  36.3 9.7 %collective-permute-start.5 = (bf16[4,32,1024]{2,1,0:T(8,128)(2,1)}, bf16[4,32,1024]{2,1,0:T(8,128)(2,1)}, u32[]{:S(2)}, u32[]{:S(2)}) collective-permute-start(bf16[4,32,1024]{2,1,0:T(8,128)(2,1)} %collective-permute-done.4.refs_2_), channel_id=1, source_target_pairs={{0,1},{1,0},{2,3},{3,2},{4,5},{5,4},{6,7},{7,6},{8,9},{9,8},{10,11... | collective-permute-start | bytes 786440 | tf_op jit(solution)/shard_map/ppermute | solution.py:620
  36.3 9.7 %collective-permute-start.8 = (bf16[4,32,1024]{2,1,0:T(8,128)(2,1)S(1)}, bf16[4,32,1024]{2,1,0:T(8,128)(2,1)}, u32[]{:S(2)}, u32[]{:S(2)}) collective-permute-start(bf16[4,32,1024]{2,1,0:T(8,128)(2,1)S(1)} %collective-permute-done.6.refs_4_), channel_id=1, source_target_pairs={{0,1},{1,0},{2,3},{3,2},{4,5},{5,4},{6,7},{7,6},{8,9},{9,8},{10,11... | collective-permute-start | bytes 786440 | tf_op jit(solution)/shard_map/ppermute | solution.py:620
  55.0 13.3 %collective-permute-start.19 = (bf16[1056,256]{1,0:T(8,128)(2,1)S(1)}, bf16[1056,256]{1,0:T(8,128)(2,1)S(1)}, u32[]{:S(2)}, u32[]{:S(2)}) collective-permute-start(bf16[1056,256]{1,0:T(8,128)(2,1)S(1)} %get-tuple-element.56), channel_id=1, source_target_pairs={{0,4},{4,0},{8,12},{12,8},{16,20},{20,16},{24,28},{28,24},{1,5},{5... | collective-permute-start | bytes 1622024 | tf_op jit(solution)/shard_map/ppermute | solution.py:556
  56.7 14.9 %collective-permute-start.13 = (bf16[1024,256]{1,0:T(8,128)(2,1)S(1)}, bf16[1024,256]{1,0:T(8,128)(2,1)S(1)}, u32[]{:S(2)}, u32[]{:S(2)}) collective-permute-start(bf16[1024,256]{1,0:T(8,128)(2,1)S(1)} %get-tuple-element.50), channel_id=1, source_target_pairs={{0,8},{4,12},{24,16},{28,20},{1,9},{5,13},{25,17},{29,21},{2,10},{... | collective-permute-start | bytes 1572872 | tf_op jit(solution)/shard_map/ppermute | solution.py:553
  59.3 23.9 %collective-permute-start.15 = (bf16[1056,256]{1,0:T(8,128)(2,1)S(1)}, bf16[1056,256]{1,0:T(8,128)(2,1)S(1)}, u32[]{:S(2)}, u32[]{:S(2)}) collective-permute-start(bf16[1056,256]{1,0:T(8,128)(2,1)S(1)} %get-tuple-element.52.own_ref), channel_id=1, source_target_pairs={{0,8},{4,12},{24,16},{28,20},{1,9},{5,13},{25,17},{29,21},{2,10},{... | collective-permute-start | bytes 1622024 | tf_op jit(solution)/shard_map/ppermute | solution.py:553
  60.7 32.1 %collective-permute-start.18 = (bf16[1056,256]{1,0:T(8,128)(2,1)}, bf16[1056,256]{1,0:T(8,128)(2,1)}, u32[]{:S(2)}, u32[]{:S(2)}) collective-permute-start(bf16[1056,256]{1,0:T(8,128)(2,1)} %get-tuple-element.51.own_ref), channel_id=1, source_target_pairs={{0,8},{4,12},{24,16},{28,20},{1,9},{5,13},{25,17},{29,21},{2,10},{... | collective-permute-start | bytes 1622024 | tf_op jit(solution)/shard_map/ppermute | solution.py:553
  69.3 27.9 %collective-permute-start.20 = (bf16[1056,256]{1,0:T(8,128)(2,1)}, bf16[1056,256]{1,0:T(8,128)(2,1)}, u32[]{:S(2)}, u32[]{:S(2)}) collective-permute-start(bf16[1056,256]{1,0:T(8,128)(2,1)} %onward.4), channel_id=1, source_target_pairs={{8,0},{12,4},{16,24},{20,28},{9,1},{13,5},{17,25},{21,29},{10,2},{... | collective-permute-start | bytes 1622024 | tf_op jit(solution)/shard_map/ppermute | solution.py:553
  71.8 28.3 %collective-permute-start.14 = (bf16[1024,256]{1,0:T(8,128)(2,1)S(1)}, bf16[1024,256]{1,0:T(8,128)(2,1)S(1)}, u32[]{:S(2)}, u32[]{:S(2)}) collective-permute-start(bf16[1024,256]{1,0:T(8,128)(2,1)S(1)} %add_convert_fusion.refs_6_), channel_id=1, source_target_pairs={{8,16},{12,20},{16,8},{20,12},{9,17},{13,21},{17,9},{21,13},{10,18... | collective-permute-start | bytes 1572872 | tf_op jit(solution)/shard_map/ppermute | solution.py:553
  72.5 27.8 %collective-permute-start.17 = (bf16[1056,256]{1,0:T(8,128)(2,1)}, bf16[1056,256]{1,0:T(8,128)(2,1)}, u32[]{:S(2)}, u32[]{:S(2)}) collective-permute-start(bf16[1056,256]{1,0:T(8,128)(2,1)} %get-tuple-element.53), channel_id=1, source_target_pairs={{0,4},{4,0},{8,12},{12,8},{16,20},{20,16},{24,28},{28,24},{1,5},{5... | collective-permute-start | bytes 1622024 | tf_op jit(solution)/shard_map/ppermute | solution.py:556
  85.3 15.1 %collective-permute-start.16 = (bf16[1056,256]{1,0:T(8,128)(2,1)}, bf16[1056,256]{1,0:T(8,128)(2,1)}, u32[]{:S(2)}, u32[]{:S(2)}) collective-permute-start(bf16[1056,256]{1,0:T(8,128)(2,1)} %onward.3), channel_id=1, source_target_pairs={{8,24},{12,28},{16,0},{20,4},{9,25},{13,29},{17,1},{21,5},{10,26},... | collective-permute-start | bytes 1622024 | tf_op jit(solution)/shard_map/ppermute | solution.py:553
  92.8 14.3 %collective-permute-start.21 = (bf16[1056,256]{1,0:T(8,128)(2,1)}, bf16[1056,256]{1,0:T(8,128)(2,1)S(1)}, u32[]{:S(2)}, u32[]{:S(2)}) collective-permute-start(bf16[1056,256]{1,0:T(8,128)(2,1)} %onward.4), channel_id=1, source_target_pairs={{0,8},{4,12},{24,16},{28,20},{1,9},{5,13},{25,17},{29,21},{2,10},{... | collective-permute-start | bytes 1622024 | tf_op jit(solution)/shard_map/ppermute | solution.py:553
  99.4 14.3 %collective-permute-start.22 = (bf16[1056,256]{1,0:T(8,128)(2,1)S(1)}, bf16[1056,256]{1,0:T(8,128)(2,1)S(1)}, u32[]{:S(2)}, u32[]{:S(2)}) collective-permute-start(bf16[1056,256]{1,0:T(8,128)(2,1)S(1)} %onward.5), channel_id=1, source_target_pairs={{8,16},{12,20},{16,8},{20,12},{9,17},{13,21},{17,9},{21,13},{10,18... | collective-permute-start | bytes 1622024 | tf_op jit(solution)/shard_map/ppermute | solution.py:553
  100.4 13.4 %collective-permute-start.23 = (bf16[1024,256]{1,0:T(8,128)(2,1)S(1)}, bf16[1024,256]{1,0:T(8,128)(2,1)S(1)}, u32[]{:S(2)}, u32[]{:S(2)}) collective-permute-start(bf16[1024,256]{1,0:T(8,128)(2,1)S(1)} %multiply_convert_fusion), channel_id=1, source_target_pairs={{8,0},{12,4},{16,24},{20,28},{9,1},{13,5},{17,25},{21,29},{10,2},{... | collective-permute-start | bytes 1572872 | tf_op jit(solution)/shard_map/ppermute | solution.py:553
  123.4 25.7 %collective-permute-start.35 = (bf16[528,256]{1,0:T(8,128)(2,1)S(1)}, bf16[528,256]{1,0:T(8,128)(2,1)S(1)}, u32[]{:S(2)}, u32[]{:S(2)}) collective-permute-start(bf16[528,256]{1,0:T(8,128)(2,1)S(1)} %get-tuple-element.72), channel_id=1, source_target_pairs={{8,16},{12,20},{16,8},{20,12},{9,17},{13,21},{17,9},{21,13},{10,18... | collective-permute-start | bytes 811016 | tf_op jit(solution)/shard_map/ppermute | solution.py:553
  124.1 10.9 %collective-permute-start.38 = (bf16[528,256]{1,0:T(8,128)(2,1)S(1)}, bf16[528,256]{1,0:T(8,128)(2,1)S(1)}, u32[]{:S(2)}, u32[]{:S(2)}) collective-permute-start(bf16[528,256]{1,0:T(8,128)(2,1)S(1)} %get-tuple-element.72), channel_id=1, source_target_pairs={{0,8},{4,12},{8,0},{12,4},{16,24},{20,28},{24,16},{28,20},{1,9},{5... | collective-permute-start | bytes 811016 | tf_op jit(solution)/shard_map/ppermute | solution.py:553
  129.2 29.2 %collective-permute-start.37 = (bf16[528,256]{1,0:T(8,128)(2,1)S(1)}, bf16[528,256]{1,0:T(8,128)(2,1)S(1)}, u32[]{:S(2)}, u32[]{:S(2)}) collective-permute-start(bf16[528,256]{1,0:T(8,128)(2,1)S(1)} %get-tuple-element.72), channel_id=1, source_target_pairs={{0,4},{4,0},{8,12},{12,8},{16,20},{20,16},{24,28},{28,24},{1,5},{5... | collective-permute-start | bytes 811016 | tf_op jit(solution)/shard_map/ppermute | solution.py:556
  132.1 16.3 %collective-permute-start.26 = (bf16[512,256]{1,0:T(8,128)(2,1)}, bf16[512,256]{1,0:T(8,128)(2,1)S(1)}, u32[]{:S(2)}, u32[]{:S(2)}) collective-permute-start(bf16[512,256]{1,0:T(8,128)(2,1)} %get-tuple-element.64), channel_id=1, source_target_pairs={{0,4},{4,0},{8,12},{12,8},{16,20},{20,16},{24,28},{28,24},{1,5},{5... | collective-permute-start | bytes 786440 | tf_op jit(solution)/shard_map/ppermute | solution.py:556
  132.9 19.4 %collective-permute-start.28 = (bf16[512,256]{1,0:T(8,128)(2,1)S(1)}, bf16[512,256]{1,0:T(8,128)(2,1)S(1)}, u32[]{:S(2)}, u32[]{:S(2)}) collective-permute-start(bf16[512,256]{1,0:T(8,128)(2,1)S(1)} %collective-permute-done.27), channel_id=1, source_target_pairs={{8,16},{12,20},{16,8},{20,12},{9,17},{13,21},{17,9},{21,13},{10,18... | collective-permute-start | bytes 786440 | tf_op jit(solution)/shard_map/ppermute | solution.py:553
  135.0 12.3 %collective-permute-start.25 = (bf16[512,256]{1,0:T(8,128)(2,1)S(1)}, bf16[512,256]{1,0:T(8,128)(2,1)S(1)}, u32[]{:S(2)}, u32[]{:S(2)}) collective-permute-start(bf16[512,256]{1,0:T(8,128)(2,1)S(1)} %collective-permute-done.24), channel_id=1, source_target_pairs={{8,0},{12,4},{16,24},{20,28},{9,1},{13,5},{17,25},{21,29},{10,2},{... | collective-permute-start | bytes 786440 | tf_op jit(solution)/shard_map/ppermute | solution.py:553
  147.3 22.6 %collective-permute-start.30 = (bf16[512,256]{1,0:T(8,128)(2,1)S(1)}, bf16[512,256]{1,0:T(8,128)(2,1)S(1)}, u32[]{:S(2)}, u32[]{:S(2)}) collective-permute-start(bf16[512,256]{1,0:T(8,128)(2,1)S(1)} %collective-permute-done.27), channel_id=1, source_target_pairs={{0,4},{4,0},{8,12},{12,8},{16,20},{20,16},{24,28},{28,24},{1,5},{5... | collective-permute-start | bytes 786440 | tf_op jit(solution)/shard_map/ppermute | solution.py:556
  148.4 12.3 %collective-permute-start.39 = (bf16[528,256]{1,0:T(8,128)(2,1)S(1)}, bf16[528,256]{1,0:T(8,128)(2,1)S(1)}, u32[]{:S(2)}, u32[]{:S(2)}) collective-permute-start(bf16[528,256]{1,0:T(8,128)(2,1)S(1)} %collective-permute-done.38), channel_id=1, source_target_pairs={{8,16},{12,20},{16,8},{20,12},{9,17},{13,21},{17,9},{21,13},{10,18... | collective-permute-start | bytes 811016 | tf_op jit(solution)/shard_map/ppermute | solution.py:553
  152.3 24.7 %collective-permute-start.41 = (bf16[528,256]{1,0:T(8,128)(2,1)S(1)}, bf16[528,256]{1,0:T(8,128)(2,1)S(1)}, u32[]{:S(2)}, u32[]{:S(2)}) collective-permute-start(bf16[528,256]{1,0:T(8,128)(2,1)S(1)} %collective-permute-done.38), channel_id=1, source_target_pairs={{0,4},{4,0},{8,12},{12,8},{16,20},{20,16},{24,28},{28,24},{1,5},{5... | collective-permute-start | bytes 811016 | tf_op jit(solution)/shard_map/ppermute | solution.py:556
  158.0 14.0 %collective-permute-start.31 = (bf16[512,256]{1,0:T(8,128)(2,1)S(1)}, bf16[512,256]{1,0:T(8,128)(2,1)S(1)}, u32[]{:S(2)}, u32[]{:S(2)}) collective-permute-start(bf16[512,256]{1,0:T(8,128)(2,1)S(1)} %broadcast_select_fusion.3), channel_id=1, source_target_pairs={{0,4},{4,0},{8,12},{12,8},{16,20},{20,16},{24,28},{28,24},{1,5},{5... | collective-permute-start | bytes 786440 | tf_op jit(solution)/shard_map/ppermute | solution.py:556
  158.5 10.1 %collective-permute-start.29 = (bf16[512,256]{1,0:T(8,128)(2,1)S(1)}, bf16[512,256]{1,0:T(8,128)(2,1)S(1)}, u32[]{:S(2)}, u32[]{:S(2)}) collective-permute-start(bf16[512,256]{1,0:T(8,128)(2,1)S(1)} %collective-permute-done.28), channel_id=1, source_target_pairs={{8,0},{12,4},{16,24},{20,28},{9,1},{13,5},{17,25},{21,29},{10,2},{... | collective-permute-start | bytes 786440 | tf_op jit(solution)/shard_map/ppermute | solution.py:553
  160.7 18.3 %collective-permute-start.42 = (bf16[528,256]{1,0:T(8,128)(2,1)S(1)}, bf16[528,256]{1,0:T(8,128)(2,1)S(1)}, u32[]{:S(2)}, u32[]{:S(2)}) collective-permute-start(bf16[528,256]{1,0:T(8,128)(2,1)S(1)} %broadcast_select_fusion.1), channel_id=1, source_target_pairs={{0,4},{4,0},{8,12},{12,8},{16,20},{20,16},{24,28},{28,24},{1,5},{5... | collective-permute-start | bytes 811016 | tf_op jit(solution)/shard_map/ppermute | solution.py:556
  169.9 10.1 %collective-permute-start.32 = (bf16[512,256]{1,0:T(8,128)(2,1)S(1)}, bf16[512,256]{1,0:T(8,128)(2,1)S(1)}, u32[]{:S(2)}, u32[]{:S(2)}) collective-permute-start(bf16[512,256]{1,0:T(8,128)(2,1)S(1)} %broadcast_select_fusion.2), channel_id=1, source_target_pairs={{0,4},{4,0},{8,12},{12,8},{16,20},{20,16},{24,28},{28,24},{1,5},{5... | collective-permute-start | bytes 786440 | tf_op jit(solution)/shard_map/ppermute | solution.py:556
  200.2 14.3 %all-to-all-start = ((bf16[8,32,512]{2,1,0:T(8,128)(2,1)}), bf16[8,32,512]{2,1,0:T(8,128)(2,1)S(1)}, u32[]{:S(2)}, u32[]{:S(2)}) async-start(bf16[8,32,512]{2,1,0:T(8,128)(2,1)} %multiply_convert_fusion.1), calls=%async_computation | async-start | bytes 524288 | tf_op jit(solution)/shard_map/all_to_all | solution.py:743
  (33 other events, 361.3 us)

commit v6 on v1

--- a/solution.py
+++ b/solution.py
@@ -201,11 +201,12 @@
 def project_kernel(ranks, place_ref, factor_ref, *refs):
     hidden = [refs[x * ranks : (x + 1) * ranks] for x in range(PAIR)]
     refs = refs[PAIR * ranks :]
-    own_x, x_far, own_bc, other_bc, own_dt, other_dt = refs[:6]
-    far_refs = refs[6 : 6 + LINE // 2]
-    near_refs = refs[6 + LINE // 2 : 6 + LINE]
-    sent_refs = refs[6 + LINE : 6 + LINE + LINE // 2]
-    bc_ref, largest_ref, quant_ref, near_dt, all_dt = refs[6 + LINE + LINE // 2 :]
+    own_x, other_x, refs = (refs[0], refs[1 : 1 + LINE // 2], refs[1 + LINE // 2 :])
+    own_bc, other_bc, own_dt, other_dt = refs[:4]
+    far_refs, near_refs, sent_refs = (
+        refs[4 + at : 4 + at + LINE // 2] for at in range(0, 3 * LINE // 2, LINE // 2)
+    )
+    bc_ref, largest_ref, quant_ref, near_dt, all_dt = refs[4 + 3 * LINE // 2 :]
     side, z = (place_ref[1], place_ref[2])
     factor = factor_ref[0]
     depth = own_x.shape[0]
@@ -267,8 +268,8 @@
         for m in range(LINE // 2):
             owner = z ^ (m + LINE // 2)
             run = side * LINE + owner
-            other = x_far[:, columns(owner % (LINE // 2))]
-            far_refs[m][at_rows] = both(own_x[:, columns(run)], other).astype(jnp.bfloat16)
+            product = both(own_x[:, columns(run)], other_x[m][...])
+            far_refs[m][at_rows] = product.astype(jnp.bfloat16)
             far_refs[m][extra_rows] = steps_of(all_dt, run)
             for out_refs, way in ((near_refs, side), (sent_refs, 1 - side)):
                 run = way * LINE + (z ^ m)
@@ -285,8 +286,8 @@
 def project(place, factor, hidden, w_x, weights):
     line, own, wide = hidden[0].shape
     ranks = len(hidden) // PAIR
-    depth, x_wide = (weights[0].shape[0], 2 * weights[0].shape[1])
-    channels, maps_wide = (x_wide // LINE, weights[1].shape[1])
+    depth, channels = weights[0].shape
+    x_wide, maps_wide = (LINE * channels, weights[LINE // 2].shape[1])
     tokens = line * PAIR * ranks * own
     extra = tokens // channels * ROWS
     dt_shape = (weights[-1].shape[0] // ROWS, ROWS, tokens // CUTS)
@@ -582,17 +583,15 @@
     ).reshape(channels, STATE)
 
     tie = lax.optimization_barrier
-    half_run = LINE // 2 * channels
-    opposite = (z // (LINE // 2)) ^ 1
-    at = ((1 - side) * 2 + opposite) * half_run
-    x_sent = lax.dynamic_slice_in_dim(w_x, at, half_run, axis=1)
-    x_sent, hidden_in = tie((x_sent, hidden_in))
-    x_far = across(x_sent)
-    x_far, maps_sent, dt_sent = tie(
-        (x_far, pick(w_bc, 1, 1 - side).reshape(depth, 2 * STATE), w_dt.T)
-    )
-    bc_other, dt_other = (across(maps_sent), across(dt_sent))
+    def sent_columns(m):
+        run = (1 - side) * LINE + (z ^ m)
+        return lax.dynamic_slice_in_dim(w_x, run * channels, channels, axis=1)
+
+    x_sent, hidden_in = tie((sent_columns(LINE - 1), hidden_in))
+    swapped = [across(x_sent)]
     bc_own = pick(w_bc, 1, side).reshape(depth, 2 * STATE)
+    maps_sent = pick(w_bc, 1, 1 - side).reshape(depth, 2 * STATE)
+    dt_sent = w_dt.T
 
     def line_columns(m):
         return lax.dynamic_slice_in_dim(hidden_in, (z ^ m) * PAIR * depth, PAIR * depth, axis=1)
@@ -601,7 +600,12 @@
     for m in range(1, LINE):
         arrived.append(along(line_columns(m), [(s, s ^ m) for s in range(LINE)]))
     stacked = jnp.stack(arrived)
+    stacked, x_sent, maps_sent, dt_sent = tie(
+        (stacked, sent_columns(LINE - 2), maps_sent, dt_sent)
+    )
     beyond_pair = across(stacked)
+    swapped.insert(0, across(x_sent))
+    bc_other, dt_other = (across(maps_sent), across(dt_sent))
     beyond_pair, small, start_state, bc_own, dt_sent = tie(
         (beyond_pair, small, start_state, bc_own, dt_sent)
     )
@@ -622,7 +626,7 @@
     middle = [(next_start, next_end), (next_end, next_start)]
     over_middle = [(next_start, end), (next_end, start)]
     beside_pairs = [(s, s ^ 1) for s in range(LINE)]
-    weights = (x_far, bc_own, bc_other, dt_sent, dt_other)
+    weights = (*swapped, bc_own, bc_other, dt_sent, dt_other)
     over, far, mine, near, mine_sent, near_sent, maps, largest = project(
         place, factor, rows, w_x, weights
     )

time: 194 us -> 197 us (1.015)
  waiting for transfers between devices: 91.8 us -> 98.9 us
  starting transfers between devices: 52.8 us -> 49.1 us
    ppermute x10 -> x11, waiting for transfers between devices: 20 us -> 27.8 us  [across(): return lax.ppermute(value, 'seq', [(s, s ^ 1) for s in range(count)])]
    ppermute x10 -> x11, starting transfers between devices: 15.4 us -> 10.8 us  [across(): return lax.ppermute(value, 'seq', [(s, s ^ 1) for s in range(count)])]
    ppermute x17, waiting for transfers between devices: 54 us -> 56.9 us  [along(): return lax.ppermute(value, 'seq', moves)]
    ppermute x6, waiting for transfers between devices: 2.75 us -> 0.02 us  [by_heads(): ours.append(lax.ppermute(ours[j - bit], 'tensor', pairs))]
    unnamed x32 -> x34, local copies, waits for them, and re-layouts: 6.93 us -> 6.91 us
  transfers between devices with their start and end apart: 38 -> 39, of which waited for: 18 -> 16; matrix products, arithmetic and copies ran while one was open for 9% -> 8% of each run, Pallas kernels for 2% -> 2%
where the time goes in v6:
time: 197 us; the launch traced here: 196 us
  waiting for transfers between devices  98.9 us (50%)
  starting transfers between devices  49.1 us (25%)
  Pallas kernels  18.5 us (9%)
  local copies, waits for them, and re-layouts  14.6 us (7%)
  other arithmetic  9.05 us (5%)
  matrix products  3.68 us (2%)
    ppermute x17, waiting for transfers between devices, along(): return lax.ppermute(value, 'seq', moves)  56.9 us
    ppermute x11, waiting for transfers between devices, across(): return lax.ppermute(value, 'seq', [(s, s ^ 1) for s in range(count)])  27.8 us
    ppermute x17, starting transfers between devices, along(): return lax.ppermute(value, 'seq', moves)  27.6 us
    ppermute x11, starting transfers between devices, across(): return lax.ppermute(value, 'seq', [(s, s ^ 1) for s in range(count)])  10.8 us
    pallas_call x1, Pallas kernels, scan(): pl.pallas_call(scan_kernel, in_specs=[SMEM, SMEM] + [VMEM] * (len(sums) +...  8.64 us
    all_to_all x1, waiting for transfers between devices, by_heads(): lax.all_to_all(final.astype(bf16), 'seq', split_axis=0, concat_axis=0, ti...  7.62 us
    unnamed x34, local copies, waits for them, and re-layouts  6.91 us
    pallas_call x1, Pallas kernels, project(): pl.pallas_call(functools.partial(project_kernel, ranks), in_specs=[SMEM,...  5.7 us
  transfers between devices with their start and end apart: 39, of which 16 were waited for; matrix products, arithmetic and copies ran while one was open for 8% of the time, Pallas kernels for 2%

profile of v6, /device:TPU:0, one launch (start us, length us, event | category | flops | bytes accessed | tf_op | source)
XLA Modules:
  0.0 195.7 jit_solution(18367384154116729317)
XLA Ops:
  0.7 2.0 %constant_dynamic-slice_fusion.6 = (bf16[512,256]{1,0:T(8,128)(2,1)}, bf16[512,256]{1,0:T(8,128)(2,1)}) fusion(bf16[512,2048]{1,0:T(8,128)(2,1)} %refs_8_.1, s32[]{:T(128)S(6)} %select_n.127, s32[]{:T(128)S(6)} %select_n.122), kind=kLoop, calls=%fused_computation.60 | loop fusion | bytes 1048584 | tf_op jit(solution)/shard_map/dynamic_slice | solution.py:588
  2.8 1.6 dynamic-slice_bitcast_fusion
  4.3 3.0 %collective-permute-start = (bf16[32,1024]{1,0:T(8,128)(2,1)}, bf16[32,1024]{1,0:T(8,128)(2,1)S(1)}, u32[]{:S(2)}, u32[]{:S(2)}) collective-permute-start(bf16[32,1024]{1,0:T(8,128)(2,1)} %get-tuple-element.69), channel_id=1, source_target_pairs={{0,8},{4,12},{8,0},{12,4},{16,24},{20,28},{24,16},{28,20},{1,9},{5... | collective-permute-start | bytes 196616 | tf_op jit(solution)/shard_map/ppermute | solution.py:548
  7.4 2.6 %collective-permute-start.1 = (bf16[32,1024]{1,0:T(8,128)(2,1)S(1)}, bf16[32,1024]{1,0:T(8,128)(2,1)}, u32[]{:S(2)}, u32[]{:S(2)}) collective-permute-start(bf16[32,1024]{1,0:T(8,128)(2,1)S(1)} %get-tuple-element.68), channel_id=1, source_target_pairs={{0,16},{4,20},{8,24},{12,28},{16,0},{20,4},{24,8},{28,12},{1,17},{... | collective-permute-start | bytes 196616 | tf_op jit(solution)/shard_map/ppermute | solution.py:548
  9.9 1.7 collective-permute-start.11
  19.8 1.6 collective-permute-start.4
  22.5 4.6 %collective-permute-done.6.refs_4_ = bf16[4,32,1024]{2,1,0:T(8,128)(2,1)S(1)} collective-permute-done((bf16[4,32,1024]{2,1,0:T(8,128)(2,1)S(1)}, bf16[4,32,1024]{2,1,0:T(8,128)(2,1)S(1)}, u32[]{:S(2)}, u32[]{:S(2)}) %collective-permute-start.6) | collective-permute-done | bytes 262176 | tf_op jit(solution)/shard_map/ppermute | solution.py:551
  27.1 1.5 collective-permute-start.8
  29.5 3.0 %collective-permute-done.13.refs_14_ = bf16[32,512]{1,0:T(8,128)(2,1)S(1)} collective-permute-done((bf16[32,512]{1,0:T(8,128)(2,1)S(1)}, bf16[32,512]{1,0:T(8,128)(2,1)S(1)}, u32[]{:S(2)}, u32[]{:S(2)}) %collective-permute-start.13) | collective-permute-done | bytes 32800 | tf_op jit(solution)/shard_map/ppermute | solution.py:551
  35.6 5.9 %collective-permute-done.12.refs_12_ = bf16[512,256]{1,0:T(8,128)(2,1)} collective-permute-done((bf16[512,256]{1,0:T(8,128)(2,1)}, bf16[512,256]{1,0:T(8,128)(2,1)}, u32[]{:S(2)}, u32[]{:S(2)}) %collective-permute-start.12) | collective-permute-done | bytes 262176 | tf_op jit(solution)/shard_map/ppermute | solution.py:551
  41.6 1.6 copy-done.7
  44.1 5.7 %project.1 = (bf16[1056,256]{1,0:T(8,128)(2,1)}, bf16[1056,256]{1,0:T(8,128)(2,1)S(1)}, bf16[1056,256]{1,0:T(8,128)(2,1)S(1)}, bf16[1056,256]{1,0:T(8,128)(2,1)S...) custom-call(s32[7]{0:T(128)S(1)} %stack.43.place_ref, ...), custom_call_target="tpu_custom_call" | custom-call | flops 2684354560 | bytes 4194304 | tf_op jit(solution)/shard_map/project/pallas_call | solution.py:298
  51.5 2.5 %collective-permute-start.14 = (bf16[1024,256]{1,0:T(8,128)(2,1)S(1)}, bf16[1024,256]{1,0:T(8,128)(2,1)S(1)}, u32[]{:S(2)}, u32[]{:S(2)}) collective-permute-start(bf16[1024,256]{1,0:T(8,128)(2,1)S(1)} %get-tuple-element.42), channel_id=1, source_target_pairs={{0,8},{4,12},{24,16},{28,20},{1,9},{5,13},{25,17},{29,21},{2,10},{... | collective-permute-start | bytes 1572872 | tf_op jit(solution)/shard_map/ppermute | solution.py:548
  55.3 2.1 %collective-permute-start.19 = (bf16[1056,256]{1,0:T(8,128)(2,1)}, bf16[1056,256]{1,0:T(8,128)(2,1)}, u32[]{:S(2)}, u32[]{:S(2)}) collective-permute-start(bf16[1056,256]{1,0:T(8,128)(2,1)} %get-tuple-element.43.own_ref), channel_id=1, source_target_pairs={{0,8},{4,12},{24,16},{28,20},{1,9},{5,13},{25,17},{29,21},{2,10},{... | collective-permute-start | bytes 1622024 | tf_op jit(solution)/shard_map/ppermute | solution.py:548
  57.4 7.1 %collective-permute-done.20.received_ref = bf16[1056,256]{1,0:T(8,128)(2,1)S(1)} collective-permute-done((bf16[1056,256]{1,0:T(8,128)(2,1)S(1)}, bf16[1056,256]{1,0:T(8,128)(2,1)S(1)}, u32[]{:S(2)}, u32[]{:S(2)}) %collective-permute-start.20) | collective-permute-done | bytes 540704 | tf_op jit(solution)/shard_map/ppermute | solution.py:551
  68.5 9.4 %collective-permute-done.16.received_ref = bf16[1056,256]{1,0:T(8,128)(2,1)S(1)} collective-permute-done((bf16[1056,256]{1,0:T(8,128)(2,1)S(1)}, bf16[1056,256]{1,0:T(8,128)(2,1)S(1)}, u32[]{:S(2)}, u32[]{:S(2)}) %collective-permute-start.16) | collective-permute-done | bytes 540704 | tf_op jit(solution)/shard_map/ppermute | solution.py:548
  77.9 2.0 %onward.3 = bf16[1056,256]{1,0:T(8,128)(2,1)} custom-call(bf16[1056,256]{1,0:T(8,128)(2,1)} %get-tuple-element.43.own_ref, bf16[1056,256]{1,0:T(8,128)(2,1)S(1)} %collective-permute-done.16.received_ref), custom_call_target="tpu_custom_call" | custom-call | flops 270336 | bytes 1622016 | tf_op jit(solution)/shard_map/onward/pallas_call | solution.py:333
  81.1 6.8 %collective-permute-done.19.received_ref = bf16[1056,256]{1,0:T(8,128)(2,1)} collective-permute-done((bf16[1056,256]{1,0:T(8,128)(2,1)}, bf16[1056,256]{1,0:T(8,128)(2,1)}, u32[]{:S(2)}, u32[]{:S(2)}) %collective-permute-start.19) | collective-permute-done | bytes 540704 | tf_op jit(solution)/shard_map/ppermute | solution.py:548
  88.0 4.4 %collective-permute-start.22 = (bf16[1056,256]{1,0:T(8,128)(2,1)}, bf16[1056,256]{1,0:T(8,128)(2,1)S(1)}, u32[]{:S(2)}, u32[]{:S(2)}) collective-permute-start(bf16[1056,256]{1,0:T(8,128)(2,1)} %onward.4), channel_id=1, source_target_pairs={{0,8},{4,12},{24,16},{28,20},{1,9},{5,13},{25,17},{29,21},{2,10},{... | collective-permute-start | bytes 1622024 | tf_op jit(solution)/shard_map/ppermute | solution.py:548
  98.2 4.7 %collective-permute-done.22.refs_3_ = bf16[1056,256]{1,0:T(8,128)(2,1)S(1)} collective-permute-done((bf16[1056,256]{1,0:T(8,128)(2,1)}, bf16[1056,256]{1,0:T(8,128)(2,1)S(1)}, u32[]{:S(2)}, u32[]{:S(2)}) %collective-permute-start.22) | collective-permute-done | bytes 540704 | tf_op jit(solution)/shard_map/ppermute | solution.py:548
  102.9 7.4 %collective-permute-done.24.refs_8_ = bf16[1024,256]{1,0:T(8,128)(2,1)S(1)} collective-permute-done((bf16[1024,256]{1,0:T(8,128)(2,1)S(1)}, bf16[1024,256]{1,0:T(8,128)(2,1)S(1)}, u32[]{:S(2)}, u32[]{:S(2)}) %collective-permute-start.24) | collective-permute-done | bytes 524320 | tf_op jit(solution)/shard_map/ppermute | solution.py:548
  111.4 8.6 %scan.1 = bf16[1040,256]{1,0:T(8,128)(2,1)S(1)} custom-call(s32[7]{0:T(128)S(1)} %stack.43.place_ref, f32[1]{0:T(128)} %bitcast.3.scale_ref, bf16[1056,256]{1,0:T(8,128)(2,1)S(1)} %copy-done.6, bf16[1056,256]{1,0:T(8,128)(2,1)} %collective-permute-done.18.refs_1_, bf16[1056,256]{1,0:T(8,128)(2,1)} %collective-permute-done.21.refs_2_, ...), custom_call_target="tpu_custom_call" | custom-call | flops 268435456 | bytes 2097152 | tf_op jit(solution)/shard_map/scan/pallas_call | solution.py:493
  121.5 1.5 collective-permute-start.28
  125.2 8.7 %collective-permute-done.28 = bf16[1040,256]{1,0:T(8,128)(2,1)S(1)} collective-permute-done((bf16[1040,256]{1,0:T(8,128)(2,1)S(1)}, bf16[1040,256]{1,0:T(8,128)(2,1)S(1)}, u32[]{:S(2)}, u32[]{:S(2)}) %collective-permute-start.28) | collective-permute-done | bytes 532512 | tf_op jit(solution)/shard_map/ppermute | solution.py:548
  135.2 8.6 %collective-permute-done.26 = bf16[1040,256]{1,0:T(8,128)(2,1)S(1)} collective-permute-done((bf16[1040,256]{1,0:T(8,128)(2,1)}, bf16[1040,256]{1,0:T(8,128)(2,1)S(1)}, u32[]{:S(2)}, u32[]{:S(2)}) %collective-permute-start.26) | collective-permute-done | bytes 532512 | tf_op jit(solution)/shard_map/ppermute | solution.py:548
  147.3 10.1 %collective-permute-done.30 = bf16[1040,256]{1,0:T(8,128)(2,1)S(1)} collective-permute-done((bf16[1040,256]{1,0:T(8,128)(2,1)S(1)}, bf16[1040,256]{1,0:T(8,128)(2,1)S(1)}, u32[]{:S(2)}, u32[]{:S(2)}) %collective-permute-start.30) | collective-permute-done | bytes 532512 | tf_op jit(solution)/shard_map/ppermute | solution.py:548
  157.5 1.7 collective-permute-start.33
  160.6 7.1 %collective-permute-done.33 = bf16[1040,256]{1,0:T(8,128)(2,1)S(1)} collective-permute-done((bf16[1040,256]{1,0:T(8,128)(2,1)S(1)}, bf16[1040,256]{1,0:T(8,128)(2,1)S(1)}, u32[]{:S(2)}, u32[]{:S(2)}) %collective-permute-start.33) | collective-permute-done | bytes 532512 | tf_op jit(solution)/shard_map/ppermute | solution.py:551
  170.7 1.7 add_convert_fusion.2
  175.1 5.5 %collective-permute-done.35 = bf16[256,512]{1,0:T(8,128)(2,1)S(1)} collective-permute-done((bf16[256,512]{1,0:T(8,128)(2,1)}, bf16[256,512]{1,0:T(8,128)(2,1)S(1)}, u32[]{:S(2)}, u32[]{:S(2)}) %collective-permute-start.35) | collective-permute-done | bytes 262176 | tf_op jit(solution)/shard_map/ppermute | solution.py:718
  182.5 4.2 %all-to-all-start = ((bf16[8,32,512]{2,1,0:T(8,128)(2,1)}), bf16[8,32,512]{2,1,0:T(8,128)(2,1)S(1)}, u32[]{:S(2)}, u32[]{:S(2)}) async-start(bf16[8,32,512]{2,1,0:T(8,128)(2,1)} %multiply_convert_fusion.1), calls=%async_computation | async-start | bytes 524288 | tf_op jit(solution)/shard_map/all_to_all | solution.py:724
  187.3 7.6 %all-to-all-done = bf16[8,32,512]{2,1,0:T(8,128)(2,1)S(1)} async-done(((bf16[8,32,512]{2,1,0:T(8,128)(2,1)}), bf16[8,32,512]{2,1,0:T(8,128)(2,1)S(1)}, u32[]{:S(2)}, u32[]{:S(2)}) %all-to-all-start) | async-done | bytes 262176 | tf_op jit(solution)/shard_map/all_to_all | solution.py:724
  (138 shorter events, 47.0 us)
Async XLA Ops:
  4.3 12.5 %collective-permute-start = (bf16[32,1024]{1,0:T(8,128)(2,1)}, bf16[32,1024]{1,0:T(8,128)(2,1)S(1)}, u32[]{:S(2)}, u32[]{:S(2)}) collective-permute-start(bf16[32,1024]{1,0:T(8,128)(2,1)} %get-tuple-element.69), channel_id=1, source_target_pairs={{0,8},{4,12},{8,0},{12,4},{16,24},{20,28},{24,16},{28,20},{1,9},{5... | collective-permute-start | bytes 196616 | tf_op jit(solution)/shard_map/ppermute | solution.py:548
  7.4 9.5 %collective-permute-start.1 = (bf16[32,1024]{1,0:T(8,128)(2,1)S(1)}, bf16[32,1024]{1,0:T(8,128)(2,1)}, u32[]{:S(2)}, u32[]{:S(2)}) collective-permute-start(bf16[32,1024]{1,0:T(8,128)(2,1)S(1)} %get-tuple-element.68), channel_id=1, source_target_pairs={{0,16},{4,20},{8,24},{12,28},{16,0},{20,4},{24,8},{28,12},{1,17},{... | collective-permute-start | bytes 196616 | tf_op jit(solution)/shard_map/ppermute | solution.py:548
  9.9 22.6 %collective-permute-start.11 = (bf16[512,256]{1,0:T(8,128)(2,1)}, bf16[512,256]{1,0:T(8,128)(2,1)S(1)}, u32[]{:S(2)}, u32[]{:S(2)}) collective-permute-start(bf16[512,256]{1,0:T(8,128)(2,1)} %get-tuple-element.37), channel_id=1, source_target_pairs={{0,4},{4,0},{8,12},{12,8},{16,20},{20,16},{24,28},{28,24},{1,5},{5... | collective-permute-start | bytes 786440 | tf_op jit(solution)/shard_map/ppermute | solution.py:551
  17.8 9.3 %collective-permute-start.6 = (bf16[4,32,1024]{2,1,0:T(8,128)(2,1)S(1)}, bf16[4,32,1024]{2,1,0:T(8,128)(2,1)S(1)}, u32[]{:S(2)}, u32[]{:S(2)}) collective-permute-start(bf16[4,32,1024]{2,1,0:T(8,128)(2,1)S(1)} %pad_maximum_fusion.refs_0_), channel_id=1, source_target_pairs={{0,4},{4,0},{8,12},{12,8},{16,20},{20,16},{24,28},{28,24},{1,5},{5... | collective-permute-start | bytes 786440 | tf_op jit(solution)/shard_map/ppermute | solution.py:551
  19.8 13.6 %collective-permute-start.4 = (bf16[4,32,1024]{2,1,0:T(8,128)(2,1)S(1)}, bf16[4,32,1024]{2,1,0:T(8,128)(2,1)}, u32[]{:S(2)}, u32[]{:S(2)}) collective-permute-start(bf16[4,32,1024]{2,1,0:T(8,128)(2,1)S(1)} %pad_maximum_fusion.refs_0_), channel_id=1, source_target_pairs={{0,2},{1,3},{2,0},{3,1},{4,6},{5,7},{6,4},{7,5},{8,10},{9,11},{10,... | collective-permute-start | bytes 786440 | tf_op jit(solution)/shard_map/ppermute | solution.py:618
  21.3 12.3 %collective-permute-start.10 = (bf16[512,256]{1,0:T(8,128)(2,1)}, bf16[512,256]{1,0:T(8,128)(2,1)S(1)}, u32[]{:S(2)}, u32[]{:S(2)}) collective-permute-start(bf16[512,256]{1,0:T(8,128)(2,1)} %get-tuple-element.36), channel_id=1, source_target_pairs={{0,4},{4,0},{8,12},{12,8},{16,20},{20,16},{24,28},{28,24},{1,5},{5... | collective-permute-start | bytes 786440 | tf_op jit(solution)/shard_map/ppermute | solution.py:551
  27.1 7.5 %collective-permute-start.8 = (bf16[4,32,1024]{2,1,0:T(8,128)(2,1)S(1)}, bf16[4,32,1024]{2,1,0:T(8,128)(2,1)}, u32[]{:S(2)}, u32[]{:S(2)}) collective-permute-start(bf16[4,32,1024]{2,1,0:T(8,128)(2,1)S(1)} %collective-permute-done.6.refs_4_), channel_id=1, source_target_pairs={{0,2},{1,3},{2,0},{3,1},{4,6},{5,7},{6,4},{7,5},{8,10},{9,11},{10,... | collective-permute-start | bytes 786440 | tf_op jit(solution)/shard_map/ppermute | solution.py:618
  32.5 9.0 %collective-permute-start.3 = (bf16[4,32,1024]{2,1,0:T(8,128)(2,1)S(1)}, bf16[4,32,1024]{2,1,0:T(8,128)(2,1)}, u32[]{:S(2)}, u32[]{:S(2)}) collective-permute-start(bf16[4,32,1024]{2,1,0:T(8,128)(2,1)S(1)} %pad_maximum_fusion.refs_0_), channel_id=1, source_target_pairs={{0,1},{1,0},{2,3},{3,2},{4,5},{5,4},{6,7},{7,6},{8,9},{9,8},{10,11... | collective-permute-start | bytes 786440 | tf_op jit(solution)/shard_map/ppermute | solution.py:618
  32.5 9.0 %collective-permute-start.12 = (bf16[512,256]{1,0:T(8,128)(2,1)}, bf16[512,256]{1,0:T(8,128)(2,1)}, u32[]{:S(2)}, u32[]{:S(2)}) collective-permute-start(bf16[512,256]{1,0:T(8,128)(2,1)} %bitcast.62), channel_id=1, source_target_pairs={{0,4},{4,0},{8,12},{12,8},{16,20},{20,16},{24,28},{28,24},{1,5},{5... | collective-permute-start | bytes 786440 | tf_op jit(solution)/shard_map/ppermute | solution.py:551
  33.4 8.2 %collective-permute-start.7 = (bf16[4,32,1024]{2,1,0:T(8,128)(2,1)S(1)}, bf16[4,32,1024]{2,1,0:T(8,128)(2,1)}, u32[]{:S(2)}, u32[]{:S(2)}) collective-permute-start(bf16[4,32,1024]{2,1,0:T(8,128)(2,1)S(1)} %collective-permute-done.6.refs_4_), channel_id=1, source_target_pairs={{0,1},{1,0},{2,3},{3,2},{4,5},{5,4},{6,7},{7,6},{8,9},{9,8},{10,11... | collective-permute-start | bytes 786440 | tf_op jit(solution)/shard_map/ppermute | solution.py:618
  34.3 7.2 %collective-permute-start.5 = (bf16[4,32,1024]{2,1,0:T(8,128)(2,1)}, bf16[4,32,1024]{2,1,0:T(8,128)(2,1)}, u32[]{:S(2)}, u32[]{:S(2)}) collective-permute-start(bf16[4,32,1024]{2,1,0:T(8,128)(2,1)} %collective-permute-done.4.refs_2_), channel_id=1, source_target_pairs={{0,1},{1,0},{2,3},{3,2},{4,5},{5,4},{6,7},{7,6},{8,9},{9,8},{10,11... | collective-permute-start | bytes 786440 | tf_op jit(solution)/shard_map/ppermute | solution.py:618
  50.6 13.9 %collective-permute-start.20 = (bf16[1056,256]{1,0:T(8,128)(2,1)S(1)}, bf16[1056,256]{1,0:T(8,128)(2,1)S(1)}, u32[]{:S(2)}, u32[]{:S(2)}) collective-permute-start(bf16[1056,256]{1,0:T(8,128)(2,1)S(1)} %get-tuple-element.48), channel_id=1, source_target_pairs={{0,4},{4,0},{8,12},{12,8},{16,20},{20,16},{24,28},{28,24},{1,5},{5... | collective-permute-start | bytes 1622024 | tf_op jit(solution)/shard_map/ppermute | solution.py:551
  51.5 15.3 %collective-permute-start.14 = (bf16[1024,256]{1,0:T(8,128)(2,1)S(1)}, bf16[1024,256]{1,0:T(8,128)(2,1)S(1)}, u32[]{:S(2)}, u32[]{:S(2)}) collective-permute-start(bf16[1024,256]{1,0:T(8,128)(2,1)S(1)} %get-tuple-element.42), channel_id=1, source_target_pairs={{0,8},{4,12},{24,16},{28,20},{1,9},{5,13},{25,17},{29,21},{2,10},{... | collective-permute-start | bytes 1572872 | tf_op jit(solution)/shard_map/ppermute | solution.py:548
  54.0 23.9 %collective-permute-start.16 = (bf16[1056,256]{1,0:T(8,128)(2,1)S(1)}, bf16[1056,256]{1,0:T(8,128)(2,1)S(1)}, u32[]{:S(2)}, u32[]{:S(2)}) collective-permute-start(bf16[1056,256]{1,0:T(8,128)(2,1)S(1)} %get-tuple-element.44.own_ref), channel_id=1, source_target_pairs={{0,8},{4,12},{24,16},{28,20},{1,9},{5,13},{25,17},{29,21},{2,10},{... | collective-permute-start | bytes 1622024 | tf_op jit(solution)/shard_map/ppermute | solution.py:548
  55.3 32.7 %collective-permute-start.19 = (bf16[1056,256]{1,0:T(8,128)(2,1)}, bf16[1056,256]{1,0:T(8,128)(2,1)}, u32[]{:S(2)}, u32[]{:S(2)}) collective-permute-start(bf16[1056,256]{1,0:T(8,128)(2,1)} %get-tuple-element.43.own_ref), channel_id=1, source_target_pairs={{0,8},{4,12},{24,16},{28,20},{1,9},{5,13},{25,17},{29,21},{2,10},{... | collective-permute-start | bytes 1622024 | tf_op jit(solution)/shard_map/ppermute | solution.py:548
  65.4 27.0 %collective-permute-start.21 = (bf16[1056,256]{1,0:T(8,128)(2,1)}, bf16[1056,256]{1,0:T(8,128)(2,1)}, u32[]{:S(2)}, u32[]{:S(2)}) collective-permute-start(bf16[1056,256]{1,0:T(8,128)(2,1)} %onward.4), channel_id=1, source_target_pairs={{8,0},{12,4},{16,24},{20,28},{9,1},{13,5},{17,25},{21,29},{10,2},{... | collective-permute-start | bytes 1622024 | tf_op jit(solution)/shard_map/ppermute | solution.py:548
  66.9 28.5 %collective-permute-start.15 = (bf16[1024,256]{1,0:T(8,128)(2,1)S(1)}, bf16[1024,256]{1,0:T(8,128)(2,1)S(1)}, u32[]{:S(2)}, u32[]{:S(2)}) collective-permute-start(bf16[1024,256]{1,0:T(8,128)(2,1)S(1)} %add_convert_fusion.1.refs_6_), channel_id=1, source_target_pairs={{8,16},{12,20},{16,8},{20,12},{9,17},{13,21},{17,9},{21,13},{10,18... | collective-permute-start | bytes 1572872 | tf_op jit(solution)/shard_map/ppermute | solution.py:548
  67.6 28.0 %collective-permute-start.18 = (bf16[1056,256]{1,0:T(8,128)(2,1)}, bf16[1056,256]{1,0:T(8,128)(2,1)}, u32[]{:S(2)}, u32[]{:S(2)}) collective-permute-start(bf16[1056,256]{1,0:T(8,128)(2,1)} %get-tuple-element.45), channel_id=1, source_target_pairs={{0,4},{4,0},{8,12},{12,8},{16,20},{20,16},{24,28},{28,24},{1,5},{5... | collective-permute-start | bytes 1622024 | tf_op jit(solution)/shard_map/ppermute | solution.py:551
  79.9 16.8 %collective-permute-start.17 = (bf16[1056,256]{1,0:T(8,128)(2,1)}, bf16[1056,256]{1,0:T(8,128)(2,1)}, u32[]{:S(2)}, u32[]{:S(2)}) collective-permute-start(bf16[1056,256]{1,0:T(8,128)(2,1)} %onward.3), channel_id=1, source_target_pairs={{8,24},{12,28},{16,0},{20,4},{9,25},{13,29},{17,1},{21,5},{10,26},... | collective-permute-start | bytes 1622024 | tf_op jit(solution)/shard_map/ppermute | solution.py:548
  88.0 14.9 %collective-permute-start.22 = (bf16[1056,256]{1,0:T(8,128)(2,1)}, bf16[1056,256]{1,0:T(8,128)(2,1)S(1)}, u32[]{:S(2)}, u32[]{:S(2)}) collective-permute-start(bf16[1056,256]{1,0:T(8,128)(2,1)} %onward.4), channel_id=1, source_target_pairs={{0,8},{4,12},{24,16},{28,20},{1,9},{5,13},{25,17},{29,21},{2,10},{... | collective-permute-start | bytes 1622024 | tf_op jit(solution)/shard_map/ppermute | solution.py:548
  94.7 15.6 %collective-permute-start.23 = (bf16[1056,256]{1,0:T(8,128)(2,1)S(1)}, bf16[1056,256]{1,0:T(8,128)(2,1)S(1)}, u32[]{:S(2)}, u32[]{:S(2)}) collective-permute-start(bf16[1056,256]{1,0:T(8,128)(2,1)S(1)} %onward.5), channel_id=1, source_target_pairs={{8,16},{12,20},{16,8},{20,12},{9,17},{13,21},{17,9},{21,13},{10,18... | collective-permute-start | bytes 1622024 | tf_op jit(solution)/shard_map/ppermute | solution.py:548
  96.7 13.6 %collective-permute-start.24 = (bf16[1024,256]{1,0:T(8,128)(2,1)S(1)}, bf16[1024,256]{1,0:T(8,128)(2,1)S(1)}, u32[]{:S(2)}, u32[]{:S(2)}) collective-permute-start(bf16[1024,256]{1,0:T(8,128)(2,1)S(1)} %multiply_convert_fusion), channel_id=1, source_target_pairs={{8,0},{12,4},{16,24},{20,28},{9,1},{13,5},{17,25},{21,29},{10,2},{... | collective-permute-start | bytes 1572872 | tf_op jit(solution)/shard_map/ppermute | solution.py:548
  121.5 12.5 %collective-permute-start.28 = (bf16[1040,256]{1,0:T(8,128)(2,1)S(1)}, bf16[1040,256]{1,0:T(8,128)(2,1)S(1)}, u32[]{:S(2)}, u32[]{:S(2)}) collective-permute-start(bf16[1040,256]{1,0:T(8,128)(2,1)S(1)} %scan.1), channel_id=1, source_target_pairs={{0,8},{4,12},{8,0},{12,4},{16,24},{20,28},{24,16},{28,20},{1,9},{5... | collective-permute-start | bytes 1597448 | tf_op jit(solution)/shard_map/ppermute | solution.py:548
  123.0 21.0 %collective-permute-start.27 = (bf16[1040,256]{1,0:T(8,128)(2,1)S(1)}, bf16[1040,256]{1,0:T(8,128)(2,1)S(1)}, u32[]{:S(2)}, u32[]{:S(2)}) collective-permute-start(bf16[1040,256]{1,0:T(8,128)(2,1)S(1)} %scan.1), channel_id=1, source_target_pairs={{0,4},{4,0},{8,12},{12,8},{16,20},{20,16},{24,28},{28,24},{1,5},{5... | collective-permute-start | bytes 1597448 | tf_op jit(solution)/shard_map/ppermute | solution.py:551
  123.9 20.0 %collective-permute-start.26 = (bf16[1040,256]{1,0:T(8,128)(2,1)}, bf16[1040,256]{1,0:T(8,128)(2,1)S(1)}, u32[]{:S(2)}, u32[]{:S(2)}) collective-permute-start(bf16[1040,256]{1,0:T(8,128)(2,1)} %collective-permute-done.25), channel_id=1, source_target_pairs={{8,0},{12,4},{16,24},{20,28},{9,1},{13,5},{17,25},{21,29},{10,2},{... | collective-permute-start | bytes 1597448 | tf_op jit(solution)/shard_map/ppermute | solution.py:548
  133.9 11.2 %collective-permute-start.29 = (bf16[1040,256]{1,0:T(8,128)(2,1)S(1)}, bf16[1040,256]{1,0:T(8,128)(2,1)S(1)}, u32[]{:S(2)}, u32[]{:S(2)}) collective-permute-start(bf16[1040,256]{1,0:T(8,128)(2,1)S(1)} %collective-permute-done.28), channel_id=1, source_target_pairs={{8,16},{12,20},{16,8},{20,12},{9,17},{13,21},{17,9},{21,13},{10,18... | collective-permute-start | bytes 1597448 | tf_op jit(solution)/shard_map/ppermute | solution.py:548
  134.6 22.9 %collective-permute-start.31 = (bf16[1040,256]{1,0:T(8,128)(2,1)S(1)}, bf16[1040,256]{1,0:T(8,128)(2,1)S(1)}, u32[]{:S(2)}, u32[]{:S(2)}) collective-permute-start(bf16[1040,256]{1,0:T(8,128)(2,1)S(1)} %collective-permute-done.28), channel_id=1, source_target_pairs={{0,4},{4,0},{8,12},{12,8},{16,20},{20,16},{24,28},{28,24},{1,5},{5... | collective-permute-start | bytes 1597448 | tf_op jit(solution)/shard_map/ppermute | solution.py:551
  143.9 15.3 %collective-permute-start.32 = (bf16[1040,256]{1,0:T(8,128)(2,1)S(1)}, bf16[1040,256]{1,0:T(8,128)(2,1)S(1)}, u32[]{:S(2)}, u32[]{:S(2)}) collective-permute-start(bf16[1040,256]{1,0:T(8,128)(2,1)S(1)} %broadcast_select_fusion.1), channel_id=1, source_target_pairs={{0,4},{4,0},{8,12},{12,8},{16,20},{20,16},{24,28},{28,24},{1,5},{5... | collective-permute-start | bytes 1597448 | tf_op jit(solution)/shard_map/ppermute | solution.py:551
  145.1 12.3 %collective-permute-start.30 = (bf16[1040,256]{1,0:T(8,128)(2,1)S(1)}, bf16[1040,256]{1,0:T(8,128)(2,1)S(1)}, u32[]{:S(2)}, u32[]{:S(2)}) collective-permute-start(bf16[1040,256]{1,0:T(8,128)(2,1)S(1)} %collective-permute-done.29), channel_id=1, source_target_pairs={{8,0},{12,4},{16,24},{20,28},{9,1},{13,5},{17,25},{21,29},{10,2},{... | collective-permute-start | bytes 1597448 | tf_op jit(solution)/shard_map/ppermute | solution.py:548
  157.5 10.2 %collective-permute-start.33 = (bf16[1040,256]{1,0:T(8,128)(2,1)S(1)}, bf16[1040,256]{1,0:T(8,128)(2,1)S(1)}, u32[]{:S(2)}, u32[]{:S(2)}) collective-permute-start(bf16[1040,256]{1,0:T(8,128)(2,1)S(1)} %broadcast_select_fusion), channel_id=1, source_target_pairs={{0,4},{4,0},{8,12},{12,8},{16,20},{20,16},{24,28},{28,24},{1,5},{5... | collective-permute-start | bytes 1597448 | tf_op jit(solution)/shard_map/ppermute | solution.py:551
  172.4 8.3 %collective-permute-start.35 = (bf16[256,512]{1,0:T(8,128)(2,1)}, bf16[256,512]{1,0:T(8,128)(2,1)S(1)}, u32[]{:S(2)}, u32[]{:S(2)}) collective-permute-start(bf16[256,512]{1,0:T(8,128)(2,1)} %add_convert_fusion.2), channel_id=1, source_target_pairs={{0,2},{1,3},{2,0},{3,1},{4,6},{5,7},{6,4},{7,5},{8,10},{9,11},{10,... | collective-permute-start | bytes 786440 | tf_op jit(solution)/shard_map/ppermute | solution.py:718
  182.5 12.4 %all-to-all-start = ((bf16[8,32,512]{2,1,0:T(8,128)(2,1)}), bf16[8,32,512]{2,1,0:T(8,128)(2,1)S(1)}, u32[]{:S(2)}, u32[]{:S(2)}) async-start(bf16[8,32,512]{2,1,0:T(8,128)(2,1)} %multiply_convert_fusion.1), calls=%async_computation | async-start | bytes 524288 | tf_op jit(solution)/shard_map/all_to_all | solution.py:724
  (21 other events, 303.7 us)

commit v7 on v1

--- a/solution.py
+++ b/solution.py
@@ -201,11 +201,11 @@
 def project_kernel(ranks, place_ref, factor_ref, *refs):
     hidden = [refs[x * ranks : (x + 1) * ranks] for x in range(PAIR)]
     refs = refs[PAIR * ranks :]
-    own_x, x_far, own_bc, other_bc, own_dt, other_dt = refs[:6]
-    far_refs = refs[6 : 6 + LINE // 2]
-    near_refs = refs[6 + LINE // 2 : 6 + LINE]
-    sent_refs = refs[6 + LINE : 6 + LINE + LINE // 2]
-    bc_ref, largest_ref, quant_ref, near_dt, all_dt = refs[6 + LINE + LINE // 2 :]
+    own_x, x_far, own_bc, own_dt, rest = refs[:5]
+    far_refs, near_refs, sent_refs = (
+        refs[5 + at : 5 + at + LINE // 2] for at in range(0, 3 * LINE // 2, LINE // 2)
+    )
+    bc_ref, largest_ref, quant_ref, near_dt, all_dt = refs[5 + 3 * LINE // 2 :]
     side, z = (place_ref[1], place_ref[2])
     factor = factor_ref[0]
     depth = own_x.shape[0]
@@ -221,6 +221,10 @@
                     quant_ref[half, block, j] = scaled.astype(jnp.bfloat16)
                     top = jnp.max(jnp.abs(values).reshape(-1, ROWS, depth), axis=0)
                     largest = top if largest is None else jnp.maximum(largest, top)
+    step_rows = own_dt.shape[0]
+    other_dt = jnp.concatenate(
+        [rest[at : at + step_rows] for at in range(depth, rest.shape[0], step_rows)], axis=1
+    )
     width = largest_ref.shape[1]
     top = largest[:, :width]
     for at in range(width, depth, width):
@@ -262,8 +266,8 @@
         extra_rows = slice(tokens + cut * extra, tokens + (cut + 1) * extra)
         ours = nt_dot(own_dt[...], near)
         near_dt[...] = ours.reshape(near_dt.shape)
-        all_dt[...] = (ours + nt_dot(other_dt[...], far)).reshape(all_dt.shape)
-        bc_ref[at_rows] = both(own_bc[...], other_bc[...]).astype(jnp.bfloat16)
+        all_dt[...] = (ours + nt_dot(other_dt, far)).reshape(all_dt.shape)
+        bc_ref[at_rows] = both(own_bc[...], rest[:depth]).astype(jnp.bfloat16)
         for m in range(LINE // 2):
             owner = z ^ (m + LINE // 2)
             run = side * LINE + owner
@@ -289,7 +293,7 @@
     channels, maps_wide = (x_wide // LINE, weights[1].shape[1])
     tokens = line * PAIR * ranks * own
     extra = tokens // channels * ROWS
-    dt_shape = (weights[-1].shape[0] // ROWS, ROWS, tokens // CUTS)
+    dt_shape = (weights[2].shape[0] // ROWS, ROWS, tokens // CUTS)
     payload = jax.ShapeDtypeStruct((tokens + extra, channels), jnp.bfloat16)
     maps = jax.ShapeDtypeStruct((tokens, maps_wide), jnp.bfloat16)
     largest = jax.ShapeDtypeStruct((ROWS, 128), jnp.float32)
@@ -393,7 +397,13 @@
 
     up = lax.broadcasted_iota(jnp.int32, (SPAN, SPAN), 0)
     across = lax.broadcasted_iota(jnp.int32, (SPAN, SPAN), 1)
-    lane = lax.broadcasted_iota(jnp.int32, (SPAN, channels), 1)
+    together = SPAN // HEAD_DIM
+    insides = [
+        ((across >= h * HEAD_DIM) & (across < (h + 1) * HEAD_DIM))
+        .astype(jnp.float32)
+        .astype(jnp.bfloat16)
+        for h in range(together)
+    ]
     lower = up >= across
     upper = (up <= across).astype(jnp.float32)
     lanes = across[:ROWS]
@@ -438,24 +448,33 @@
         ).T
 
         def spread(row):
-            result = jnp.broadcast_to(turned[:, row : row + 1], (SPAN, channels))
-            for h in range(1, heads):
-                result = jnp.where(lane >= h * HEAD_DIM, turned[:, row + h : row + h + 1], result)
-            return result
+            tiles = []
+            for first in range(row, row + heads, together):
+                tile = jnp.broadcast_to(turned[:, first : first + 1], across.shape)
+                for h in range(1, together):
+                    column = turned[:, first + h : first + h + 1]
+                    tile = jnp.where(across >= h * HEAD_DIM, column, tile)
+                tiles.append(tile)
+            return jnp.concatenate(tiles, axis=1)
 
         inner = jnp.where(lower, nt_dot(out_map, in_map), 0.0)
         x_wide = x_act.astype(jnp.float32)
-        weights, spaced = ([], [])
-        for h in range(heads):
-            gap = jnp.where(lower, turned[:, h : h + 1] - cum[h : h + 1], 0.0)
-            weights.append((inner * jnp.exp(gap) * step[h : h + 1]).astype(jnp.bfloat16))
-            inside = (lane >= h * HEAD_DIM) & (lane < (h + 1) * HEAD_DIM)
-            spaced.append(jnp.where(inside, x_wide, 0.0).astype(jnp.bfloat16))
-        local_part = jnp.dot(
-            jnp.concatenate(weights, axis=1),
-            jnp.concatenate(spaced, axis=0),
-            preferred_element_type=jnp.float32,
-        )
+        local_tiles = []
+        for first in range(0, heads, together):
+            weights, spaced = ([], [])
+            tile = x_act[:, first * HEAD_DIM : (first + together) * HEAD_DIM]
+            for h in range(first, first + together):
+                gap = jnp.where(lower, turned[:, h : h + 1] - cum[h : h + 1], 0.0)
+                weights.append((inner * jnp.exp(gap) * step[h : h + 1]).astype(jnp.bfloat16))
+                spaced.append(tile * insides[h - first])
+            local_tiles.append(
+                jnp.dot(
+                    jnp.concatenate(weights, axis=1),
+                    jnp.concatenate(spaced, axis=0),
+                    preferred_element_type=jnp.float32,
+                )
+            )
+        local_part = jnp.concatenate(local_tiles, axis=1)
         grown = spread(2 * ROWS)
         x_weighted = (x_wide * spread(ROWS)).astype(jnp.bfloat16)
         added = lax.dot_general(
@@ -588,10 +607,11 @@
     x_sent = lax.dynamic_slice_in_dim(w_x, at, half_run, axis=1)
     x_sent, hidden_in = tie((x_sent, hidden_in))
     x_far = across(x_sent)
-    x_far, maps_sent, dt_sent = tie(
-        (x_far, pick(w_bc, 1, 1 - side).reshape(depth, 2 * STATE), w_dt.T)
-    )
-    bc_other, dt_other = (across(maps_sent), across(dt_sent))
+    dt_rows = w_dt.T
+    dt_cut = [dt_rows[:, at : at + 2 * STATE] for at in range(0, depth, 2 * STATE)]
+    maps_sent = pick(w_bc, 1, 1 - side).reshape(depth, 2 * STATE)
+    x_far, rest_sent = tie((x_far, jnp.concatenate([maps_sent, *dt_cut], axis=0)))
+    rest_other = across(rest_sent)
     bc_own = pick(w_bc, 1, side).reshape(depth, 2 * STATE)
 
     def line_columns(m):
@@ -602,8 +622,8 @@
         arrived.append(along(line_columns(m), [(s, s ^ m) for s in range(LINE)]))
     stacked = jnp.stack(arrived)
     beyond_pair = across(stacked)
-    beyond_pair, small, start_state, bc_own, dt_sent = tie(
-        (beyond_pair, small, start_state, bc_own, dt_sent)
+    beyond_pair, small, start_state, bc_own, dt_rows = tie(
+        (beyond_pair, small, start_state, bc_own, dt_rows)
     )
     rows = []
     for mine in (stacked, beyond_pair):
@@ -622,7 +642,7 @@
     middle = [(next_start, next_end), (next_end, next_start)]
     over_middle = [(next_start, end), (next_end, start)]
     beside_pairs = [(s, s ^ 1) for s in range(LINE)]
-    weights = (x_far, bc_own, bc_other, dt_sent, dt_other)
+    weights = (x_far, bc_own, dt_rows, rest_other)
     over, far, mine, near, mine_sent, near_sent, maps, largest = project(
         place, factor, rows, w_x, weights
     )

time: 194 us -> 192 us (0.990)
  local copies, waits for them, and re-layouts: 15.6 us -> 18.6 us
  starting transfers between devices: 52.8 us -> 49.9 us
  other arithmetic: 9.05 us -> 6.55 us
    ppermute x10 -> x9, starting transfers between devices: 15.4 us -> 10.1 us  [across(): return lax.ppermute(value, 'seq', [(s, s ^ 1) for s in range(count)])]
    unnamed x32 -> x38, local copies, waits for them, and re-layouts: 6.93 us -> 9.12 us
    ppermute x10 -> x9, waiting for transfers between devices: 20 us -> 20.8 us  [across(): return lax.ppermute(value, 'seq', [(s, s ^ 1) for s in range(count)])]
  transfers between devices with their start and end apart: 38 -> 37, of which waited for: 18 -> 19; matrix products, arithmetic and copies ran while one was open for 9% -> 8% of each run, Pallas kernels for 2% -> 2%
where the time goes in v7:
time: 192 us; the launch traced here: 191 us
  waiting for transfers between devices  92.1 us (48%)
  starting transfers between devices  49.9 us (26%)
  local copies, waits for them, and re-layouts  18.6 us (10%)
  Pallas kernels  18.3 us (10%)
  other arithmetic  6.55 us (3%)
  matrix products  3.66 us (2%)
    ppermute x17, waiting for transfers between devices, along(): return lax.ppermute(value, 'seq', moves)  54.4 us
    ppermute x17, starting transfers between devices, along(): return lax.ppermute(value, 'seq', moves)  28 us
    ppermute x9, waiting for transfers between devices, across(): return lax.ppermute(value, 'seq', [(s, s ^ 1) for s in range(count)])  20.8 us
    ppermute x9, starting transfers between devices, across(): return lax.ppermute(value, 'seq', [(s, s ^ 1) for s in range(count)])  10.1 us
    unnamed x38, local copies, waits for them, and re-layouts  9.12 us
    pallas_call x1, Pallas kernels, scan(): pl.pallas_call(scan_kernel, in_specs=[SMEM, SMEM] + [VMEM] * (len(sums) +...  8.49 us
    all_to_all x1, waiting for transfers between devices, by_heads(): lax.all_to_all(final.astype(bf16), 'seq', split_axis=0, concat_axis=0, ti...  7.62 us
    ppermute x1, waiting for transfers between devices, by_heads(): received = lax.ppermute(sent.astype(bf16), 'tensor', pairs)  6.89 us
  transfers between devices with their start and end apart: 37, of which 19 were waited for; matrix products, arithmetic and copies ran while one was open for 8% of the time, Pallas kernels for 2%

profile of v7, /device:TPU:0, one launch (start us, length us, event | category | flops | bytes accessed | tf_op | source)
XLA Modules:
  0.0 191.1 jit_solution(4845763996926801992)
XLA Ops:
  0.8 2.0 %constant_dynamic-slice_fusion.9 = bf16[512,512]{1,0:T(8,128)(2,1)} fusion(bf16[512,2048]{1,0:T(8,128)(2,1)} %refs_8_.1, s32[]{:T(128)S(6)} %select_n.123), kind=kLoop, calls=%fused_computation.64 | loop fusion | bytes 1048580 | tf_op jit(solution)/shard_map/dynamic_slice | solution.py:607
  3.7 3.1 %collective-permute-start = (bf16[32,1024]{1,0:T(8,128)(2,1)S(1)}, bf16[32,1024]{1,0:T(8,128)(2,1)S(1)}, u32[]{:S(2)}, u32[]{:S(2)}) collective-permute-start(bf16[32,1024]{1,0:T(8,128)(2,1)S(1)} %get-tuple-element.63), channel_id=1, source_target_pairs={{0,8},{4,12},{8,0},{12,4},{16,24},{20,28},{24,16},{28,20},{1,9},{5... | collective-permute-start | bytes 196616 | tf_op jit(solution)/shard_map/ppermute | solution.py:566
  6.8 2.6 %collective-permute-start.1 = (bf16[32,1024]{1,0:T(8,128)(2,1)S(1)}, bf16[32,1024]{1,0:T(8,128)(2,1)S(1)}, u32[]{:S(2)}, u32[]{:S(2)}) collective-permute-start(bf16[32,1024]{1,0:T(8,128)(2,1)S(1)} %get-tuple-element.62), channel_id=1, source_target_pairs={{0,16},{4,20},{8,24},{12,28},{16,0},{20,4},{24,8},{28,12},{1,17},{... | collective-permute-start | bytes 196616 | tf_op jit(solution)/shard_map/ppermute | solution.py:566
  9.4 1.7 collective-permute-start.10
  15.5 1.6 collective-permute-start.6
  17.1 2.2 %constant_dynamic-slice_fusion.2 = (bf16[512,1,2,128]{3,2,1,0:T(2,128)(2,1)}, bf16[512,1,2,128]{3,2,1,0:T(2,128)(2,1)}) fusion(bf16[512,2,2,128]{3,2,1,0:T(2,128)(2,1)} %param.18, s32[]{:T(128)S(6)} %select_n.132, s32[]{:T(128)S(6)} %select_n.129), kind=kLoop, calls=%fused_computation.57 | loop fusion | bytes 1048584 | tf_op jit(solution)/shard_map/jit(dynamic_index_in_dim)/dynamic_slice | solution.py:562
  21.6 1.6 collective-permute-start.4
  23.2 5.3 %collective-permute-done.6.refs_4_ = bf16[4,32,1024]{2,1,0:T(8,128)(2,1)} collective-permute-done((bf16[4,32,1024]{2,1,0:T(8,128)(2,1)S(1)}, bf16[4,32,1024]{2,1,0:T(8,128)(2,1)}, u32[]{:S(2)}, u32[]{:S(2)}) %collective-permute-start.6) | collective-permute-done | bytes 262176 | tf_op jit(solution)/shard_map/ppermute | solution.py:569
  36.6 2.9 %collective-permute-done.11.refs_12_ = bf16[576,256]{1,0:T(8,128)(2,1)S(1)} collective-permute-done((bf16[576,256]{1,0:T(8,128)(2,1)}, bf16[576,256]{1,0:T(8,128)(2,1)S(1)}, u32[]{:S(2)}, u32[]{:S(2)}) %collective-permute-start.11) | collective-permute-done | bytes 294944 | tf_op jit(solution)/shard_map/ppermute | solution.py:569
  39.5 1.6 copy-done.7
  42.1 5.7 %project.1 = (bf16[1056,256]{1,0:T(8,128)(2,1)}, bf16[1056,256]{1,0:T(8,128)(2,1)S(1)}, bf16[1056,256]{1,0:T(8,128)(2,1)S(1)}, bf16[1056,256]{1,0:T(8,128)(2,1)S...) custom-call(s32[7]{0:T(128)S(1)} %stack.43.place_ref, ...), custom_call_target="tpu_custom_call" | custom-call | flops 2684354560 | bytes 4194304 | tf_op jit(solution)/shard_map/project/pallas_call | solution.py:301
  50.1 2.5 %collective-permute-start.12 = (bf16[1024,256]{1,0:T(8,128)(2,1)S(1)}, bf16[1024,256]{1,0:T(8,128)(2,1)S(1)}, u32[]{:S(2)}, u32[]{:S(2)}) collective-permute-start(bf16[1024,256]{1,0:T(8,128)(2,1)S(1)} %get-tuple-element.38), channel_id=1, source_target_pairs={{0,8},{4,12},{24,16},{28,20},{1,9},{5,13},{25,17},{29,21},{2,10},{... | collective-permute-start | bytes 1572872 | tf_op jit(solution)/shard_map/ppermute | solution.py:566
  53.9 2.1 %collective-permute-start.17 = (bf16[1056,256]{1,0:T(8,128)(2,1)}, bf16[1056,256]{1,0:T(8,128)(2,1)}, u32[]{:S(2)}, u32[]{:S(2)}) collective-permute-start(bf16[1056,256]{1,0:T(8,128)(2,1)} %get-tuple-element.39.own_ref), channel_id=1, source_target_pairs={{0,8},{4,12},{24,16},{28,20},{1,9},{5,13},{25,17},{29,21},{2,10},{... | collective-permute-start | bytes 1622024 | tf_op jit(solution)/shard_map/ppermute | solution.py:566
  56.1 4.6 %collective-permute-done.18.received_ref = bf16[1056,256]{1,0:T(8,128)(2,1)S(1)} collective-permute-done((bf16[1056,256]{1,0:T(8,128)(2,1)S(1)}, bf16[1056,256]{1,0:T(8,128)(2,1)S(1)}, u32[]{:S(2)}, u32[]{:S(2)}) %collective-permute-start.18) | collective-permute-done | bytes 540704 | tf_op jit(solution)/shard_map/ppermute | solution.py:569
  62.9 2.1 %collective-permute-done.12 = bf16[1024,256]{1,0:T(8,128)(2,1)S(1)} collective-permute-done((bf16[1024,256]{1,0:T(8,128)(2,1)S(1)}, bf16[1024,256]{1,0:T(8,128)(2,1)S(1)}, u32[]{:S(2)}, u32[]{:S(2)}) %collective-permute-start.12) | collective-permute-done | bytes 524320 | tf_op jit(solution)/shard_map/ppermute | solution.py:566
  66.4 10.2 %collective-permute-done.14.received_ref = bf16[1056,256]{1,0:T(8,128)(2,1)S(1)} collective-permute-done((bf16[1056,256]{1,0:T(8,128)(2,1)S(1)}, bf16[1056,256]{1,0:T(8,128)(2,1)S(1)}, u32[]{:S(2)}, u32[]{:S(2)}) %collective-permute-start.14) | collective-permute-done | bytes 540704 | tf_op jit(solution)/shard_map/ppermute | solution.py:566
  76.5 2.0 %onward.3 = bf16[1056,256]{1,0:T(8,128)(2,1)} custom-call(bf16[1056,256]{1,0:T(8,128)(2,1)} %get-tuple-element.39.own_ref, bf16[1056,256]{1,0:T(8,128)(2,1)S(1)} %collective-permute-done.14.received_ref), custom_call_target="tpu_custom_call" | custom-call | flops 270336 | bytes 1622016 | tf_op jit(solution)/shard_map/onward/pallas_call | solution.py:336
  79.8 4.8 %collective-permute-done.17.received_ref = bf16[1056,256]{1,0:T(8,128)(2,1)} collective-permute-done((bf16[1056,256]{1,0:T(8,128)(2,1)}, bf16[1056,256]{1,0:T(8,128)(2,1)}, u32[]{:S(2)}, u32[]{:S(2)}) %collective-permute-start.17) | collective-permute-done | bytes 540704 | tf_op jit(solution)/shard_map/ppermute | solution.py:566
  84.6 4.4 %collective-permute-start.20 = (bf16[1056,256]{1,0:T(8,128)(2,1)}, bf16[1056,256]{1,0:T(8,128)(2,1)S(1)}, u32[]{:S(2)}, u32[]{:S(2)}) collective-permute-start(bf16[1056,256]{1,0:T(8,128)(2,1)} %onward.4), channel_id=1, source_target_pairs={{0,8},{4,12},{24,16},{28,20},{1,9},{5,13},{25,17},{29,21},{2,10},{... | collective-permute-start | bytes 1622024 | tf_op jit(solution)/shard_map/ppermute | solution.py:566
  93.7 3.8 %collective-permute-done.20.refs_3_ = bf16[1056,256]{1,0:T(8,128)(2,1)S(1)} collective-permute-done((bf16[1056,256]{1,0:T(8,128)(2,1)}, bf16[1056,256]{1,0:T(8,128)(2,1)S(1)}, u32[]{:S(2)}, u32[]{:S(2)}) %collective-permute-start.20) | collective-permute-done | bytes 540704 | tf_op jit(solution)/shard_map/ppermute | solution.py:566
  97.5 6.7 %collective-permute-done.22.refs_8_ = bf16[1024,256]{1,0:T(8,128)(2,1)S(1)} collective-permute-done((bf16[1024,256]{1,0:T(8,128)(2,1)S(1)}, bf16[1024,256]{1,0:T(8,128)(2,1)S(1)}, u32[]{:S(2)}, u32[]{:S(2)}) %collective-permute-start.22) | collective-permute-done | bytes 524320 | tf_op jit(solution)/shard_map/ppermute | solution.py:566
  105.3 8.5 %scan.1 = bf16[1040,256]{1,0:T(8,128)(2,1)S(1)} custom-call(s32[7]{0:T(128)S(1)} %stack.43.place_ref, f32[1]{0:T(128)} %bitcast.3.scale_ref, bf16[1056,256]{1,0:T(8,128)(2,1)S(1)} %copy-done.6, bf16[1056,256]{1,0:T(8,128)(2,1)} %collective-permute-done.16.refs_1_, bf16[1056,256]{1,0:T(8,128)(2,1)} %collective-permute-done.19.refs_2_, ...), custom_call_target="tpu_custom_call" | custom-call | flops 268435456 | bytes 2097152 | tf_op jit(solution)/shard_map/scan/pallas_call | solution.py:511
  115.2 1.8 collective-permute-start.26
  118.9 8.5 %collective-permute-done.26 = bf16[1040,256]{1,0:T(8,128)(2,1)S(1)} collective-permute-done((bf16[1040,256]{1,0:T(8,128)(2,1)S(1)}, bf16[1040,256]{1,0:T(8,128)(2,1)S(1)}, u32[]{:S(2)}, u32[]{:S(2)}) %collective-permute-start.26) | collective-permute-done | bytes 532512 | tf_op jit(solution)/shard_map/ppermute | solution.py:566
  128.9 7.0 %collective-permute-done.24 = bf16[1040,256]{1,0:T(8,128)(2,1)S(1)} collective-permute-done((bf16[1040,256]{1,0:T(8,128)(2,1)}, bf16[1040,256]{1,0:T(8,128)(2,1)S(1)}, u32[]{:S(2)}, u32[]{:S(2)}) %collective-permute-start.24) | collective-permute-done | bytes 532512 | tf_op jit(solution)/shard_map/ppermute | solution.py:566
  139.3 10.1 %collective-permute-done.28 = bf16[1040,256]{1,0:T(8,128)(2,1)S(1)} collective-permute-done((bf16[1040,256]{1,0:T(8,128)(2,1)S(1)}, bf16[1040,256]{1,0:T(8,128)(2,1)S(1)}, u32[]{:S(2)}, u32[]{:S(2)}) %collective-permute-start.28) | collective-permute-done | bytes 532512 | tf_op jit(solution)/shard_map/ppermute | solution.py:566
  149.6 1.6 collective-permute-start.31
  152.5 8.1 %collective-permute-done.31 = bf16[1040,256]{1,0:T(8,128)(2,1)S(1)} collective-permute-done((bf16[1040,256]{1,0:T(8,128)(2,1)S(1)}, bf16[1040,256]{1,0:T(8,128)(2,1)S(1)}, u32[]{:S(2)}, u32[]{:S(2)}) %collective-permute-start.31) | collective-permute-done | bytes 532512 | tf_op jit(solution)/shard_map/ppermute | solution.py:569
  162.8 3.1 %collective-permute-start.35 = (f32[8,128]{1,0:T(8,128)S(1)}, f32[8,128]{1,0:T(8,128)S(1)}, u32[]{:S(2)}, u32[]{:S(2)}) collective-permute-start(f32[8,128]{1,0:T(8,128)S(1)} %add.280), channel_id=1, source_target_pairs={{0,2},{1,3},{2,0},{3,1},{4,6},{5,7},{6,4},{7,5},{8,10},{9,11},{10,... | collective-permute-start | bytes 12296 | tf_op jit(solution)/shard_map/ppermute | solution.py:735
  168.9 6.9 %collective-permute-done.33 = bf16[256,512]{1,0:T(8,128)(2,1)S(1)} collective-permute-done((bf16[256,512]{1,0:T(8,128)(2,1)}, bf16[256,512]{1,0:T(8,128)(2,1)S(1)}, u32[]{:S(2)}, u32[]{:S(2)}) %collective-permute-start.33) | collective-permute-done | bytes 262176 | tf_op jit(solution)/shard_map/ppermute | solution.py:734
  177.7 4.4 %all-to-all-start = ((bf16[8,32,512]{2,1,0:T(8,128)(2,1)}), bf16[8,32,512]{2,1,0:T(8,128)(2,1)S(1)}, u32[]{:S(2)}, u32[]{:S(2)}) async-start(bf16[8,32,512]{2,1,0:T(8,128)(2,1)} %multiply_convert_fusion.1), calls=%async_computation | async-start | bytes 524288 | tf_op jit(solution)/shard_map/all_to_all | solution.py:740
  182.7 7.6 %all-to-all-done = bf16[8,32,512]{2,1,0:T(8,128)(2,1)S(1)} async-done(((bf16[8,32,512]{2,1,0:T(8,128)(2,1)}), bf16[8,32,512]{2,1,0:T(8,128)(2,1)S(1)}, u32[]{:S(2)}, u32[]{:S(2)}) %all-to-all-start) | async-done | bytes 262176 | tf_op jit(solution)/shard_map/all_to_all | solution.py:740
  (140 shorter events, 48.3 us)
Async XLA Ops:
  3.7 10.4 %collective-permute-start = (bf16[32,1024]{1,0:T(8,128)(2,1)S(1)}, bf16[32,1024]{1,0:T(8,128)(2,1)S(1)}, u32[]{:S(2)}, u32[]{:S(2)}) collective-permute-start(bf16[32,1024]{1,0:T(8,128)(2,1)S(1)} %get-tuple-element.63), channel_id=1, source_target_pairs={{0,8},{4,12},{8,0},{12,4},{16,24},{20,28},{24,16},{28,20},{1,9},{5... | collective-permute-start | bytes 196616 | tf_op jit(solution)/shard_map/ppermute | solution.py:566
  6.8 7.4 %collective-permute-start.1 = (bf16[32,1024]{1,0:T(8,128)(2,1)S(1)}, bf16[32,1024]{1,0:T(8,128)(2,1)S(1)}, u32[]{:S(2)}, u32[]{:S(2)}) collective-permute-start(bf16[32,1024]{1,0:T(8,128)(2,1)S(1)} %get-tuple-element.62), channel_id=1, source_target_pairs={{0,16},{4,20},{8,24},{12,28},{16,0},{20,4},{24,8},{28,12},{1,17},{... | collective-permute-start | bytes 196616 | tf_op jit(solution)/shard_map/ppermute | solution.py:566
  9.4 6.1 %collective-permute-start.2 = (bf16[32,1024]{1,0:T(8,128)(2,1)S(1)}, bf16[32,1024]{1,0:T(8,128)(2,1)S(1)}, u32[]{:S(2)}, u32[]{:S(2)}) collective-permute-start(bf16[32,1024]{1,0:T(8,128)(2,1)S(1)} %get-tuple-element.61), channel_id=1, source_target_pairs={{0,24},{4,28},{8,16},{12,20},{16,8},{20,12},{24,0},{28,4},{1,25},{... | collective-permute-start | bytes 196616 | tf_op jit(solution)/shard_map/ppermute | solution.py:566
  9.4 22.3 %collective-permute-start.10 = (bf16[512,512]{1,0:T(8,128)(2,1)}, bf16[512,512]{1,0:T(8,128)(2,1)S(1)}, u32[]{:S(2)}, u32[]{:S(2)}) collective-permute-start(bf16[512,512]{1,0:T(8,128)(2,1)} %constant_dynamic-slice_fusion.9), channel_id=1, source_target_pairs={{0,4},{4,0},{8,12},{12,8},{16,20},{20,16},{24,28},{28,24},{1,5},{5... | collective-permute-start | bytes 1572872 | tf_op jit(solution)/shard_map/ppermute | solution.py:569
  15.5 12.9 %collective-permute-start.6 = (bf16[4,32,1024]{2,1,0:T(8,128)(2,1)S(1)}, bf16[4,32,1024]{2,1,0:T(8,128)(2,1)}, u32[]{:S(2)}, u32[]{:S(2)}) collective-permute-start(bf16[4,32,1024]{2,1,0:T(8,128)(2,1)S(1)} %pad_maximum_fusion.1.refs_0_), channel_id=1, source_target_pairs={{0,4},{4,0},{8,12},{12,8},{16,20},{20,16},{24,28},{28,24},{1,5},{5... | collective-permute-start | bytes 786440 | tf_op jit(solution)/shard_map/ppermute | solution.py:569
  21.6 12.9 %collective-permute-start.4 = (bf16[4,32,1024]{2,1,0:T(8,128)(2,1)S(1)}, bf16[4,32,1024]{2,1,0:T(8,128)(2,1)}, u32[]{:S(2)}, u32[]{:S(2)}) collective-permute-start(bf16[4,32,1024]{2,1,0:T(8,128)(2,1)S(1)} %pad_maximum_fusion.1.refs_0_), channel_id=1, source_target_pairs={{0,2},{1,3},{2,0},{3,1},{4,6},{5,7},{6,4},{7,5},{8,10},{9,11},{10,... | collective-permute-start | bytes 786440 | tf_op jit(solution)/shard_map/ppermute | solution.py:634
  28.4 6.9 %collective-permute-start.8 = (bf16[4,32,1024]{2,1,0:T(8,128)(2,1)}, bf16[4,32,1024]{2,1,0:T(8,128)(2,1)}, u32[]{:S(2)}, u32[]{:S(2)}) collective-permute-start(bf16[4,32,1024]{2,1,0:T(8,128)(2,1)} %collective-permute-done.6.refs_4_), channel_id=1, source_target_pairs={{0,2},{1,3},{2,0},{3,1},{4,6},{5,7},{6,4},{7,5},{8,10},{9,11},{10,... | collective-permute-start | bytes 786440 | tf_op jit(solution)/shard_map/ppermute | solution.py:634
  32.5 7.0 %collective-permute-start.11 = (bf16[576,256]{1,0:T(8,128)(2,1)}, bf16[576,256]{1,0:T(8,128)(2,1)S(1)}, u32[]{:S(2)}, u32[]{:S(2)}) collective-permute-start(bf16[576,256]{1,0:T(8,128)(2,1)} %pad_maximum_fusion), channel_id=1, source_target_pairs={{0,4},{4,0},{8,12},{12,8},{16,20},{20,16},{24,28},{28,24},{1,5},{5... | collective-permute-start | bytes 884744 | tf_op jit(solution)/shard_map/ppermute | solution.py:569
  35.3 4.2 %collective-permute-start.9 = (bf16[4,32,1024]{2,1,0:T(8,128)(2,1)}, bf16[4,32,1024]{2,1,0:T(8,128)(2,1)}, u32[]{:S(2)}, u32[]{:S(2)}) collective-permute-start(bf16[4,32,1024]{2,1,0:T(8,128)(2,1)} %collective-permute-done.8.refs_6_), channel_id=1, source_target_pairs={{0,1},{1,0},{2,3},{3,2},{4,5},{5,4},{6,7},{7,6},{8,9},{9,8},{10,11... | collective-permute-start | bytes 786440 | tf_op jit(solution)/shard_map/ppermute | solution.py:634
  48.6 12.0 %collective-permute-start.18 = (bf16[1056,256]{1,0:T(8,128)(2,1)S(1)}, bf16[1056,256]{1,0:T(8,128)(2,1)S(1)}, u32[]{:S(2)}, u32[]{:S(2)}) collective-permute-start(bf16[1056,256]{1,0:T(8,128)(2,1)S(1)} %get-tuple-element.44), channel_id=1, source_target_pairs={{0,4},{4,0},{8,12},{12,8},{16,20},{20,16},{24,28},{28,24},{1,5},{5... | collective-permute-start | bytes 1622024 | tf_op jit(solution)/shard_map/ppermute | solution.py:569
  50.1 14.8 %collective-permute-start.12 = (bf16[1024,256]{1,0:T(8,128)(2,1)S(1)}, bf16[1024,256]{1,0:T(8,128)(2,1)S(1)}, u32[]{:S(2)}, u32[]{:S(2)}) collective-permute-start(bf16[1024,256]{1,0:T(8,128)(2,1)S(1)} %get-tuple-element.38), channel_id=1, source_target_pairs={{0,8},{4,12},{24,16},{28,20},{1,9},{5,13},{25,17},{29,21},{2,10},{... | collective-permute-start | bytes 1572872 | tf_op jit(solution)/shard_map/ppermute | solution.py:566
  52.6 23.9 %collective-permute-start.14 = (bf16[1056,256]{1,0:T(8,128)(2,1)S(1)}, bf16[1056,256]{1,0:T(8,128)(2,1)S(1)}, u32[]{:S(2)}, u32[]{:S(2)}) collective-permute-start(bf16[1056,256]{1,0:T(8,128)(2,1)S(1)} %get-tuple-element.40.own_ref), channel_id=1, source_target_pairs={{0,8},{4,12},{24,16},{28,20},{1,9},{5,13},{25,17},{29,21},{2,10},{... | collective-permute-start | bytes 1622024 | tf_op jit(solution)/shard_map/ppermute | solution.py:566
  53.9 30.7 %collective-permute-start.17 = (bf16[1056,256]{1,0:T(8,128)(2,1)}, bf16[1056,256]{1,0:T(8,128)(2,1)}, u32[]{:S(2)}, u32[]{:S(2)}) collective-permute-start(bf16[1056,256]{1,0:T(8,128)(2,1)} %get-tuple-element.39.own_ref), channel_id=1, source_target_pairs={{0,8},{4,12},{24,16},{28,20},{1,9},{5,13},{25,17},{29,21},{2,10},{... | collective-permute-start | bytes 1622024 | tf_op jit(solution)/shard_map/ppermute | solution.py:566
  61.6 27.5 %collective-permute-start.19 = (bf16[1056,256]{1,0:T(8,128)(2,1)}, bf16[1056,256]{1,0:T(8,128)(2,1)}, u32[]{:S(2)}, u32[]{:S(2)}) collective-permute-start(bf16[1056,256]{1,0:T(8,128)(2,1)} %onward.4), channel_id=1, source_target_pairs={{8,0},{12,4},{16,24},{20,28},{9,1},{13,5},{17,25},{21,29},{10,2},{... | collective-permute-start | bytes 1622024 | tf_op jit(solution)/shard_map/ppermute | solution.py:566
  65.1 27.0 %collective-permute-start.13 = (bf16[1024,256]{1,0:T(8,128)(2,1)S(1)}, bf16[1024,256]{1,0:T(8,128)(2,1)S(1)}, u32[]{:S(2)}, u32[]{:S(2)}) collective-permute-start(bf16[1024,256]{1,0:T(8,128)(2,1)S(1)} %add_convert_fusion.1.refs_6_), channel_id=1, source_target_pairs={{8,16},{12,20},{16,8},{20,12},{9,17},{13,21},{17,9},{21,13},{10,18... | collective-permute-start | bytes 1572872 | tf_op jit(solution)/shard_map/ppermute | solution.py:566
  65.8 26.5 %collective-permute-start.16 = (bf16[1056,256]{1,0:T(8,128)(2,1)}, bf16[1056,256]{1,0:T(8,128)(2,1)}, u32[]{:S(2)}, u32[]{:S(2)}) collective-permute-start(bf16[1056,256]{1,0:T(8,128)(2,1)} %get-tuple-element.41), channel_id=1, source_target_pairs={{0,4},{4,0},{8,12},{12,8},{16,20},{20,16},{24,28},{28,24},{1,5},{5... | collective-permute-start | bytes 1622024 | tf_op jit(solution)/shard_map/ppermute | solution.py:569
  78.5 13.7 %collective-permute-start.15 = (bf16[1056,256]{1,0:T(8,128)(2,1)}, bf16[1056,256]{1,0:T(8,128)(2,1)}, u32[]{:S(2)}, u32[]{:S(2)}) collective-permute-start(bf16[1056,256]{1,0:T(8,128)(2,1)} %onward.3), channel_id=1, source_target_pairs={{8,24},{12,28},{16,0},{20,4},{9,25},{13,29},{17,1},{21,5},{10,26},... | collective-permute-start | bytes 1622024 | tf_op jit(solution)/shard_map/ppermute | solution.py:566
  84.6 12.9 %collective-permute-start.20 = (bf16[1056,256]{1,0:T(8,128)(2,1)}, bf16[1056,256]{1,0:T(8,128)(2,1)S(1)}, u32[]{:S(2)}, u32[]{:S(2)}) collective-permute-start(bf16[1056,256]{1,0:T(8,128)(2,1)} %onward.4), channel_id=1, source_target_pairs={{0,8},{4,12},{24,16},{28,20},{1,9},{5,13},{25,17},{29,21},{2,10},{... | collective-permute-start | bytes 1622024 | tf_op jit(solution)/shard_map/ppermute | solution.py:566
  91.3 12.9 %collective-permute-start.21 = (bf16[1056,256]{1,0:T(8,128)(2,1)S(1)}, bf16[1056,256]{1,0:T(8,128)(2,1)S(1)}, u32[]{:S(2)}, u32[]{:S(2)}) collective-permute-start(bf16[1056,256]{1,0:T(8,128)(2,1)S(1)} %onward.5), channel_id=1, source_target_pairs={{8,16},{12,20},{16,8},{20,12},{9,17},{13,21},{17,9},{21,13},{10,18... | collective-permute-start | bytes 1622024 | tf_op jit(solution)/shard_map/ppermute | solution.py:566
  92.2 12.0 %collective-permute-start.22 = (bf16[1024,256]{1,0:T(8,128)(2,1)S(1)}, bf16[1024,256]{1,0:T(8,128)(2,1)S(1)}, u32[]{:S(2)}, u32[]{:S(2)}) collective-permute-start(bf16[1024,256]{1,0:T(8,128)(2,1)S(1)} %multiply_convert_fusion), channel_id=1, source_target_pairs={{8,0},{12,4},{16,24},{20,28},{9,1},{13,5},{17,25},{21,29},{10,2},{... | collective-permute-start | bytes 1572872 | tf_op jit(solution)/shard_map/ppermute | solution.py:566
  115.2 12.1 %collective-permute-start.26 = (bf16[1040,256]{1,0:T(8,128)(2,1)S(1)}, bf16[1040,256]{1,0:T(8,128)(2,1)S(1)}, u32[]{:S(2)}, u32[]{:S(2)}) collective-permute-start(bf16[1040,256]{1,0:T(8,128)(2,1)S(1)} %scan.1), channel_id=1, source_target_pairs={{0,8},{4,12},{8,0},{12,4},{16,24},{20,28},{24,16},{28,20},{1,9},{5... | collective-permute-start | bytes 1597448 | tf_op jit(solution)/shard_map/ppermute | solution.py:566
  117.1 19.0 %collective-permute-start.25 = (bf16[1040,256]{1,0:T(8,128)(2,1)S(1)}, bf16[1040,256]{1,0:T(8,128)(2,1)S(1)}, u32[]{:S(2)}, u32[]{:S(2)}) collective-permute-start(bf16[1040,256]{1,0:T(8,128)(2,1)S(1)} %scan.1), channel_id=1, source_target_pairs={{0,4},{4,0},{8,12},{12,8},{16,20},{20,16},{24,28},{28,24},{1,5},{5... | collective-permute-start | bytes 1597448 | tf_op jit(solution)/shard_map/ppermute | solution.py:569
  117.6 18.3 %collective-permute-start.24 = (bf16[1040,256]{1,0:T(8,128)(2,1)}, bf16[1040,256]{1,0:T(8,128)(2,1)S(1)}, u32[]{:S(2)}, u32[]{:S(2)}) collective-permute-start(bf16[1040,256]{1,0:T(8,128)(2,1)} %collective-permute-done.23), channel_id=1, source_target_pairs={{8,0},{12,4},{16,24},{20,28},{9,1},{13,5},{17,25},{21,29},{10,2},{... | collective-permute-start | bytes 1597448 | tf_op jit(solution)/shard_map/ppermute | solution.py:566
  127.4 9.8 %collective-permute-start.27 = (bf16[1040,256]{1,0:T(8,128)(2,1)S(1)}, bf16[1040,256]{1,0:T(8,128)(2,1)S(1)}, u32[]{:S(2)}, u32[]{:S(2)}) collective-permute-start(bf16[1040,256]{1,0:T(8,128)(2,1)S(1)} %collective-permute-done.26), channel_id=1, source_target_pairs={{8,16},{12,20},{16,8},{20,12},{9,17},{13,21},{17,9},{21,13},{10,18... | collective-permute-start | bytes 1597448 | tf_op jit(solution)/shard_map/ppermute | solution.py:566
  128.0 21.5 %collective-permute-start.29 = (bf16[1040,256]{1,0:T(8,128)(2,1)S(1)}, bf16[1040,256]{1,0:T(8,128)(2,1)S(1)}, u32[]{:S(2)}, u32[]{:S(2)}) collective-permute-start(bf16[1040,256]{1,0:T(8,128)(2,1)S(1)} %collective-permute-done.26), channel_id=1, source_target_pairs={{0,4},{4,0},{8,12},{12,8},{16,20},{20,16},{24,28},{28,24},{1,5},{5... | collective-permute-start | bytes 1597448 | tf_op jit(solution)/shard_map/ppermute | solution.py:569
  136.0 15.1 %collective-permute-start.30 = (bf16[1040,256]{1,0:T(8,128)(2,1)S(1)}, bf16[1040,256]{1,0:T(8,128)(2,1)S(1)}, u32[]{:S(2)}, u32[]{:S(2)}) collective-permute-start(bf16[1040,256]{1,0:T(8,128)(2,1)S(1)} %broadcast_select_fusion.1), channel_id=1, source_target_pairs={{0,4},{4,0},{8,12},{12,8},{16,20},{20,16},{24,28},{28,24},{1,5},{5... | collective-permute-start | bytes 1597448 | tf_op jit(solution)/shard_map/ppermute | solution.py:569
  137.1 12.3 %collective-permute-start.28 = (bf16[1040,256]{1,0:T(8,128)(2,1)S(1)}, bf16[1040,256]{1,0:T(8,128)(2,1)S(1)}, u32[]{:S(2)}, u32[]{:S(2)}) collective-permute-start(bf16[1040,256]{1,0:T(8,128)(2,1)S(1)} %collective-permute-done.27), channel_id=1, source_target_pairs={{8,0},{12,4},{16,24},{20,28},{9,1},{13,5},{17,25},{21,29},{10,2},{... | collective-permute-start | bytes 1597448 | tf_op jit(solution)/shard_map/ppermute | solution.py:566
  149.6 11.0 %collective-permute-start.31 = (bf16[1040,256]{1,0:T(8,128)(2,1)S(1)}, bf16[1040,256]{1,0:T(8,128)(2,1)S(1)}, u32[]{:S(2)}, u32[]{:S(2)}) collective-permute-start(bf16[1040,256]{1,0:T(8,128)(2,1)S(1)} %broadcast_select_fusion), channel_id=1, source_target_pairs={{0,4},{4,0},{8,12},{12,8},{16,20},{20,16},{24,28},{28,24},{1,5},{5... | collective-permute-start | bytes 1597448 | tf_op jit(solution)/shard_map/ppermute | solution.py:569
  160.9 5.1 %collective-permute-start.32 = (bf16[512,512]{1,0:T(8,128)(2,1)S(1)}, bf16[512,512]{1,0:T(8,128)(2,1)S(1)}, u32[]{:S(2)}, u32[]{:S(2)}) collective-permute-start(bf16[512,512]{1,0:T(8,128)(2,1)S(1)} %add_convert_fusion), channel_id=1, source_target_pairs={{0,1},{1,0},{2,3},{3,2},{4,5},{5,4},{6,7},{7,6},{8,9},{9,8},{10,11... | collective-permute-start | bytes 1572872 | tf_op jit(solution)/shard_map/ppermute | solution.py:724
  162.8 4.7 %collective-permute-start.35 = (f32[8,128]{1,0:T(8,128)S(1)}, f32[8,128]{1,0:T(8,128)S(1)}, u32[]{:S(2)}, u32[]{:S(2)}) collective-permute-start(f32[8,128]{1,0:T(8,128)S(1)} %add.280), channel_id=1, source_target_pairs={{0,2},{1,3},{2,0},{3,1},{4,6},{5,7},{6,4},{7,5},{8,10},{9,11},{10,... | collective-permute-start | bytes 12296 | tf_op jit(solution)/shard_map/ppermute | solution.py:735
  167.6 8.3 %collective-permute-start.33 = (bf16[256,512]{1,0:T(8,128)(2,1)}, bf16[256,512]{1,0:T(8,128)(2,1)S(1)}, u32[]{:S(2)}, u32[]{:S(2)}) collective-permute-start(bf16[256,512]{1,0:T(8,128)(2,1)} %add_convert_fusion.2), channel_id=1, source_target_pairs={{0,2},{1,3},{2,0},{3,1},{4,6},{5,7},{6,4},{7,5},{8,10},{9,11},{10,... | collective-permute-start | bytes 786440 | tf_op jit(solution)/shard_map/ppermute | solution.py:734
  177.7 12.6 %all-to-all-start = ((bf16[8,32,512]{2,1,0:T(8,128)(2,1)}), bf16[8,32,512]{2,1,0:T(8,128)(2,1)S(1)}, u32[]{:S(2)}, u32[]{:S(2)}) async-start(bf16[8,32,512]{2,1,0:T(8,128)(2,1)} %multiply_convert_fusion.1), calls=%async_computation | async-start | bytes 524288 | tf_op jit(solution)/shard_map/all_to_all | solution.py:740
  (21 other events, 307.3 us)

commit v8 on v7

--- a/solution.py
+++ b/solution.py
@@ -318,13 +318,14 @@
     )(place, factor, *hidden, w_x, *weights)
 
 
-def onward_kernel(own_ref, received_ref, out_ref):
-    rows, channels = own_ref.shape
+def onward_kernel(*refs):
+    share_refs, out_ref = (refs[:-1], refs[-1])
+    rows, channels = out_ref.shape
     tokens = rows * channels // (channels + ROWS)
-    total = own_ref[:tokens].astype(jnp.float32) + received_ref[:tokens].astype(jnp.float32)
+    total = sum(ref[:tokens].astype(jnp.float32) for ref in share_refs)
     out_ref[:tokens] = total.astype(jnp.bfloat16)
     upper = lax.broadcasted_iota(jnp.int32, (ROWS, channels), 0) < ROWS // 2
-    extra = own_ref[tokens:].astype(jnp.float32) + received_ref[tokens:].astype(jnp.float32)
+    extra = sum(ref[tokens:].astype(jnp.float32) for ref in share_refs)
     pieces = []
     for at in range(0, rows - tokens, ROWS):
         piece = extra[at : at + ROWS]
@@ -332,18 +333,21 @@
     out_ref[tokens:] = jnp.concatenate(pieces, axis=0).astype(jnp.bfloat16)
 
 
-def onward(own, received):
+def onward(*shares):
+    own = shares[0]
     return pl.pallas_call(
         onward_kernel,
-        in_specs=[VMEM, VMEM],
+        in_specs=[VMEM] * len(shares),
         out_specs=VMEM,
         out_shape=jax.ShapeDtypeStruct(own.shape, own.dtype),
         compiler_params=pltpu.CompilerParams(vmem_limit_bytes=8 * 2**20),
         cost_estimate=pl.CostEstimate(
-            flops=own.size, bytes_accessed=6 * own.size, transcendentals=0
+            flops=len(shares) * own.size,
+            bytes_accessed=2 * (len(shares) + 1) * own.size,
+            transcendentals=0,
         ),
         name="onward",
-    )(own, received)
+    )(*shares)
 
 
 def turned_rank(rank, ranks):
@@ -660,13 +664,15 @@
     sent_end = onward(over, hop_far)
     got_end = along(sent_end, over_middle)
     hop_over, near_out, unused = tie((hop_over, near_out, sent_end))
-    got_next = along(onward(far, hop_over), middle)
-    map_done, got_end, got_mine = tie((map_done, got_end, got_mine))
+    sent_next = onward(far, hop_over)
+    got_next = along(sent_next, middle)
+    near_sum = onward(mine, got_mine, near_out, near_in)
+    map_done, unused = tie((map_done, sent_next))
     map_done = along(map_done, outward)
     gained = scan(
         place,
         in_scale,
-        [mine, got_mine, near_out, near_in, got_end, got_next],
+        [near_sum, got_end, got_next],
         [map_sum, map_far, map_done],
         small,
         largest,

time: 192 us -> 197 us (1.026)
  waiting for transfers between devices: 92.1 us -> 97.7 us
    ppermute x17, waiting for transfers between devices: 54.4 us -> 58.6 us  [along(): return lax.ppermute(value, 'seq', moves)]
    unnamed x38 -> x36, local copies, waits for them, and re-layouts: 9.12 us -> 7.33 us
    pallas_call x3 -> x4, Pallas kernels: 4.14 us -> 4.96 us  [onward(): pl.pallas_call(onward_kernel, in_specs=[VMEM] * len(shares), out_specs=VM...]
  transfers between devices with their start and end apart: 37 -> 37, of which waited for: 19 -> 21; matrix products, arithmetic and copies ran while one was open for 8% -> 8% of each run, Pallas kernels for 2% -> 3%
where the time goes in v8:
time: 197 us; the launch traced here: 196 us
  waiting for transfers between devices  97.7 us (50%)
  starting transfers between devices  50.4 us (26%)
  Pallas kernels  18.7 us (9%)
  local copies, waits for them, and re-layouts  16.8 us (9%)
  other arithmetic  6.55 us (3%)
  matrix products  3.67 us (2%)
    ppermute x17, waiting for transfers between devices, along(): return lax.ppermute(value, 'seq', moves)  58.6 us
    ppermute x17, starting transfers between devices, along(): return lax.ppermute(value, 'seq', moves)  29.7 us
    ppermute x9, waiting for transfers between devices, across(): return lax.ppermute(value, 'seq', [(s, s ^ 1) for s in range(count)])  22.2 us
    ppermute x9, starting transfers between devices, across(): return lax.ppermute(value, 'seq', [(s, s ^ 1) for s in range(count)])  10.1 us
    all_to_all x1, waiting for transfers between devices, by_heads(): lax.all_to_all(final.astype(bf16), 'seq', split_axis=0, concat_axis=0, ti...  7.62 us
    pallas_call x1, Pallas kernels, scan(): pl.pallas_call(scan_kernel, in_specs=[SMEM, SMEM] + [VMEM] * (len(sums) +...  7.44 us
    unnamed x36, local copies, waits for them, and re-layouts  7.33 us
    ppermute x1, waiting for transfers between devices, by_heads(): received = lax.ppermute(sent.astype(bf16), 'tensor', pairs)  6.89 us
  transfers between devices with their start and end apart: 37, of which 21 were waited for; matrix products, arithmetic and copies ran while one was open for 8% of the time, Pallas kernels for 3%

profile of v8, /device:TPU:0, one launch (start us, length us, event | category | flops | bytes accessed | tf_op | source)
XLA Modules:
  0.0 195.7 jit_solution(7109552635335499955)
XLA Ops:
  0.8 2.0 %constant_dynamic-slice_fusion.9 = bf16[512,512]{1,0:T(8,128)(2,1)} fusion(bf16[512,2048]{1,0:T(8,128)(2,1)} %refs_8_.1, s32[]{:T(128)S(6)} %select_n.123), kind=kLoop, calls=%fused_computation.64 | loop fusion | bytes 1048580 | tf_op jit(solution)/shard_map/dynamic_slice | solution.py:611
  3.7 3.1 %collective-permute-start = (bf16[32,1024]{1,0:T(8,128)(2,1)S(1)}, bf16[32,1024]{1,0:T(8,128)(2,1)S(1)}, u32[]{:S(2)}, u32[]{:S(2)}) collective-permute-start(bf16[32,1024]{1,0:T(8,128)(2,1)S(1)} %get-tuple-element.59), channel_id=1, source_target_pairs={{0,8},{4,12},{8,0},{12,4},{16,24},{20,28},{24,16},{28,20},{1,9},{5... | collective-permute-start | bytes 196616 | tf_op jit(solution)/shard_map/ppermute | solution.py:570
  6.8 2.6 %collective-permute-start.1 = (bf16[32,1024]{1,0:T(8,128)(2,1)S(1)}, bf16[32,1024]{1,0:T(8,128)(2,1)S(1)}, u32[]{:S(2)}, u32[]{:S(2)}) collective-permute-start(bf16[32,1024]{1,0:T(8,128)(2,1)S(1)} %get-tuple-element.58), channel_id=1, source_target_pairs={{0,16},{4,20},{8,24},{12,28},{16,0},{20,4},{24,8},{28,12},{1,17},{... | collective-permute-start | bytes 196616 | tf_op jit(solution)/shard_map/ppermute | solution.py:570
  9.4 1.7 collective-permute-start.10
  17.1 2.2 %constant_dynamic-slice_fusion.2 = (bf16[512,1,2,128]{3,2,1,0:T(2,128)(2,1)}, bf16[512,1,2,128]{3,2,1,0:T(2,128)(2,1)}) fusion(bf16[512,2,2,128]{3,2,1,0:T(2,128)(2,1)} %param.18, s32[]{:T(128)S(6)} %select_n.132, s32[]{:T(128)S(6)} %select_n.129), kind=kLoop, calls=%fused_computation.57 | loop fusion | bytes 1048584 | tf_op jit(solution)/shard_map/jit(dynamic_index_in_dim)/dynamic_slice | solution.py:566
  21.6 1.6 collective-permute-start.4
  23.2 5.3 %collective-permute-done.6.refs_4_ = bf16[4,32,1024]{2,1,0:T(8,128)(2,1)} collective-permute-done((bf16[4,32,1024]{2,1,0:T(8,128)(2,1)S(1)}, bf16[4,32,1024]{2,1,0:T(8,128)(2,1)}, u32[]{:S(2)}, u32[]{:S(2)}) %collective-permute-start.6) | collective-permute-done | bytes 262176 | tf_op jit(solution)/shard_map/ppermute | solution.py:573
  36.6 2.9 %collective-permute-done.11.refs_12_ = bf16[576,256]{1,0:T(8,128)(2,1)S(1)} collective-permute-done((bf16[576,256]{1,0:T(8,128)(2,1)}, bf16[576,256]{1,0:T(8,128)(2,1)S(1)}, u32[]{:S(2)}, u32[]{:S(2)}) %collective-permute-start.11) | collective-permute-done | bytes 294944 | tf_op jit(solution)/shard_map/ppermute | solution.py:573
  39.5 1.6 copy-done.5
  42.1 6.3 %project.1 = (bf16[1056,256]{1,0:T(8,128)(2,1)}, bf16[1056,256]{1,0:T(8,128)(2,1)}, bf16[1056,256]{1,0:T(8,128)(2,1)S(1)}, bf16[1056,256]{1,0:T(8,128)(2,1)S(1)}...) custom-call(s32[7]{0:T(128)S(1)} %stack.43.place_ref, ...), custom_call_target="tpu_custom_call" | custom-call | flops 2684354560 | bytes 4194304 | tf_op jit(solution)/shard_map/project/pallas_call | solution.py:301
  49.9 2.5 %collective-permute-start.20 = (bf16[1024,256]{1,0:T(8,128)(2,1)S(1)}, bf16[1024,256]{1,0:T(8,128)(2,1)S(1)}, u32[]{:S(2)}, u32[]{:S(2)}) collective-permute-start(bf16[1024,256]{1,0:T(8,128)(2,1)S(1)} %get-tuple-element.43), channel_id=1, source_target_pairs={{0,8},{4,12},{24,16},{28,20},{1,9},{5,13},{25,17},{29,21},{2,10},{... | collective-permute-start | bytes 1572872 | tf_op jit(solution)/shard_map/ppermute | solution.py:570
  52.4 2.1 %collective-permute-start.16 = (bf16[1056,256]{1,0:T(8,128)(2,1)}, bf16[1056,256]{1,0:T(8,128)(2,1)}, u32[]{:S(2)}, u32[]{:S(2)}) collective-permute-start(bf16[1056,256]{1,0:T(8,128)(2,1)} %get-tuple-element.40.refs_0_), channel_id=1, source_target_pairs={{0,8},{4,12},{24,16},{28,20},{1,9},{5,13},{25,17},{29,21},{2,10},{... | collective-permute-start | bytes 1622024 | tf_op jit(solution)/shard_map/ppermute | solution.py:570
  54.5 2.1 %collective-permute-start.13 = (bf16[1056,256]{1,0:T(8,128)(2,1)}, bf16[1056,256]{1,0:T(8,128)(2,1)}, u32[]{:S(2)}, u32[]{:S(2)}) collective-permute-start(bf16[1056,256]{1,0:T(8,128)(2,1)} %get-tuple-element.37.refs_0_), channel_id=1, source_target_pairs={{0,8},{4,12},{24,16},{28,20},{1,9},{5,13},{25,17},{29,21},{2,10},{... | collective-permute-start | bytes 1622024 | tf_op jit(solution)/shard_map/ppermute | solution.py:570
  56.6 3.8 %collective-permute-done.14.refs_1_ = bf16[1056,256]{1,0:T(8,128)(2,1)S(1)} collective-permute-done((bf16[1056,256]{1,0:T(8,128)(2,1)S(1)}, bf16[1056,256]{1,0:T(8,128)(2,1)S(1)}, u32[]{:S(2)}, u32[]{:S(2)}) %collective-permute-start.14) | collective-permute-done | bytes 540704 | tf_op jit(solution)/shard_map/ppermute | solution.py:573
  62.7 2.1 %collective-permute-done.20 = bf16[1024,256]{1,0:T(8,128)(2,1)S(1)} collective-permute-done((bf16[1024,256]{1,0:T(8,128)(2,1)S(1)}, bf16[1024,256]{1,0:T(8,128)(2,1)S(1)}, u32[]{:S(2)}, u32[]{:S(2)}) %collective-permute-start.20) | collective-permute-done | bytes 524320 | tf_op jit(solution)/shard_map/ppermute | solution.py:570
  66.2 10.2 %collective-permute-done.16.refs_1_ = bf16[1056,256]{1,0:T(8,128)(2,1)} collective-permute-done((bf16[1056,256]{1,0:T(8,128)(2,1)}, bf16[1056,256]{1,0:T(8,128)(2,1)}, u32[]{:S(2)}, u32[]{:S(2)}) %collective-permute-start.16) | collective-permute-done | bytes 540704 | tf_op jit(solution)/shard_map/ppermute | solution.py:570
  76.4 4.4 %collective-permute-start.17 = (bf16[1056,256]{1,0:T(8,128)(2,1)}, bf16[1056,256]{1,0:T(8,128)(2,1)S(1)}, u32[]{:S(2)}, u32[]{:S(2)}) collective-permute-start(bf16[1056,256]{1,0:T(8,128)(2,1)} %onward.4), channel_id=1, source_target_pairs={{0,8},{4,12},{24,16},{28,20},{1,9},{5,13},{25,17},{29,21},{2,10},{... | collective-permute-start | bytes 1622024 | tf_op jit(solution)/shard_map/ppermute | solution.py:570
  82.2 5.8 %collective-permute-done.13.refs_1_ = bf16[1056,256]{1,0:T(8,128)(2,1)} collective-permute-done((bf16[1056,256]{1,0:T(8,128)(2,1)}, bf16[1056,256]{1,0:T(8,128)(2,1)}, u32[]{:S(2)}, u32[]{:S(2)}) %collective-permute-start.13) | collective-permute-done | bytes 540704 | tf_op jit(solution)/shard_map/ppermute | solution.py:570
  93.0 2.9 %collective-permute-done.17.refs_3_ = bf16[1056,256]{1,0:T(8,128)(2,1)S(1)} collective-permute-done((bf16[1056,256]{1,0:T(8,128)(2,1)}, bf16[1056,256]{1,0:T(8,128)(2,1)S(1)}, u32[]{:S(2)}, u32[]{:S(2)}) %collective-permute-start.17) | collective-permute-done | bytes 540704 | tf_op jit(solution)/shard_map/ppermute | solution.py:570
  97.3 6.9 %collective-permute-done.18.refs_1_ = bf16[1056,256]{1,0:T(8,128)(2,1)S(1)} collective-permute-done((bf16[1056,256]{1,0:T(8,128)(2,1)S(1)}, bf16[1056,256]{1,0:T(8,128)(2,1)S(1)}, u32[]{:S(2)}, u32[]{:S(2)}) %collective-permute-start.18) | collective-permute-done | bytes 540704 | tf_op jit(solution)/shard_map/ppermute | solution.py:570
  104.2 5.3 %collective-permute-done.22.refs_5_ = bf16[1024,256]{1,0:T(8,128)(2,1)S(1)} collective-permute-done((bf16[1024,256]{1,0:T(8,128)(2,1)S(1)}, bf16[1024,256]{1,0:T(8,128)(2,1)S(1)}, u32[]{:S(2)}, u32[]{:S(2)}) %collective-permute-start.22) | collective-permute-done | bytes 524320 | tf_op jit(solution)/shard_map/ppermute | solution.py:570
  110.6 7.4 %scan.1 = bf16[1040,256]{1,0:T(8,128)(2,1)S(1)} custom-call(s32[7]{0:T(128)S(1)} %stack.43.place_ref, f32[1]{0:T(128)} %bitcast.3.scale_ref, bf16[1056,256]{1,0:T(8,128)(2,1)S(1)} %onward.6.refs_0_, bf16[1056,256]{1,0:T(8,128)(2,1)S(1)} %collective-permute-done.18.refs_1_, bf16[1056,256]{1,0:T(8,128)(2,1)S(1)} %collective-permute-done.19.refs_2_, ...), custom_call_target="tpu_custom_call" | custom-call | flops 268435456 | bytes 2097152 | tf_op jit(solution)/shard_map/scan/pallas_call | solution.py:515
  119.5 2.8 %collective-permute-start.26 = (bf16[1040,256]{1,0:T(8,128)(2,1)S(1)}, bf16[1040,256]{1,0:T(8,128)(2,1)S(1)}, u32[]{:S(2)}, u32[]{:S(2)}) collective-permute-start(bf16[1040,256]{1,0:T(8,128)(2,1)S(1)} %scan.1), channel_id=1, source_target_pairs={{0,8},{4,12},{8,0},{12,4},{16,24},{20,28},{24,16},{28,20},{1,9},{5... | collective-permute-start | bytes 1597448 | tf_op jit(solution)/shard_map/ppermute | solution.py:570
  124.1 9.5 %collective-permute-done.26 = bf16[1040,256]{1,0:T(8,128)(2,1)S(1)} collective-permute-done((bf16[1040,256]{1,0:T(8,128)(2,1)S(1)}, bf16[1040,256]{1,0:T(8,128)(2,1)S(1)}, u32[]{:S(2)}, u32[]{:S(2)}) %collective-permute-start.26) | collective-permute-done | bytes 532512 | tf_op jit(solution)/shard_map/ppermute | solution.py:570
  135.4 5.5 %collective-permute-done.24 = bf16[1040,256]{1,0:T(8,128)(2,1)S(1)} collective-permute-done((bf16[1040,256]{1,0:T(8,128)(2,1)}, bf16[1040,256]{1,0:T(8,128)(2,1)S(1)}, u32[]{:S(2)}, u32[]{:S(2)}) %collective-permute-start.24) | collective-permute-done | bytes 532512 | tf_op jit(solution)/shard_map/ppermute | solution.py:570
  144.3 8.9 %collective-permute-done.28 = bf16[1040,256]{1,0:T(8,128)(2,1)S(1)} collective-permute-done((bf16[1040,256]{1,0:T(8,128)(2,1)S(1)}, bf16[1040,256]{1,0:T(8,128)(2,1)S(1)}, u32[]{:S(2)}, u32[]{:S(2)}) %collective-permute-start.28) | collective-permute-done | bytes 532512 | tf_op jit(solution)/shard_map/ppermute | solution.py:570
  154.9 5.1 %collective-permute-done.30 = bf16[1040,256]{1,0:T(8,128)(2,1)S(1)} collective-permute-done((bf16[1040,256]{1,0:T(8,128)(2,1)S(1)}, bf16[1040,256]{1,0:T(8,128)(2,1)S(1)}, u32[]{:S(2)}, u32[]{:S(2)}) %collective-permute-start.30) | collective-permute-done | bytes 532512 | tf_op jit(solution)/shard_map/ppermute | solution.py:573
  161.3 5.2 %collective-permute-done.31 = bf16[1040,256]{1,0:T(8,128)(2,1)S(1)} collective-permute-done((bf16[1040,256]{1,0:T(8,128)(2,1)S(1)}, bf16[1040,256]{1,0:T(8,128)(2,1)S(1)}, u32[]{:S(2)}, u32[]{:S(2)}) %collective-permute-start.31) | collective-permute-done | bytes 532512 | tf_op jit(solution)/shard_map/ppermute | solution.py:573
  168.8 2.2 %collective-permute-start.35 = (f32[8,128]{1,0:T(8,128)S(1)}, f32[8,128]{1,0:T(8,128)S(1)}, u32[]{:S(2)}, u32[]{:S(2)}) collective-permute-start(f32[8,128]{1,0:T(8,128)S(1)} %add.280), channel_id=1, source_target_pairs={{0,2},{1,3},{2,0},{3,1},{4,6},{5,7},{6,4},{7,5},{8,10},{9,11},{10,... | collective-permute-start | bytes 12296 | tf_op jit(solution)/shard_map/ppermute | solution.py:741
  173.9 6.9 %collective-permute-done.33 = bf16[256,512]{1,0:T(8,128)(2,1)S(1)} collective-permute-done((bf16[256,512]{1,0:T(8,128)(2,1)}, bf16[256,512]{1,0:T(8,128)(2,1)S(1)}, u32[]{:S(2)}, u32[]{:S(2)}) %collective-permute-start.33) | collective-permute-done | bytes 262176 | tf_op jit(solution)/shard_map/ppermute | solution.py:740
  182.7 4.1 %all-to-all-start = ((bf16[8,32,512]{2,1,0:T(8,128)(2,1)}), bf16[8,32,512]{2,1,0:T(8,128)(2,1)S(1)}, u32[]{:S(2)}, u32[]{:S(2)}) async-start(bf16[8,32,512]{2,1,0:T(8,128)(2,1)} %multiply_convert_fusion.1), calls=%async_computation | async-start | bytes 524288 | tf_op jit(solution)/shard_map/all_to_all | solution.py:746
  187.4 7.6 %all-to-all-done = bf16[8,32,512]{2,1,0:T(8,128)(2,1)S(1)} async-done(((bf16[8,32,512]{2,1,0:T(8,128)(2,1)}), bf16[8,32,512]{2,1,0:T(8,128)(2,1)S(1)}, u32[]{:S(2)}, u32[]{:S(2)}) %all-to-all-start) | async-done | bytes 262176 | tf_op jit(solution)/shard_map/all_to_all | solution.py:746
  (139 shorter events, 51.2 us)
Async XLA Ops:
  3.7 10.4 %collective-permute-start = (bf16[32,1024]{1,0:T(8,128)(2,1)S(1)}, bf16[32,1024]{1,0:T(8,128)(2,1)S(1)}, u32[]{:S(2)}, u32[]{:S(2)}) collective-permute-start(bf16[32,1024]{1,0:T(8,128)(2,1)S(1)} %get-tuple-element.59), channel_id=1, source_target_pairs={{0,8},{4,12},{8,0},{12,4},{16,24},{20,28},{24,16},{28,20},{1,9},{5... | collective-permute-start | bytes 196616 | tf_op jit(solution)/shard_map/ppermute | solution.py:570
  6.8 7.4 %collective-permute-start.1 = (bf16[32,1024]{1,0:T(8,128)(2,1)S(1)}, bf16[32,1024]{1,0:T(8,128)(2,1)S(1)}, u32[]{:S(2)}, u32[]{:S(2)}) collective-permute-start(bf16[32,1024]{1,0:T(8,128)(2,1)S(1)} %get-tuple-element.58), channel_id=1, source_target_pairs={{0,16},{4,20},{8,24},{12,28},{16,0},{20,4},{24,8},{28,12},{1,17},{... | collective-permute-start | bytes 196616 | tf_op jit(solution)/shard_map/ppermute | solution.py:570
  9.4 6.1 %collective-permute-start.2 = (bf16[32,1024]{1,0:T(8,128)(2,1)S(1)}, bf16[32,1024]{1,0:T(8,128)(2,1)S(1)}, u32[]{:S(2)}, u32[]{:S(2)}) collective-permute-start(bf16[32,1024]{1,0:T(8,128)(2,1)S(1)} %get-tuple-element.57), channel_id=1, source_target_pairs={{0,24},{4,28},{8,16},{12,20},{16,8},{20,12},{24,0},{28,4},{1,25},{... | collective-permute-start | bytes 196616 | tf_op jit(solution)/shard_map/ppermute | solution.py:570
  9.4 22.3 %collective-permute-start.10 = (bf16[512,512]{1,0:T(8,128)(2,1)}, bf16[512,512]{1,0:T(8,128)(2,1)S(1)}, u32[]{:S(2)}, u32[]{:S(2)}) collective-permute-start(bf16[512,512]{1,0:T(8,128)(2,1)} %constant_dynamic-slice_fusion.9), channel_id=1, source_target_pairs={{0,4},{4,0},{8,12},{12,8},{16,20},{20,16},{24,28},{28,24},{1,5},{5... | collective-permute-start | bytes 1572872 | tf_op jit(solution)/shard_map/ppermute | solution.py:573
  15.5 12.9 %collective-permute-start.6 = (bf16[4,32,1024]{2,1,0:T(8,128)(2,1)S(1)}, bf16[4,32,1024]{2,1,0:T(8,128)(2,1)}, u32[]{:S(2)}, u32[]{:S(2)}) collective-permute-start(bf16[4,32,1024]{2,1,0:T(8,128)(2,1)S(1)} %pad_maximum_fusion.1.refs_0_), channel_id=1, source_target_pairs={{0,4},{4,0},{8,12},{12,8},{16,20},{20,16},{24,28},{28,24},{1,5},{5... | collective-permute-start | bytes 786440 | tf_op jit(solution)/shard_map/ppermute | solution.py:573
  21.6 12.9 %collective-permute-start.4 = (bf16[4,32,1024]{2,1,0:T(8,128)(2,1)S(1)}, bf16[4,32,1024]{2,1,0:T(8,128)(2,1)}, u32[]{:S(2)}, u32[]{:S(2)}) collective-permute-start(bf16[4,32,1024]{2,1,0:T(8,128)(2,1)S(1)} %pad_maximum_fusion.1.refs_0_), channel_id=1, source_target_pairs={{0,2},{1,3},{2,0},{3,1},{4,6},{5,7},{6,4},{7,5},{8,10},{9,11},{10,... | collective-permute-start | bytes 786440 | tf_op jit(solution)/shard_map/ppermute | solution.py:638
  28.5 6.9 %collective-permute-start.8 = (bf16[4,32,1024]{2,1,0:T(8,128)(2,1)}, bf16[4,32,1024]{2,1,0:T(8,128)(2,1)}, u32[]{:S(2)}, u32[]{:S(2)}) collective-permute-start(bf16[4,32,1024]{2,1,0:T(8,128)(2,1)} %collective-permute-done.6.refs_4_), channel_id=1, source_target_pairs={{0,2},{1,3},{2,0},{3,1},{4,6},{5,7},{6,4},{7,5},{8,10},{9,11},{10,... | collective-permute-start | bytes 786440 | tf_op jit(solution)/shard_map/ppermute | solution.py:638
  32.5 7.0 %collective-permute-start.11 = (bf16[576,256]{1,0:T(8,128)(2,1)}, bf16[576,256]{1,0:T(8,128)(2,1)S(1)}, u32[]{:S(2)}, u32[]{:S(2)}) collective-permute-start(bf16[576,256]{1,0:T(8,128)(2,1)} %pad_maximum_fusion), channel_id=1, source_target_pairs={{0,4},{4,0},{8,12},{12,8},{16,20},{20,16},{24,28},{28,24},{1,5},{5... | collective-permute-start | bytes 884744 | tf_op jit(solution)/shard_map/ppermute | solution.py:573
  35.3 4.2 %collective-permute-start.9 = (bf16[4,32,1024]{2,1,0:T(8,128)(2,1)}, bf16[4,32,1024]{2,1,0:T(8,128)(2,1)}, u32[]{:S(2)}, u32[]{:S(2)}) collective-permute-start(bf16[4,32,1024]{2,1,0:T(8,128)(2,1)} %collective-permute-done.8.refs_6_), channel_id=1, source_target_pairs={{0,1},{1,0},{2,3},{3,2},{4,5},{5,4},{6,7},{7,6},{8,9},{9,8},{10,11... | collective-permute-start | bytes 786440 | tf_op jit(solution)/shard_map/ppermute | solution.py:638
  48.4 12.0 %collective-permute-start.14 = (bf16[1056,256]{1,0:T(8,128)(2,1)S(1)}, bf16[1056,256]{1,0:T(8,128)(2,1)S(1)}, u32[]{:S(2)}, u32[]{:S(2)}) collective-permute-start(bf16[1056,256]{1,0:T(8,128)(2,1)S(1)} %get-tuple-element.39), channel_id=1, source_target_pairs={{0,4},{4,0},{8,12},{12,8},{16,20},{20,16},{24,28},{28,24},{1,5},{5... | collective-permute-start | bytes 1622024 | tf_op jit(solution)/shard_map/ppermute | solution.py:573
  49.9 14.8 %collective-permute-start.20 = (bf16[1024,256]{1,0:T(8,128)(2,1)S(1)}, bf16[1024,256]{1,0:T(8,128)(2,1)S(1)}, u32[]{:S(2)}, u32[]{:S(2)}) collective-permute-start(bf16[1024,256]{1,0:T(8,128)(2,1)S(1)} %get-tuple-element.43), channel_id=1, source_target_pairs={{0,8},{4,12},{24,16},{28,20},{1,9},{5,13},{25,17},{29,21},{2,10},{... | collective-permute-start | bytes 1572872 | tf_op jit(solution)/shard_map/ppermute | solution.py:570
  52.4 24.0 %collective-permute-start.16 = (bf16[1056,256]{1,0:T(8,128)(2,1)}, bf16[1056,256]{1,0:T(8,128)(2,1)}, u32[]{:S(2)}, u32[]{:S(2)}) collective-permute-start(bf16[1056,256]{1,0:T(8,128)(2,1)} %get-tuple-element.40.refs_0_), channel_id=1, source_target_pairs={{0,8},{4,12},{24,16},{28,20},{1,9},{5,13},{25,17},{29,21},{2,10},{... | collective-permute-start | bytes 1622024 | tf_op jit(solution)/shard_map/ppermute | solution.py:570
  54.5 33.5 %collective-permute-start.13 = (bf16[1056,256]{1,0:T(8,128)(2,1)}, bf16[1056,256]{1,0:T(8,128)(2,1)}, u32[]{:S(2)}, u32[]{:S(2)}) collective-permute-start(bf16[1056,256]{1,0:T(8,128)(2,1)} %get-tuple-element.37.refs_0_), channel_id=1, source_target_pairs={{0,8},{4,12},{24,16},{28,20},{1,9},{5,13},{25,17},{29,21},{2,10},{... | collective-permute-start | bytes 1622024 | tf_op jit(solution)/shard_map/ppermute | solution.py:570
  61.4 27.9 %collective-permute-start.15 = (bf16[1056,256]{1,0:T(8,128)(2,1)}, bf16[1056,256]{1,0:T(8,128)(2,1)}, u32[]{:S(2)}, u32[]{:S(2)}) collective-permute-start(bf16[1056,256]{1,0:T(8,128)(2,1)} %onward.4), channel_id=1, source_target_pairs={{8,0},{12,4},{16,24},{20,28},{9,1},{13,5},{17,25},{21,29},{10,2},{... | collective-permute-start | bytes 1622024 | tf_op jit(solution)/shard_map/ppermute | solution.py:570
  64.9 26.5 %collective-permute-start.21 = (bf16[1024,256]{1,0:T(8,128)(2,1)S(1)}, bf16[1024,256]{1,0:T(8,128)(2,1)S(1)}, u32[]{:S(2)}, u32[]{:S(2)}) collective-permute-start(bf16[1024,256]{1,0:T(8,128)(2,1)S(1)} %add_convert_fusion.1.refs_3_), channel_id=1, source_target_pairs={{8,16},{12,20},{16,8},{20,12},{9,17},{13,21},{17,9},{21,13},{10,18... | collective-permute-start | bytes 1572872 | tf_op jit(solution)/shard_map/ppermute | solution.py:570
  65.6 27.4 %collective-permute-start.12 = (bf16[1056,256]{1,0:T(8,128)(2,1)}, bf16[1056,256]{1,0:T(8,128)(2,1)S(1)}, u32[]{:S(2)}, u32[]{:S(2)}) collective-permute-start(bf16[1056,256]{1,0:T(8,128)(2,1)} %copy-done.7), channel_id=1, source_target_pairs={{0,4},{4,0},{8,12},{12,8},{16,20},{20,16},{24,28},{28,24},{1,5},{5... | collective-permute-start | bytes 1622024 | tf_op jit(solution)/shard_map/ppermute | solution.py:573
  76.4 19.6 %collective-permute-start.17 = (bf16[1056,256]{1,0:T(8,128)(2,1)}, bf16[1056,256]{1,0:T(8,128)(2,1)S(1)}, u32[]{:S(2)}, u32[]{:S(2)}) collective-permute-start(bf16[1056,256]{1,0:T(8,128)(2,1)} %onward.4), channel_id=1, source_target_pairs={{0,8},{4,12},{24,16},{28,20},{1,9},{5,13},{25,17},{29,21},{2,10},{... | collective-permute-start | bytes 1622024 | tf_op jit(solution)/shard_map/ppermute | solution.py:570
  88.0 16.2 %collective-permute-start.18 = (bf16[1056,256]{1,0:T(8,128)(2,1)S(1)}, bf16[1056,256]{1,0:T(8,128)(2,1)S(1)}, u32[]{:S(2)}, u32[]{:S(2)}) collective-permute-start(bf16[1056,256]{1,0:T(8,128)(2,1)S(1)} %onward.5), channel_id=1, source_target_pairs={{8,24},{12,28},{16,0},{20,4},{9,25},{13,29},{17,1},{21,5},{10,26},... | collective-permute-start | bytes 1622024 | tf_op jit(solution)/shard_map/ppermute | solution.py:570
  90.7 18.9 %collective-permute-start.19 = (bf16[1056,256]{1,0:T(8,128)(2,1)S(1)}, bf16[1056,256]{1,0:T(8,128)(2,1)S(1)}, u32[]{:S(2)}, u32[]{:S(2)}) collective-permute-start(bf16[1056,256]{1,0:T(8,128)(2,1)S(1)} %onward.7), channel_id=1, source_target_pairs={{8,16},{12,20},{16,8},{20,12},{9,17},{13,21},{17,9},{21,13},{10,18... | collective-permute-start | bytes 1622024 | tf_op jit(solution)/shard_map/ppermute | solution.py:570
  91.5 18.0 %collective-permute-start.22 = (bf16[1024,256]{1,0:T(8,128)(2,1)S(1)}, bf16[1024,256]{1,0:T(8,128)(2,1)S(1)}, u32[]{:S(2)}, u32[]{:S(2)}) collective-permute-start(bf16[1024,256]{1,0:T(8,128)(2,1)S(1)} %multiply_convert_fusion), channel_id=1, source_target_pairs={{8,0},{12,4},{16,24},{20,28},{9,1},{13,5},{17,25},{21,29},{10,2},{... | collective-permute-start | bytes 1572872 | tf_op jit(solution)/shard_map/ppermute | solution.py:570
  118.0 4.8 %collective-permute-start.23 = (bf16[1040,256]{1,0:T(8,128)(2,1)S(1)}, bf16[1040,256]{1,0:T(8,128)(2,1)}, u32[]{:S(2)}, u32[]{:S(2)}) collective-permute-start(bf16[1040,256]{1,0:T(8,128)(2,1)S(1)} %scan.1), channel_id=1, source_target_pairs={{8,16},{12,20},{16,8},{20,12},{9,17},{13,21},{17,9},{21,13},{10,18... | collective-permute-start | bytes 1597448 | tf_op jit(solution)/shard_map/ppermute | solution.py:570
  119.5 14.2 %collective-permute-start.26 = (bf16[1040,256]{1,0:T(8,128)(2,1)S(1)}, bf16[1040,256]{1,0:T(8,128)(2,1)S(1)}, u32[]{:S(2)}, u32[]{:S(2)}) collective-permute-start(bf16[1040,256]{1,0:T(8,128)(2,1)S(1)} %scan.1), channel_id=1, source_target_pairs={{0,8},{4,12},{8,0},{12,4},{16,24},{20,28},{24,16},{28,20},{1,9},{5... | collective-permute-start | bytes 1597448 | tf_op jit(solution)/shard_map/ppermute | solution.py:570
  122.3 18.7 %collective-permute-start.25 = (bf16[1040,256]{1,0:T(8,128)(2,1)S(1)}, bf16[1040,256]{1,0:T(8,128)(2,1)S(1)}, u32[]{:S(2)}, u32[]{:S(2)}) collective-permute-start(bf16[1040,256]{1,0:T(8,128)(2,1)S(1)} %scan.1), channel_id=1, source_target_pairs={{0,4},{4,0},{8,12},{12,8},{16,20},{20,16},{24,28},{28,24},{1,5},{5... | collective-permute-start | bytes 1597448 | tf_op jit(solution)/shard_map/ppermute | solution.py:573
  122.8 18.1 %collective-permute-start.24 = (bf16[1040,256]{1,0:T(8,128)(2,1)}, bf16[1040,256]{1,0:T(8,128)(2,1)S(1)}, u32[]{:S(2)}, u32[]{:S(2)}) collective-permute-start(bf16[1040,256]{1,0:T(8,128)(2,1)} %collective-permute-done.23), channel_id=1, source_target_pairs={{8,0},{12,4},{16,24},{20,28},{9,1},{13,5},{17,25},{21,29},{10,2},{... | collective-permute-start | bytes 1597448 | tf_op jit(solution)/shard_map/ppermute | solution.py:570
  133.7 8.4 %collective-permute-start.27 = (bf16[1040,256]{1,0:T(8,128)(2,1)S(1)}, bf16[1040,256]{1,0:T(8,128)(2,1)S(1)}, u32[]{:S(2)}, u32[]{:S(2)}) collective-permute-start(bf16[1040,256]{1,0:T(8,128)(2,1)S(1)} %collective-permute-done.26), channel_id=1, source_target_pairs={{8,16},{12,20},{16,8},{20,12},{9,17},{13,21},{17,9},{21,13},{10,18... | collective-permute-start | bytes 1597448 | tf_op jit(solution)/shard_map/ppermute | solution.py:570
  134.4 19.0 %collective-permute-start.29 = (bf16[1040,256]{1,0:T(8,128)(2,1)S(1)}, bf16[1040,256]{1,0:T(8,128)(2,1)S(1)}, u32[]{:S(2)}, u32[]{:S(2)}) collective-permute-start(bf16[1040,256]{1,0:T(8,128)(2,1)S(1)} %collective-permute-done.26), channel_id=1, source_target_pairs={{0,4},{4,0},{8,12},{12,8},{16,20},{20,16},{24,28},{28,24},{1,5},{5... | collective-permute-start | bytes 1597448 | tf_op jit(solution)/shard_map/ppermute | solution.py:573
  141.0 19.0 %collective-permute-start.30 = (bf16[1040,256]{1,0:T(8,128)(2,1)S(1)}, bf16[1040,256]{1,0:T(8,128)(2,1)S(1)}, u32[]{:S(2)}, u32[]{:S(2)}) collective-permute-start(bf16[1040,256]{1,0:T(8,128)(2,1)S(1)} %broadcast_select_fusion.1), channel_id=1, source_target_pairs={{0,4},{4,0},{8,12},{12,8},{16,20},{20,16},{24,28},{28,24},{1,5},{5... | collective-permute-start | bytes 1597448 | tf_op jit(solution)/shard_map/ppermute | solution.py:573
  142.1 11.2 %collective-permute-start.28 = (bf16[1040,256]{1,0:T(8,128)(2,1)S(1)}, bf16[1040,256]{1,0:T(8,128)(2,1)S(1)}, u32[]{:S(2)}, u32[]{:S(2)}) collective-permute-start(bf16[1040,256]{1,0:T(8,128)(2,1)S(1)} %collective-permute-done.27), channel_id=1, source_target_pairs={{8,0},{12,4},{16,24},{20,28},{9,1},{13,5},{17,25},{21,29},{10,2},{... | collective-permute-start | bytes 1597448 | tf_op jit(solution)/shard_map/ppermute | solution.py:570
  153.3 13.2 %collective-permute-start.31 = (bf16[1040,256]{1,0:T(8,128)(2,1)S(1)}, bf16[1040,256]{1,0:T(8,128)(2,1)S(1)}, u32[]{:S(2)}, u32[]{:S(2)}) collective-permute-start(bf16[1040,256]{1,0:T(8,128)(2,1)S(1)} %broadcast_select_fusion), channel_id=1, source_target_pairs={{0,4},{4,0},{8,12},{12,8},{16,20},{20,16},{24,28},{28,24},{1,5},{5... | collective-permute-start | bytes 1597448 | tf_op jit(solution)/shard_map/ppermute | solution.py:573
  166.8 4.2 %collective-permute-start.32 = (bf16[512,512]{1,0:T(8,128)(2,1)S(1)}, bf16[512,512]{1,0:T(8,128)(2,1)S(1)}, u32[]{:S(2)}, u32[]{:S(2)}) collective-permute-start(bf16[512,512]{1,0:T(8,128)(2,1)S(1)} %add_convert_fusion), channel_id=1, source_target_pairs={{0,1},{1,0},{2,3},{3,2},{4,5},{5,4},{6,7},{7,6},{8,9},{9,8},{10,11... | collective-permute-start | bytes 1572872 | tf_op jit(solution)/shard_map/ppermute | solution.py:730
  172.6 8.3 %collective-permute-start.33 = (bf16[256,512]{1,0:T(8,128)(2,1)}, bf16[256,512]{1,0:T(8,128)(2,1)S(1)}, u32[]{:S(2)}, u32[]{:S(2)}) collective-permute-start(bf16[256,512]{1,0:T(8,128)(2,1)} %add_convert_fusion.2), channel_id=1, source_target_pairs={{0,2},{1,3},{2,0},{3,1},{4,6},{5,7},{6,4},{7,5},{8,10},{9,11},{10,... | collective-permute-start | bytes 786440 | tf_op jit(solution)/shard_map/ppermute | solution.py:740
  182.7 12.3 %all-to-all-start = ((bf16[8,32,512]{2,1,0:T(8,128)(2,1)}), bf16[8,32,512]{2,1,0:T(8,128)(2,1)S(1)}, u32[]{:S(2)}, u32[]{:S(2)}) async-start(bf16[8,32,512]{2,1,0:T(8,128)(2,1)} %multiply_convert_fusion.1), calls=%async_computation | async-start | bytes 524288 | tf_op jit(solution)/shard_map/all_to_all | solution.py:746
  (20 other events, 324.9 us)

commit v9 on v8

--- a/solution.py
+++ b/solution.py
@@ -657,15 +657,17 @@
     near = onward(near, across(near_sent))
     got_mine = across(mine_sent)
     near_out = along(near, outward)
-    near_in = along(near, inward)
     map_sum = (maps.astype(f32) + map_hop.astype(f32)).astype(bf16)
     map_far = along(map_sum, middle)
     map_done = ((map_sum.astype(f32) + map_far.astype(f32)) * in_scale).astype(bf16)
     sent_end = onward(over, hop_far)
     got_end = along(sent_end, over_middle)
+    near, unused = tie((near, sent_end))
+    near_in = along(near, inward)
     hop_over, near_out, unused = tie((hop_over, near_out, sent_end))
     sent_next = onward(far, hop_over)
     got_next = along(sent_next, middle)
+    got_end, near_in = tie((got_end, near_in))
     near_sum = onward(mine, got_mine, near_out, near_in)
     map_done, unused = tie((map_done, sent_next))
     map_done = along(map_done, outward)

time: 197 us -> 192 us (0.975)
  waiting for transfers between devices: 97.7 us -> 88.8 us
  starting transfers between devices: 50.4 us -> 54.5 us
    ppermute x17, waiting for transfers between devices: 58.6 us -> 52.1 us  [along(): return lax.ppermute(value, 'seq', moves)]
    ppermute x9, waiting for transfers between devices: 22.2 us -> 19.8 us  [across(): return lax.ppermute(value, 'seq', [(s, s ^ 1) for s in range(count)])]
    ppermute x9, starting transfers between devices: 10.1 us -> 12.4 us  [across(): return lax.ppermute(value, 'seq', [(s, s ^ 1) for s in range(count)])]
  transfers between devices with their start and end apart: 37 -> 37, of which waited for: 21 -> 19; matrix products, arithmetic and copies ran while one was open for 8% -> 8% of each run, Pallas kernels for 3% -> 3%
where the time goes in v9:
time: 192 us; the launch traced here: 191 us
  waiting for transfers between devices  88.8 us (46%)
  starting transfers between devices  54.5 us (28%)
  Pallas kernels  18.7 us (10%)
  local copies, waits for them, and re-layouts  16.8 us (9%)
  other arithmetic  6.55 us (3%)
  matrix products  3.69 us (2%)
    ppermute x17, waiting for transfers between devices, along(): return lax.ppermute(value, 'seq', moves)  52.1 us
    ppermute x17, starting transfers between devices, along(): return lax.ppermute(value, 'seq', moves)  28.8 us
    ppermute x9, waiting for transfers between devices, across(): return lax.ppermute(value, 'seq', [(s, s ^ 1) for s in range(count)])  19.8 us
    ppermute x9, starting transfers between devices, across(): return lax.ppermute(value, 'seq', [(s, s ^ 1) for s in range(count)])  12.4 us
    all_to_all x1, waiting for transfers between devices, by_heads(): lax.all_to_all(final.astype(bf16), 'seq', split_axis=0, concat_axis=0, ti...  7.62 us
    pallas_call x1, Pallas kernels, scan(): pl.pallas_call(scan_kernel, in_specs=[SMEM, SMEM] + [VMEM] * (len(sums) +...  7.44 us
    unnamed x36, local copies, waits for them, and re-layouts  7.33 us
    ppermute x1, waiting for transfers between devices, by_heads(): received = lax.ppermute(sent.astype(bf16), 'tensor', pairs)  6.89 us
  transfers between devices with their start and end apart: 37, of which 19 were waited for; matrix products, arithmetic and copies ran while one was open for 8% of the time, Pallas kernels for 3%

profile of v9, /device:TPU:0, one launch (start us, length us, event | category | flops | bytes accessed | tf_op | source)
XLA Modules:
  0.0 191.0 jit_solution(2114057302046880093)
XLA Ops:
  0.8 2.0 %constant_dynamic-slice_fusion.9 = bf16[512,512]{1,0:T(8,128)(2,1)} fusion(bf16[512,2048]{1,0:T(8,128)(2,1)} %refs_8_.1, s32[]{:T(128)S(6)} %select_n.123), kind=kLoop, calls=%fused_computation.64 | loop fusion | bytes 1048580 | tf_op jit(solution)/shard_map/dynamic_slice | solution.py:611
  3.7 3.1 %collective-permute-start = (bf16[32,1024]{1,0:T(8,128)(2,1)S(1)}, bf16[32,1024]{1,0:T(8,128)(2,1)S(1)}, u32[]{:S(2)}, u32[]{:S(2)}) collective-permute-start(bf16[32,1024]{1,0:T(8,128)(2,1)S(1)} %get-tuple-element.65), channel_id=1, source_target_pairs={{0,8},{4,12},{8,0},{12,4},{16,24},{20,28},{24,16},{28,20},{1,9},{5... | collective-permute-start | bytes 196616 | tf_op jit(solution)/shard_map/ppermute | solution.py:570
  6.8 2.6 %collective-permute-start.1 = (bf16[32,1024]{1,0:T(8,128)(2,1)S(1)}, bf16[32,1024]{1,0:T(8,128)(2,1)S(1)}, u32[]{:S(2)}, u32[]{:S(2)}) collective-permute-start(bf16[32,1024]{1,0:T(8,128)(2,1)S(1)} %get-tuple-element.64), channel_id=1, source_target_pairs={{0,16},{4,20},{8,24},{12,28},{16,0},{20,4},{24,8},{28,12},{1,17},{... | collective-permute-start | bytes 196616 | tf_op jit(solution)/shard_map/ppermute | solution.py:570
  9.4 1.7 collective-permute-start.10
  15.5 1.6 collective-permute-start.6
  17.1 2.2 %constant_dynamic-slice_fusion.2 = (bf16[512,1,2,128]{3,2,1,0:T(2,128)(2,1)}, bf16[512,1,2,128]{3,2,1,0:T(2,128)(2,1)}) fusion(bf16[512,2,2,128]{3,2,1,0:T(2,128)(2,1)} %param.18, s32[]{:T(128)S(6)} %select_n.132, s32[]{:T(128)S(6)} %select_n.129), kind=kLoop, calls=%fused_computation.57 | loop fusion | bytes 1048584 | tf_op jit(solution)/shard_map/jit(dynamic_index_in_dim)/dynamic_slice | solution.py:566
  21.6 1.6 collective-permute-start.4
  23.2 5.3 %collective-permute-done.6.refs_4_ = bf16[4,32,1024]{2,1,0:T(8,128)(2,1)} collective-permute-done((bf16[4,32,1024]{2,1,0:T(8,128)(2,1)S(1)}, bf16[4,32,1024]{2,1,0:T(8,128)(2,1)}, u32[]{:S(2)}, u32[]{:S(2)}) %collective-permute-start.6) | collective-permute-done | bytes 262176 | tf_op jit(solution)/shard_map/ppermute | solution.py:573
  36.6 2.9 %collective-permute-done.11.refs_12_ = bf16[576,256]{1,0:T(8,128)(2,1)S(1)} collective-permute-done((bf16[576,256]{1,0:T(8,128)(2,1)}, bf16[576,256]{1,0:T(8,128)(2,1)S(1)}, u32[]{:S(2)}, u32[]{:S(2)}) %collective-permute-start.11) | collective-permute-done | bytes 294944 | tf_op jit(solution)/shard_map/ppermute | solution.py:573
  39.5 1.6 copy-done.5
  42.1 6.3 %project.1 = (bf16[1056,256]{1,0:T(8,128)(2,1)}, bf16[1056,256]{1,0:T(8,128)(2,1)}, bf16[1056,256]{1,0:T(8,128)(2,1)S(1)}, bf16[1056,256]{1,0:T(8,128)(2,1)S(1)}...) custom-call(s32[7]{0:T(128)S(1)} %stack.43.place_ref, ...), custom_call_target="tpu_custom_call" | custom-call | flops 2684354560 | bytes 4194304 | tf_op jit(solution)/shard_map/project/pallas_call | solution.py:301
  49.9 2.5 %collective-permute-start.20 = (bf16[1024,256]{1,0:T(8,128)(2,1)S(1)}, bf16[1024,256]{1,0:T(8,128)(2,1)S(1)}, u32[]{:S(2)}, u32[]{:S(2)}) collective-permute-start(bf16[1024,256]{1,0:T(8,128)(2,1)S(1)} %get-tuple-element.49), channel_id=1, source_target_pairs={{0,8},{4,12},{24,16},{28,20},{1,9},{5,13},{25,17},{29,21},{2,10},{... | collective-permute-start | bytes 1572872 | tf_op jit(solution)/shard_map/ppermute | solution.py:570
  52.4 2.1 %collective-permute-start.16 = (bf16[1056,256]{1,0:T(8,128)(2,1)}, bf16[1056,256]{1,0:T(8,128)(2,1)}, u32[]{:S(2)}, u32[]{:S(2)}) collective-permute-start(bf16[1056,256]{1,0:T(8,128)(2,1)} %get-tuple-element.43.refs_0_), channel_id=1, source_target_pairs={{0,8},{4,12},{24,16},{28,20},{1,9},{5,13},{25,17},{29,21},{2,10},{... | collective-permute-start | bytes 1622024 | tf_op jit(solution)/shard_map/ppermute | solution.py:570
  54.5 2.1 %collective-permute-start.13 = (bf16[1056,256]{1,0:T(8,128)(2,1)}, bf16[1056,256]{1,0:T(8,128)(2,1)}, u32[]{:S(2)}, u32[]{:S(2)}) collective-permute-start(bf16[1056,256]{1,0:T(8,128)(2,1)} %get-tuple-element.40.refs_0_), channel_id=1, source_target_pairs={{0,8},{4,12},{24,16},{28,20},{1,9},{5,13},{25,17},{29,21},{2,10},{... | collective-permute-start | bytes 1622024 | tf_op jit(solution)/shard_map/ppermute | solution.py:570
  56.6 3.8 %collective-permute-done.14.refs_1_ = bf16[1056,256]{1,0:T(8,128)(2,1)S(1)} collective-permute-done((bf16[1056,256]{1,0:T(8,128)(2,1)S(1)}, bf16[1056,256]{1,0:T(8,128)(2,1)S(1)}, u32[]{:S(2)}, u32[]{:S(2)}) %collective-permute-start.14) | collective-permute-done | bytes 540704 | tf_op jit(solution)/shard_map/ppermute | solution.py:573
  62.7 2.1 %collective-permute-done.20 = bf16[1024,256]{1,0:T(8,128)(2,1)S(1)} collective-permute-done((bf16[1024,256]{1,0:T(8,128)(2,1)S(1)}, bf16[1024,256]{1,0:T(8,128)(2,1)S(1)}, u32[]{:S(2)}, u32[]{:S(2)}) %collective-permute-start.20) | collective-permute-done | bytes 524320 | tf_op jit(solution)/shard_map/ppermute | solution.py:570
  66.2 10.2 %collective-permute-done.16.refs_1_ = bf16[1056,256]{1,0:T(8,128)(2,1)} collective-permute-done((bf16[1056,256]{1,0:T(8,128)(2,1)}, bf16[1056,256]{1,0:T(8,128)(2,1)}, u32[]{:S(2)}, u32[]{:S(2)}) %collective-permute-start.16) | collective-permute-done | bytes 540704 | tf_op jit(solution)/shard_map/ppermute | solution.py:570
  79.1 5.3 %collective-permute-done.13.refs_1_ = bf16[1056,256]{1,0:T(8,128)(2,1)} collective-permute-done((bf16[1056,256]{1,0:T(8,128)(2,1)}, bf16[1056,256]{1,0:T(8,128)(2,1)}, u32[]{:S(2)}, u32[]{:S(2)}) %collective-permute-start.13) | collective-permute-done | bytes 540704 | tf_op jit(solution)/shard_map/ppermute | solution.py:570
  84.4 4.4 %collective-permute-start.18 = (bf16[1056,256]{1,0:T(8,128)(2,1)}, bf16[1056,256]{1,0:T(8,128)(2,1)S(1)}, u32[]{:S(2)}, u32[]{:S(2)}) collective-permute-start(bf16[1056,256]{1,0:T(8,128)(2,1)} %onward.4), channel_id=1, source_target_pairs={{0,8},{4,12},{24,16},{28,20},{1,9},{5,13},{25,17},{29,21},{2,10},{... | collective-permute-start | bytes 1622024 | tf_op jit(solution)/shard_map/ppermute | solution.py:570
  92.5 4.7 %collective-permute-done.18.refs_3_ = bf16[1056,256]{1,0:T(8,128)(2,1)S(1)} collective-permute-done((bf16[1056,256]{1,0:T(8,128)(2,1)}, bf16[1056,256]{1,0:T(8,128)(2,1)S(1)}, u32[]{:S(2)}, u32[]{:S(2)}) %collective-permute-start.18) | collective-permute-done | bytes 540704 | tf_op jit(solution)/shard_map/ppermute | solution.py:570
  98.6 4.4 %collective-permute-done.22.refs_5_ = bf16[1024,256]{1,0:T(8,128)(2,1)S(1)} collective-permute-done((bf16[1024,256]{1,0:T(8,128)(2,1)S(1)}, bf16[1024,256]{1,0:T(8,128)(2,1)S(1)}, u32[]{:S(2)}, u32[]{:S(2)}) %collective-permute-start.22) | collective-permute-done | bytes 524320 | tf_op jit(solution)/shard_map/ppermute | solution.py:570
  104.0 7.4 %scan.1 = bf16[1040,256]{1,0:T(8,128)(2,1)S(1)} custom-call(s32[7]{0:T(128)S(1)} %stack.43.place_ref, f32[1]{0:T(128)} %bitcast.3.scale_ref, bf16[1056,256]{1,0:T(8,128)(2,1)S(1)} %onward.6.refs_0_, bf16[1056,256]{1,0:T(8,128)(2,1)S(1)} %collective-permute-done.17.refs_1_, bf16[1056,256]{1,0:T(8,128)(2,1)S(1)} %collective-permute-done.19.refs_2_, ...), custom_call_target="tpu_custom_call" | custom-call | flops 268435456 | bytes 2097152 | tf_op jit(solution)/shard_map/scan/pallas_call | solution.py:515
  112.9 1.8 collective-permute-start.26
  117.4 7.6 %collective-permute-done.26 = bf16[1040,256]{1,0:T(8,128)(2,1)S(1)} collective-permute-done((bf16[1040,256]{1,0:T(8,128)(2,1)S(1)}, bf16[1040,256]{1,0:T(8,128)(2,1)S(1)}, u32[]{:S(2)}, u32[]{:S(2)}) %collective-permute-start.26) | collective-permute-done | bytes 532512 | tf_op jit(solution)/shard_map/ppermute | solution.py:570
  127.5 6.4 %collective-permute-done.24 = bf16[1040,256]{1,0:T(8,128)(2,1)S(1)} collective-permute-done((bf16[1040,256]{1,0:T(8,128)(2,1)}, bf16[1040,256]{1,0:T(8,128)(2,1)S(1)}, u32[]{:S(2)}, u32[]{:S(2)}) %collective-permute-start.24) | collective-permute-done | bytes 532512 | tf_op jit(solution)/shard_map/ppermute | solution.py:570
  133.9 2.5 %collective-permute-start.30 = (bf16[1040,256]{1,0:T(8,128)(2,1)S(1)}, bf16[1040,256]{1,0:T(8,128)(2,1)S(1)}, u32[]{:S(2)}, u32[]{:S(2)}) collective-permute-start(bf16[1040,256]{1,0:T(8,128)(2,1)S(1)} %broadcast_select_fusion.1), channel_id=1, source_target_pairs={{0,4},{4,0},{8,12},{12,8},{16,20},{20,16},{24,28},{28,24},{1,5},{5... | collective-permute-start | bytes 1597448 | tf_op jit(solution)/shard_map/ppermute | solution.py:573
  139.1 10.1 %collective-permute-done.28 = bf16[1040,256]{1,0:T(8,128)(2,1)S(1)} collective-permute-done((bf16[1040,256]{1,0:T(8,128)(2,1)S(1)}, bf16[1040,256]{1,0:T(8,128)(2,1)S(1)}, u32[]{:S(2)}, u32[]{:S(2)}) %collective-permute-start.28) | collective-permute-done | bytes 532512 | tf_op jit(solution)/shard_map/ppermute | solution.py:570
  151.1 7.8 %collective-permute-done.31 = bf16[1040,256]{1,0:T(8,128)(2,1)S(1)} collective-permute-done((bf16[1040,256]{1,0:T(8,128)(2,1)S(1)}, bf16[1040,256]{1,0:T(8,128)(2,1)S(1)}, u32[]{:S(2)}, u32[]{:S(2)}) %collective-permute-start.31) | collective-permute-done | bytes 532512 | tf_op jit(solution)/shard_map/ppermute | solution.py:573
  161.2 3.5 %collective-permute-start.35 = (f32[8,128]{1,0:T(8,128)S(1)}, f32[8,128]{1,0:T(8,128)S(1)}, u32[]{:S(2)}, u32[]{:S(2)}) collective-permute-start(f32[8,128]{1,0:T(8,128)S(1)} %add.280), channel_id=1, source_target_pairs={{0,2},{1,3},{2,0},{3,1},{4,6},{5,7},{6,4},{7,5},{8,10},{9,11},{10,... | collective-permute-start | bytes 12296 | tf_op jit(solution)/shard_map/ppermute | solution.py:743
  167.7 6.9 %collective-permute-done.33 = bf16[256,512]{1,0:T(8,128)(2,1)S(1)} collective-permute-done((bf16[256,512]{1,0:T(8,128)(2,1)}, bf16[256,512]{1,0:T(8,128)(2,1)S(1)}, u32[]{:S(2)}, u32[]{:S(2)}) %collective-permute-start.33) | collective-permute-done | bytes 262176 | tf_op jit(solution)/shard_map/ppermute | solution.py:742
  176.5 5.6 %all-to-all-start = ((bf16[8,32,512]{2,1,0:T(8,128)(2,1)}), bf16[8,32,512]{2,1,0:T(8,128)(2,1)S(1)}, u32[]{:S(2)}, u32[]{:S(2)}) async-start(bf16[8,32,512]{2,1,0:T(8,128)(2,1)} %multiply_convert_fusion.1), calls=%async_computation | async-start | bytes 524288 | tf_op jit(solution)/shard_map/all_to_all | solution.py:748
  182.6 7.6 %all-to-all-done = bf16[8,32,512]{2,1,0:T(8,128)(2,1)S(1)} async-done(((bf16[8,32,512]{2,1,0:T(8,128)(2,1)}), bf16[8,32,512]{2,1,0:T(8,128)(2,1)S(1)}, u32[]{:S(2)}, u32[]{:S(2)}) %all-to-all-start) | async-done | bytes 262176 | tf_op jit(solution)/shard_map/all_to_all | solution.py:748
  (139 shorter events, 49.4 us)
Async XLA Ops:
  3.7 10.4 %collective-permute-start = (bf16[32,1024]{1,0:T(8,128)(2,1)S(1)}, bf16[32,1024]{1,0:T(8,128)(2,1)S(1)}, u32[]{:S(2)}, u32[]{:S(2)}) collective-permute-start(bf16[32,1024]{1,0:T(8,128)(2,1)S(1)} %get-tuple-element.65), channel_id=1, source_target_pairs={{0,8},{4,12},{8,0},{12,4},{16,24},{20,28},{24,16},{28,20},{1,9},{5... | collective-permute-start | bytes 196616 | tf_op jit(solution)/shard_map/ppermute | solution.py:570
  6.8 7.4 %collective-permute-start.1 = (bf16[32,1024]{1,0:T(8,128)(2,1)S(1)}, bf16[32,1024]{1,0:T(8,128)(2,1)S(1)}, u32[]{:S(2)}, u32[]{:S(2)}) collective-permute-start(bf16[32,1024]{1,0:T(8,128)(2,1)S(1)} %get-tuple-element.64), channel_id=1, source_target_pairs={{0,16},{4,20},{8,24},{12,28},{16,0},{20,4},{24,8},{28,12},{1,17},{... | collective-permute-start | bytes 196616 | tf_op jit(solution)/shard_map/ppermute | solution.py:570
  9.4 6.1 %collective-permute-start.2 = (bf16[32,1024]{1,0:T(8,128)(2,1)S(1)}, bf16[32,1024]{1,0:T(8,128)(2,1)S(1)}, u32[]{:S(2)}, u32[]{:S(2)}) collective-permute-start(bf16[32,1024]{1,0:T(8,128)(2,1)S(1)} %get-tuple-element.63), channel_id=1, source_target_pairs={{0,24},{4,28},{8,16},{12,20},{16,8},{20,12},{24,0},{28,4},{1,25},{... | collective-permute-start | bytes 196616 | tf_op jit(solution)/shard_map/ppermute | solution.py:570
  9.4 22.3 %collective-permute-start.10 = (bf16[512,512]{1,0:T(8,128)(2,1)}, bf16[512,512]{1,0:T(8,128)(2,1)S(1)}, u32[]{:S(2)}, u32[]{:S(2)}) collective-permute-start(bf16[512,512]{1,0:T(8,128)(2,1)} %constant_dynamic-slice_fusion.9), channel_id=1, source_target_pairs={{0,4},{4,0},{8,12},{12,8},{16,20},{20,16},{24,28},{28,24},{1,5},{5... | collective-permute-start | bytes 1572872 | tf_op jit(solution)/shard_map/ppermute | solution.py:573
  15.5 12.9 %collective-permute-start.6 = (bf16[4,32,1024]{2,1,0:T(8,128)(2,1)S(1)}, bf16[4,32,1024]{2,1,0:T(8,128)(2,1)}, u32[]{:S(2)}, u32[]{:S(2)}) collective-permute-start(bf16[4,32,1024]{2,1,0:T(8,128)(2,1)S(1)} %pad_maximum_fusion.1.refs_0_), channel_id=1, source_target_pairs={{0,4},{4,0},{8,12},{12,8},{16,20},{20,16},{24,28},{28,24},{1,5},{5... | collective-permute-start | bytes 786440 | tf_op jit(solution)/shard_map/ppermute | solution.py:573
  21.6 12.9 %collective-permute-start.4 = (bf16[4,32,1024]{2,1,0:T(8,128)(2,1)S(1)}, bf16[4,32,1024]{2,1,0:T(8,128)(2,1)}, u32[]{:S(2)}, u32[]{:S(2)}) collective-permute-start(bf16[4,32,1024]{2,1,0:T(8,128)(2,1)S(1)} %pad_maximum_fusion.1.refs_0_), channel_id=1, source_target_pairs={{0,2},{1,3},{2,0},{3,1},{4,6},{5,7},{6,4},{7,5},{8,10},{9,11},{10,... | collective-permute-start | bytes 786440 | tf_op jit(solution)/shard_map/ppermute | solution.py:638
  28.5 6.9 %collective-permute-start.8 = (bf16[4,32,1024]{2,1,0:T(8,128)(2,1)}, bf16[4,32,1024]{2,1,0:T(8,128)(2,1)}, u32[]{:S(2)}, u32[]{:S(2)}) collective-permute-start(bf16[4,32,1024]{2,1,0:T(8,128)(2,1)} %collective-permute-done.6.refs_4_), channel_id=1, source_target_pairs={{0,2},{1,3},{2,0},{3,1},{4,6},{5,7},{6,4},{7,5},{8,10},{9,11},{10,... | collective-permute-start | bytes 786440 | tf_op jit(solution)/shard_map/ppermute | solution.py:638
  32.5 7.0 %collective-permute-start.11 = (bf16[576,256]{1,0:T(8,128)(2,1)}, bf16[576,256]{1,0:T(8,128)(2,1)S(1)}, u32[]{:S(2)}, u32[]{:S(2)}) collective-permute-start(bf16[576,256]{1,0:T(8,128)(2,1)} %pad_maximum_fusion), channel_id=1, source_target_pairs={{0,4},{4,0},{8,12},{12,8},{16,20},{20,16},{24,28},{28,24},{1,5},{5... | collective-permute-start | bytes 884744 | tf_op jit(solution)/shard_map/ppermute | solution.py:573
  48.4 12.0 %collective-permute-start.14 = (bf16[1056,256]{1,0:T(8,128)(2,1)S(1)}, bf16[1056,256]{1,0:T(8,128)(2,1)S(1)}, u32[]{:S(2)}, u32[]{:S(2)}) collective-permute-start(bf16[1056,256]{1,0:T(8,128)(2,1)S(1)} %get-tuple-element.42), channel_id=1, source_target_pairs={{0,4},{4,0},{8,12},{12,8},{16,20},{20,16},{24,28},{28,24},{1,5},{5... | collective-permute-start | bytes 1622024 | tf_op jit(solution)/shard_map/ppermute | solution.py:573
  49.9 14.8 %collective-permute-start.20 = (bf16[1024,256]{1,0:T(8,128)(2,1)S(1)}, bf16[1024,256]{1,0:T(8,128)(2,1)S(1)}, u32[]{:S(2)}, u32[]{:S(2)}) collective-permute-start(bf16[1024,256]{1,0:T(8,128)(2,1)S(1)} %get-tuple-element.49), channel_id=1, source_target_pairs={{0,8},{4,12},{24,16},{28,20},{1,9},{5,13},{25,17},{29,21},{2,10},{... | collective-permute-start | bytes 1572872 | tf_op jit(solution)/shard_map/ppermute | solution.py:570
  52.4 24.0 %collective-permute-start.16 = (bf16[1056,256]{1,0:T(8,128)(2,1)}, bf16[1056,256]{1,0:T(8,128)(2,1)}, u32[]{:S(2)}, u32[]{:S(2)}) collective-permute-start(bf16[1056,256]{1,0:T(8,128)(2,1)} %get-tuple-element.43.refs_0_), channel_id=1, source_target_pairs={{0,8},{4,12},{24,16},{28,20},{1,9},{5,13},{25,17},{29,21},{2,10},{... | collective-permute-start | bytes 1622024 | tf_op jit(solution)/shard_map/ppermute | solution.py:570
  54.5 29.9 %collective-permute-start.13 = (bf16[1056,256]{1,0:T(8,128)(2,1)}, bf16[1056,256]{1,0:T(8,128)(2,1)}, u32[]{:S(2)}, u32[]{:S(2)}) collective-permute-start(bf16[1056,256]{1,0:T(8,128)(2,1)} %get-tuple-element.40.refs_0_), channel_id=1, source_target_pairs={{0,8},{4,12},{24,16},{28,20},{1,9},{5,13},{25,17},{29,21},{2,10},{... | collective-permute-start | bytes 1622024 | tf_op jit(solution)/shard_map/ppermute | solution.py:570
  61.4 27.4 %collective-permute-start.15 = (bf16[1056,256]{1,0:T(8,128)(2,1)}, bf16[1056,256]{1,0:T(8,128)(2,1)}, u32[]{:S(2)}, u32[]{:S(2)}) collective-permute-start(bf16[1056,256]{1,0:T(8,128)(2,1)} %onward.4), channel_id=1, source_target_pairs={{8,0},{12,4},{16,24},{20,28},{9,1},{13,5},{17,25},{21,29},{10,2},{... | collective-permute-start | bytes 1622024 | tf_op jit(solution)/shard_map/ppermute | solution.py:570
  64.9 26.0 %collective-permute-start.21 = (bf16[1024,256]{1,0:T(8,128)(2,1)S(1)}, bf16[1024,256]{1,0:T(8,128)(2,1)S(1)}, u32[]{:S(2)}, u32[]{:S(2)}) collective-permute-start(bf16[1024,256]{1,0:T(8,128)(2,1)S(1)} %add_convert_fusion.1.refs_3_), channel_id=1, source_target_pairs={{8,16},{12,20},{16,8},{20,12},{9,17},{13,21},{17,9},{21,13},{10,18... | collective-permute-start | bytes 1572872 | tf_op jit(solution)/shard_map/ppermute | solution.py:570
  65.6 31.7 %collective-permute-start.12 = (bf16[1056,256]{1,0:T(8,128)(2,1)}, bf16[1056,256]{1,0:T(8,128)(2,1)S(1)}, u32[]{:S(2)}, u32[]{:S(2)}) collective-permute-start(bf16[1056,256]{1,0:T(8,128)(2,1)} %copy-done.7), channel_id=1, source_target_pairs={{0,4},{4,0},{8,12},{12,8},{16,20},{20,16},{24,28},{28,24},{1,5},{5... | collective-permute-start | bytes 1622024 | tf_op jit(solution)/shard_map/ppermute | solution.py:573
  77.8 19.5 %collective-permute-start.17 = (bf16[1056,256]{1,0:T(8,128)(2,1)S(1)}, bf16[1056,256]{1,0:T(8,128)(2,1)S(1)}, u32[]{:S(2)}, u32[]{:S(2)}) collective-permute-start(bf16[1056,256]{1,0:T(8,128)(2,1)S(1)} %onward.5), channel_id=1, source_target_pairs={{8,24},{12,28},{16,0},{20,4},{9,25},{13,29},{17,1},{21,5},{10,26},... | collective-permute-start | bytes 1622024 | tf_op jit(solution)/shard_map/ppermute | solution.py:570
  84.4 12.9 %collective-permute-start.18 = (bf16[1056,256]{1,0:T(8,128)(2,1)}, bf16[1056,256]{1,0:T(8,128)(2,1)S(1)}, u32[]{:S(2)}, u32[]{:S(2)}) collective-permute-start(bf16[1056,256]{1,0:T(8,128)(2,1)} %onward.4), channel_id=1, source_target_pairs={{0,8},{4,12},{24,16},{28,20},{1,9},{5,13},{25,17},{29,21},{2,10},{... | collective-permute-start | bytes 1622024 | tf_op jit(solution)/shard_map/ppermute | solution.py:570
  90.2 12.8 %collective-permute-start.19 = (bf16[1056,256]{1,0:T(8,128)(2,1)S(1)}, bf16[1056,256]{1,0:T(8,128)(2,1)S(1)}, u32[]{:S(2)}, u32[]{:S(2)}) collective-permute-start(bf16[1056,256]{1,0:T(8,128)(2,1)S(1)} %onward.7), channel_id=1, source_target_pairs={{8,16},{12,20},{16,8},{20,12},{9,17},{13,21},{17,9},{21,13},{10,18... | collective-permute-start | bytes 1622024 | tf_op jit(solution)/shard_map/ppermute | solution.py:570
  91.1 11.9 %collective-permute-start.22 = (bf16[1024,256]{1,0:T(8,128)(2,1)S(1)}, bf16[1024,256]{1,0:T(8,128)(2,1)S(1)}, u32[]{:S(2)}, u32[]{:S(2)}) collective-permute-start(bf16[1024,256]{1,0:T(8,128)(2,1)S(1)} %multiply_convert_fusion), channel_id=1, source_target_pairs={{8,0},{12,4},{16,24},{20,28},{9,1},{13,5},{17,25},{21,29},{10,2},{... | collective-permute-start | bytes 1572872 | tf_op jit(solution)/shard_map/ppermute | solution.py:570
  111.5 4.6 %collective-permute-start.23 = (bf16[1040,256]{1,0:T(8,128)(2,1)S(1)}, bf16[1040,256]{1,0:T(8,128)(2,1)}, u32[]{:S(2)}, u32[]{:S(2)}) collective-permute-start(bf16[1040,256]{1,0:T(8,128)(2,1)S(1)} %scan.1), channel_id=1, source_target_pairs={{8,16},{12,20},{16,8},{20,12},{9,17},{13,21},{17,9},{21,13},{10,18... | collective-permute-start | bytes 1597448 | tf_op jit(solution)/shard_map/ppermute | solution.py:570
  112.9 12.0 %collective-permute-start.26 = (bf16[1040,256]{1,0:T(8,128)(2,1)S(1)}, bf16[1040,256]{1,0:T(8,128)(2,1)S(1)}, u32[]{:S(2)}, u32[]{:S(2)}) collective-permute-start(bf16[1040,256]{1,0:T(8,128)(2,1)S(1)} %scan.1), channel_id=1, source_target_pairs={{0,8},{4,12},{8,0},{12,4},{16,24},{20,28},{24,16},{28,20},{1,9},{5... | collective-permute-start | bytes 1597448 | tf_op jit(solution)/shard_map/ppermute | solution.py:570
  114.8 19.1 %collective-permute-start.25 = (bf16[1040,256]{1,0:T(8,128)(2,1)S(1)}, bf16[1040,256]{1,0:T(8,128)(2,1)S(1)}, u32[]{:S(2)}, u32[]{:S(2)}) collective-permute-start(bf16[1040,256]{1,0:T(8,128)(2,1)S(1)} %scan.1), channel_id=1, source_target_pairs={{0,4},{4,0},{8,12},{12,8},{16,20},{20,16},{24,28},{28,24},{1,5},{5... | collective-permute-start | bytes 1597448 | tf_op jit(solution)/shard_map/ppermute | solution.py:573
  116.1 17.8 %collective-permute-start.24 = (bf16[1040,256]{1,0:T(8,128)(2,1)}, bf16[1040,256]{1,0:T(8,128)(2,1)S(1)}, u32[]{:S(2)}, u32[]{:S(2)}) collective-permute-start(bf16[1040,256]{1,0:T(8,128)(2,1)} %collective-permute-done.23), channel_id=1, source_target_pairs={{8,0},{12,4},{16,24},{20,28},{9,1},{13,5},{17,25},{21,29},{10,2},{... | collective-permute-start | bytes 1597448 | tf_op jit(solution)/shard_map/ppermute | solution.py:570
  124.9 11.9 %collective-permute-start.27 = (bf16[1040,256]{1,0:T(8,128)(2,1)S(1)}, bf16[1040,256]{1,0:T(8,128)(2,1)S(1)}, u32[]{:S(2)}, u32[]{:S(2)}) collective-permute-start(bf16[1040,256]{1,0:T(8,128)(2,1)S(1)} %collective-permute-done.26), channel_id=1, source_target_pairs={{8,16},{12,20},{16,8},{20,12},{9,17},{13,21},{17,9},{21,13},{10,18... | collective-permute-start | bytes 1597448 | tf_op jit(solution)/shard_map/ppermute | solution.py:570
  125.6 23.7 %collective-permute-start.29 = (bf16[1040,256]{1,0:T(8,128)(2,1)S(1)}, bf16[1040,256]{1,0:T(8,128)(2,1)S(1)}, u32[]{:S(2)}, u32[]{:S(2)}) collective-permute-start(bf16[1040,256]{1,0:T(8,128)(2,1)S(1)} %collective-permute-done.26), channel_id=1, source_target_pairs={{0,4},{4,0},{8,12},{12,8},{16,20},{20,16},{24,28},{28,24},{1,5},{5... | collective-permute-start | bytes 1597448 | tf_op jit(solution)/shard_map/ppermute | solution.py:573
  133.9 15.8 %collective-permute-start.30 = (bf16[1040,256]{1,0:T(8,128)(2,1)S(1)}, bf16[1040,256]{1,0:T(8,128)(2,1)S(1)}, u32[]{:S(2)}, u32[]{:S(2)}) collective-permute-start(bf16[1040,256]{1,0:T(8,128)(2,1)S(1)} %broadcast_select_fusion.1), channel_id=1, source_target_pairs={{0,4},{4,0},{8,12},{12,8},{16,20},{20,16},{24,28},{28,24},{1,5},{5... | collective-permute-start | bytes 1597448 | tf_op jit(solution)/shard_map/ppermute | solution.py:573
  136.9 12.3 %collective-permute-start.28 = (bf16[1040,256]{1,0:T(8,128)(2,1)S(1)}, bf16[1040,256]{1,0:T(8,128)(2,1)S(1)}, u32[]{:S(2)}, u32[]{:S(2)}) collective-permute-start(bf16[1040,256]{1,0:T(8,128)(2,1)S(1)} %collective-permute-done.27), channel_id=1, source_target_pairs={{8,0},{12,4},{16,24},{20,28},{9,1},{13,5},{17,25},{21,29},{10,2},{... | collective-permute-start | bytes 1597448 | tf_op jit(solution)/shard_map/ppermute | solution.py:570
  149.3 9.6 %collective-permute-start.31 = (bf16[1040,256]{1,0:T(8,128)(2,1)S(1)}, bf16[1040,256]{1,0:T(8,128)(2,1)S(1)}, u32[]{:S(2)}, u32[]{:S(2)}) collective-permute-start(bf16[1040,256]{1,0:T(8,128)(2,1)S(1)} %broadcast_select_fusion), channel_id=1, source_target_pairs={{0,4},{4,0},{8,12},{12,8},{16,20},{20,16},{24,28},{28,24},{1,5},{5... | collective-permute-start | bytes 1597448 | tf_op jit(solution)/shard_map/ppermute | solution.py:573
  159.2 5.5 %collective-permute-start.32 = (bf16[512,512]{1,0:T(8,128)(2,1)S(1)}, bf16[512,512]{1,0:T(8,128)(2,1)S(1)}, u32[]{:S(2)}, u32[]{:S(2)}) collective-permute-start(bf16[512,512]{1,0:T(8,128)(2,1)S(1)} %add_convert_fusion), channel_id=1, source_target_pairs={{0,1},{1,0},{2,3},{3,2},{4,5},{5,4},{6,7},{7,6},{8,9},{9,8},{10,11... | collective-permute-start | bytes 1572872 | tf_op jit(solution)/shard_map/ppermute | solution.py:732
  161.2 5.1 %collective-permute-start.35 = (f32[8,128]{1,0:T(8,128)S(1)}, f32[8,128]{1,0:T(8,128)S(1)}, u32[]{:S(2)}, u32[]{:S(2)}) collective-permute-start(f32[8,128]{1,0:T(8,128)S(1)} %add.280), channel_id=1, source_target_pairs={{0,2},{1,3},{2,0},{3,1},{4,6},{5,7},{6,4},{7,5},{8,10},{9,11},{10,... | collective-permute-start | bytes 12296 | tf_op jit(solution)/shard_map/ppermute | solution.py:743
  166.3 8.3 %collective-permute-start.33 = (bf16[256,512]{1,0:T(8,128)(2,1)}, bf16[256,512]{1,0:T(8,128)(2,1)S(1)}, u32[]{:S(2)}, u32[]{:S(2)}) collective-permute-start(bf16[256,512]{1,0:T(8,128)(2,1)} %add_convert_fusion.2), channel_id=1, source_target_pairs={{0,2},{1,3},{2,0},{3,1},{4,6},{5,7},{6,4},{7,5},{8,10},{9,11},{10,... | collective-permute-start | bytes 786440 | tf_op jit(solution)/shard_map/ppermute | solution.py:742
  176.5 13.8 %all-to-all-start = ((bf16[8,32,512]{2,1,0:T(8,128)(2,1)}), bf16[8,32,512]{2,1,0:T(8,128)(2,1)S(1)}, u32[]{:S(2)}, u32[]{:S(2)}) async-start(bf16[8,32,512]{2,1,0:T(8,128)(2,1)} %multiply_convert_fusion.1), calls=%async_computation | async-start | bytes 524288 | tf_op jit(solution)/shard_map/all_to_all | solution.py:748
  (20 other events, 320.4 us)

commit v10 on v9

--- a/solution.py
+++ b/solution.py
@@ -731,7 +731,6 @@
     pairs = [(t, t ^ 1) for t in range(ranks)]
     received = lax.ppermute(first_sum(1 - keeps).astype(bf16), "tensor", pairs)
     kept = first_sum(keeps)
-    squares = squares + lax.ppermute(squares, "tensor", pairs)
     bit = 2
     while bit < ranks:
         run //= 2
@@ -739,9 +738,12 @@
         pairs = [(t, t ^ bit) for t in range(ranks)]
         sent = run_of(kept, 1 - keeps, run) + run_of(received, 1 - keeps, run).astype(f32)
         kept = run_of(kept, keeps, run) + run_of(received, keeps, run).astype(f32)
-        received = lax.ppermute(sent.astype(bf16), "tensor", pairs)
+        sent = sent.astype(bf16)
         squares = squares + lax.ppermute(squares, "tensor", pairs)
+        squares, unused = tie((squares, sent))
+        received = lax.ppermute(sent, "tensor", pairs)
         bit *= 2
+    squares = squares + lax.ppermute(squares, "tensor", [(t, t ^ 1) for t in range(ranks)])
     mean_sq = squares.reshape(count, ranks, own) / (HEADS * HEAD_DIM)
     factors = lax.rsqrt(pick(mean_sq, 1, rank) + epsilon)
     final = (kept + received.astype(f32)).reshape(count, own, -1) * factors[:, :, None]

time: 192 us -> 193 us (level)
    ppermute x1 -> x2, starting transfers between devices: 0.01 us -> 2.16 us  [the longest x1 2.09 us: by_heads(): received = lax.ppermute(sent, 'tensor', pairs)]
    ppermute x1 -> x2, waiting for transfers between devices: 6.89 us -> 5.61 us  [the longest x1 5.61 us: by_heads(): received = lax.ppermute(sent, 'tensor', pairs)]
    ppermute x2 -> x1, starting transfers between devices: 4.09 us -> 3.61 us  [by_heads(): squares = squares + lax.ppermute(squares, 'tensor', pairs)]
where the time goes in v10:
time: 193 us; the launch traced here: 192 us
  waiting for transfers between devices  88.5 us (46%)
  starting transfers between devices  56.2 us (29%)
  Pallas kernels  18.7 us (10%)
  local copies, waits for them, and re-layouts  16.8 us (9%)
  other arithmetic  5.93 us (3%)
  matrix products  3.69 us (2%)
    ppermute x17, waiting for transfers between devices, along(): return lax.ppermute(value, 'seq', moves)  52.1 us
    ppermute x17, starting transfers between devices, along(): return lax.ppermute(value, 'seq', moves)  28.8 us
    ppermute x9, waiting for transfers between devices, across(): return lax.ppermute(value, 'seq', [(s, s ^ 1) for s in range(count)])  19.8 us
    ppermute x9, starting transfers between devices, across(): return lax.ppermute(value, 'seq', [(s, s ^ 1) for s in range(count)])  12.4 us
    all_to_all x1, waiting for transfers between devices, by_heads(): lax.all_to_all(final.astype(bf16), 'seq', split_axis=0, concat_axis=0, ti...  8.32 us
    pallas_call x1, Pallas kernels, scan(): pl.pallas_call(scan_kernel, in_specs=[SMEM, SMEM] + [VMEM] * (len(sums) +...  7.44 us
    unnamed x36, local copies, waits for them, and re-layouts  7.32 us
    pallas_call x1, Pallas kernels, project(): pl.pallas_call(functools.partial(project_kernel, ranks), in_specs=[SMEM,...  6.27 us
  transfers between devices with their start and end apart: 37, of which 19 were waited for; matrix products, arithmetic and copies ran while one was open for 8% of the time, Pallas kernels for 3%

profile of v10, /device:TPU:0, one launch (start us, length us, event | category | flops | bytes accessed | tf_op | source)
XLA Modules:
  0.0 191.7 jit_solution(13097818717450554936)
XLA Ops:
  0.8 2.0 %constant_dynamic-slice_fusion.9 = bf16[512,512]{1,0:T(8,128)(2,1)} fusion(bf16[512,2048]{1,0:T(8,128)(2,1)} %refs_8_.1, s32[]{:T(128)S(6)} %select_n.123), kind=kLoop, calls=%fused_computation.64 | loop fusion | bytes 1048580 | tf_op jit(solution)/shard_map/dynamic_slice | solution.py:611
  3.7 3.1 %collective-permute-start = (bf16[32,1024]{1,0:T(8,128)(2,1)S(1)}, bf16[32,1024]{1,0:T(8,128)(2,1)S(1)}, u32[]{:S(2)}, u32[]{:S(2)}) collective-permute-start(bf16[32,1024]{1,0:T(8,128)(2,1)S(1)} %get-tuple-element.67), channel_id=1, source_target_pairs={{0,8},{4,12},{8,0},{12,4},{16,24},{20,28},{24,16},{28,20},{1,9},{5... | collective-permute-start | bytes 196616 | tf_op jit(solution)/shard_map/ppermute | solution.py:570
  6.8 2.6 %collective-permute-start.1 = (bf16[32,1024]{1,0:T(8,128)(2,1)S(1)}, bf16[32,1024]{1,0:T(8,128)(2,1)S(1)}, u32[]{:S(2)}, u32[]{:S(2)}) collective-permute-start(bf16[32,1024]{1,0:T(8,128)(2,1)S(1)} %get-tuple-element.66), channel_id=1, source_target_pairs={{0,16},{4,20},{8,24},{12,28},{16,0},{20,4},{24,8},{28,12},{1,17},{... | collective-permute-start | bytes 196616 | tf_op jit(solution)/shard_map/ppermute | solution.py:570
  9.4 1.7 collective-permute-start.10
  17.1 2.2 %constant_dynamic-slice_fusion.2 = (bf16[512,1,2,128]{3,2,1,0:T(2,128)(2,1)}, bf16[512,1,2,128]{3,2,1,0:T(2,128)(2,1)}) fusion(bf16[512,2,2,128]{3,2,1,0:T(2,128)(2,1)} %param.18, s32[]{:T(128)S(6)} %select_n.132, s32[]{:T(128)S(6)} %select_n.129), kind=kLoop, calls=%fused_computation.57 | loop fusion | bytes 1048584 | tf_op jit(solution)/shard_map/jit(dynamic_index_in_dim)/dynamic_slice | solution.py:566
  21.6 1.6 collective-permute-start.4
  23.2 5.3 %collective-permute-done.6.refs_4_ = bf16[4,32,1024]{2,1,0:T(8,128)(2,1)} collective-permute-done((bf16[4,32,1024]{2,1,0:T(8,128)(2,1)S(1)}, bf16[4,32,1024]{2,1,0:T(8,128)(2,1)}, u32[]{:S(2)}, u32[]{:S(2)}) %collective-permute-start.6) | collective-permute-done | bytes 262176 | tf_op jit(solution)/shard_map/ppermute | solution.py:573
  36.6 2.9 %collective-permute-done.11.refs_12_ = bf16[576,256]{1,0:T(8,128)(2,1)S(1)} collective-permute-done((bf16[576,256]{1,0:T(8,128)(2,1)}, bf16[576,256]{1,0:T(8,128)(2,1)S(1)}, u32[]{:S(2)}, u32[]{:S(2)}) %collective-permute-start.11) | collective-permute-done | bytes 294944 | tf_op jit(solution)/shard_map/ppermute | solution.py:573
  39.5 1.6 copy-done.5
  42.1 6.3 %project.1 = (bf16[1056,256]{1,0:T(8,128)(2,1)}, bf16[1056,256]{1,0:T(8,128)(2,1)}, bf16[1056,256]{1,0:T(8,128)(2,1)S(1)}, bf16[1056,256]{1,0:T(8,128)(2,1)S(1)}...) custom-call(s32[7]{0:T(128)S(1)} %stack.43.place_ref, ...), custom_call_target="tpu_custom_call" | custom-call | flops 2684354560 | bytes 4194304 | tf_op jit(solution)/shard_map/project/pallas_call | solution.py:301
  49.9 2.5 %collective-permute-start.20 = (bf16[1024,256]{1,0:T(8,128)(2,1)S(1)}, bf16[1024,256]{1,0:T(8,128)(2,1)S(1)}, u32[]{:S(2)}, u32[]{:S(2)}) collective-permute-start(bf16[1024,256]{1,0:T(8,128)(2,1)S(1)} %get-tuple-element.50), channel_id=1, source_target_pairs={{0,8},{4,12},{24,16},{28,20},{1,9},{5,13},{25,17},{29,21},{2,10},{... | collective-permute-start | bytes 1572872 | tf_op jit(solution)/shard_map/ppermute | solution.py:570
  52.4 2.1 %collective-permute-start.16 = (bf16[1056,256]{1,0:T(8,128)(2,1)}, bf16[1056,256]{1,0:T(8,128)(2,1)}, u32[]{:S(2)}, u32[]{:S(2)}) collective-permute-start(bf16[1056,256]{1,0:T(8,128)(2,1)} %get-tuple-element.44.refs_0_), channel_id=1, source_target_pairs={{0,8},{4,12},{24,16},{28,20},{1,9},{5,13},{25,17},{29,21},{2,10},{... | collective-permute-start | bytes 1622024 | tf_op jit(solution)/shard_map/ppermute | solution.py:570
  54.5 2.1 %collective-permute-start.13 = (bf16[1056,256]{1,0:T(8,128)(2,1)}, bf16[1056,256]{1,0:T(8,128)(2,1)}, u32[]{:S(2)}, u32[]{:S(2)}) collective-permute-start(bf16[1056,256]{1,0:T(8,128)(2,1)} %get-tuple-element.41.refs_0_), channel_id=1, source_target_pairs={{0,8},{4,12},{24,16},{28,20},{1,9},{5,13},{25,17},{29,21},{2,10},{... | collective-permute-start | bytes 1622024 | tf_op jit(solution)/shard_map/ppermute | solution.py:570
  56.6 3.8 %collective-permute-done.14.refs_1_ = bf16[1056,256]{1,0:T(8,128)(2,1)S(1)} collective-permute-done((bf16[1056,256]{1,0:T(8,128)(2,1)S(1)}, bf16[1056,256]{1,0:T(8,128)(2,1)S(1)}, u32[]{:S(2)}, u32[]{:S(2)}) %collective-permute-start.14) | collective-permute-done | bytes 540704 | tf_op jit(solution)/shard_map/ppermute | solution.py:573
  62.7 2.1 %collective-permute-done.20 = bf16[1024,256]{1,0:T(8,128)(2,1)S(1)} collective-permute-done((bf16[1024,256]{1,0:T(8,128)(2,1)S(1)}, bf16[1024,256]{1,0:T(8,128)(2,1)S(1)}, u32[]{:S(2)}, u32[]{:S(2)}) %collective-permute-start.20) | collective-permute-done | bytes 524320 | tf_op jit(solution)/shard_map/ppermute | solution.py:570
  66.2 10.2 %collective-permute-done.16.refs_1_ = bf16[1056,256]{1,0:T(8,128)(2,1)} collective-permute-done((bf16[1056,256]{1,0:T(8,128)(2,1)}, bf16[1056,256]{1,0:T(8,128)(2,1)}, u32[]{:S(2)}, u32[]{:S(2)}) %collective-permute-start.16) | collective-permute-done | bytes 540704 | tf_op jit(solution)/shard_map/ppermute | solution.py:570
  79.1 5.3 %collective-permute-done.13.refs_1_ = bf16[1056,256]{1,0:T(8,128)(2,1)} collective-permute-done((bf16[1056,256]{1,0:T(8,128)(2,1)}, bf16[1056,256]{1,0:T(8,128)(2,1)}, u32[]{:S(2)}, u32[]{:S(2)}) %collective-permute-start.13) | collective-permute-done | bytes 540704 | tf_op jit(solution)/shard_map/ppermute | solution.py:570
  84.4 4.4 %collective-permute-start.18 = (bf16[1056,256]{1,0:T(8,128)(2,1)}, bf16[1056,256]{1,0:T(8,128)(2,1)S(1)}, u32[]{:S(2)}, u32[]{:S(2)}) collective-permute-start(bf16[1056,256]{1,0:T(8,128)(2,1)} %onward.4), channel_id=1, source_target_pairs={{0,8},{4,12},{24,16},{28,20},{1,9},{5,13},{25,17},{29,21},{2,10},{... | collective-permute-start | bytes 1622024 | tf_op jit(solution)/shard_map/ppermute | solution.py:570
  92.5 4.7 %collective-permute-done.18.refs_3_ = bf16[1056,256]{1,0:T(8,128)(2,1)S(1)} collective-permute-done((bf16[1056,256]{1,0:T(8,128)(2,1)}, bf16[1056,256]{1,0:T(8,128)(2,1)S(1)}, u32[]{:S(2)}, u32[]{:S(2)}) %collective-permute-start.18) | collective-permute-done | bytes 540704 | tf_op jit(solution)/shard_map/ppermute | solution.py:570
  98.6 4.4 %collective-permute-done.22.refs_5_ = bf16[1024,256]{1,0:T(8,128)(2,1)S(1)} collective-permute-done((bf16[1024,256]{1,0:T(8,128)(2,1)S(1)}, bf16[1024,256]{1,0:T(8,128)(2,1)S(1)}, u32[]{:S(2)}, u32[]{:S(2)}) %collective-permute-start.22) | collective-permute-done | bytes 524320 | tf_op jit(solution)/shard_map/ppermute | solution.py:570
  104.0 7.4 %scan.1 = bf16[1040,256]{1,0:T(8,128)(2,1)S(1)} custom-call(s32[7]{0:T(128)S(1)} %stack.43.place_ref, f32[1]{0:T(128)} %bitcast.3.scale_ref, bf16[1056,256]{1,0:T(8,128)(2,1)S(1)} %onward.6.refs_0_, bf16[1056,256]{1,0:T(8,128)(2,1)S(1)} %collective-permute-done.17.refs_1_, bf16[1056,256]{1,0:T(8,128)(2,1)S(1)} %collective-permute-done.19.refs_2_, ...), custom_call_target="tpu_custom_call" | custom-call | flops 268435456 | bytes 2097152 | tf_op jit(solution)/shard_map/scan/pallas_call | solution.py:515
  112.9 1.8 collective-permute-start.26
  117.4 7.6 %collective-permute-done.26 = bf16[1040,256]{1,0:T(8,128)(2,1)S(1)} collective-permute-done((bf16[1040,256]{1,0:T(8,128)(2,1)S(1)}, bf16[1040,256]{1,0:T(8,128)(2,1)S(1)}, u32[]{:S(2)}, u32[]{:S(2)}) %collective-permute-start.26) | collective-permute-done | bytes 532512 | tf_op jit(solution)/shard_map/ppermute | solution.py:570
  127.5 6.4 %collective-permute-done.24 = bf16[1040,256]{1,0:T(8,128)(2,1)S(1)} collective-permute-done((bf16[1040,256]{1,0:T(8,128)(2,1)}, bf16[1040,256]{1,0:T(8,128)(2,1)S(1)}, u32[]{:S(2)}, u32[]{:S(2)}) %collective-permute-start.24) | collective-permute-done | bytes 532512 | tf_op jit(solution)/shard_map/ppermute | solution.py:570
  133.9 2.5 %collective-permute-start.30 = (bf16[1040,256]{1,0:T(8,128)(2,1)S(1)}, bf16[1040,256]{1,0:T(8,128)(2,1)S(1)}, u32[]{:S(2)}, u32[]{:S(2)}) collective-permute-start(bf16[1040,256]{1,0:T(8,128)(2,1)S(1)} %broadcast_select_fusion.1), channel_id=1, source_target_pairs={{0,4},{4,0},{8,12},{12,8},{16,20},{20,16},{24,28},{28,24},{1,5},{5... | collective-permute-start | bytes 1597448 | tf_op jit(solution)/shard_map/ppermute | solution.py:573
  139.1 10.1 %collective-permute-done.28 = bf16[1040,256]{1,0:T(8,128)(2,1)S(1)} collective-permute-done((bf16[1040,256]{1,0:T(8,128)(2,1)S(1)}, bf16[1040,256]{1,0:T(8,128)(2,1)S(1)}, u32[]{:S(2)}, u32[]{:S(2)}) %collective-permute-start.28) | collective-permute-done | bytes 532512 | tf_op jit(solution)/shard_map/ppermute | solution.py:570
  151.1 7.8 %collective-permute-done.31 = bf16[1040,256]{1,0:T(8,128)(2,1)S(1)} collective-permute-done((bf16[1040,256]{1,0:T(8,128)(2,1)S(1)}, bf16[1040,256]{1,0:T(8,128)(2,1)S(1)}, u32[]{:S(2)}, u32[]{:S(2)}) %collective-permute-start.31) | collective-permute-done | bytes 532512 | tf_op jit(solution)/shard_map/ppermute | solution.py:573
  159.3 3.6 %collective-permute-start.34 = (f32[8,128]{1,0:T(8,128)S(1)}, f32[8,128]{1,0:T(8,128)S(1)}, u32[]{:S(2)}, u32[]{:S(2)}) collective-permute-start(f32[8,128]{1,0:T(8,128)S(1)} %fusion.40), channel_id=1, source_target_pairs={{0,2},{1,3},{2,0},{3,1},{4,6},{5,7},{6,4},{7,5},{8,10},{9,11},{10,... | collective-permute-start | bytes 12296 | tf_op jit(solution)/shard_map/ppermute | solution.py:742
  165.5 2.1 %collective-permute-start.33 = (bf16[256,512]{1,0:T(8,128)(2,1)S(1)}, bf16[256,512]{1,0:T(8,128)(2,1)}, u32[]{:S(2)}, u32[]{:S(2)}) collective-permute-start(bf16[256,512]{1,0:T(8,128)(2,1)S(1)} %add_convert_fusion.2), channel_id=1, source_target_pairs={{0,2},{1,3},{2,0},{3,1},{4,6},{5,7},{6,4},{7,5},{8,10},{9,11},{10,... | collective-permute-start | bytes 786440 | tf_op jit(solution)/shard_map/ppermute | solution.py:744
  169.0 5.6 %collective-permute-done.33 = bf16[256,512]{1,0:T(8,128)(2,1)} collective-permute-done((bf16[256,512]{1,0:T(8,128)(2,1)S(1)}, bf16[256,512]{1,0:T(8,128)(2,1)}, u32[]{:S(2)}, u32[]{:S(2)}) %collective-permute-start.33) | collective-permute-done | bytes 262176 | tf_op jit(solution)/shard_map/ppermute | solution.py:744
  176.5 5.6 %all-to-all-start = ((bf16[8,32,512]{2,1,0:T(8,128)(2,1)}), bf16[8,32,512]{2,1,0:T(8,128)(2,1)S(1)}, u32[]{:S(2)}, u32[]{:S(2)}) async-start(bf16[8,32,512]{2,1,0:T(8,128)(2,1)} %multiply_convert_fusion.1), calls=%async_computation | async-start | bytes 524288 | tf_op jit(solution)/shard_map/all_to_all | solution.py:750
  182.7 8.3 %all-to-all-done = bf16[8,32,512]{2,1,0:T(8,128)(2,1)S(1)} async-done(((bf16[8,32,512]{2,1,0:T(8,128)(2,1)}), bf16[8,32,512]{2,1,0:T(8,128)(2,1)S(1)}, u32[]{:S(2)}, u32[]{:S(2)}) %all-to-all-start) | async-done | bytes 262176 | tf_op jit(solution)/shard_map/all_to_all | solution.py:750
  (139 shorter events, 50.1 us)
Async XLA Ops:
  3.7 10.4 %collective-permute-start = (bf16[32,1024]{1,0:T(8,128)(2,1)S(1)}, bf16[32,1024]{1,0:T(8,128)(2,1)S(1)}, u32[]{:S(2)}, u32[]{:S(2)}) collective-permute-start(bf16[32,1024]{1,0:T(8,128)(2,1)S(1)} %get-tuple-element.67), channel_id=1, source_target_pairs={{0,8},{4,12},{8,0},{12,4},{16,24},{20,28},{24,16},{28,20},{1,9},{5... | collective-permute-start | bytes 196616 | tf_op jit(solution)/shard_map/ppermute | solution.py:570
  6.8 7.4 %collective-permute-start.1 = (bf16[32,1024]{1,0:T(8,128)(2,1)S(1)}, bf16[32,1024]{1,0:T(8,128)(2,1)S(1)}, u32[]{:S(2)}, u32[]{:S(2)}) collective-permute-start(bf16[32,1024]{1,0:T(8,128)(2,1)S(1)} %get-tuple-element.66), channel_id=1, source_target_pairs={{0,16},{4,20},{8,24},{12,28},{16,0},{20,4},{24,8},{28,12},{1,17},{... | collective-permute-start | bytes 196616 | tf_op jit(solution)/shard_map/ppermute | solution.py:570
  9.4 6.1 %collective-permute-start.2 = (bf16[32,1024]{1,0:T(8,128)(2,1)S(1)}, bf16[32,1024]{1,0:T(8,128)(2,1)S(1)}, u32[]{:S(2)}, u32[]{:S(2)}) collective-permute-start(bf16[32,1024]{1,0:T(8,128)(2,1)S(1)} %get-tuple-element.65), channel_id=1, source_target_pairs={{0,24},{4,28},{8,16},{12,20},{16,8},{20,12},{24,0},{28,4},{1,25},{... | collective-permute-start | bytes 196616 | tf_op jit(solution)/shard_map/ppermute | solution.py:570
  9.4 22.3 %collective-permute-start.10 = (bf16[512,512]{1,0:T(8,128)(2,1)}, bf16[512,512]{1,0:T(8,128)(2,1)S(1)}, u32[]{:S(2)}, u32[]{:S(2)}) collective-permute-start(bf16[512,512]{1,0:T(8,128)(2,1)} %constant_dynamic-slice_fusion.9), channel_id=1, source_target_pairs={{0,4},{4,0},{8,12},{12,8},{16,20},{20,16},{24,28},{28,24},{1,5},{5... | collective-permute-start | bytes 1572872 | tf_op jit(solution)/shard_map/ppermute | solution.py:573
  15.5 12.9 %collective-permute-start.6 = (bf16[4,32,1024]{2,1,0:T(8,128)(2,1)S(1)}, bf16[4,32,1024]{2,1,0:T(8,128)(2,1)}, u32[]{:S(2)}, u32[]{:S(2)}) collective-permute-start(bf16[4,32,1024]{2,1,0:T(8,128)(2,1)S(1)} %pad_maximum_fusion.1.refs_0_), channel_id=1, source_target_pairs={{0,4},{4,0},{8,12},{12,8},{16,20},{20,16},{24,28},{28,24},{1,5},{5... | collective-permute-start | bytes 786440 | tf_op jit(solution)/shard_map/ppermute | solution.py:573
  21.6 12.9 %collective-permute-start.4 = (bf16[4,32,1024]{2,1,0:T(8,128)(2,1)S(1)}, bf16[4,32,1024]{2,1,0:T(8,128)(2,1)}, u32[]{:S(2)}, u32[]{:S(2)}) collective-permute-start(bf16[4,32,1024]{2,1,0:T(8,128)(2,1)S(1)} %pad_maximum_fusion.1.refs_0_), channel_id=1, source_target_pairs={{0,2},{1,3},{2,0},{3,1},{4,6},{5,7},{6,4},{7,5},{8,10},{9,11},{10,... | collective-permute-start | bytes 786440 | tf_op jit(solution)/shard_map/ppermute | solution.py:638
  28.5 6.9 %collective-permute-start.8 = (bf16[4,32,1024]{2,1,0:T(8,128)(2,1)}, bf16[4,32,1024]{2,1,0:T(8,128)(2,1)}, u32[]{:S(2)}, u32[]{:S(2)}) collective-permute-start(bf16[4,32,1024]{2,1,0:T(8,128)(2,1)} %collective-permute-done.6.refs_4_), channel_id=1, source_target_pairs={{0,2},{1,3},{2,0},{3,1},{4,6},{5,7},{6,4},{7,5},{8,10},{9,11},{10,... | collective-permute-start | bytes 786440 | tf_op jit(solution)/shard_map/ppermute | solution.py:638
  32.5 7.0 %collective-permute-start.11 = (bf16[576,256]{1,0:T(8,128)(2,1)}, bf16[576,256]{1,0:T(8,128)(2,1)S(1)}, u32[]{:S(2)}, u32[]{:S(2)}) collective-permute-start(bf16[576,256]{1,0:T(8,128)(2,1)} %pad_maximum_fusion), channel_id=1, source_target_pairs={{0,4},{4,0},{8,12},{12,8},{16,20},{20,16},{24,28},{28,24},{1,5},{5... | collective-permute-start | bytes 884744 | tf_op jit(solution)/shard_map/ppermute | solution.py:573
  48.4 12.0 %collective-permute-start.14 = (bf16[1056,256]{1,0:T(8,128)(2,1)S(1)}, bf16[1056,256]{1,0:T(8,128)(2,1)S(1)}, u32[]{:S(2)}, u32[]{:S(2)}) collective-permute-start(bf16[1056,256]{1,0:T(8,128)(2,1)S(1)} %get-tuple-element.43), channel_id=1, source_target_pairs={{0,4},{4,0},{8,12},{12,8},{16,20},{20,16},{24,28},{28,24},{1,5},{5... | collective-permute-start | bytes 1622024 | tf_op jit(solution)/shard_map/ppermute | solution.py:573
  49.9 14.8 %collective-permute-start.20 = (bf16[1024,256]{1,0:T(8,128)(2,1)S(1)}, bf16[1024,256]{1,0:T(8,128)(2,1)S(1)}, u32[]{:S(2)}, u32[]{:S(2)}) collective-permute-start(bf16[1024,256]{1,0:T(8,128)(2,1)S(1)} %get-tuple-element.50), channel_id=1, source_target_pairs={{0,8},{4,12},{24,16},{28,20},{1,9},{5,13},{25,17},{29,21},{2,10},{... | collective-permute-start | bytes 1572872 | tf_op jit(solution)/shard_map/ppermute | solution.py:570
  52.4 24.0 %collective-permute-start.16 = (bf16[1056,256]{1,0:T(8,128)(2,1)}, bf16[1056,256]{1,0:T(8,128)(2,1)}, u32[]{:S(2)}, u32[]{:S(2)}) collective-permute-start(bf16[1056,256]{1,0:T(8,128)(2,1)} %get-tuple-element.44.refs_0_), channel_id=1, source_target_pairs={{0,8},{4,12},{24,16},{28,20},{1,9},{5,13},{25,17},{29,21},{2,10},{... | collective-permute-start | bytes 1622024 | tf_op jit(solution)/shard_map/ppermute | solution.py:570
  54.5 29.9 %collective-permute-start.13 = (bf16[1056,256]{1,0:T(8,128)(2,1)}, bf16[1056,256]{1,0:T(8,128)(2,1)}, u32[]{:S(2)}, u32[]{:S(2)}) collective-permute-start(bf16[1056,256]{1,0:T(8,128)(2,1)} %get-tuple-element.41.refs_0_), channel_id=1, source_target_pairs={{0,8},{4,12},{24,16},{28,20},{1,9},{5,13},{25,17},{29,21},{2,10},{... | collective-permute-start | bytes 1622024 | tf_op jit(solution)/shard_map/ppermute | solution.py:570
  61.4 27.4 %collective-permute-start.15 = (bf16[1056,256]{1,0:T(8,128)(2,1)}, bf16[1056,256]{1,0:T(8,128)(2,1)}, u32[]{:S(2)}, u32[]{:S(2)}) collective-permute-start(bf16[1056,256]{1,0:T(8,128)(2,1)} %onward.4), channel_id=1, source_target_pairs={{8,0},{12,4},{16,24},{20,28},{9,1},{13,5},{17,25},{21,29},{10,2},{... | collective-permute-start | bytes 1622024 | tf_op jit(solution)/shard_map/ppermute | solution.py:570
  64.9 26.0 %collective-permute-start.21 = (bf16[1024,256]{1,0:T(8,128)(2,1)S(1)}, bf16[1024,256]{1,0:T(8,128)(2,1)S(1)}, u32[]{:S(2)}, u32[]{:S(2)}) collective-permute-start(bf16[1024,256]{1,0:T(8,128)(2,1)S(1)} %add_convert_fusion.1.refs_3_), channel_id=1, source_target_pairs={{8,16},{12,20},{16,8},{20,12},{9,17},{13,21},{17,9},{21,13},{10,18... | collective-permute-start | bytes 1572872 | tf_op jit(solution)/shard_map/ppermute | solution.py:570
  65.6 31.7 %collective-permute-start.12 = (bf16[1056,256]{1,0:T(8,128)(2,1)}, bf16[1056,256]{1,0:T(8,128)(2,1)S(1)}, u32[]{:S(2)}, u32[]{:S(2)}) collective-permute-start(bf16[1056,256]{1,0:T(8,128)(2,1)} %copy-done.7), channel_id=1, source_target_pairs={{0,4},{4,0},{8,12},{12,8},{16,20},{20,16},{24,28},{28,24},{1,5},{5... | collective-permute-start | bytes 1622024 | tf_op jit(solution)/shard_map/ppermute | solution.py:573
  77.8 19.5 %collective-permute-start.17 = (bf16[1056,256]{1,0:T(8,128)(2,1)S(1)}, bf16[1056,256]{1,0:T(8,128)(2,1)S(1)}, u32[]{:S(2)}, u32[]{:S(2)}) collective-permute-start(bf16[1056,256]{1,0:T(8,128)(2,1)S(1)} %onward.5), channel_id=1, source_target_pairs={{8,24},{12,28},{16,0},{20,4},{9,25},{13,29},{17,1},{21,5},{10,26},... | collective-permute-start | bytes 1622024 | tf_op jit(solution)/shard_map/ppermute | solution.py:570
  84.4 12.9 %collective-permute-start.18 = (bf16[1056,256]{1,0:T(8,128)(2,1)}, bf16[1056,256]{1,0:T(8,128)(2,1)S(1)}, u32[]{:S(2)}, u32[]{:S(2)}) collective-permute-start(bf16[1056,256]{1,0:T(8,128)(2,1)} %onward.4), channel_id=1, source_target_pairs={{0,8},{4,12},{24,16},{28,20},{1,9},{5,13},{25,17},{29,21},{2,10},{... | collective-permute-start | bytes 1622024 | tf_op jit(solution)/shard_map/ppermute | solution.py:570
  90.2 12.8 %collective-permute-start.19 = (bf16[1056,256]{1,0:T(8,128)(2,1)S(1)}, bf16[1056,256]{1,0:T(8,128)(2,1)S(1)}, u32[]{:S(2)}, u32[]{:S(2)}) collective-permute-start(bf16[1056,256]{1,0:T(8,128)(2,1)S(1)} %onward.7), channel_id=1, source_target_pairs={{8,16},{12,20},{16,8},{20,12},{9,17},{13,21},{17,9},{21,13},{10,18... | collective-permute-start | bytes 1622024 | tf_op jit(solution)/shard_map/ppermute | solution.py:570
  91.1 11.9 %collective-permute-start.22 = (bf16[1024,256]{1,0:T(8,128)(2,1)S(1)}, bf16[1024,256]{1,0:T(8,128)(2,1)S(1)}, u32[]{:S(2)}, u32[]{:S(2)}) collective-permute-start(bf16[1024,256]{1,0:T(8,128)(2,1)S(1)} %multiply_convert_fusion), channel_id=1, source_target_pairs={{8,0},{12,4},{16,24},{20,28},{9,1},{13,5},{17,25},{21,29},{10,2},{... | collective-permute-start | bytes 1572872 | tf_op jit(solution)/shard_map/ppermute | solution.py:570
  111.5 4.6 %collective-permute-start.23 = (bf16[1040,256]{1,0:T(8,128)(2,1)S(1)}, bf16[1040,256]{1,0:T(8,128)(2,1)}, u32[]{:S(2)}, u32[]{:S(2)}) collective-permute-start(bf16[1040,256]{1,0:T(8,128)(2,1)S(1)} %scan.1), channel_id=1, source_target_pairs={{8,16},{12,20},{16,8},{20,12},{9,17},{13,21},{17,9},{21,13},{10,18... | collective-permute-start | bytes 1597448 | tf_op jit(solution)/shard_map/ppermute | solution.py:570
  112.9 12.0 %collective-permute-start.26 = (bf16[1040,256]{1,0:T(8,128)(2,1)S(1)}, bf16[1040,256]{1,0:T(8,128)(2,1)S(1)}, u32[]{:S(2)}, u32[]{:S(2)}) collective-permute-start(bf16[1040,256]{1,0:T(8,128)(2,1)S(1)} %scan.1), channel_id=1, source_target_pairs={{0,8},{4,12},{8,0},{12,4},{16,24},{20,28},{24,16},{28,20},{1,9},{5... | collective-permute-start | bytes 1597448 | tf_op jit(solution)/shard_map/ppermute | solution.py:570
  114.8 19.1 %collective-permute-start.25 = (bf16[1040,256]{1,0:T(8,128)(2,1)S(1)}, bf16[1040,256]{1,0:T(8,128)(2,1)S(1)}, u32[]{:S(2)}, u32[]{:S(2)}) collective-permute-start(bf16[1040,256]{1,0:T(8,128)(2,1)S(1)} %scan.1), channel_id=1, source_target_pairs={{0,4},{4,0},{8,12},{12,8},{16,20},{20,16},{24,28},{28,24},{1,5},{5... | collective-permute-start | bytes 1597448 | tf_op jit(solution)/shard_map/ppermute | solution.py:573
  116.1 17.8 %collective-permute-start.24 = (bf16[1040,256]{1,0:T(8,128)(2,1)}, bf16[1040,256]{1,0:T(8,128)(2,1)S(1)}, u32[]{:S(2)}, u32[]{:S(2)}) collective-permute-start(bf16[1040,256]{1,0:T(8,128)(2,1)} %collective-permute-done.23), channel_id=1, source_target_pairs={{8,0},{12,4},{16,24},{20,28},{9,1},{13,5},{17,25},{21,29},{10,2},{... | collective-permute-start | bytes 1597448 | tf_op jit(solution)/shard_map/ppermute | solution.py:570
  124.9 11.9 %collective-permute-start.27 = (bf16[1040,256]{1,0:T(8,128)(2,1)S(1)}, bf16[1040,256]{1,0:T(8,128)(2,1)S(1)}, u32[]{:S(2)}, u32[]{:S(2)}) collective-permute-start(bf16[1040,256]{1,0:T(8,128)(2,1)S(1)} %collective-permute-done.26), channel_id=1, source_target_pairs={{8,16},{12,20},{16,8},{20,12},{9,17},{13,21},{17,9},{21,13},{10,18... | collective-permute-start | bytes 1597448 | tf_op jit(solution)/shard_map/ppermute | solution.py:570
  125.6 23.7 %collective-permute-start.29 = (bf16[1040,256]{1,0:T(8,128)(2,1)S(1)}, bf16[1040,256]{1,0:T(8,128)(2,1)S(1)}, u32[]{:S(2)}, u32[]{:S(2)}) collective-permute-start(bf16[1040,256]{1,0:T(8,128)(2,1)S(1)} %collective-permute-done.26), channel_id=1, source_target_pairs={{0,4},{4,0},{8,12},{12,8},{16,20},{20,16},{24,28},{28,24},{1,5},{5... | collective-permute-start | bytes 1597448 | tf_op jit(solution)/shard_map/ppermute | solution.py:573
  133.9 15.8 %collective-permute-start.30 = (bf16[1040,256]{1,0:T(8,128)(2,1)S(1)}, bf16[1040,256]{1,0:T(8,128)(2,1)S(1)}, u32[]{:S(2)}, u32[]{:S(2)}) collective-permute-start(bf16[1040,256]{1,0:T(8,128)(2,1)S(1)} %broadcast_select_fusion.1), channel_id=1, source_target_pairs={{0,4},{4,0},{8,12},{12,8},{16,20},{20,16},{24,28},{28,24},{1,5},{5... | collective-permute-start | bytes 1597448 | tf_op jit(solution)/shard_map/ppermute | solution.py:573
  136.9 12.3 %collective-permute-start.28 = (bf16[1040,256]{1,0:T(8,128)(2,1)S(1)}, bf16[1040,256]{1,0:T(8,128)(2,1)S(1)}, u32[]{:S(2)}, u32[]{:S(2)}) collective-permute-start(bf16[1040,256]{1,0:T(8,128)(2,1)S(1)} %collective-permute-done.27), channel_id=1, source_target_pairs={{8,0},{12,4},{16,24},{20,28},{9,1},{13,5},{17,25},{21,29},{10,2},{... | collective-permute-start | bytes 1597448 | tf_op jit(solution)/shard_map/ppermute | solution.py:570
  149.3 9.6 %collective-permute-start.31 = (bf16[1040,256]{1,0:T(8,128)(2,1)S(1)}, bf16[1040,256]{1,0:T(8,128)(2,1)S(1)}, u32[]{:S(2)}, u32[]{:S(2)}) collective-permute-start(bf16[1040,256]{1,0:T(8,128)(2,1)S(1)} %broadcast_select_fusion), channel_id=1, source_target_pairs={{0,4},{4,0},{8,12},{12,8},{16,20},{20,16},{24,28},{28,24},{1,5},{5... | collective-permute-start | bytes 1597448 | tf_op jit(solution)/shard_map/ppermute | solution.py:573
  159.2 5.3 %collective-permute-start.32 = (bf16[512,512]{1,0:T(8,128)(2,1)S(1)}, bf16[512,512]{1,0:T(8,128)(2,1)S(1)}, u32[]{:S(2)}, u32[]{:S(2)}) collective-permute-start(bf16[512,512]{1,0:T(8,128)(2,1)S(1)} %add_convert_fusion), channel_id=1, source_target_pairs={{0,1},{1,0},{2,3},{3,2},{4,5},{5,4},{6,7},{7,6},{8,9},{9,8},{10,11... | collective-permute-start | bytes 1572872 | tf_op jit(solution)/shard_map/ppermute | solution.py:732
  159.3 5.2 %collective-permute-start.34 = (f32[8,128]{1,0:T(8,128)S(1)}, f32[8,128]{1,0:T(8,128)S(1)}, u32[]{:S(2)}, u32[]{:S(2)}) collective-permute-start(f32[8,128]{1,0:T(8,128)S(1)} %fusion.40), channel_id=1, source_target_pairs={{0,2},{1,3},{2,0},{3,1},{4,6},{5,7},{6,4},{7,5},{8,10},{9,11},{10,... | collective-permute-start | bytes 12296 | tf_op jit(solution)/shard_map/ppermute | solution.py:742
  165.5 9.1 %collective-permute-start.33 = (bf16[256,512]{1,0:T(8,128)(2,1)S(1)}, bf16[256,512]{1,0:T(8,128)(2,1)}, u32[]{:S(2)}, u32[]{:S(2)}) collective-permute-start(bf16[256,512]{1,0:T(8,128)(2,1)S(1)} %add_convert_fusion.2), channel_id=1, source_target_pairs={{0,2},{1,3},{2,0},{3,1},{4,6},{5,7},{6,4},{7,5},{8,10},{9,11},{10,... | collective-permute-start | bytes 786440 | tf_op jit(solution)/shard_map/ppermute | solution.py:744
  176.5 14.5 %all-to-all-start = ((bf16[8,32,512]{2,1,0:T(8,128)(2,1)}), bf16[8,32,512]{2,1,0:T(8,128)(2,1)S(1)}, u32[]{:S(2)}, u32[]{:S(2)}) async-start(bf16[8,32,512]{2,1,0:T(8,128)(2,1)} %multiply_convert_fusion.1), calls=%async_computation | async-start | bytes 524288 | tf_op jit(solution)/shard_map/all_to_all | solution.py:750
  (20 other events, 320.7 us)

commit v11 on v9

--- a/solution.py
+++ b/solution.py
@@ -614,8 +614,7 @@
     dt_rows = w_dt.T
     dt_cut = [dt_rows[:, at : at + 2 * STATE] for at in range(0, depth, 2 * STATE)]
     maps_sent = pick(w_bc, 1, 1 - side).reshape(depth, 2 * STATE)
-    x_far, rest_sent = tie((x_far, jnp.concatenate([maps_sent, *dt_cut], axis=0)))
-    rest_other = across(rest_sent)
+    rest_other = across(jnp.concatenate([maps_sent, *dt_cut], axis=0))
     bc_own = pick(w_bc, 1, side).reshape(depth, 2 * STATE)
 
     def line_columns(m):

time: 192 us -> 204 us (1.062)
  waiting for transfers between devices: 88.8 us -> 108 us
  local copies, waits for them, and re-layouts: 16.8 us -> 11.8 us
    ppermute x9, waiting for transfers between devices: 19.8 us -> 31.3 us  [across(): return lax.ppermute(value, 'seq', [(s, s ^ 1) for s in range(count)])]
    ppermute x6, waiting for transfers between devices: 1.33 us -> 5.85 us  [by_heads(): ours.append(lax.ppermute(ours[j - bit], 'tensor', pairs))]
    ppermute x17, waiting for transfers between devices: 52.1 us -> 55.8 us  [along(): return lax.ppermute(value, 'seq', moves)]
    unnamed x36 -> x38, local copies, waits for them, and re-layouts: 7.33 us -> 3.73 us
  transfers between devices with their start and end apart: 37 -> 37, of which waited for: 19 -> 16; matrix products, arithmetic and copies ran while one was open for 8% -> 6% of each run, Pallas kernels for 3% -> 2%
where the time goes in v11:
time: 204 us; the launch traced here: 203 us
  waiting for transfers between devices  108 us (53%)
  starting transfers between devices  52.8 us (26%)
  Pallas kernels  18.9 us (9%)
  local copies, waits for them, and re-layouts  11.8 us (6%)
  other arithmetic  6.15 us (3%)
  matrix products  3.68 us (2%)
    ppermute x17, waiting for transfers between devices, along(): return lax.ppermute(value, 'seq', moves)  55.8 us
    ppermute x9, waiting for transfers between devices, across(): return lax.ppermute(value, 'seq', [(s, s ^ 1) for s in range(count)])  31.3 us
    ppermute x17, starting transfers between devices, along(): return lax.ppermute(value, 'seq', moves)  28.8 us
    ppermute x9, starting transfers between devices, across(): return lax.ppermute(value, 'seq', [(s, s ^ 1) for s in range(count)])  13.1 us
    all_to_all x1, waiting for transfers between devices, by_heads(): lax.all_to_all(final.astype(bf16), 'seq', split_axis=0, concat_axis=0, ti...  7.62 us
    pallas_call x1, Pallas kernels, scan(): pl.pallas_call(scan_kernel, in_specs=[SMEM, SMEM] + [VMEM] * (len(sums) +...  7.45 us
    pallas_call x1, Pallas kernels, project(): pl.pallas_call(functools.partial(project_kernel, ranks), in_specs=[SMEM,...  6.44 us
    ppermute x1, waiting for transfers between devices, by_heads(): received = lax.ppermute(sent.astype(bf16), 'tensor', pairs)  6.39 us
  transfers between devices with their start and end apart: 37, of which 16 were waited for; matrix products, arithmetic and copies ran while one was open for 6% of the time, Pallas kernels for 2%

profile of v11, /device:TPU:0, one launch (start us, length us, event | category | flops | bytes accessed | tf_op | source)
XLA Modules:
  0.0 203.3 jit_solution(5818435774070666801)
XLA Ops:
  0.8 2.0 constant_dynamic-slice_fusion.9
  3.8 3.1 %collective-permute-start = (bf16[32,1024]{1,0:T(8,128)(2,1)S(1)}, bf16[32,1024]{1,0:T(8,128)(2,1)S(1)}, u32[]{:S(2)}, u32[]{:S(2)}) collective-permute-start(bf16[32,1024]{1,0:T(8,128)(2,1)S(1)} %get-tuple-element.61), channel_id=1, source_target_pairs={{0,8},{4,12},{8,0},{12,4},{16,24},{20,28},{24,16},{28,20},{1,9},{5... | collective-permute-start | bytes 196616 | tf_op jit(solution)/shard_map/ppermute | solution.py:570
  6.8 2.6 %collective-permute-start.1 = (bf16[32,1024]{1,0:T(8,128)(2,1)S(1)}, bf16[32,1024]{1,0:T(8,128)(2,1)S(1)}, u32[]{:S(2)}, u32[]{:S(2)}) collective-permute-start(bf16[32,1024]{1,0:T(8,128)(2,1)S(1)} %get-tuple-element.60), channel_id=1, source_target_pairs={{0,16},{4,20},{8,24},{12,28},{16,0},{20,4},{24,8},{28,12},{1,17},{... | collective-permute-start | bytes 196616 | tf_op jit(solution)/shard_map/ppermute | solution.py:570
  9.4 2.1 %constant_dynamic-slice_fusion.2 = (bf16[512,1,2,128]{3,2,1,0:T(2,128)(2,1)S(1)}, bf16[512,1,2,128]{3,2,1,0:T(2,128)(2,1)}) fusion(bf16[512,2,2,128]{3,2,1,0:T(2,128)(2,1)} %param.18, s32[]{:T(128)S(6)} %select_n.132, s32[]{:T(128)S(6)} %select_n.129), kind=kLoop, calls=%fused_computation.57 | loop fusion | bytes 1048584 | tf_op jit(solution)/shard_map/jit(dynamic_index_in_dim)/dynamic_slice | solution.py:566
  12.3 1.7 collective-permute-start.11
  15.6 1.6 collective-permute-start.6
  19.5 1.6 collective-permute-start.4
  21.0 16.7 %collective-permute-done.6.refs_4_ = bf16[4,32,1024]{2,1,0:T(8,128)(2,1)} collective-permute-done((bf16[4,32,1024]{2,1,0:T(8,128)(2,1)S(1)}, bf16[4,32,1024]{2,1,0:T(8,128)(2,1)}, u32[]{:S(2)}, u32[]{:S(2)}) %collective-permute-start.6) | collective-permute-done | bytes 262176 | tf_op jit(solution)/shard_map/ppermute | solution.py:573
  39.8 4.8 %collective-permute-done.8.refs_6_ = bf16[4,32,1024]{2,1,0:T(8,128)(2,1)} collective-permute-done((bf16[4,32,1024]{2,1,0:T(8,128)(2,1)}, bf16[4,32,1024]{2,1,0:T(8,128)(2,1)}, u32[]{:S(2)}, u32[]{:S(2)}) %collective-permute-start.8) | collective-permute-done | bytes 262176 | tf_op jit(solution)/shard_map/ppermute | solution.py:637
  46.4 1.6 copy-done.5
  48.0 6.4 %project.1 = (bf16[1056,256]{1,0:T(8,128)(2,1)}, bf16[1056,256]{1,0:T(8,128)(2,1)}, bf16[1056,256]{1,0:T(8,128)(2,1)S(1)}, bf16[1056,256]{1,0:T(8,128)(2,1)S(1)}...) custom-call(s32[7]{0:T(128)S(1)} %stack.43.place_ref, ...), custom_call_target="tpu_custom_call" | custom-call | flops 2684354560 | bytes 4194304 | tf_op jit(solution)/shard_map/project/pallas_call | solution.py:301
  55.8 2.5 %collective-permute-start.20 = (bf16[1024,256]{1,0:T(8,128)(2,1)S(1)}, bf16[1024,256]{1,0:T(8,128)(2,1)S(1)}, u32[]{:S(2)}, u32[]{:S(2)}) collective-permute-start(bf16[1024,256]{1,0:T(8,128)(2,1)S(1)} %get-tuple-element.45), channel_id=1, source_target_pairs={{0,8},{4,12},{24,16},{28,20},{1,9},{5,13},{25,17},{29,21},{2,10},{... | collective-permute-start | bytes 1572872 | tf_op jit(solution)/shard_map/ppermute | solution.py:570
  58.4 2.1 %collective-permute-start.16 = (bf16[1056,256]{1,0:T(8,128)(2,1)}, bf16[1056,256]{1,0:T(8,128)(2,1)}, u32[]{:S(2)}, u32[]{:S(2)}) collective-permute-start(bf16[1056,256]{1,0:T(8,128)(2,1)} %get-tuple-element.39.refs_0_), channel_id=1, source_target_pairs={{0,8},{4,12},{24,16},{28,20},{1,9},{5,13},{25,17},{29,21},{2,10},{... | collective-permute-start | bytes 1622024 | tf_op jit(solution)/shard_map/ppermute | solution.py:570
  60.5 2.1 %collective-permute-start.13 = (bf16[1056,256]{1,0:T(8,128)(2,1)}, bf16[1056,256]{1,0:T(8,128)(2,1)}, u32[]{:S(2)}, u32[]{:S(2)}) collective-permute-start(bf16[1056,256]{1,0:T(8,128)(2,1)} %get-tuple-element.36.refs_0_), channel_id=1, source_target_pairs={{0,8},{4,12},{24,16},{28,20},{1,9},{5,13},{25,17},{29,21},{2,10},{... | collective-permute-start | bytes 1622024 | tf_op jit(solution)/shard_map/ppermute | solution.py:570
  62.6 6.3 %collective-permute-done.14.refs_1_ = bf16[1056,256]{1,0:T(8,128)(2,1)S(1)} collective-permute-done((bf16[1056,256]{1,0:T(8,128)(2,1)S(1)}, bf16[1056,256]{1,0:T(8,128)(2,1)S(1)}, u32[]{:S(2)}, u32[]{:S(2)}) %collective-permute-start.14) | collective-permute-done | bytes 540704 | tf_op jit(solution)/shard_map/ppermute | solution.py:573
  73.3 9.0 %collective-permute-done.16.refs_1_ = bf16[1056,256]{1,0:T(8,128)(2,1)} collective-permute-done((bf16[1056,256]{1,0:T(8,128)(2,1)}, bf16[1056,256]{1,0:T(8,128)(2,1)}, u32[]{:S(2)}, u32[]{:S(2)}) %collective-permute-start.16) | collective-permute-done | bytes 540704 | tf_op jit(solution)/shard_map/ppermute | solution.py:570
  85.0 7.8 %collective-permute-done.13.refs_1_ = bf16[1056,256]{1,0:T(8,128)(2,1)} collective-permute-done((bf16[1056,256]{1,0:T(8,128)(2,1)}, bf16[1056,256]{1,0:T(8,128)(2,1)}, u32[]{:S(2)}, u32[]{:S(2)}) %collective-permute-start.13) | collective-permute-done | bytes 540704 | tf_op jit(solution)/shard_map/ppermute | solution.py:570
  92.8 4.4 %collective-permute-start.18 = (bf16[1056,256]{1,0:T(8,128)(2,1)}, bf16[1056,256]{1,0:T(8,128)(2,1)S(1)}, u32[]{:S(2)}, u32[]{:S(2)}) collective-permute-start(bf16[1056,256]{1,0:T(8,128)(2,1)} %onward.4), channel_id=1, source_target_pairs={{0,8},{4,12},{24,16},{28,20},{1,9},{5,13},{25,17},{29,21},{2,10},{... | collective-permute-start | bytes 1622024 | tf_op jit(solution)/shard_map/ppermute | solution.py:570
  101.0 7.2 %collective-permute-done.18.refs_3_ = bf16[1056,256]{1,0:T(8,128)(2,1)S(1)} collective-permute-done((bf16[1056,256]{1,0:T(8,128)(2,1)}, bf16[1056,256]{1,0:T(8,128)(2,1)S(1)}, u32[]{:S(2)}, u32[]{:S(2)}) %collective-permute-start.18) | collective-permute-done | bytes 540704 | tf_op jit(solution)/shard_map/ppermute | solution.py:570
  109.5 4.4 %collective-permute-done.22.refs_5_ = bf16[1024,256]{1,0:T(8,128)(2,1)S(1)} collective-permute-done((bf16[1024,256]{1,0:T(8,128)(2,1)S(1)}, bf16[1024,256]{1,0:T(8,128)(2,1)S(1)}, u32[]{:S(2)}, u32[]{:S(2)}) %collective-permute-start.22) | collective-permute-done | bytes 524320 | tf_op jit(solution)/shard_map/ppermute | solution.py:570
  115.0 7.5 %scan.1 = bf16[1040,256]{1,0:T(8,128)(2,1)S(1)} custom-call(s32[7]{0:T(128)S(1)} %stack.43.place_ref, f32[1]{0:T(128)} %bitcast.3.scale_ref, bf16[1056,256]{1,0:T(8,128)(2,1)S(1)} %onward.6.refs_0_, bf16[1056,256]{1,0:T(8,128)(2,1)S(1)} %collective-permute-done.17.refs_1_, bf16[1056,256]{1,0:T(8,128)(2,1)S(1)} %collective-permute-done.19.refs_2_, ...), custom_call_target="tpu_custom_call" | custom-call | flops 268435456 | bytes 2097152 | tf_op jit(solution)/shard_map/scan/pallas_call | solution.py:515
  123.9 1.8 collective-permute-start.26
  128.3 7.6 %collective-permute-done.26 = bf16[1040,256]{1,0:T(8,128)(2,1)S(1)} collective-permute-done((bf16[1040,256]{1,0:T(8,128)(2,1)S(1)}, bf16[1040,256]{1,0:T(8,128)(2,1)S(1)}, u32[]{:S(2)}, u32[]{:S(2)}) %collective-permute-start.26) | collective-permute-done | bytes 532512 | tf_op jit(solution)/shard_map/ppermute | solution.py:570
  136.6 2.1 %collective-permute-start.29 = (bf16[1040,256]{1,0:T(8,128)(2,1)S(1)}, bf16[1040,256]{1,0:T(8,128)(2,1)S(1)}, u32[]{:S(2)}, u32[]{:S(2)}) collective-permute-start(bf16[1040,256]{1,0:T(8,128)(2,1)S(1)} %collective-permute-done.26), channel_id=1, source_target_pairs={{0,4},{4,0},{8,12},{12,8},{16,20},{20,16},{24,28},{28,24},{1,5},{5... | collective-permute-start | bytes 1597448 | tf_op jit(solution)/shard_map/ppermute | solution.py:573
  139.2 8.1 %collective-permute-done.24 = bf16[1040,256]{1,0:T(8,128)(2,1)S(1)} collective-permute-done((bf16[1040,256]{1,0:T(8,128)(2,1)}, bf16[1040,256]{1,0:T(8,128)(2,1)S(1)}, u32[]{:S(2)}, u32[]{:S(2)}) %collective-permute-start.24) | collective-permute-done | bytes 532512 | tf_op jit(solution)/shard_map/ppermute | solution.py:570
  147.4 2.8 %collective-permute-start.30 = (bf16[1040,256]{1,0:T(8,128)(2,1)S(1)}, bf16[1040,256]{1,0:T(8,128)(2,1)S(1)}, u32[]{:S(2)}, u32[]{:S(2)}) collective-permute-start(bf16[1040,256]{1,0:T(8,128)(2,1)S(1)} %broadcast_select_fusion.1), channel_id=1, source_target_pairs={{0,4},{4,0},{8,12},{12,8},{16,20},{20,16},{24,28},{28,24},{1,5},{5... | collective-permute-start | bytes 1597448 | tf_op jit(solution)/shard_map/ppermute | solution.py:573
  152.9 10.8 %collective-permute-done.28 = bf16[1040,256]{1,0:T(8,128)(2,1)S(1)} collective-permute-done((bf16[1040,256]{1,0:T(8,128)(2,1)S(1)}, bf16[1040,256]{1,0:T(8,128)(2,1)S(1)}, u32[]{:S(2)}, u32[]{:S(2)}) %collective-permute-start.28) | collective-permute-done | bytes 532512 | tf_op jit(solution)/shard_map/ppermute | solution.py:570
  165.7 8.4 %collective-permute-done.31 = bf16[1040,256]{1,0:T(8,128)(2,1)S(1)} collective-permute-done((bf16[1040,256]{1,0:T(8,128)(2,1)S(1)}, bf16[1040,256]{1,0:T(8,128)(2,1)S(1)}, u32[]{:S(2)}, u32[]{:S(2)}) %collective-permute-start.31) | collective-permute-done | bytes 532512 | tf_op jit(solution)/shard_map/ppermute | solution.py:573
  177.9 1.7 add_convert_fusion.2
  181.5 6.4 %collective-permute-done.33 = bf16[256,512]{1,0:T(8,128)(2,1)S(1)} collective-permute-done((bf16[256,512]{1,0:T(8,128)(2,1)}, bf16[256,512]{1,0:T(8,128)(2,1)S(1)}, u32[]{:S(2)}, u32[]{:S(2)}) %collective-permute-start.33) | collective-permute-done | bytes 262176 | tf_op jit(solution)/shard_map/ppermute | solution.py:741
  189.8 4.6 %all-to-all-start = ((bf16[8,32,512]{2,1,0:T(8,128)(2,1)}), bf16[8,32,512]{2,1,0:T(8,128)(2,1)S(1)}, u32[]{:S(2)}, u32[]{:S(2)}) async-start(bf16[8,32,512]{2,1,0:T(8,128)(2,1)} %multiply_convert_fusion.1), calls=%async_computation | async-start | bytes 524288 | tf_op jit(solution)/shard_map/all_to_all | solution.py:747
  194.9 7.6 %all-to-all-done = bf16[8,32,512]{2,1,0:T(8,128)(2,1)S(1)} async-done(((bf16[8,32,512]{2,1,0:T(8,128)(2,1)}), bf16[8,32,512]{2,1,0:T(8,128)(2,1)S(1)}, u32[]{:S(2)}, u32[]{:S(2)}) %all-to-all-start) | async-done | bytes 262176 | tf_op jit(solution)/shard_map/all_to_all | solution.py:747
  (141 shorter events, 41.9 us)
Async XLA Ops:
  3.8 11.0 %collective-permute-start = (bf16[32,1024]{1,0:T(8,128)(2,1)S(1)}, bf16[32,1024]{1,0:T(8,128)(2,1)S(1)}, u32[]{:S(2)}, u32[]{:S(2)}) collective-permute-start(bf16[32,1024]{1,0:T(8,128)(2,1)S(1)} %get-tuple-element.61), channel_id=1, source_target_pairs={{0,8},{4,12},{8,0},{12,4},{16,24},{20,28},{24,16},{28,20},{1,9},{5... | collective-permute-start | bytes 196616 | tf_op jit(solution)/shard_map/ppermute | solution.py:570
  6.8 7.9 %collective-permute-start.1 = (bf16[32,1024]{1,0:T(8,128)(2,1)S(1)}, bf16[32,1024]{1,0:T(8,128)(2,1)S(1)}, u32[]{:S(2)}, u32[]{:S(2)}) collective-permute-start(bf16[32,1024]{1,0:T(8,128)(2,1)S(1)} %get-tuple-element.60), channel_id=1, source_target_pairs={{0,16},{4,20},{8,24},{12,28},{16,0},{20,4},{24,8},{28,12},{1,17},{... | collective-permute-start | bytes 196616 | tf_op jit(solution)/shard_map/ppermute | solution.py:570
  9.4 6.1 %collective-permute-start.2 = (bf16[32,1024]{1,0:T(8,128)(2,1)S(1)}, bf16[32,1024]{1,0:T(8,128)(2,1)S(1)}, u32[]{:S(2)}, u32[]{:S(2)}) collective-permute-start(bf16[32,1024]{1,0:T(8,128)(2,1)S(1)} %get-tuple-element.59), channel_id=1, source_target_pairs={{0,24},{4,28},{8,16},{12,20},{16,8},{20,12},{24,0},{28,4},{1,25},{... | collective-permute-start | bytes 196616 | tf_op jit(solution)/shard_map/ppermute | solution.py:570
  12.3 26.9 %collective-permute-start.11 = (bf16[576,256]{1,0:T(8,128)(2,1)}, bf16[576,256]{1,0:T(8,128)(2,1)S(1)}, u32[]{:S(2)}, u32[]{:S(2)}) collective-permute-start(bf16[576,256]{1,0:T(8,128)(2,1)} %pad_maximum_fusion), channel_id=1, source_target_pairs={{0,4},{4,0},{8,12},{12,8},{16,20},{20,16},{24,28},{28,24},{1,5},{5... | collective-permute-start | bytes 884744 | tf_op jit(solution)/shard_map/ppermute | solution.py:573
  14.0 31.3 %collective-permute-start.10 = (bf16[512,512]{1,0:T(8,128)(2,1)}, bf16[512,512]{1,0:T(8,128)(2,1)}, u32[]{:S(2)}, u32[]{:S(2)}) collective-permute-start(bf16[512,512]{1,0:T(8,128)(2,1)} %constant_dynamic-slice_fusion.9), channel_id=1, source_target_pairs={{0,4},{4,0},{8,12},{12,8},{16,20},{20,16},{24,28},{28,24},{1,5},{5... | collective-permute-start | bytes 1572872 | tf_op jit(solution)/shard_map/ppermute | solution.py:573
  15.6 22.1 %collective-permute-start.6 = (bf16[4,32,1024]{2,1,0:T(8,128)(2,1)S(1)}, bf16[4,32,1024]{2,1,0:T(8,128)(2,1)}, u32[]{:S(2)}, u32[]{:S(2)}) collective-permute-start(bf16[4,32,1024]{2,1,0:T(8,128)(2,1)S(1)} %pad_maximum_fusion.1.refs_0_), channel_id=1, source_target_pairs={{0,4},{4,0},{8,12},{12,8},{16,20},{20,16},{24,28},{28,24},{1,5},{5... | collective-permute-start | bytes 786440 | tf_op jit(solution)/shard_map/ppermute | solution.py:573
  19.5 20.3 %collective-permute-start.4 = (bf16[4,32,1024]{2,1,0:T(8,128)(2,1)S(1)}, bf16[4,32,1024]{2,1,0:T(8,128)(2,1)}, u32[]{:S(2)}, u32[]{:S(2)}) collective-permute-start(bf16[4,32,1024]{2,1,0:T(8,128)(2,1)S(1)} %pad_maximum_fusion.1.refs_0_), channel_id=1, source_target_pairs={{0,2},{1,3},{2,0},{3,1},{4,6},{5,7},{6,4},{7,5},{8,10},{9,11},{10,... | collective-permute-start | bytes 786440 | tf_op jit(solution)/shard_map/ppermute | solution.py:637
  37.7 6.9 %collective-permute-start.8 = (bf16[4,32,1024]{2,1,0:T(8,128)(2,1)}, bf16[4,32,1024]{2,1,0:T(8,128)(2,1)}, u32[]{:S(2)}, u32[]{:S(2)}) collective-permute-start(bf16[4,32,1024]{2,1,0:T(8,128)(2,1)} %collective-permute-done.6.refs_4_), channel_id=1, source_target_pairs={{0,2},{1,3},{2,0},{3,1},{4,6},{5,7},{6,4},{7,5},{8,10},{9,11},{10,... | collective-permute-start | bytes 786440 | tf_op jit(solution)/shard_map/ppermute | solution.py:637
  39.2 6.1 %collective-permute-start.3 = (bf16[4,32,1024]{2,1,0:T(8,128)(2,1)S(1)}, bf16[4,32,1024]{2,1,0:T(8,128)(2,1)}, u32[]{:S(2)}, u32[]{:S(2)}) collective-permute-start(bf16[4,32,1024]{2,1,0:T(8,128)(2,1)S(1)} %pad_maximum_fusion.1.refs_0_), channel_id=1, source_target_pairs={{0,1},{1,0},{2,3},{3,2},{4,5},{5,4},{6,7},{7,6},{8,9},{9,8},{10,11... | collective-permute-start | bytes 786440 | tf_op jit(solution)/shard_map/ppermute | solution.py:637
  39.2 6.1 %collective-permute-start.7 = (bf16[4,32,1024]{2,1,0:T(8,128)(2,1)}, bf16[4,32,1024]{2,1,0:T(8,128)(2,1)}, u32[]{:S(2)}, u32[]{:S(2)}) collective-permute-start(bf16[4,32,1024]{2,1,0:T(8,128)(2,1)} %collective-permute-done.6.refs_4_), channel_id=1, source_target_pairs={{0,1},{1,0},{2,3},{3,2},{4,5},{5,4},{6,7},{7,6},{8,9},{9,8},{10,11... | collective-permute-start | bytes 786440 | tf_op jit(solution)/shard_map/ppermute | solution.py:637
  39.7 5.6 %collective-permute-start.5 = (bf16[4,32,1024]{2,1,0:T(8,128)(2,1)}, bf16[4,32,1024]{2,1,0:T(8,128)(2,1)}, u32[]{:S(2)}, u32[]{:S(2)}) collective-permute-start(bf16[4,32,1024]{2,1,0:T(8,128)(2,1)} %collective-permute-done.4.refs_2_), channel_id=1, source_target_pairs={{0,1},{1,0},{2,3},{3,2},{4,5},{5,4},{6,7},{7,6},{8,9},{9,8},{10,11... | collective-permute-start | bytes 786440 | tf_op jit(solution)/shard_map/ppermute | solution.py:637
  54.5 14.4 %collective-permute-start.14 = (bf16[1056,256]{1,0:T(8,128)(2,1)S(1)}, bf16[1056,256]{1,0:T(8,128)(2,1)S(1)}, u32[]{:S(2)}, u32[]{:S(2)}) collective-permute-start(bf16[1056,256]{1,0:T(8,128)(2,1)S(1)} %get-tuple-element.38), channel_id=1, source_target_pairs={{0,4},{4,0},{8,12},{12,8},{16,20},{20,16},{24,28},{28,24},{1,5},{5... | collective-permute-start | bytes 1622024 | tf_op jit(solution)/shard_map/ppermute | solution.py:573
  55.8 15.3 %collective-permute-start.20 = (bf16[1024,256]{1,0:T(8,128)(2,1)S(1)}, bf16[1024,256]{1,0:T(8,128)(2,1)S(1)}, u32[]{:S(2)}, u32[]{:S(2)}) collective-permute-start(bf16[1024,256]{1,0:T(8,128)(2,1)S(1)} %get-tuple-element.45), channel_id=1, source_target_pairs={{0,8},{4,12},{24,16},{28,20},{1,9},{5,13},{25,17},{29,21},{2,10},{... | collective-permute-start | bytes 1572872 | tf_op jit(solution)/shard_map/ppermute | solution.py:570
  58.4 24.0 %collective-permute-start.16 = (bf16[1056,256]{1,0:T(8,128)(2,1)}, bf16[1056,256]{1,0:T(8,128)(2,1)}, u32[]{:S(2)}, u32[]{:S(2)}) collective-permute-start(bf16[1056,256]{1,0:T(8,128)(2,1)} %get-tuple-element.39.refs_0_), channel_id=1, source_target_pairs={{0,8},{4,12},{24,16},{28,20},{1,9},{5,13},{25,17},{29,21},{2,10},{... | collective-permute-start | bytes 1622024 | tf_op jit(solution)/shard_map/ppermute | solution.py:570
  60.5 32.3 %collective-permute-start.13 = (bf16[1056,256]{1,0:T(8,128)(2,1)}, bf16[1056,256]{1,0:T(8,128)(2,1)}, u32[]{:S(2)}, u32[]{:S(2)}) collective-permute-start(bf16[1056,256]{1,0:T(8,128)(2,1)} %get-tuple-element.36.refs_0_), channel_id=1, source_target_pairs={{0,8},{4,12},{24,16},{28,20},{1,9},{5,13},{25,17},{29,21},{2,10},{... | collective-permute-start | bytes 1622024 | tf_op jit(solution)/shard_map/ppermute | solution.py:570
  69.8 27.4 %collective-permute-start.15 = (bf16[1056,256]{1,0:T(8,128)(2,1)}, bf16[1056,256]{1,0:T(8,128)(2,1)}, u32[]{:S(2)}, u32[]{:S(2)}) collective-permute-start(bf16[1056,256]{1,0:T(8,128)(2,1)} %onward.4), channel_id=1, source_target_pairs={{8,0},{12,4},{16,24},{20,28},{9,1},{13,5},{17,25},{21,29},{10,2},{... | collective-permute-start | bytes 1622024 | tf_op jit(solution)/shard_map/ppermute | solution.py:570
  71.3 28.0 %collective-permute-start.21 = (bf16[1024,256]{1,0:T(8,128)(2,1)S(1)}, bf16[1024,256]{1,0:T(8,128)(2,1)S(1)}, u32[]{:S(2)}, u32[]{:S(2)}) collective-permute-start(bf16[1024,256]{1,0:T(8,128)(2,1)S(1)} %add_convert_fusion.1.refs_3_), channel_id=1, source_target_pairs={{8,16},{12,20},{16,8},{20,12},{9,17},{13,21},{17,9},{21,13},{10,18... | collective-permute-start | bytes 1572872 | tf_op jit(solution)/shard_map/ppermute | solution.py:570
  72.0 36.2 %collective-permute-start.12 = (bf16[1056,256]{1,0:T(8,128)(2,1)}, bf16[1056,256]{1,0:T(8,128)(2,1)S(1)}, u32[]{:S(2)}, u32[]{:S(2)}) collective-permute-start(bf16[1056,256]{1,0:T(8,128)(2,1)} %copy-done.7), channel_id=1, source_target_pairs={{0,4},{4,0},{8,12},{12,8},{16,20},{20,16},{24,28},{28,24},{1,5},{5... | collective-permute-start | bytes 1622024 | tf_op jit(solution)/shard_map/ppermute | solution.py:573
  83.7 24.5 %collective-permute-start.17 = (bf16[1056,256]{1,0:T(8,128)(2,1)S(1)}, bf16[1056,256]{1,0:T(8,128)(2,1)S(1)}, u32[]{:S(2)}, u32[]{:S(2)}) collective-permute-start(bf16[1056,256]{1,0:T(8,128)(2,1)S(1)} %onward.5), channel_id=1, source_target_pairs={{8,24},{12,28},{16,0},{20,4},{9,25},{13,29},{17,1},{21,5},{10,26},... | collective-permute-start | bytes 1622024 | tf_op jit(solution)/shard_map/ppermute | solution.py:570
  92.8 15.4 %collective-permute-start.18 = (bf16[1056,256]{1,0:T(8,128)(2,1)}, bf16[1056,256]{1,0:T(8,128)(2,1)S(1)}, u32[]{:S(2)}, u32[]{:S(2)}) collective-permute-start(bf16[1056,256]{1,0:T(8,128)(2,1)} %onward.4), channel_id=1, source_target_pairs={{0,8},{4,12},{24,16},{28,20},{1,9},{5,13},{25,17},{29,21},{2,10},{... | collective-permute-start | bytes 1622024 | tf_op jit(solution)/shard_map/ppermute | solution.py:570
  98.6 15.3 %collective-permute-start.19 = (bf16[1056,256]{1,0:T(8,128)(2,1)S(1)}, bf16[1056,256]{1,0:T(8,128)(2,1)S(1)}, u32[]{:S(2)}, u32[]{:S(2)}) collective-permute-start(bf16[1056,256]{1,0:T(8,128)(2,1)S(1)} %onward.7), channel_id=1, source_target_pairs={{8,16},{12,20},{16,8},{20,12},{9,17},{13,21},{17,9},{21,13},{10,18... | collective-permute-start | bytes 1622024 | tf_op jit(solution)/shard_map/ppermute | solution.py:570
  99.5 14.4 %collective-permute-start.22 = (bf16[1024,256]{1,0:T(8,128)(2,1)S(1)}, bf16[1024,256]{1,0:T(8,128)(2,1)S(1)}, u32[]{:S(2)}, u32[]{:S(2)}) collective-permute-start(bf16[1024,256]{1,0:T(8,128)(2,1)S(1)} %multiply_convert_fusion), channel_id=1, source_target_pairs={{8,0},{12,4},{16,24},{20,28},{9,1},{13,5},{17,25},{21,29},{10,2},{... | collective-permute-start | bytes 1572872 | tf_op jit(solution)/shard_map/ppermute | solution.py:570
  123.9 12.0 %collective-permute-start.26 = (bf16[1040,256]{1,0:T(8,128)(2,1)S(1)}, bf16[1040,256]{1,0:T(8,128)(2,1)S(1)}, u32[]{:S(2)}, u32[]{:S(2)}) collective-permute-start(bf16[1040,256]{1,0:T(8,128)(2,1)S(1)} %scan.1), channel_id=1, source_target_pairs={{0,8},{4,12},{8,0},{12,4},{16,24},{20,28},{24,16},{28,20},{1,9},{5... | collective-permute-start | bytes 1597448 | tf_op jit(solution)/shard_map/ppermute | solution.py:570
  125.7 21.7 %collective-permute-start.25 = (bf16[1040,256]{1,0:T(8,128)(2,1)S(1)}, bf16[1040,256]{1,0:T(8,128)(2,1)S(1)}, u32[]{:S(2)}, u32[]{:S(2)}) collective-permute-start(bf16[1040,256]{1,0:T(8,128)(2,1)S(1)} %scan.1), channel_id=1, source_target_pairs={{0,4},{4,0},{8,12},{12,8},{16,20},{20,16},{24,28},{28,24},{1,5},{5... | collective-permute-start | bytes 1597448 | tf_op jit(solution)/shard_map/ppermute | solution.py:573
  127.0 20.3 %collective-permute-start.24 = (bf16[1040,256]{1,0:T(8,128)(2,1)}, bf16[1040,256]{1,0:T(8,128)(2,1)S(1)}, u32[]{:S(2)}, u32[]{:S(2)}) collective-permute-start(bf16[1040,256]{1,0:T(8,128)(2,1)} %collective-permute-done.23), channel_id=1, source_target_pairs={{8,0},{12,4},{16,24},{20,28},{9,1},{13,5},{17,25},{21,29},{10,2},{... | collective-permute-start | bytes 1597448 | tf_op jit(solution)/shard_map/ppermute | solution.py:570
  135.9 14.8 %collective-permute-start.27 = (bf16[1040,256]{1,0:T(8,128)(2,1)S(1)}, bf16[1040,256]{1,0:T(8,128)(2,1)S(1)}, u32[]{:S(2)}, u32[]{:S(2)}) collective-permute-start(bf16[1040,256]{1,0:T(8,128)(2,1)S(1)} %collective-permute-done.26), channel_id=1, source_target_pairs={{8,16},{12,20},{16,8},{20,12},{9,17},{13,21},{17,9},{21,13},{10,18... | collective-permute-start | bytes 1597448 | tf_op jit(solution)/shard_map/ppermute | solution.py:570
  136.6 27.2 %collective-permute-start.29 = (bf16[1040,256]{1,0:T(8,128)(2,1)S(1)}, bf16[1040,256]{1,0:T(8,128)(2,1)S(1)}, u32[]{:S(2)}, u32[]{:S(2)}) collective-permute-start(bf16[1040,256]{1,0:T(8,128)(2,1)S(1)} %collective-permute-done.26), channel_id=1, source_target_pairs={{0,4},{4,0},{8,12},{12,8},{16,20},{20,16},{24,28},{28,24},{1,5},{5... | collective-permute-start | bytes 1597448 | tf_op jit(solution)/shard_map/ppermute | solution.py:573
  147.4 16.9 %collective-permute-start.30 = (bf16[1040,256]{1,0:T(8,128)(2,1)S(1)}, bf16[1040,256]{1,0:T(8,128)(2,1)S(1)}, u32[]{:S(2)}, u32[]{:S(2)}) collective-permute-start(bf16[1040,256]{1,0:T(8,128)(2,1)S(1)} %broadcast_select_fusion.1), channel_id=1, source_target_pairs={{0,4},{4,0},{8,12},{12,8},{16,20},{20,16},{24,28},{28,24},{1,5},{5... | collective-permute-start | bytes 1597448 | tf_op jit(solution)/shard_map/ppermute | solution.py:573
  150.7 13.0 %collective-permute-start.28 = (bf16[1040,256]{1,0:T(8,128)(2,1)S(1)}, bf16[1040,256]{1,0:T(8,128)(2,1)S(1)}, u32[]{:S(2)}, u32[]{:S(2)}) collective-permute-start(bf16[1040,256]{1,0:T(8,128)(2,1)S(1)} %collective-permute-done.27), channel_id=1, source_target_pairs={{8,0},{12,4},{16,24},{20,28},{9,1},{13,5},{17,25},{21,29},{10,2},{... | collective-permute-start | bytes 1597448 | tf_op jit(solution)/shard_map/ppermute | solution.py:570
  163.8 10.3 %collective-permute-start.31 = (bf16[1040,256]{1,0:T(8,128)(2,1)S(1)}, bf16[1040,256]{1,0:T(8,128)(2,1)S(1)}, u32[]{:S(2)}, u32[]{:S(2)}) collective-permute-start(bf16[1040,256]{1,0:T(8,128)(2,1)S(1)} %broadcast_select_fusion), channel_id=1, source_target_pairs={{0,4},{4,0},{8,12},{12,8},{16,20},{20,16},{24,28},{28,24},{1,5},{5... | collective-permute-start | bytes 1597448 | tf_op jit(solution)/shard_map/ppermute | solution.py:573
  179.6 8.3 %collective-permute-start.33 = (bf16[256,512]{1,0:T(8,128)(2,1)}, bf16[256,512]{1,0:T(8,128)(2,1)S(1)}, u32[]{:S(2)}, u32[]{:S(2)}) collective-permute-start(bf16[256,512]{1,0:T(8,128)(2,1)} %add_convert_fusion.2), channel_id=1, source_target_pairs={{0,2},{1,3},{2,0},{3,1},{4,6},{5,7},{6,4},{7,5},{8,10},{9,11},{10,... | collective-permute-start | bytes 786440 | tf_op jit(solution)/shard_map/ppermute | solution.py:741
  189.8 12.8 %all-to-all-start = ((bf16[8,32,512]{2,1,0:T(8,128)(2,1)}), bf16[8,32,512]{2,1,0:T(8,128)(2,1)S(1)}, u32[]{:S(2)}, u32[]{:S(2)}) async-start(bf16[8,32,512]{2,1,0:T(8,128)(2,1)} %multiply_convert_fusion.1), calls=%async_computation | async-start | bytes 524288 | tf_op jit(solution)/shard_map/all_to_all | solution.py:747
  (21 other events, 366.2 us)

commit v12 on v11

--- a/solution.py
+++ b/solution.py
@@ -609,8 +609,6 @@
     opposite = (z // (LINE // 2)) ^ 1
     at = ((1 - side) * 2 + opposite) * half_run
     x_sent = lax.dynamic_slice_in_dim(w_x, at, half_run, axis=1)
-    x_sent, hidden_in = tie((x_sent, hidden_in))
-    x_far = across(x_sent)
     dt_rows = w_dt.T
     dt_cut = [dt_rows[:, at : at + 2 * STATE] for at in range(0, depth, 2 * STATE)]
     maps_sent = pick(w_bc, 1, 1 - side).reshape(depth, 2 * STATE)
@@ -624,7 +622,9 @@
     for m in range(1, LINE):
         arrived.append(along(line_columns(m), [(s, s ^ m) for s in range(LINE)]))
     stacked = jnp.stack(arrived)
+    stacked, x_sent = tie((stacked, x_sent))
     beyond_pair = across(stacked)
+    x_far = across(x_sent)
     beyond_pair, small, start_state, bc_own, dt_rows = tie(
         (beyond_pair, small, start_state, bc_own, dt_rows)
     )

time: 204 us -> 192 us (0.941)
  waiting for transfers between devices: 108 us -> 94.9 us
    ppermute x9, waiting for transfers between devices: 31.3 us -> 21 us  [across(): return lax.ppermute(value, 'seq', [(s, s ^ 1) for s in range(count)])]
    unnamed x38 -> x40, local copies, waits for them, and re-layouts: 3.73 us -> 4.54 us
  transfers between devices with their start and end apart: 37 -> 37, of which waited for: 16 -> 16; matrix products, arithmetic and copies ran while one was open for 6% -> 7% of each run, Pallas kernels for 2% -> 3%
where the time goes in v12:
time: 192 us; the launch traced here: 191 us
  waiting for transfers between devices  94.9 us (49%)
  starting transfers between devices  53.4 us (28%)
  Pallas kernels  18.8 us (10%)
  local copies, waits for them, and re-layouts  12.7 us (7%)
  other arithmetic  5.21 us (3%)
  matrix products  3.7 us (2%)
  between operations  1.92 us (1%)
    ppermute x17, waiting for transfers between devices, along(): return lax.ppermute(value, 'seq', moves)  54.4 us
    ppermute x17, starting transfers between devices, along(): return lax.ppermute(value, 'seq', moves)  28.8 us
    ppermute x9, waiting for transfers between devices, across(): return lax.ppermute(value, 'seq', [(s, s ^ 1) for s in range(count)])  21 us
    ppermute x9, starting transfers between devices, across(): return lax.ppermute(value, 'seq', [(s, s ^ 1) for s in range(count)])  12.8 us
    all_to_all x1, waiting for transfers between devices, by_heads(): lax.all_to_all(final.astype(bf16), 'seq', split_axis=0, concat_axis=0, ti...  7.62 us
    pallas_call x1, Pallas kernels, scan(): pl.pallas_call(scan_kernel, in_specs=[SMEM, SMEM] + [VMEM] * (len(sums) +...  7.46 us
    ppermute x1, waiting for transfers between devices, by_heads(): received = lax.ppermute(sent.astype(bf16), 'tensor', pairs)  6.42 us
    pallas_call x1, Pallas kernels, project(): pl.pallas_call(functools.partial(project_kernel, ranks), in_specs=[SMEM,...  6.42 us
  transfers between devices with their start and end apart: 37, of which 16 were waited for; matrix products, arithmetic and copies ran while one was open for 7% of the time, Pallas kernels for 3%

profile of v12, /device:TPU:0, one launch (start us, length us, event | category | flops | bytes accessed | tf_op | source)
XLA Modules:
  0.0 190.6 jit_solution(15932406218327931157)
XLA Ops:
  1.9 3.1 %collective-permute-start = (bf16[32,1024]{1,0:T(8,128)(2,1)S(1)}, bf16[32,1024]{1,0:T(8,128)(2,1)S(1)}, u32[]{:S(2)}, u32[]{:S(2)}) collective-permute-start(bf16[32,1024]{1,0:T(8,128)(2,1)S(1)} %get-tuple-element.59), channel_id=1, source_target_pairs={{0,8},{4,12},{8,0},{12,4},{16,24},{20,28},{24,16},{28,20},{1,9},{5... | collective-permute-start | bytes 196616 | tf_op jit(solution)/shard_map/ppermute | solution.py:570
  4.9 2.6 %collective-permute-start.1 = (bf16[32,1024]{1,0:T(8,128)(2,1)S(1)}, bf16[32,1024]{1,0:T(8,128)(2,1)S(1)}, u32[]{:S(2)}, u32[]{:S(2)}) collective-permute-start(bf16[32,1024]{1,0:T(8,128)(2,1)S(1)} %get-tuple-element.61), channel_id=1, source_target_pairs={{0,16},{4,20},{8,24},{12,28},{16,0},{20,4},{24,8},{28,12},{1,17},{... | collective-permute-start | bytes 196616 | tf_op jit(solution)/shard_map/ppermute | solution.py:570
  7.5 2.1 %constant_dynamic-slice_fusion.2 = (bf16[512,1,2,128]{3,2,1,0:T(2,128)(2,1)S(1)}, bf16[512,1,2,128]{3,2,1,0:T(2,128)(2,1)}) fusion(bf16[512,2,2,128]{3,2,1,0:T(2,128)(2,1)} %param.18, s32[]{:T(128)S(6)} %select_n.132, s32[]{:T(128)S(6)} %select_n.129), kind=kLoop, calls=%fused_computation.57 | loop fusion | bytes 1048584 | tf_op jit(solution)/shard_map/jit(dynamic_index_in_dim)/dynamic_slice | solution.py:566
  10.4 1.7 collective-permute-start.11
  12.6 1.9 constant_dynamic-slice_fusion.6
  17.5 1.6 collective-permute-start.4
  20.5 5.8 %collective-permute-done.6.refs_4_ = bf16[4,32,1024]{2,1,0:T(8,128)(2,1)} collective-permute-done((bf16[4,32,1024]{2,1,0:T(8,128)(2,1)S(1)}, bf16[4,32,1024]{2,1,0:T(8,128)(2,1)}, u32[]{:S(2)}, u32[]{:S(2)}) %collective-permute-start.6) | collective-permute-done | bytes 262176 | tf_op jit(solution)/shard_map/ppermute | solution.py:573
  26.3 1.7 collective-permute-start.8
  28.7 4.4 %collective-permute-done.8.refs_6_ = bf16[4,32,1024]{2,1,0:T(8,128)(2,1)} collective-permute-done((bf16[4,32,1024]{2,1,0:T(8,128)(2,1)}, bf16[4,32,1024]{2,1,0:T(8,128)(2,1)}, u32[]{:S(2)}, u32[]{:S(2)}) %collective-permute-start.8) | collective-permute-done | bytes 262176 | tf_op jit(solution)/shard_map/ppermute | solution.py:637
  33.8 2.0 %collective-permute-done.10.refs_9_ = bf16[512,512]{1,0:T(8,128)(2,1)} collective-permute-done((bf16[512,512]{1,0:T(8,128)(2,1)}, bf16[512,512]{1,0:T(8,128)(2,1)}, u32[]{:S(2)}, u32[]{:S(2)}) %collective-permute-start.10) | collective-permute-done | bytes 524320 | tf_op jit(solution)/shard_map/ppermute | solution.py:573
  35.8 1.6 copy-done.5
  37.4 6.4 %project.1 = (bf16[1056,256]{1,0:T(8,128)(2,1)}, bf16[1056,256]{1,0:T(8,128)(2,1)}, bf16[1056,256]{1,0:T(8,128)(2,1)S(1)}, bf16[1056,256]{1,0:T(8,128)(2,1)S(1)}...) custom-call(s32[7]{0:T(128)S(1)} %stack.43.place_ref, ...), custom_call_target="tpu_custom_call" | custom-call | flops 2684354560 | bytes 4194304 | tf_op jit(solution)/shard_map/project/pallas_call | solution.py:301
  45.4 2.5 %collective-permute-start.20 = (bf16[1024,256]{1,0:T(8,128)(2,1)S(1)}, bf16[1024,256]{1,0:T(8,128)(2,1)S(1)}, u32[]{:S(2)}, u32[]{:S(2)}) collective-permute-start(bf16[1024,256]{1,0:T(8,128)(2,1)S(1)} %get-tuple-element.45), channel_id=1, source_target_pairs={{0,8},{4,12},{24,16},{28,20},{1,9},{5,13},{25,17},{29,21},{2,10},{... | collective-permute-start | bytes 1572872 | tf_op jit(solution)/shard_map/ppermute | solution.py:570
  47.9 2.1 %collective-permute-start.16 = (bf16[1056,256]{1,0:T(8,128)(2,1)}, bf16[1056,256]{1,0:T(8,128)(2,1)}, u32[]{:S(2)}, u32[]{:S(2)}) collective-permute-start(bf16[1056,256]{1,0:T(8,128)(2,1)} %get-tuple-element.39.refs_0_), channel_id=1, source_target_pairs={{0,8},{4,12},{24,16},{28,20},{1,9},{5,13},{25,17},{29,21},{2,10},{... | collective-permute-start | bytes 1622024 | tf_op jit(solution)/shard_map/ppermute | solution.py:570
  50.0 2.1 %collective-permute-start.13 = (bf16[1056,256]{1,0:T(8,128)(2,1)}, bf16[1056,256]{1,0:T(8,128)(2,1)}, u32[]{:S(2)}, u32[]{:S(2)}) collective-permute-start(bf16[1056,256]{1,0:T(8,128)(2,1)} %get-tuple-element.36.refs_0_), channel_id=1, source_target_pairs={{0,8},{4,12},{24,16},{28,20},{1,9},{5,13},{25,17},{29,21},{2,10},{... | collective-permute-start | bytes 1622024 | tf_op jit(solution)/shard_map/ppermute | solution.py:570
  52.1 5.2 %collective-permute-done.14.refs_1_ = bf16[1056,256]{1,0:T(8,128)(2,1)S(1)} collective-permute-done((bf16[1056,256]{1,0:T(8,128)(2,1)S(1)}, bf16[1056,256]{1,0:T(8,128)(2,1)S(1)}, u32[]{:S(2)}, u32[]{:S(2)}) %collective-permute-start.14) | collective-permute-done | bytes 540704 | tf_op jit(solution)/shard_map/ppermute | solution.py:573
  62.2 9.8 %collective-permute-done.16.refs_1_ = bf16[1056,256]{1,0:T(8,128)(2,1)} collective-permute-done((bf16[1056,256]{1,0:T(8,128)(2,1)}, bf16[1056,256]{1,0:T(8,128)(2,1)}, u32[]{:S(2)}, u32[]{:S(2)}) %collective-permute-start.16) | collective-permute-done | bytes 540704 | tf_op jit(solution)/shard_map/ppermute | solution.py:570
  74.6 7.1 %collective-permute-done.13.refs_1_ = bf16[1056,256]{1,0:T(8,128)(2,1)} collective-permute-done((bf16[1056,256]{1,0:T(8,128)(2,1)}, bf16[1056,256]{1,0:T(8,128)(2,1)}, u32[]{:S(2)}, u32[]{:S(2)}) %collective-permute-start.13) | collective-permute-done | bytes 540704 | tf_op jit(solution)/shard_map/ppermute | solution.py:570
  81.7 4.4 %collective-permute-start.18 = (bf16[1056,256]{1,0:T(8,128)(2,1)}, bf16[1056,256]{1,0:T(8,128)(2,1)S(1)}, u32[]{:S(2)}, u32[]{:S(2)}) collective-permute-start(bf16[1056,256]{1,0:T(8,128)(2,1)} %onward.4), channel_id=1, source_target_pairs={{0,8},{4,12},{24,16},{28,20},{1,9},{5,13},{25,17},{29,21},{2,10},{... | collective-permute-start | bytes 1622024 | tf_op jit(solution)/shard_map/ppermute | solution.py:570
  89.9 6.5 %collective-permute-done.18.refs_3_ = bf16[1056,256]{1,0:T(8,128)(2,1)S(1)} collective-permute-done((bf16[1056,256]{1,0:T(8,128)(2,1)}, bf16[1056,256]{1,0:T(8,128)(2,1)S(1)}, u32[]{:S(2)}, u32[]{:S(2)}) %collective-permute-start.18) | collective-permute-done | bytes 540704 | tf_op jit(solution)/shard_map/ppermute | solution.py:570
  97.7 4.4 %collective-permute-done.22.refs_5_ = bf16[1024,256]{1,0:T(8,128)(2,1)S(1)} collective-permute-done((bf16[1024,256]{1,0:T(8,128)(2,1)S(1)}, bf16[1024,256]{1,0:T(8,128)(2,1)S(1)}, u32[]{:S(2)}, u32[]{:S(2)}) %collective-permute-start.22) | collective-permute-done | bytes 524320 | tf_op jit(solution)/shard_map/ppermute | solution.py:570
  103.2 7.5 %scan.1 = bf16[1040,256]{1,0:T(8,128)(2,1)S(1)} custom-call(s32[7]{0:T(128)S(1)} %stack.43.place_ref, f32[1]{0:T(128)} %bitcast.3.scale_ref, bf16[1056,256]{1,0:T(8,128)(2,1)S(1)} %onward.6.refs_0_, bf16[1056,256]{1,0:T(8,128)(2,1)S(1)} %collective-permute-done.17.refs_1_, bf16[1056,256]{1,0:T(8,128)(2,1)S(1)} %collective-permute-done.19.refs_2_, ...), custom_call_target="tpu_custom_call" | custom-call | flops 268435456 | bytes 2097152 | tf_op jit(solution)/shard_map/scan/pallas_call | solution.py:515
  112.1 1.8 collective-permute-start.26
  116.5 7.6 %collective-permute-done.26 = bf16[1040,256]{1,0:T(8,128)(2,1)S(1)} collective-permute-done((bf16[1040,256]{1,0:T(8,128)(2,1)S(1)}, bf16[1040,256]{1,0:T(8,128)(2,1)S(1)}, u32[]{:S(2)}, u32[]{:S(2)}) %collective-permute-start.26) | collective-permute-done | bytes 532512 | tf_op jit(solution)/shard_map/ppermute | solution.py:570
  124.8 1.8 collective-permute-start.29
  127.0 7.8 %collective-permute-done.24 = bf16[1040,256]{1,0:T(8,128)(2,1)S(1)} collective-permute-done((bf16[1040,256]{1,0:T(8,128)(2,1)}, bf16[1040,256]{1,0:T(8,128)(2,1)S(1)}, u32[]{:S(2)}, u32[]{:S(2)}) %collective-permute-start.24) | collective-permute-done | bytes 532512 | tf_op jit(solution)/shard_map/ppermute | solution.py:570
  134.9 2.8 %collective-permute-start.30 = (bf16[1040,256]{1,0:T(8,128)(2,1)S(1)}, bf16[1040,256]{1,0:T(8,128)(2,1)S(1)}, u32[]{:S(2)}, u32[]{:S(2)}) collective-permute-start(bf16[1040,256]{1,0:T(8,128)(2,1)S(1)} %broadcast_select_fusion.1), channel_id=1, source_target_pairs={{0,4},{4,0},{8,12},{12,8},{16,20},{20,16},{24,28},{28,24},{1,5},{5... | collective-permute-start | bytes 1597448 | tf_op jit(solution)/shard_map/ppermute | solution.py:573
  140.4 10.5 %collective-permute-done.28 = bf16[1040,256]{1,0:T(8,128)(2,1)S(1)} collective-permute-done((bf16[1040,256]{1,0:T(8,128)(2,1)S(1)}, bf16[1040,256]{1,0:T(8,128)(2,1)S(1)}, u32[]{:S(2)}, u32[]{:S(2)}) %collective-permute-start.28) | collective-permute-done | bytes 532512 | tf_op jit(solution)/shard_map/ppermute | solution.py:570
  152.8 8.0 %collective-permute-done.31 = bf16[1040,256]{1,0:T(8,128)(2,1)S(1)} collective-permute-done((bf16[1040,256]{1,0:T(8,128)(2,1)S(1)}, bf16[1040,256]{1,0:T(8,128)(2,1)S(1)}, u32[]{:S(2)}, u32[]{:S(2)}) %collective-permute-start.31) | collective-permute-done | bytes 532512 | tf_op jit(solution)/shard_map/ppermute | solution.py:573
  168.1 6.4 %collective-permute-done.33 = bf16[256,512]{1,0:T(8,128)(2,1)S(1)} collective-permute-done((bf16[256,512]{1,0:T(8,128)(2,1)}, bf16[256,512]{1,0:T(8,128)(2,1)S(1)}, u32[]{:S(2)}, u32[]{:S(2)}) %collective-permute-start.33) | collective-permute-done | bytes 262176 | tf_op jit(solution)/shard_map/ppermute | solution.py:741
  176.4 5.3 %all-to-all-start = ((bf16[8,32,512]{2,1,0:T(8,128)(2,1)}), bf16[8,32,512]{2,1,0:T(8,128)(2,1)S(1)}, u32[]{:S(2)}, u32[]{:S(2)}) async-start(bf16[8,32,512]{2,1,0:T(8,128)(2,1)} %multiply_convert_fusion.1), calls=%async_computation | async-start | bytes 524288 | tf_op jit(solution)/shard_map/all_to_all | solution.py:747
  182.3 7.6 %all-to-all-done = bf16[8,32,512]{2,1,0:T(8,128)(2,1)S(1)} async-done(((bf16[8,32,512]{2,1,0:T(8,128)(2,1)}), bf16[8,32,512]{2,1,0:T(8,128)(2,1)S(1)}, u32[]{:S(2)}, u32[]{:S(2)}) %all-to-all-start) | async-done | bytes 262176 | tf_op jit(solution)/shard_map/all_to_all | solution.py:747
  (143 shorter events, 42.6 us)
Async XLA Ops:
  1.9 12.6 %collective-permute-start = (bf16[32,1024]{1,0:T(8,128)(2,1)S(1)}, bf16[32,1024]{1,0:T(8,128)(2,1)S(1)}, u32[]{:S(2)}, u32[]{:S(2)}) collective-permute-start(bf16[32,1024]{1,0:T(8,128)(2,1)S(1)} %get-tuple-element.59), channel_id=1, source_target_pairs={{0,8},{4,12},{8,0},{12,4},{16,24},{20,28},{24,16},{28,20},{1,9},{5... | collective-permute-start | bytes 196616 | tf_op jit(solution)/shard_map/ppermute | solution.py:570
  4.9 9.5 %collective-permute-start.1 = (bf16[32,1024]{1,0:T(8,128)(2,1)S(1)}, bf16[32,1024]{1,0:T(8,128)(2,1)S(1)}, u32[]{:S(2)}, u32[]{:S(2)}) collective-permute-start(bf16[32,1024]{1,0:T(8,128)(2,1)S(1)} %get-tuple-element.61), channel_id=1, source_target_pairs={{0,16},{4,20},{8,24},{12,28},{16,0},{20,4},{24,8},{28,12},{1,17},{... | collective-permute-start | bytes 196616 | tf_op jit(solution)/shard_map/ppermute | solution.py:570
  7.5 6.9 %collective-permute-start.2 = (bf16[32,1024]{1,0:T(8,128)(2,1)S(1)}, bf16[32,1024]{1,0:T(8,128)(2,1)S(1)}, u32[]{:S(2)}, u32[]{:S(2)}) collective-permute-start(bf16[32,1024]{1,0:T(8,128)(2,1)S(1)} %get-tuple-element.60), channel_id=1, source_target_pairs={{0,24},{4,28},{8,16},{12,20},{16,8},{20,12},{24,0},{28,4},{1,25},{... | collective-permute-start | bytes 196616 | tf_op jit(solution)/shard_map/ppermute | solution.py:570
  10.4 17.6 %collective-permute-start.11 = (bf16[576,256]{1,0:T(8,128)(2,1)}, bf16[576,256]{1,0:T(8,128)(2,1)S(1)}, u32[]{:S(2)}, u32[]{:S(2)}) collective-permute-start(bf16[576,256]{1,0:T(8,128)(2,1)} %pad_maximum_fusion), channel_id=1, source_target_pairs={{0,4},{4,0},{8,12},{12,8},{16,20},{20,16},{24,28},{28,24},{1,5},{5... | collective-permute-start | bytes 884744 | tf_op jit(solution)/shard_map/ppermute | solution.py:573
  14.5 11.8 %collective-permute-start.6 = (bf16[4,32,1024]{2,1,0:T(8,128)(2,1)S(1)}, bf16[4,32,1024]{2,1,0:T(8,128)(2,1)}, u32[]{:S(2)}, u32[]{:S(2)}) collective-permute-start(bf16[4,32,1024]{2,1,0:T(8,128)(2,1)S(1)} %pad_maximum_fusion.1.refs_0_), channel_id=1, source_target_pairs={{0,4},{4,0},{8,12},{12,8},{16,20},{20,16},{24,28},{28,24},{1,5},{5... | collective-permute-start | bytes 786440 | tf_op jit(solution)/shard_map/ppermute | solution.py:573
  17.5 11.0 %collective-permute-start.4 = (bf16[4,32,1024]{2,1,0:T(8,128)(2,1)S(1)}, bf16[4,32,1024]{2,1,0:T(8,128)(2,1)}, u32[]{:S(2)}, u32[]{:S(2)}) collective-permute-start(bf16[4,32,1024]{2,1,0:T(8,128)(2,1)S(1)} %pad_maximum_fusion.1.refs_0_), channel_id=1, source_target_pairs={{0,2},{1,3},{2,0},{3,1},{4,6},{5,7},{6,4},{7,5},{8,10},{9,11},{10,... | collective-permute-start | bytes 786440 | tf_op jit(solution)/shard_map/ppermute | solution.py:637
  19.1 16.7 %collective-permute-start.10 = (bf16[512,512]{1,0:T(8,128)(2,1)}, bf16[512,512]{1,0:T(8,128)(2,1)}, u32[]{:S(2)}, u32[]{:S(2)}) collective-permute-start(bf16[512,512]{1,0:T(8,128)(2,1)} %constant_dynamic-slice_fusion.6), channel_id=1, source_target_pairs={{0,4},{4,0},{8,12},{12,8},{16,20},{20,16},{24,28},{28,24},{1,5},{5... | collective-permute-start | bytes 1572872 | tf_op jit(solution)/shard_map/ppermute | solution.py:573
  26.3 6.7 %collective-permute-start.8 = (bf16[4,32,1024]{2,1,0:T(8,128)(2,1)}, bf16[4,32,1024]{2,1,0:T(8,128)(2,1)}, u32[]{:S(2)}, u32[]{:S(2)}) collective-permute-start(bf16[4,32,1024]{2,1,0:T(8,128)(2,1)} %collective-permute-done.6.refs_4_), channel_id=1, source_target_pairs={{0,2},{1,3},{2,0},{3,1},{4,6},{5,7},{6,4},{7,5},{8,10},{9,11},{10,... | collective-permute-start | bytes 786440 | tf_op jit(solution)/shard_map/ppermute | solution.py:637
  28.1 5.7 %collective-permute-start.3 = (bf16[4,32,1024]{2,1,0:T(8,128)(2,1)S(1)}, bf16[4,32,1024]{2,1,0:T(8,128)(2,1)}, u32[]{:S(2)}, u32[]{:S(2)}) collective-permute-start(bf16[4,32,1024]{2,1,0:T(8,128)(2,1)S(1)} %pad_maximum_fusion.1.refs_0_), channel_id=1, source_target_pairs={{0,1},{1,0},{2,3},{3,2},{4,5},{5,4},{6,7},{7,6},{8,9},{9,8},{10,11... | collective-permute-start | bytes 786440 | tf_op jit(solution)/shard_map/ppermute | solution.py:637
  28.1 5.7 %collective-permute-start.7 = (bf16[4,32,1024]{2,1,0:T(8,128)(2,1)}, bf16[4,32,1024]{2,1,0:T(8,128)(2,1)}, u32[]{:S(2)}, u32[]{:S(2)}) collective-permute-start(bf16[4,32,1024]{2,1,0:T(8,128)(2,1)} %collective-permute-done.6.refs_4_), channel_id=1, source_target_pairs={{0,1},{1,0},{2,3},{3,2},{4,5},{5,4},{6,7},{7,6},{8,9},{9,8},{10,11... | collective-permute-start | bytes 786440 | tf_op jit(solution)/shard_map/ppermute | solution.py:637
  28.6 5.2 %collective-permute-start.5 = (bf16[4,32,1024]{2,1,0:T(8,128)(2,1)}, bf16[4,32,1024]{2,1,0:T(8,128)(2,1)}, u32[]{:S(2)}, u32[]{:S(2)}) collective-permute-start(bf16[4,32,1024]{2,1,0:T(8,128)(2,1)} %collective-permute-done.4.refs_2_), channel_id=1, source_target_pairs={{0,1},{1,0},{2,3},{3,2},{4,5},{5,4},{6,7},{7,6},{8,9},{9,8},{10,11... | collective-permute-start | bytes 786440 | tf_op jit(solution)/shard_map/ppermute | solution.py:637
  43.8 13.5 %collective-permute-start.14 = (bf16[1056,256]{1,0:T(8,128)(2,1)S(1)}, bf16[1056,256]{1,0:T(8,128)(2,1)S(1)}, u32[]{:S(2)}, u32[]{:S(2)}) collective-permute-start(bf16[1056,256]{1,0:T(8,128)(2,1)S(1)} %get-tuple-element.38), channel_id=1, source_target_pairs={{0,4},{4,0},{8,12},{12,8},{16,20},{20,16},{24,28},{28,24},{1,5},{5... | collective-permute-start | bytes 1622024 | tf_op jit(solution)/shard_map/ppermute | solution.py:573
  45.4 14.9 %collective-permute-start.20 = (bf16[1024,256]{1,0:T(8,128)(2,1)S(1)}, bf16[1024,256]{1,0:T(8,128)(2,1)S(1)}, u32[]{:S(2)}, u32[]{:S(2)}) collective-permute-start(bf16[1024,256]{1,0:T(8,128)(2,1)S(1)} %get-tuple-element.45), channel_id=1, source_target_pairs={{0,8},{4,12},{24,16},{28,20},{1,9},{5,13},{25,17},{29,21},{2,10},{... | collective-permute-start | bytes 1572872 | tf_op jit(solution)/shard_map/ppermute | solution.py:570
  47.9 24.0 %collective-permute-start.16 = (bf16[1056,256]{1,0:T(8,128)(2,1)}, bf16[1056,256]{1,0:T(8,128)(2,1)}, u32[]{:S(2)}, u32[]{:S(2)}) collective-permute-start(bf16[1056,256]{1,0:T(8,128)(2,1)} %get-tuple-element.39.refs_0_), channel_id=1, source_target_pairs={{0,8},{4,12},{24,16},{28,20},{1,9},{5,13},{25,17},{29,21},{2,10},{... | collective-permute-start | bytes 1622024 | tf_op jit(solution)/shard_map/ppermute | solution.py:570
  50.0 31.7 %collective-permute-start.13 = (bf16[1056,256]{1,0:T(8,128)(2,1)}, bf16[1056,256]{1,0:T(8,128)(2,1)}, u32[]{:S(2)}, u32[]{:S(2)}) collective-permute-start(bf16[1056,256]{1,0:T(8,128)(2,1)} %get-tuple-element.36.refs_0_), channel_id=1, source_target_pairs={{0,8},{4,12},{24,16},{28,20},{1,9},{5,13},{25,17},{29,21},{2,10},{... | collective-permute-start | bytes 1622024 | tf_op jit(solution)/shard_map/ppermute | solution.py:570
  58.2 27.9 %collective-permute-start.15 = (bf16[1056,256]{1,0:T(8,128)(2,1)}, bf16[1056,256]{1,0:T(8,128)(2,1)}, u32[]{:S(2)}, u32[]{:S(2)}) collective-permute-start(bf16[1056,256]{1,0:T(8,128)(2,1)} %onward.4), channel_id=1, source_target_pairs={{8,0},{12,4},{16,24},{20,28},{9,1},{13,5},{17,25},{21,29},{10,2},{... | collective-permute-start | bytes 1622024 | tf_op jit(solution)/shard_map/ppermute | solution.py:570
  60.4 27.8 %collective-permute-start.21 = (bf16[1024,256]{1,0:T(8,128)(2,1)S(1)}, bf16[1024,256]{1,0:T(8,128)(2,1)S(1)}, u32[]{:S(2)}, u32[]{:S(2)}) collective-permute-start(bf16[1024,256]{1,0:T(8,128)(2,1)S(1)} %add_convert_fusion.1.refs_3_), channel_id=1, source_target_pairs={{8,16},{12,20},{16,8},{20,12},{9,17},{13,21},{17,9},{21,13},{10,18... | collective-permute-start | bytes 1572872 | tf_op jit(solution)/shard_map/ppermute | solution.py:570
  61.1 35.3 %collective-permute-start.12 = (bf16[1056,256]{1,0:T(8,128)(2,1)}, bf16[1056,256]{1,0:T(8,128)(2,1)S(1)}, u32[]{:S(2)}, u32[]{:S(2)}) collective-permute-start(bf16[1056,256]{1,0:T(8,128)(2,1)} %copy-done.7), channel_id=1, source_target_pairs={{0,4},{4,0},{8,12},{12,8},{16,20},{20,16},{24,28},{28,24},{1,5},{5... | collective-permute-start | bytes 1622024 | tf_op jit(solution)/shard_map/ppermute | solution.py:573
  73.3 23.1 %collective-permute-start.17 = (bf16[1056,256]{1,0:T(8,128)(2,1)S(1)}, bf16[1056,256]{1,0:T(8,128)(2,1)S(1)}, u32[]{:S(2)}, u32[]{:S(2)}) collective-permute-start(bf16[1056,256]{1,0:T(8,128)(2,1)S(1)} %onward.5), channel_id=1, source_target_pairs={{8,24},{12,28},{16,0},{20,4},{9,25},{13,29},{17,1},{21,5},{10,26},... | collective-permute-start | bytes 1622024 | tf_op jit(solution)/shard_map/ppermute | solution.py:570
  81.7 14.7 %collective-permute-start.18 = (bf16[1056,256]{1,0:T(8,128)(2,1)}, bf16[1056,256]{1,0:T(8,128)(2,1)S(1)}, u32[]{:S(2)}, u32[]{:S(2)}) collective-permute-start(bf16[1056,256]{1,0:T(8,128)(2,1)} %onward.4), channel_id=1, source_target_pairs={{0,8},{4,12},{24,16},{28,20},{1,9},{5,13},{25,17},{29,21},{2,10},{... | collective-permute-start | bytes 1622024 | tf_op jit(solution)/shard_map/ppermute | solution.py:570
  87.5 14.6 %collective-permute-start.19 = (bf16[1056,256]{1,0:T(8,128)(2,1)S(1)}, bf16[1056,256]{1,0:T(8,128)(2,1)S(1)}, u32[]{:S(2)}, u32[]{:S(2)}) collective-permute-start(bf16[1056,256]{1,0:T(8,128)(2,1)S(1)} %onward.7), channel_id=1, source_target_pairs={{8,16},{12,20},{16,8},{20,12},{9,17},{13,21},{17,9},{21,13},{10,18... | collective-permute-start | bytes 1622024 | tf_op jit(solution)/shard_map/ppermute | solution.py:570
  88.4 13.7 %collective-permute-start.22 = (bf16[1024,256]{1,0:T(8,128)(2,1)S(1)}, bf16[1024,256]{1,0:T(8,128)(2,1)S(1)}, u32[]{:S(2)}, u32[]{:S(2)}) collective-permute-start(bf16[1024,256]{1,0:T(8,128)(2,1)S(1)} %multiply_convert_fusion), channel_id=1, source_target_pairs={{8,0},{12,4},{16,24},{20,28},{9,1},{13,5},{17,25},{21,29},{10,2},{... | collective-permute-start | bytes 1572872 | tf_op jit(solution)/shard_map/ppermute | solution.py:570
  112.1 12.0 %collective-permute-start.26 = (bf16[1040,256]{1,0:T(8,128)(2,1)S(1)}, bf16[1040,256]{1,0:T(8,128)(2,1)S(1)}, u32[]{:S(2)}, u32[]{:S(2)}) collective-permute-start(bf16[1040,256]{1,0:T(8,128)(2,1)S(1)} %scan.1), channel_id=1, source_target_pairs={{0,8},{4,12},{8,0},{12,4},{16,24},{20,28},{24,16},{28,20},{1,9},{5... | collective-permute-start | bytes 1597448 | tf_op jit(solution)/shard_map/ppermute | solution.py:570
  113.9 20.9 %collective-permute-start.25 = (bf16[1040,256]{1,0:T(8,128)(2,1)S(1)}, bf16[1040,256]{1,0:T(8,128)(2,1)S(1)}, u32[]{:S(2)}, u32[]{:S(2)}) collective-permute-start(bf16[1040,256]{1,0:T(8,128)(2,1)S(1)} %scan.1), channel_id=1, source_target_pairs={{0,4},{4,0},{8,12},{12,8},{16,20},{20,16},{24,28},{28,24},{1,5},{5... | collective-permute-start | bytes 1597448 | tf_op jit(solution)/shard_map/ppermute | solution.py:573
  115.2 19.6 %collective-permute-start.24 = (bf16[1040,256]{1,0:T(8,128)(2,1)}, bf16[1040,256]{1,0:T(8,128)(2,1)S(1)}, u32[]{:S(2)}, u32[]{:S(2)}) collective-permute-start(bf16[1040,256]{1,0:T(8,128)(2,1)} %collective-permute-done.23), channel_id=1, source_target_pairs={{8,0},{12,4},{16,24},{20,28},{9,1},{13,5},{17,25},{21,29},{10,2},{... | collective-permute-start | bytes 1597448 | tf_op jit(solution)/shard_map/ppermute | solution.py:570
  124.1 14.0 %collective-permute-start.27 = (bf16[1040,256]{1,0:T(8,128)(2,1)S(1)}, bf16[1040,256]{1,0:T(8,128)(2,1)S(1)}, u32[]{:S(2)}, u32[]{:S(2)}) collective-permute-start(bf16[1040,256]{1,0:T(8,128)(2,1)S(1)} %collective-permute-done.26), channel_id=1, source_target_pairs={{8,16},{12,20},{16,8},{20,12},{9,17},{13,21},{17,9},{21,13},{10,18... | collective-permute-start | bytes 1597448 | tf_op jit(solution)/shard_map/ppermute | solution.py:570
  124.8 26.1 %collective-permute-start.29 = (bf16[1040,256]{1,0:T(8,128)(2,1)S(1)}, bf16[1040,256]{1,0:T(8,128)(2,1)S(1)}, u32[]{:S(2)}, u32[]{:S(2)}) collective-permute-start(bf16[1040,256]{1,0:T(8,128)(2,1)S(1)} %collective-permute-done.26), channel_id=1, source_target_pairs={{0,4},{4,0},{8,12},{12,8},{16,20},{20,16},{24,28},{28,24},{1,5},{5... | collective-permute-start | bytes 1597448 | tf_op jit(solution)/shard_map/ppermute | solution.py:573
  134.9 16.6 %collective-permute-start.30 = (bf16[1040,256]{1,0:T(8,128)(2,1)S(1)}, bf16[1040,256]{1,0:T(8,128)(2,1)S(1)}, u32[]{:S(2)}, u32[]{:S(2)}) collective-permute-start(bf16[1040,256]{1,0:T(8,128)(2,1)S(1)} %broadcast_select_fusion.1), channel_id=1, source_target_pairs={{0,4},{4,0},{8,12},{12,8},{16,20},{20,16},{24,28},{28,24},{1,5},{5... | collective-permute-start | bytes 1597448 | tf_op jit(solution)/shard_map/ppermute | solution.py:573
  138.2 12.7 %collective-permute-start.28 = (bf16[1040,256]{1,0:T(8,128)(2,1)S(1)}, bf16[1040,256]{1,0:T(8,128)(2,1)S(1)}, u32[]{:S(2)}, u32[]{:S(2)}) collective-permute-start(bf16[1040,256]{1,0:T(8,128)(2,1)S(1)} %collective-permute-done.27), channel_id=1, source_target_pairs={{8,0},{12,4},{16,24},{20,28},{9,1},{13,5},{17,25},{21,29},{10,2},{... | collective-permute-start | bytes 1597448 | tf_op jit(solution)/shard_map/ppermute | solution.py:570
  150.9 9.9 %collective-permute-start.31 = (bf16[1040,256]{1,0:T(8,128)(2,1)S(1)}, bf16[1040,256]{1,0:T(8,128)(2,1)S(1)}, u32[]{:S(2)}, u32[]{:S(2)}) collective-permute-start(bf16[1040,256]{1,0:T(8,128)(2,1)S(1)} %broadcast_select_fusion), channel_id=1, source_target_pairs={{0,4},{4,0},{8,12},{12,8},{16,20},{20,16},{24,28},{28,24},{1,5},{5... | collective-permute-start | bytes 1597448 | tf_op jit(solution)/shard_map/ppermute | solution.py:573
  166.3 8.3 %collective-permute-start.33 = (bf16[256,512]{1,0:T(8,128)(2,1)}, bf16[256,512]{1,0:T(8,128)(2,1)S(1)}, u32[]{:S(2)}, u32[]{:S(2)}) collective-permute-start(bf16[256,512]{1,0:T(8,128)(2,1)} %add_convert_fusion.2), channel_id=1, source_target_pairs={{0,2},{1,3},{2,0},{3,1},{4,6},{5,7},{6,4},{7,5},{8,10},{9,11},{10,... | collective-permute-start | bytes 786440 | tf_op jit(solution)/shard_map/ppermute | solution.py:741
  176.4 13.5 %all-to-all-start = ((bf16[8,32,512]{2,1,0:T(8,128)(2,1)}), bf16[8,32,512]{2,1,0:T(8,128)(2,1)S(1)}, u32[]{:S(2)}, u32[]{:S(2)}) async-start(bf16[8,32,512]{2,1,0:T(8,128)(2,1)} %multiply_convert_fusion.1), calls=%async_computation | async-start | bytes 524288 | tf_op jit(solution)/shard_map/all_to_all | solution.py:747
  (22 other events, 324.7 us)

commit v13 on v12

--- a/solution.py
+++ b/solution.py
@@ -661,11 +661,11 @@
     map_done = ((map_sum.astype(f32) + map_far.astype(f32)) * in_scale).astype(bf16)
     sent_end = onward(over, hop_far)
     got_end = along(sent_end, over_middle)
-    near, unused = tie((near, sent_end))
-    near_in = along(near, inward)
     hop_over, near_out, unused = tie((hop_over, near_out, sent_end))
     sent_next = onward(far, hop_over)
     got_next = along(sent_next, middle)
+    near, unused = tie((near, sent_next))
+    near_in = along(near, inward)
     got_end, near_in = tie((got_end, near_in))
     near_sum = onward(mine, got_mine, near_out, near_in)
     map_done, unused = tie((map_done, sent_next))

time: 192 us -> 191 us (level)
    ppermute x9, starting transfers between devices: 12.8 us -> 9.71 us  [across(): return lax.ppermute(value, 'seq', [(s, s ^ 1) for s in range(count)])]
    ppermute x17, starting transfers between devices: 28.8 us -> 30.8 us  [along(): return lax.ppermute(value, 'seq', moves)]
where the time goes in v13:
time: 191 us; the launch traced here: 190 us
  waiting for transfers between devices  95.8 us (50%)
  starting transfers between devices  51.9 us (27%)
  Pallas kernels  18.8 us (10%)
  local copies, waits for them, and re-layouts  12.7 us (7%)
  other arithmetic  5.21 us (3%)
  matrix products  3.67 us (2%)
    ppermute x17, waiting for transfers between devices, along(): return lax.ppermute(value, 'seq', moves)  55.9 us
    ppermute x17, starting transfers between devices, along(): return lax.ppermute(value, 'seq', moves)  30.8 us
    ppermute x9, waiting for transfers between devices, across(): return lax.ppermute(value, 'seq', [(s, s ^ 1) for s in range(count)])  20.5 us
    ppermute x9, starting transfers between devices, across(): return lax.ppermute(value, 'seq', [(s, s ^ 1) for s in range(count)])  9.71 us
    all_to_all x1, waiting for transfers between devices, by_heads(): lax.all_to_all(final.astype(bf16), 'seq', split_axis=0, concat_axis=0, ti...  7.62 us
    pallas_call x1, Pallas kernels, scan(): pl.pallas_call(scan_kernel, in_specs=[SMEM, SMEM] + [VMEM] * (len(sums) +...  7.46 us
    pallas_call x1, Pallas kernels, project(): pl.pallas_call(functools.partial(project_kernel, ranks), in_specs=[SMEM,...  6.42 us
    ppermute x1, waiting for transfers between devices, by_heads(): received = lax.ppermute(sent.astype(bf16), 'tensor', pairs)  6.4 us
  transfers between devices with their start and end apart: 37, of which 16 were waited for; matrix products, arithmetic and copies ran while one was open for 7% of the time, Pallas kernels for 3%

profile of v13, /device:TPU:0, one launch (start us, length us, event | category | flops | bytes accessed | tf_op | source)
XLA Modules:
  0.0 190.0 jit_solution(2938073341664341267)
XLA Ops:
  1.9 3.1 %collective-permute-start = (bf16[32,1024]{1,0:T(8,128)(2,1)S(1)}, bf16[32,1024]{1,0:T(8,128)(2,1)S(1)}, u32[]{:S(2)}, u32[]{:S(2)}) collective-permute-start(bf16[32,1024]{1,0:T(8,128)(2,1)S(1)} %get-tuple-element.59), channel_id=1, source_target_pairs={{0,8},{4,12},{8,0},{12,4},{16,24},{20,28},{24,16},{28,20},{1,9},{5... | collective-permute-start | bytes 196616 | tf_op jit(solution)/shard_map/ppermute | solution.py:570
  4.9 2.6 %collective-permute-start.1 = (bf16[32,1024]{1,0:T(8,128)(2,1)S(1)}, bf16[32,1024]{1,0:T(8,128)(2,1)S(1)}, u32[]{:S(2)}, u32[]{:S(2)}) collective-permute-start(bf16[32,1024]{1,0:T(8,128)(2,1)S(1)} %get-tuple-element.61), channel_id=1, source_target_pairs={{0,16},{4,20},{8,24},{12,28},{16,0},{20,4},{24,8},{28,12},{1,17},{... | collective-permute-start | bytes 196616 | tf_op jit(solution)/shard_map/ppermute | solution.py:570
  7.5 2.1 %constant_dynamic-slice_fusion.2 = (bf16[512,1,2,128]{3,2,1,0:T(2,128)(2,1)S(1)}, bf16[512,1,2,128]{3,2,1,0:T(2,128)(2,1)}) fusion(bf16[512,2,2,128]{3,2,1,0:T(2,128)(2,1)} %param.18, s32[]{:T(128)S(6)} %select_n.132, s32[]{:T(128)S(6)} %select_n.129), kind=kLoop, calls=%fused_computation.57 | loop fusion | bytes 1048584 | tf_op jit(solution)/shard_map/jit(dynamic_index_in_dim)/dynamic_slice | solution.py:566
  10.4 1.7 collective-permute-start.11
  12.6 1.9 constant_dynamic-slice_fusion.6
  17.5 1.6 collective-permute-start.4
  20.5 5.8 %collective-permute-done.6.refs_4_ = bf16[4,32,1024]{2,1,0:T(8,128)(2,1)} collective-permute-done((bf16[4,32,1024]{2,1,0:T(8,128)(2,1)S(1)}, bf16[4,32,1024]{2,1,0:T(8,128)(2,1)}, u32[]{:S(2)}, u32[]{:S(2)}) %collective-permute-start.6) | collective-permute-done | bytes 262176 | tf_op jit(solution)/shard_map/ppermute | solution.py:573
  26.3 1.7 collective-permute-start.8
  28.7 4.4 %collective-permute-done.8.refs_6_ = bf16[4,32,1024]{2,1,0:T(8,128)(2,1)} collective-permute-done((bf16[4,32,1024]{2,1,0:T(8,128)(2,1)}, bf16[4,32,1024]{2,1,0:T(8,128)(2,1)}, u32[]{:S(2)}, u32[]{:S(2)}) %collective-permute-start.8) | collective-permute-done | bytes 262176 | tf_op jit(solution)/shard_map/ppermute | solution.py:637
  33.8 2.0 %collective-permute-done.10.refs_9_ = bf16[512,512]{1,0:T(8,128)(2,1)} collective-permute-done((bf16[512,512]{1,0:T(8,128)(2,1)}, bf16[512,512]{1,0:T(8,128)(2,1)}, u32[]{:S(2)}, u32[]{:S(2)}) %collective-permute-start.10) | collective-permute-done | bytes 524320 | tf_op jit(solution)/shard_map/ppermute | solution.py:573
  35.8 1.6 copy-done.5
  37.4 6.4 %project.1 = (bf16[1056,256]{1,0:T(8,128)(2,1)}, bf16[1056,256]{1,0:T(8,128)(2,1)}, bf16[1056,256]{1,0:T(8,128)(2,1)S(1)}, bf16[1056,256]{1,0:T(8,128)(2,1)S(1)}...) custom-call(s32[7]{0:T(128)S(1)} %stack.43.place_ref, ...), custom_call_target="tpu_custom_call" | custom-call | flops 2684354560 | bytes 4194304 | tf_op jit(solution)/shard_map/project/pallas_call | solution.py:301
  43.8 1.6 collective-permute-start.14
  45.4 2.5 %collective-permute-start.20 = (bf16[1024,256]{1,0:T(8,128)(2,1)S(1)}, bf16[1024,256]{1,0:T(8,128)(2,1)S(1)}, u32[]{:S(2)}, u32[]{:S(2)}) collective-permute-start(bf16[1024,256]{1,0:T(8,128)(2,1)S(1)} %get-tuple-element.45), channel_id=1, source_target_pairs={{0,8},{4,12},{24,16},{28,20},{1,9},{5,13},{25,17},{29,21},{2,10},{... | collective-permute-start | bytes 1572872 | tf_op jit(solution)/shard_map/ppermute | solution.py:570
  47.9 2.1 %collective-permute-start.16 = (bf16[1056,256]{1,0:T(8,128)(2,1)}, bf16[1056,256]{1,0:T(8,128)(2,1)}, u32[]{:S(2)}, u32[]{:S(2)}) collective-permute-start(bf16[1056,256]{1,0:T(8,128)(2,1)} %get-tuple-element.39.refs_0_), channel_id=1, source_target_pairs={{0,8},{4,12},{24,16},{28,20},{1,9},{5,13},{25,17},{29,21},{2,10},{... | collective-permute-start | bytes 1622024 | tf_op jit(solution)/shard_map/ppermute | solution.py:570
  50.0 2.1 %collective-permute-start.13 = (bf16[1056,256]{1,0:T(8,128)(2,1)}, bf16[1056,256]{1,0:T(8,128)(2,1)}, u32[]{:S(2)}, u32[]{:S(2)}) collective-permute-start(bf16[1056,256]{1,0:T(8,128)(2,1)} %get-tuple-element.36.refs_0_), channel_id=1, source_target_pairs={{0,8},{4,12},{24,16},{28,20},{1,9},{5,13},{25,17},{29,21},{2,10},{... | collective-permute-start | bytes 1622024 | tf_op jit(solution)/shard_map/ppermute | solution.py:570
  52.1 5.2 %collective-permute-done.14.refs_1_ = bf16[1056,256]{1,0:T(8,128)(2,1)S(1)} collective-permute-done((bf16[1056,256]{1,0:T(8,128)(2,1)S(1)}, bf16[1056,256]{1,0:T(8,128)(2,1)S(1)}, u32[]{:S(2)}, u32[]{:S(2)}) %collective-permute-start.14) | collective-permute-done | bytes 540704 | tf_op jit(solution)/shard_map/ppermute | solution.py:573
  62.2 9.8 %collective-permute-done.16.refs_1_ = bf16[1056,256]{1,0:T(8,128)(2,1)} collective-permute-done((bf16[1056,256]{1,0:T(8,128)(2,1)}, bf16[1056,256]{1,0:T(8,128)(2,1)}, u32[]{:S(2)}, u32[]{:S(2)}) %collective-permute-start.16) | collective-permute-done | bytes 540704 | tf_op jit(solution)/shard_map/ppermute | solution.py:570
  74.6 7.1 %collective-permute-done.13.refs_1_ = bf16[1056,256]{1,0:T(8,128)(2,1)} collective-permute-done((bf16[1056,256]{1,0:T(8,128)(2,1)}, bf16[1056,256]{1,0:T(8,128)(2,1)}, u32[]{:S(2)}, u32[]{:S(2)}) %collective-permute-start.13) | collective-permute-done | bytes 540704 | tf_op jit(solution)/shard_map/ppermute | solution.py:570
  83.8 7.3 %collective-permute-start.18 = (bf16[1056,256]{1,0:T(8,128)(2,1)}, bf16[1056,256]{1,0:T(8,128)(2,1)S(1)}, u32[]{:S(2)}, u32[]{:S(2)}) collective-permute-start(bf16[1056,256]{1,0:T(8,128)(2,1)} %onward.4), channel_id=1, source_target_pairs={{0,8},{4,12},{24,16},{28,20},{1,9},{5,13},{25,17},{29,21},{2,10},{... | collective-permute-start | bytes 1622024 | tf_op jit(solution)/shard_map/ppermute | solution.py:570
  92.8 8.4 %collective-permute-done.18.refs_3_ = bf16[1056,256]{1,0:T(8,128)(2,1)S(1)} collective-permute-done((bf16[1056,256]{1,0:T(8,128)(2,1)}, bf16[1056,256]{1,0:T(8,128)(2,1)S(1)}, u32[]{:S(2)}, u32[]{:S(2)}) %collective-permute-start.18) | collective-permute-done | bytes 540704 | tf_op jit(solution)/shard_map/ppermute | solution.py:570
  102.5 2.3 %collective-permute-done.22.refs_5_ = bf16[1024,256]{1,0:T(8,128)(2,1)S(1)} collective-permute-done((bf16[1024,256]{1,0:T(8,128)(2,1)S(1)}, bf16[1024,256]{1,0:T(8,128)(2,1)S(1)}, u32[]{:S(2)}, u32[]{:S(2)}) %collective-permute-start.22) | collective-permute-done | bytes 524320 | tf_op jit(solution)/shard_map/ppermute | solution.py:570
  105.9 7.5 %scan.1 = bf16[1040,256]{1,0:T(8,128)(2,1)S(1)} custom-call(s32[7]{0:T(128)S(1)} %stack.43.place_ref, f32[1]{0:T(128)} %bitcast.3.scale_ref, bf16[1056,256]{1,0:T(8,128)(2,1)S(1)} %onward.7.refs_0_, bf16[1056,256]{1,0:T(8,128)(2,1)S(1)} %collective-permute-done.17.refs_1_, bf16[1056,256]{1,0:T(8,128)(2,1)S(1)} %collective-permute-done.19.refs_2_, ...), custom_call_target="tpu_custom_call" | custom-call | flops 268435456 | bytes 2097152 | tf_op jit(solution)/shard_map/scan/pallas_call | solution.py:515
  117.5 8.7 %collective-permute-done.26 = bf16[1040,256]{1,0:T(8,128)(2,1)S(1)} collective-permute-done((bf16[1040,256]{1,0:T(8,128)(2,1)S(1)}, bf16[1040,256]{1,0:T(8,128)(2,1)S(1)}, u32[]{:S(2)}, u32[]{:S(2)}) %collective-permute-start.26) | collective-permute-done | bytes 532512 | tf_op jit(solution)/shard_map/ppermute | solution.py:570
  127.9 9.2 %collective-permute-done.24 = bf16[1040,256]{1,0:T(8,128)(2,1)S(1)} collective-permute-done((bf16[1040,256]{1,0:T(8,128)(2,1)}, bf16[1040,256]{1,0:T(8,128)(2,1)S(1)}, u32[]{:S(2)}, u32[]{:S(2)}) %collective-permute-start.24) | collective-permute-done | bytes 532512 | tf_op jit(solution)/shard_map/ppermute | solution.py:570
  140.5 9.6 %collective-permute-done.28 = bf16[1040,256]{1,0:T(8,128)(2,1)S(1)} collective-permute-done((bf16[1040,256]{1,0:T(8,128)(2,1)S(1)}, bf16[1040,256]{1,0:T(8,128)(2,1)S(1)}, u32[]{:S(2)}, u32[]{:S(2)}) %collective-permute-start.28) | collective-permute-done | bytes 532512 | tf_op jit(solution)/shard_map/ppermute | solution.py:570
  150.1 1.6 collective-permute-start.31
  153.1 7.5 %collective-permute-done.31 = bf16[1040,256]{1,0:T(8,128)(2,1)S(1)} collective-permute-done((bf16[1040,256]{1,0:T(8,128)(2,1)S(1)}, bf16[1040,256]{1,0:T(8,128)(2,1)S(1)}, u32[]{:S(2)}, u32[]{:S(2)}) %collective-permute-start.31) | collective-permute-done | bytes 532512 | tf_op jit(solution)/shard_map/ppermute | solution.py:573
  162.9 1.5 collective-permute-start.35
  167.8 6.4 %collective-permute-done.33 = bf16[256,512]{1,0:T(8,128)(2,1)S(1)} collective-permute-done((bf16[256,512]{1,0:T(8,128)(2,1)}, bf16[256,512]{1,0:T(8,128)(2,1)S(1)}, u32[]{:S(2)}, u32[]{:S(2)}) %collective-permute-start.33) | collective-permute-done | bytes 262176 | tf_op jit(solution)/shard_map/ppermute | solution.py:741
  176.1 4.9 %all-to-all-start = ((bf16[8,32,512]{2,1,0:T(8,128)(2,1)}), bf16[8,32,512]{2,1,0:T(8,128)(2,1)S(1)}, u32[]{:S(2)}, u32[]{:S(2)}) async-start(bf16[8,32,512]{2,1,0:T(8,128)(2,1)} %multiply_convert_fusion.1), calls=%async_computation | async-start | bytes 524288 | tf_op jit(solution)/shard_map/all_to_all | solution.py:747
  181.6 7.6 %all-to-all-done = bf16[8,32,512]{2,1,0:T(8,128)(2,1)S(1)} async-done(((bf16[8,32,512]{2,1,0:T(8,128)(2,1)}), bf16[8,32,512]{2,1,0:T(8,128)(2,1)S(1)}, u32[]{:S(2)}, u32[]{:S(2)}) %all-to-all-start) | async-done | bytes 262176 | tf_op jit(solution)/shard_map/all_to_all | solution.py:747
  (143 shorter events, 40.3 us)
Async XLA Ops:
  1.9 12.6 %collective-permute-start = (bf16[32,1024]{1,0:T(8,128)(2,1)S(1)}, bf16[32,1024]{1,0:T(8,128)(2,1)S(1)}, u32[]{:S(2)}, u32[]{:S(2)}) collective-permute-start(bf16[32,1024]{1,0:T(8,128)(2,1)S(1)} %get-tuple-element.59), channel_id=1, source_target_pairs={{0,8},{4,12},{8,0},{12,4},{16,24},{20,28},{24,16},{28,20},{1,9},{5... | collective-permute-start | bytes 196616 | tf_op jit(solution)/shard_map/ppermute | solution.py:570
  4.9 9.5 %collective-permute-start.1 = (bf16[32,1024]{1,0:T(8,128)(2,1)S(1)}, bf16[32,1024]{1,0:T(8,128)(2,1)S(1)}, u32[]{:S(2)}, u32[]{:S(2)}) collective-permute-start(bf16[32,1024]{1,0:T(8,128)(2,1)S(1)} %get-tuple-element.61), channel_id=1, source_target_pairs={{0,16},{4,20},{8,24},{12,28},{16,0},{20,4},{24,8},{28,12},{1,17},{... | collective-permute-start | bytes 196616 | tf_op jit(solution)/shard_map/ppermute | solution.py:570
  7.5 6.9 %collective-permute-start.2 = (bf16[32,1024]{1,0:T(8,128)(2,1)S(1)}, bf16[32,1024]{1,0:T(8,128)(2,1)S(1)}, u32[]{:S(2)}, u32[]{:S(2)}) collective-permute-start(bf16[32,1024]{1,0:T(8,128)(2,1)S(1)} %get-tuple-element.60), channel_id=1, source_target_pairs={{0,24},{4,28},{8,16},{12,20},{16,8},{20,12},{24,0},{28,4},{1,25},{... | collective-permute-start | bytes 196616 | tf_op jit(solution)/shard_map/ppermute | solution.py:570
  10.4 17.6 %collective-permute-start.11 = (bf16[576,256]{1,0:T(8,128)(2,1)}, bf16[576,256]{1,0:T(8,128)(2,1)S(1)}, u32[]{:S(2)}, u32[]{:S(2)}) collective-permute-start(bf16[576,256]{1,0:T(8,128)(2,1)} %pad_maximum_fusion), channel_id=1, source_target_pairs={{0,4},{4,0},{8,12},{12,8},{16,20},{20,16},{24,28},{28,24},{1,5},{5... | collective-permute-start | bytes 884744 | tf_op jit(solution)/shard_map/ppermute | solution.py:573
  14.5 11.8 %collective-permute-start.6 = (bf16[4,32,1024]{2,1,0:T(8,128)(2,1)S(1)}, bf16[4,32,1024]{2,1,0:T(8,128)(2,1)}, u32[]{:S(2)}, u32[]{:S(2)}) collective-permute-start(bf16[4,32,1024]{2,1,0:T(8,128)(2,1)S(1)} %pad_maximum_fusion.1.refs_0_), channel_id=1, source_target_pairs={{0,4},{4,0},{8,12},{12,8},{16,20},{20,16},{24,28},{28,24},{1,5},{5... | collective-permute-start | bytes 786440 | tf_op jit(solution)/shard_map/ppermute | solution.py:573
  17.5 11.0 %collective-permute-start.4 = (bf16[4,32,1024]{2,1,0:T(8,128)(2,1)S(1)}, bf16[4,32,1024]{2,1,0:T(8,128)(2,1)}, u32[]{:S(2)}, u32[]{:S(2)}) collective-permute-start(bf16[4,32,1024]{2,1,0:T(8,128)(2,1)S(1)} %pad_maximum_fusion.1.refs_0_), channel_id=1, source_target_pairs={{0,2},{1,3},{2,0},{3,1},{4,6},{5,7},{6,4},{7,5},{8,10},{9,11},{10,... | collective-permute-start | bytes 786440 | tf_op jit(solution)/shard_map/ppermute | solution.py:637
  19.1 16.7 %collective-permute-start.10 = (bf16[512,512]{1,0:T(8,128)(2,1)}, bf16[512,512]{1,0:T(8,128)(2,1)}, u32[]{:S(2)}, u32[]{:S(2)}) collective-permute-start(bf16[512,512]{1,0:T(8,128)(2,1)} %constant_dynamic-slice_fusion.6), channel_id=1, source_target_pairs={{0,4},{4,0},{8,12},{12,8},{16,20},{20,16},{24,28},{28,24},{1,5},{5... | collective-permute-start | bytes 1572872 | tf_op jit(solution)/shard_map/ppermute | solution.py:573
  26.3 6.7 %collective-permute-start.8 = (bf16[4,32,1024]{2,1,0:T(8,128)(2,1)}, bf16[4,32,1024]{2,1,0:T(8,128)(2,1)}, u32[]{:S(2)}, u32[]{:S(2)}) collective-permute-start(bf16[4,32,1024]{2,1,0:T(8,128)(2,1)} %collective-permute-done.6.refs_4_), channel_id=1, source_target_pairs={{0,2},{1,3},{2,0},{3,1},{4,6},{5,7},{6,4},{7,5},{8,10},{9,11},{10,... | collective-permute-start | bytes 786440 | tf_op jit(solution)/shard_map/ppermute | solution.py:637
  28.1 5.7 %collective-permute-start.3 = (bf16[4,32,1024]{2,1,0:T(8,128)(2,1)S(1)}, bf16[4,32,1024]{2,1,0:T(8,128)(2,1)}, u32[]{:S(2)}, u32[]{:S(2)}) collective-permute-start(bf16[4,32,1024]{2,1,0:T(8,128)(2,1)S(1)} %pad_maximum_fusion.1.refs_0_), channel_id=1, source_target_pairs={{0,1},{1,0},{2,3},{3,2},{4,5},{5,4},{6,7},{7,6},{8,9},{9,8},{10,11... | collective-permute-start | bytes 786440 | tf_op jit(solution)/shard_map/ppermute | solution.py:637
  28.1 5.7 %collective-permute-start.7 = (bf16[4,32,1024]{2,1,0:T(8,128)(2,1)}, bf16[4,32,1024]{2,1,0:T(8,128)(2,1)}, u32[]{:S(2)}, u32[]{:S(2)}) collective-permute-start(bf16[4,32,1024]{2,1,0:T(8,128)(2,1)} %collective-permute-done.6.refs_4_), channel_id=1, source_target_pairs={{0,1},{1,0},{2,3},{3,2},{4,5},{5,4},{6,7},{7,6},{8,9},{9,8},{10,11... | collective-permute-start | bytes 786440 | tf_op jit(solution)/shard_map/ppermute | solution.py:637
  28.6 5.2 %collective-permute-start.5 = (bf16[4,32,1024]{2,1,0:T(8,128)(2,1)}, bf16[4,32,1024]{2,1,0:T(8,128)(2,1)}, u32[]{:S(2)}, u32[]{:S(2)}) collective-permute-start(bf16[4,32,1024]{2,1,0:T(8,128)(2,1)} %collective-permute-done.4.refs_2_), channel_id=1, source_target_pairs={{0,1},{1,0},{2,3},{3,2},{4,5},{5,4},{6,7},{7,6},{8,9},{9,8},{10,11... | collective-permute-start | bytes 786440 | tf_op jit(solution)/shard_map/ppermute | solution.py:637
  43.8 13.5 %collective-permute-start.14 = (bf16[1056,256]{1,0:T(8,128)(2,1)S(1)}, bf16[1056,256]{1,0:T(8,128)(2,1)S(1)}, u32[]{:S(2)}, u32[]{:S(2)}) collective-permute-start(bf16[1056,256]{1,0:T(8,128)(2,1)S(1)} %get-tuple-element.38), channel_id=1, source_target_pairs={{0,4},{4,0},{8,12},{12,8},{16,20},{20,16},{24,28},{28,24},{1,5},{5... | collective-permute-start | bytes 1622024 | tf_op jit(solution)/shard_map/ppermute | solution.py:573
  45.4 14.9 %collective-permute-start.20 = (bf16[1024,256]{1,0:T(8,128)(2,1)S(1)}, bf16[1024,256]{1,0:T(8,128)(2,1)S(1)}, u32[]{:S(2)}, u32[]{:S(2)}) collective-permute-start(bf16[1024,256]{1,0:T(8,128)(2,1)S(1)} %get-tuple-element.45), channel_id=1, source_target_pairs={{0,8},{4,12},{24,16},{28,20},{1,9},{5,13},{25,17},{29,21},{2,10},{... | collective-permute-start | bytes 1572872 | tf_op jit(solution)/shard_map/ppermute | solution.py:570
  47.9 24.0 %collective-permute-start.16 = (bf16[1056,256]{1,0:T(8,128)(2,1)}, bf16[1056,256]{1,0:T(8,128)(2,1)}, u32[]{:S(2)}, u32[]{:S(2)}) collective-permute-start(bf16[1056,256]{1,0:T(8,128)(2,1)} %get-tuple-element.39.refs_0_), channel_id=1, source_target_pairs={{0,8},{4,12},{24,16},{28,20},{1,9},{5,13},{25,17},{29,21},{2,10},{... | collective-permute-start | bytes 1622024 | tf_op jit(solution)/shard_map/ppermute | solution.py:570
  50.0 31.7 %collective-permute-start.13 = (bf16[1056,256]{1,0:T(8,128)(2,1)}, bf16[1056,256]{1,0:T(8,128)(2,1)}, u32[]{:S(2)}, u32[]{:S(2)}) collective-permute-start(bf16[1056,256]{1,0:T(8,128)(2,1)} %get-tuple-element.36.refs_0_), channel_id=1, source_target_pairs={{0,8},{4,12},{24,16},{28,20},{1,9},{5,13},{25,17},{29,21},{2,10},{... | collective-permute-start | bytes 1622024 | tf_op jit(solution)/shard_map/ppermute | solution.py:570
  58.2 23.5 %collective-permute-start.15 = (bf16[1056,256]{1,0:T(8,128)(2,1)}, bf16[1056,256]{1,0:T(8,128)(2,1)}, u32[]{:S(2)}, u32[]{:S(2)}) collective-permute-start(bf16[1056,256]{1,0:T(8,128)(2,1)} %onward.4), channel_id=1, source_target_pairs={{8,0},{12,4},{16,24},{20,28},{9,1},{13,5},{17,25},{21,29},{10,2},{... | collective-permute-start | bytes 1622024 | tf_op jit(solution)/shard_map/ppermute | solution.py:570
  60.4 30.7 %collective-permute-start.21 = (bf16[1024,256]{1,0:T(8,128)(2,1)S(1)}, bf16[1024,256]{1,0:T(8,128)(2,1)S(1)}, u32[]{:S(2)}, u32[]{:S(2)}) collective-permute-start(bf16[1024,256]{1,0:T(8,128)(2,1)S(1)} %add_convert_fusion.1.refs_3_), channel_id=1, source_target_pairs={{8,16},{12,20},{16,8},{20,12},{9,17},{13,21},{17,9},{21,13},{10,18... | collective-permute-start | bytes 1572872 | tf_op jit(solution)/shard_map/ppermute | solution.py:570
  61.1 40.1 %collective-permute-start.12 = (bf16[1056,256]{1,0:T(8,128)(2,1)}, bf16[1056,256]{1,0:T(8,128)(2,1)S(1)}, u32[]{:S(2)}, u32[]{:S(2)}) collective-permute-start(bf16[1056,256]{1,0:T(8,128)(2,1)} %copy-done.7), channel_id=1, source_target_pairs={{0,4},{4,0},{8,12},{12,8},{16,20},{20,16},{24,28},{28,24},{1,5},{5... | collective-permute-start | bytes 1622024 | tf_op jit(solution)/shard_map/ppermute | solution.py:573
  73.3 19.5 %collective-permute-start.17 = (bf16[1056,256]{1,0:T(8,128)(2,1)S(1)}, bf16[1056,256]{1,0:T(8,128)(2,1)S(1)}, u32[]{:S(2)}, u32[]{:S(2)}) collective-permute-start(bf16[1056,256]{1,0:T(8,128)(2,1)S(1)} %onward.5), channel_id=1, source_target_pairs={{8,24},{12,28},{16,0},{20,4},{9,25},{13,29},{17,1},{21,5},{10,26},... | collective-permute-start | bytes 1622024 | tf_op jit(solution)/shard_map/ppermute | solution.py:570
  83.1 21.8 %collective-permute-start.19 = (bf16[1056,256]{1,0:T(8,128)(2,1)S(1)}, bf16[1056,256]{1,0:T(8,128)(2,1)S(1)}, u32[]{:S(2)}, u32[]{:S(2)}) collective-permute-start(bf16[1056,256]{1,0:T(8,128)(2,1)S(1)} %onward.6), channel_id=1, source_target_pairs={{8,16},{12,20},{16,8},{20,12},{9,17},{13,21},{17,9},{21,13},{10,18... | collective-permute-start | bytes 1622024 | tf_op jit(solution)/shard_map/ppermute | solution.py:570
  83.8 17.4 %collective-permute-start.18 = (bf16[1056,256]{1,0:T(8,128)(2,1)}, bf16[1056,256]{1,0:T(8,128)(2,1)S(1)}, u32[]{:S(2)}, u32[]{:S(2)}) collective-permute-start(bf16[1056,256]{1,0:T(8,128)(2,1)} %onward.4), channel_id=1, source_target_pairs={{0,8},{4,12},{24,16},{28,20},{1,9},{5,13},{25,17},{29,21},{2,10},{... | collective-permute-start | bytes 1622024 | tf_op jit(solution)/shard_map/ppermute | solution.py:570
  91.3 13.6 %collective-permute-start.22 = (bf16[1024,256]{1,0:T(8,128)(2,1)S(1)}, bf16[1024,256]{1,0:T(8,128)(2,1)S(1)}, u32[]{:S(2)}, u32[]{:S(2)}) collective-permute-start(bf16[1024,256]{1,0:T(8,128)(2,1)S(1)} %multiply_convert_fusion), channel_id=1, source_target_pairs={{8,0},{12,4},{16,24},{20,28},{9,1},{13,5},{17,25},{21,29},{10,2},{... | collective-permute-start | bytes 1572872 | tf_op jit(solution)/shard_map/ppermute | solution.py:570
  114.8 11.4 %collective-permute-start.26 = (bf16[1040,256]{1,0:T(8,128)(2,1)S(1)}, bf16[1040,256]{1,0:T(8,128)(2,1)S(1)}, u32[]{:S(2)}, u32[]{:S(2)}) collective-permute-start(bf16[1040,256]{1,0:T(8,128)(2,1)S(1)} %scan.1), channel_id=1, source_target_pairs={{0,8},{4,12},{8,0},{12,4},{16,24},{20,28},{24,16},{28,20},{1,9},{5... | collective-permute-start | bytes 1597448 | tf_op jit(solution)/shard_map/ppermute | solution.py:570
  115.7 21.5 %collective-permute-start.25 = (bf16[1040,256]{1,0:T(8,128)(2,1)S(1)}, bf16[1040,256]{1,0:T(8,128)(2,1)S(1)}, u32[]{:S(2)}, u32[]{:S(2)}) collective-permute-start(bf16[1040,256]{1,0:T(8,128)(2,1)S(1)} %scan.1), channel_id=1, source_target_pairs={{0,4},{4,0},{8,12},{12,8},{16,20},{20,16},{24,28},{28,24},{1,5},{5... | collective-permute-start | bytes 1597448 | tf_op jit(solution)/shard_map/ppermute | solution.py:573
  116.2 20.9 %collective-permute-start.24 = (bf16[1040,256]{1,0:T(8,128)(2,1)}, bf16[1040,256]{1,0:T(8,128)(2,1)S(1)}, u32[]{:S(2)}, u32[]{:S(2)}) collective-permute-start(bf16[1040,256]{1,0:T(8,128)(2,1)} %collective-permute-done.23), channel_id=1, source_target_pairs={{8,0},{12,4},{16,24},{20,28},{9,1},{13,5},{17,25},{21,29},{10,2},{... | collective-permute-start | bytes 1597448 | tf_op jit(solution)/shard_map/ppermute | solution.py:570
  126.2 12.1 %collective-permute-start.27 = (bf16[1040,256]{1,0:T(8,128)(2,1)S(1)}, bf16[1040,256]{1,0:T(8,128)(2,1)S(1)}, u32[]{:S(2)}, u32[]{:S(2)}) collective-permute-start(bf16[1040,256]{1,0:T(8,128)(2,1)S(1)} %collective-permute-done.26), channel_id=1, source_target_pairs={{8,16},{12,20},{16,8},{20,12},{9,17},{13,21},{17,9},{21,13},{10,18... | collective-permute-start | bytes 1597448 | tf_op jit(solution)/shard_map/ppermute | solution.py:570
  126.9 23.2 %collective-permute-start.29 = (bf16[1040,256]{1,0:T(8,128)(2,1)S(1)}, bf16[1040,256]{1,0:T(8,128)(2,1)S(1)}, u32[]{:S(2)}, u32[]{:S(2)}) collective-permute-start(bf16[1040,256]{1,0:T(8,128)(2,1)S(1)} %collective-permute-done.26), channel_id=1, source_target_pairs={{0,4},{4,0},{8,12},{12,8},{16,20},{20,16},{24,28},{28,24},{1,5},{5... | collective-permute-start | bytes 1597448 | tf_op jit(solution)/shard_map/ppermute | solution.py:573
  137.2 14.5 %collective-permute-start.30 = (bf16[1040,256]{1,0:T(8,128)(2,1)S(1)}, bf16[1040,256]{1,0:T(8,128)(2,1)S(1)}, u32[]{:S(2)}, u32[]{:S(2)}) collective-permute-start(bf16[1040,256]{1,0:T(8,128)(2,1)S(1)} %broadcast_select_fusion.1), channel_id=1, source_target_pairs={{0,4},{4,0},{8,12},{12,8},{16,20},{20,16},{24,28},{28,24},{1,5},{5... | collective-permute-start | bytes 1597448 | tf_op jit(solution)/shard_map/ppermute | solution.py:573
  138.3 11.8 %collective-permute-start.28 = (bf16[1040,256]{1,0:T(8,128)(2,1)S(1)}, bf16[1040,256]{1,0:T(8,128)(2,1)S(1)}, u32[]{:S(2)}, u32[]{:S(2)}) collective-permute-start(bf16[1040,256]{1,0:T(8,128)(2,1)S(1)} %collective-permute-done.27), channel_id=1, source_target_pairs={{8,0},{12,4},{16,24},{20,28},{9,1},{13,5},{17,25},{21,29},{10,2},{... | collective-permute-start | bytes 1597448 | tf_op jit(solution)/shard_map/ppermute | solution.py:570
  150.1 10.4 %collective-permute-start.31 = (bf16[1040,256]{1,0:T(8,128)(2,1)S(1)}, bf16[1040,256]{1,0:T(8,128)(2,1)S(1)}, u32[]{:S(2)}, u32[]{:S(2)}) collective-permute-start(bf16[1040,256]{1,0:T(8,128)(2,1)S(1)} %broadcast_select_fusion), channel_id=1, source_target_pairs={{0,4},{4,0},{8,12},{12,8},{16,20},{20,16},{24,28},{28,24},{1,5},{5... | collective-permute-start | bytes 1597448 | tf_op jit(solution)/shard_map/ppermute | solution.py:573
  165.9 8.3 %collective-permute-start.33 = (bf16[256,512]{1,0:T(8,128)(2,1)}, bf16[256,512]{1,0:T(8,128)(2,1)S(1)}, u32[]{:S(2)}, u32[]{:S(2)}) collective-permute-start(bf16[256,512]{1,0:T(8,128)(2,1)} %add_convert_fusion.2), channel_id=1, source_target_pairs={{0,2},{1,3},{2,0},{3,1},{4,6},{5,7},{6,4},{7,5},{8,10},{9,11},{10,... | collective-permute-start | bytes 786440 | tf_op jit(solution)/shard_map/ppermute | solution.py:741
  176.1 13.2 %all-to-all-start = ((bf16[8,32,512]{2,1,0:T(8,128)(2,1)}), bf16[8,32,512]{2,1,0:T(8,128)(2,1)S(1)}, u32[]{:S(2)}, u32[]{:S(2)}) async-start(bf16[8,32,512]{2,1,0:T(8,128)(2,1)} %multiply_convert_fusion.1), calls=%async_computation | async-start | bytes 524288 | tf_op jit(solution)/shard_map/all_to_all | solution.py:747
  (22 other events, 330.6 us)
